TPU v7x, 256 devices: a whole 4x4x8 slice. The times are simulated.
256 devices in a mesh: pipe: 16 (over z, x_lo), tensor: 4 (over x_hi, core), dp: 4 (over y).
Axes of the slice: x: 4 (x_hi: 2, x_lo: 2; x = x_hi * 2 + x_lo), y: 4, z: 8, core: 2. Of those that a mesh axis runs over, the one named last changes fastest.
Arguments:
- fwd_qkv: bfloat16 [3, 64, 256, 8192], P(None, ('pipe', 'dp'), None, 'tensor'), may hold values from -8 to 8, as said below
- fwd_segments: int32 [64, 256], P(('pipe', 'dp')), may hold values from 0 to 15, as said below
- parked: bfloat16 [3, 64, 256, 8192], P(None, ('pipe', 'dp'), 'tensor'), may hold values from -8 to 8, as said below
- bwd_segments: int32 [64, 256], P(('pipe', 'dp')), may hold values from 0 to 15, as said below
- grad_out: bfloat16 [64, 256, 8192], P(('pipe', 'dp'), None, 'tensor'), may hold values from -6 to 6
- loss_tokens: int32 [64], P(('pipe', 'dp')), may hold values from 1 to 256
Outputs:
- received: bfloat16 [64, 256, 8192], P(('pipe', 'dp'), None, 'tensor')
- grads: bfloat16 [3, 64, 256, 8192], P(None, ('pipe', 'dp'), None, 'tensor')
Inputs may be any that keep to these rules, and one draw needn't show every extreme that they name: `fwd_qkv`: Real-valued. `parked`: Real-valued. `fwd_segments`: in each slot the numbers start at 0, never fall, and change only at positions that are multiples of 16. `bwd_segments`: in each slot the numbers start at 0, never fall, and change only at positions that are multiples of 16.
All inputs are finite; a program needn't handle non-finite values.
Results may differ from a plain program's by a relative error of at most 0.0051.
Values may be sent and summed in bfloat16 or wider, within the bound.
No kernel may reach another device: no remote copies, remote signals or barrier semaphores. Data moves between devices by JAX's collectives and lax.ppermute only.
A program may use at most 128 MiB of HBM per device.

v0:
```python
import jax
import jax.numpy as jnp
from jax import lax
from jax.sharding import PartitionSpec as P

HEAD_DIM = 128
SEQ = 256


def shifted(array, axis, by):
    devices = lax.axis_size(axis)
    return lax.ppermute(array, axis, [(i, (i + by) % devices) for i in range(devices)])


def probabilities(query_heads, key_heads, segment):
    logits = jnp.einsum(
        "qhd,khd->hqk", query_heads, key_heads, preferred_element_type=jnp.float32
    ) * HEAD_DIM ** (-0.5)
    inside = segment[:, None] == segment[None, :]
    logits = jnp.where(inside[None], logits, jnp.float32(-1e30))
    highest = jnp.max(logits, axis=-1, keepdims=True)
    weights = jnp.exp(logits - highest)
    return weights / jnp.sum(weights, axis=-1, keepdims=True)


def split_rows(matrix):
    length = matrix.shape[0]
    return matrix.reshape(length, matrix.shape[1] // HEAD_DIM, HEAD_DIM)


def attend(queries, key_rows, value_rows, segment):
    probs_low = probabilities(split_rows(queries), split_rows(key_rows), segment).astype(
        jnp.bfloat16
    )
    mixed = jnp.einsum(
        "hqk,khd->qhd", probs_low, split_rows(value_rows), preferred_element_type=jnp.float32
    )
    return mixed.reshape(queries.shape).astype(jnp.bfloat16)


def attend_backward(queries, key_rows, value_rows, segment, upstream, factor):
    query_heads = split_rows(queries)
    key_heads = split_rows(key_rows)
    value_heads = split_rows(value_rows)
    upstream_heads = split_rows(upstream)
    stash_probs = probabilities(query_heads, key_heads, segment)
    stash_probs_low = stash_probs.astype(jnp.bfloat16)
    grad_value = jnp.einsum(
        "hqk,qhd->khd", stash_probs_low, upstream_heads, preferred_element_type=jnp.float32
    )
    grad_probs = jnp.einsum(
        "qhd,khd->hqk", upstream_heads, value_heads, preferred_element_type=jnp.float32
    )
    center = jnp.sum(stash_probs * grad_probs, axis=-1, keepdims=True)
    grad_logits = (stash_probs * (grad_probs - center) * HEAD_DIM ** (-0.5)).astype(jnp.bfloat16)
    grad_query = jnp.einsum(
        "hqk,khd->qhd", grad_logits, key_heads, preferred_element_type=jnp.float32
    )
    grad_key = jnp.einsum(
        "hqk,qhd->khd", grad_logits, query_heads, preferred_element_type=jnp.float32
    )
    stacked = jnp.stack([grad_query, grad_key, grad_value]) * factor
    return stacked.reshape(3, queries.shape[0], queries.shape[1]).astype(jnp.bfloat16)


def split_heads(parked_block):
    return lax.all_to_all(parked_block, "tensor", split_axis=3, concat_axis=2, tiled=True)


def fetch(parked_block):
    sections = lax.axis_size("pipe")
    leading = parked_block.shape[0]
    length = parked_block.shape[2]
    columns = parked_block.shape[3]
    pieces = parked_block.reshape(leading, sections, length // sections, columns)
    spread = lax.all_to_all(pieces, "pipe", split_axis=1, concat_axis=1, tiled=True)
    spread = jnp.flip(spread, axis=1)
    returned = lax.all_to_all(spread, "pipe", split_axis=1, concat_axis=1, tiled=True)
    return returned.reshape(leading, 1, length, columns)


def on_device(fwd_qkv, fwd_segments, parked, bwd_segments, grad_out, loss_tokens):
    forward_out = attend(fwd_qkv[0, 0], fwd_qkv[1, 0], fwd_qkv[2, 0], fwd_segments[0])
    received = shifted(forward_out[None], "pipe", 1)
    upstream = shifted(grad_out, "pipe", -1)
    token_total = lax.psum(jnp.sum(loss_tokens.astype(jnp.float32)), "dp")
    factor = jnp.float32(lax.axis_size("dp") * SEQ) / token_total
    stash = split_heads(fetch(parked))
    grads = attend_backward(
        stash[0, 0], stash[1, 0], stash[2, 0], bwd_segments[0], upstream[0], factor
    )
    return (received, grads[:, None])


def solution(mesh):
    placed = (
        P(None, ("pipe", "dp"), None, "tensor"),
        P(("pipe", "dp"), None),
        P(None, ("pipe", "dp"), "tensor", None),
        P(("pipe", "dp"), None),
        P(("pipe", "dp"), None, "tensor"),
        P(("pipe", "dp")),
    )
    return jax.shard_map(
        on_device,
        mesh=mesh,
        in_specs=placed,
        out_specs=(P(("pipe", "dp"), None, "tensor"), P(None, ("pipe", "dp"), None, "tensor")),
        check_vma=False,
    )
```

profile of v0, /device:TPU:1, one launch (start us, length us, event | category | flops | bytes accessed | tf_op | source)
XLA Modules:
  0.0 352.0 jit_solution(13992768372876619363)
XLA Ops:
  0.6 4.0 %reshape.149 = bf16[3,16,4,8192]{3,2,1,0:T(4,128)(2,1)S(1)} reshape(bf16[3,1,64,8192]{3,2,1,0:T(8,128)(2,1)} %param.8) | data formatting | bytes 6291456 | tf_op jit(solution)/shard_map/reshape | solution.py:75
  4.7 1.3 copy.94
  6.0 81.6 %all_to_all.25 = bf16[3,16,4,8192]{3,2,0,1:T(4,128)(2,1)S(1)} all-to-all(bf16[3,16,4,8192]{3,2,0,1:T(4,128)(2,1)S(1)} %copy.94), channel_id=1, replica_groups=mesh['pipe'=16,'tensor'=4,'dp'=4] {'pipe'}, dimensions={1} | all-to-all | bytes 6291456 | tf_op jit(solution)/shard_map/all_to_all | solution.py:76
  87.6 3.0 rev.4
  90.6 76.7 %all_to_all.26 = bf16[3,16,4,8192]{3,2,0,1:T(4,128)(2,1)S(1)} all-to-all(bf16[3,16,4,8192]{3,2,0,1:T(4,128)(2,1)} %rev.4), channel_id=1, replica_groups=mesh['pipe'=16,'tensor'=4,'dp'=4] {'pipe'}, dimensions={1} | all-to-all | bytes 6291456 | tf_op jit(solution)/shard_map/all_to_all | solution.py:78
  167.3 1.3 copy.95
  168.6 2.9 reshape.150
  171.6 11.2 %copy.96 = bf16[3,1,64,8192]{2,0,1,3:T(4,128)(2,1)} copy(bf16[3,1,64,8192]{3,2,0,1:T(8,128)(2,1)} %reshape.150) | data formatting | bytes 6291456 | tf_op jit(solution)/shard_map/reshape | solution.py:79
  182.8 8.6 %reshape.153 = bf16[4,2,196608]{2,1,0:T(2,128)(2,1)} reshape(bf16[8192,1,3,64]{3,2,1,0:T(4,128)(2,1)} %bitcast.46) | data formatting | bytes 6291456
  191.4 6.5 %all-to-all-start.2 = ((bf16[4,2,196608]{2,1,0:T(2,128)(2,1)}), bf16[4,2,196608]{2,1,0:T(2,128)(2,1)S(1)}, u32[]{:S(2)}, u32[]{:S(2)}) async-start(bf16[4,2,196608]{2,1,0:T(2,128)(2,1)} %reshape.153), calls=%async_computation.2 | async-start | bytes 6291456 | tf_op jit(solution)/shard_map/all_to_all | solution.py:67
  197.9 3.6 %fusion.42 = (bf16[1,1,256,2048]{3,2,1,0:T(8,128)(2,1)}, bf16[1,1,256,2048]{3,2,1,0:T(8,128)(2,1)}, bf16[1,1,256,2048]{3,2,1,0:T(8,128)(2,1)}) fusion(bf16[3,1,256,2048]{3,2,1,0:T(8,128)(2,1)} %param.6), kind=kLoop, calls=%fused_computation.45 | loop fusion | bytes 6291456 | tf_op jit(solution)/shard_map/slice | solution.py:83
  201.6 0.0 copy-start.2
  201.6 2.3 copy.122
  203.9 2.3 copy.123
  206.1 2.3 copy.91
  208.4 0.0 copy-done.2
  208.4 0.1 broadcast_compare_fusion.1
  208.5 5.0 %fusion.43 = (f32[16,256]{1,0:T(8,128)S(1)}, f32[16,256,256]{1,2,0:T(8,128)}) fusion(pred[256,256]{0,1:T(8,128)(4,1)S(1)} %broadcast_compare_fusion.1, bf16[256,16,128]{0,2,1:T(8,128)(2,1)} %bitcast.54, bf16[256,16,128]{0,2,1:T(8,128)(2,1)} %bitcast.56), kind=kOutput, calls=%fused_computation.46 | convolution fusion | flops 272630016 | bytes 6373376 | tf_op jit(solution)/shard_map/sub | solution.py:22
  213.5 4.0 %fusion.26 = bf16[16,256,128]{1,2,0:T(8,128)(2,1)} fusion(bf16[256,16,128]{0,2,1:T(8,128)(2,1)} %bitcast.55, f32[16,256,256]{1,2,0:T(8,128)} %get-tuple-element.9, f32[16,256]{1,0:T(8,128)S(1)} %get-tuple-element.8), kind=kOutput, calls=%fused_computation.29 | convolution fusion | flops 271056896 | bytes 6307840 | tf_op jit(solution)/shard_map/hqk,khd->qhd/dot_general | solution.py:35
  217.5 0.0 copy-start.3
  217.5 2.3 copy.93
  219.7 0.0 collective-permute-start
  219.8 2.3 copy.102
  222.1 3.6 %collective-permute-start.1 = (bf16[1,256,2048]{1,2,0:T(8,128)(2,1)}, bf16[1,256,2048]{1,2,0:T(8,128)(2,1)}, u32[]{:S(2)}, u32[]{:S(2)}) collective-permute-start(bf16[1,256,2048]{1,2,0:T(8,128)(2,1)} %copy.102), channel_id=1, source_target_pairs={{0,240},{16,0},{32,16},{48,32},{64,48},{80,64},{96,80},{112,96},{1... | collective-permute-start | bytes 3145736 | tf_op jit(solution)/shard_map/ppermute | solution.py:12
  226.3 11.0 %psum.7 = f32[]{:T(128)} all-reduce(f32[]{:T(128)} %bitcast.16), channel_id=1, replica_groups=mesh['pipe'=16,'tensor'=4,'dp'=4] {'dp'}, use_global_device_ids=true, to_apply=%region_5.6 | all-reduce | flops 1 | bytes 8 | tf_op jit(solution)/shard_map/psum | solution.py:86
  238.0 0.0 copy-done.3
  238.0 0.1 broadcast_compare_fusion
  238.1 39.1 %collective-permute-done = bf16[1,256,2048]{2,1,0:T(8,128)(2,1)} collective-permute-done((bf16[1,256,2048]{2,1,0:T(8,128)(2,1)}, bf16[1,256,2048]{2,1,0:T(8,128)(2,1)}, u32[]{:S(2)}, u32[]{:S(2)}) %collective-permute-start) | collective-permute-done | bytes 1048608 | tf_op jit(solution)/shard_map/ppermute | solution.py:12
  277.2 0.0 all-to-all-done.2
  277.2 6.4 %reshape.154 = bf16[8192,1,3,64]{3,2,1,0:T(4,128)(2,1)} reshape(bf16[4,2,196608]{2,1,0:T(2,128)(2,1)S(1)} %all-to-all-done.2) | data formatting | bytes 6291456
  283.6 12.0 %copy.121 = bf16[3,1,64,4,2048]{4,3,2,0,1:T(4,128)(2,1)S(1)} copy(bf16[3,1,64,4,2048]{2,0,4,3,1:T(4,128)(2,1)} %bitcast.47) | data formatting | bytes 6291456 | tf_op jit(solution)/shard_map/all_to_all | solution.py:67
  295.6 2.8 fusion.41
  298.4 0.0 copy-start
  298.4 3.4 copy.124
  301.8 2.2 reshape.151
  303.9 0.0 copy-done
  303.9 1.7 copy.125
  305.6 1.4 reshape.152
  307.0 1.8 copy.103
  308.8 0.0 copy-start.1
  308.8 0.2 copy.128
  309.1 0.0 collective-permute-done.1
  309.1 3.9 %fusion.27 = f32[16,256,256]{1,2,0:T(8,128)} fusion(bf16[256,16,128]{0,2,1:T(8,128)(2,1)} %bitcast.9, bf16[256,16,128]{2,1,0:T(8,128)(2,1)S(1)} %bitcast.50), kind=kOutput, calls=%fused_computation.30 | convolution fusion | flops 268435456 | bytes 6291456 | tf_op jit(solution)/shard_map/qhd,khd->hqk/dot_general | solution.py:51
  313.0 0.0 copy-done.1
  313.0 3.4 fusion.44
  316.5 8.5 %fusion.13 = f32[16,256,128]{1,2,0:T(8,128)} fusion(bf16[256,16,128]{0,2,1:T(8,128)(2,1)S(1)} %copy-done.1, f32[16,256,256]{1,2,0:T(8,128)} %fusion.27, f32[16,256,256]{1,2,0:T(8,128)} %get-tuple-element.11, f32[16,256]{1,0:T(8,128)S(1)} %get-tuple-element.10), kind=kOutput, calls=%fused_computation.16 | convolution fusion | flops 275779840 | bytes 11550720 | tf_op jit(solution)/shard_map/hqk,khd->qhd/dot_general | solution.py:56
  325.0 8.6 %fusion.10 = f32[16,256,128]{1,2,0:T(8,128)} fusion(bf16[256,16,128]{0,2,1:T(8,128)(2,1)S(1)} %reshape.152, f32[16,256,256]{1,2,0:T(8,128)} %fusion.27, f32[16,256,256]{1,2,0:T(8,128)} %get-tuple-element.11, f32[16,256]{1,0:T(8,128)S(1)} %get-tuple-element.10), kind=kOutput, calls=%fused_computation.15 | convolution fusion | flops 275779840 | bytes 11550720 | tf_op jit(solution)/shard_map/hqk,qhd->khd/dot_general | solution.py:59
  333.6 4.6 %fusion.15 = f32[16,256,128]{1,2,0:T(8,128)} fusion(bf16[256,16,128]{0,2,1:T(8,128)(2,1)} %bitcast.9, f32[16,256,256]{1,2,0:T(8,128)} %get-tuple-element.11, f32[16,256]{1,0:T(8,128)S(1)} %get-tuple-element.10), kind=kOutput, calls=%fused_computation.17 | convolution fusion | flops 270532608 | bytes 7356416 | tf_op jit(solution)/shard_map/hqk,qhd->khd/dot_general | solution.py:48
  338.2 1.9 copy.111
  340.2 3.0 copy.112
  343.1 2.9 copy.113
  346.0 3.6 %fusion.3 = bf16[3,1,256,2048]{3,2,1,0:T(8,128)(2,1)} fusion(f32[1,1,256,2048]{3,2,1,0:T(8,128)} %copy.113, f32[1,1,256,2048]{3,2,1,0:T(8,128)} %copy.112, f32[1,1,256,2048]{3,2,1,0:T(8,128)S(1)} %copy.111, f32[]{:T(128)S(6)} %div.23), kind=kLoop, calls=%fused_computation.4 | loop fusion | flops 6291456 | bytes 9437188 | tf_op jit(solution)/shard_map/convert_element_type | solution.py:63
  349.7 2.3 copy.133
Async XLA Ops:
  191.4 85.8 %all-to-all-start.2 = ((bf16[4,2,196608]{2,1,0:T(2,128)(2,1)}), bf16[4,2,196608]{2,1,0:T(2,128)(2,1)S(1)}, u32[]{:S(2)}, u32[]{:S(2)}) async-start(bf16[4,2,196608]{2,1,0:T(2,128)(2,1)} %reshape.153), calls=%async_computation.2 | async-start | bytes 6291456 | tf_op jit(solution)/shard_map/all_to_all | solution.py:67
  201.6 6.8 %copy-start.2 = (s32[1,256]{1,0:T(1,128)S(1)}, s32[1,256]{1,0:T(1,128)}, u32[]{:S(2)}) copy-start(s32[1,256]{1,0:T(1,128)} %param.7) | copy-start | bytes 3076
  217.5 20.5 %copy-start.3 = (s32[1,256]{1,0:T(1,128)S(1)}, s32[1,256]{1,0:T(1,128)}, u32[]{:S(2)}) copy-start(s32[1,256]{1,0:T(1,128)} %param.9) | copy-start | bytes 3076
  219.7 57.5 %collective-permute-start = (bf16[1,256,2048]{2,1,0:T(8,128)(2,1)}, bf16[1,256,2048]{2,1,0:T(8,128)(2,1)}, u32[]{:S(2)}, u32[]{:S(2)}) collective-permute-start(bf16[1,256,2048]{2,1,0:T(8,128)(2,1)} %copy.93), channel_id=1, source_target_pairs={{0,16},{16,32},{32,48},{48,64},{64,80},{80,96},{96,112},{112,128},... | collective-permute-start | bytes 3145736 | tf_op jit(solution)/shard_map/ppermute | solution.py:12
  222.1 87.0 %collective-permute-start.1 = (bf16[1,256,2048]{1,2,0:T(8,128)(2,1)}, bf16[1,256,2048]{1,2,0:T(8,128)(2,1)}, u32[]{:S(2)}, u32[]{:S(2)}) collective-permute-start(bf16[1,256,2048]{1,2,0:T(8,128)(2,1)} %copy.102), channel_id=1, source_target_pairs={{0,240},{16,0},{32,16},{48,32},{64,48},{80,64},{96,80},{112,96},{1... | collective-permute-start | bytes 3145736 | tf_op jit(solution)/shard_map/ppermute | solution.py:12
  298.4 5.5 %copy-start = (bf16[1,1,4,64,2048]{4,2,3,0,1:T(4,128)(2,1)S(1)}, bf16[1,1,4,64,2048]{4,2,3,0,1:T(4,128)(2,1)}, u32[]{:S(2)}) copy-start(bf16[1,1,4,64,2048]{4,2,3,0,1:T(4,128)(2,1)} %get-tuple-element.4) | copy-start | bytes 3145732
  308.8 4.2 %copy-start.1 = (bf16[256,16,128]{0,2,1:T(8,128)(2,1)S(1)}, bf16[256,16,128]{0,2,1:T(8,128)(2,1)}, u32[]{:S(2)}) copy-start(bf16[256,16,128]{0,2,1:T(8,128)(2,1)} %reshape.151) | copy-start | bytes 3145732
where the time goes:
time: 354 us; the launch traced here: 352 us
  blocking collectives  169 us (48%)
  local copies, waits for them, and re-layouts  89.4 us (25%)
  waiting for transfers between devices  39.1 us (11%)
  matrix products  38.1 us (11%)
  starting transfers between devices  10.1 us (3%)
  other arithmetic  3.84 us (1%)
    all_to_all x1, blocking collectives, fetch(): lax.all_to_all(pieces, 'pipe', split_axis=1, concat_axis=1, tiled=True)  81.6 us
    all_to_all x1, blocking collectives, fetch(): lax.all_to_all(spread, 'pipe', split_axis=1, concat_axis=1, tiled=True)  76.7 us
    ppermute x2, waiting for transfers between devices, shifted(): lax.ppermute(array, axis, [(i, (i + by) % devices) for i in range(devices)])  39.1 us
    unnamed x15, local copies, waits for them, and re-layouts  24.4 us
    reshape x2, local copies, waits for them, and re-layouts, fetch(): return returned.reshape(leading, 1, length, columns)  14.2 us
    all_to_all x1, local copies, waits for them, and re-layouts, split_heads(): lax.all_to_all(parked_block, 'tensor', split_axis=3, concat_axis=2, tiled...  12 us
    psum x1, blocking collectives, on_device(): token_total = lax.psum(jnp.sum(loss_tokens.astype(jnp.float32)), 'dp')  11 us
    dot_general x1, matrix products, attend_backward(): jnp.einsum('hqk,qhd->khd', grad_logits, query_heads, preferred_element_ty...  8.63 us
  transfers between devices with their start and end apart: 3, of which 1 were waited for; matrix products, arithmetic and copies ran while one was open for 16% of the time, Pallas kernels for 0%

commit v1 on v0

v1 whole, which is shorter than its diff:
```python
import functools
import math

import jax
import jax.numpy as jnp
from jax import lax
from jax.experimental import pallas as pl
from jax.experimental.pallas import tpu as pltpu
from jax.sharding import PartitionSpec as P

HEAD_DIM = 128
CHUNKS = 4
SCALE = HEAD_DIM ** (-0.5)
EXPONENT = SCALE * math.log2(math.e)
NT = (((1,), (1,)), ((), ()))
NN = (((1,), (0,)), ((), ()))
TN = (((0,), (0,)), ((), ()))


def product(left, right, dims):
    return lax.dot_general(left, right, dims, preferred_element_type=jnp.float32)


def probabilities(queries, keys, outside):
    logits = product(queries, keys, NT) + outside
    highest = jnp.max(logits, axis=1, keepdims=True)
    weights = jnp.exp2((logits - highest) * EXPONENT)
    return weights / jnp.sum(weights, axis=1, keepdims=True)


def outside_of(row_ref, column_ref):
    return jnp.where(column_ref[...] == row_ref[...], 0.0, -1e31).astype(jnp.float32)


def forward_kernel(qkv_ref, row_ref, column_ref, out_ref):
    outside = outside_of(row_ref, column_ref)
    for start in range(0, out_ref.shape[2], HEAD_DIM):
        head = slice(start, start + HEAD_DIM)
        probs = probabilities(qkv_ref[0, 0, :, head], qkv_ref[1, 0, :, head], outside)
        mixed = product(probs.astype(jnp.bfloat16), qkv_ref[2, 0, :, head], NN)
        out_ref[0, :, head] = mixed.astype(jnp.bfloat16)


def forward(qkv, row, column):
    _, _, length, width = qkv.shape
    step = width // CHUNKS
    return pl.pallas_call(
        forward_kernel,
        grid=(CHUNKS,),
        in_specs=[
            pl.BlockSpec((3, 1, length, step), lambda c: (0, 0, 0, c)),
            pl.BlockSpec((1, length), lambda c: (0, 0)),
            pl.BlockSpec((length, 1), lambda c: (0, 0)),
        ],
        out_specs=pl.BlockSpec((1, length, step), lambda c: (0, 0, c)),
        out_shape=jax.ShapeDtypeStruct((1, length, width), jnp.bfloat16),
        compiler_params=pltpu.CompilerParams(vmem_limit_bytes=32 * 1024 * 1024),
        cost_estimate=pl.CostEstimate(
            flops=4 * length * length * width,
            bytes_accessed=8 * length * width,
            transcendentals=length * length * width // HEAD_DIM,
        ),
    )(qkv, row, column)


def backward_kernel(parts, *refs):
    pieces, refs = refs[:parts], refs[parts:]
    upstream_ref, row_ref, column_ref, factor_ref = refs[:4]
    out_ref, stash = refs[-2:]
    mine = lax.axis_index("tensor")
    rows = pieces[0].shape[2]
    for k in range(parts):
        start = pl.multiple_of((mine ^ k) * rows, rows)
        stash[:, pl.ds(start, rows), :] = pieces[k][:, 0]
    outside = outside_of(row_ref, column_ref)
    factor = factor_ref[0]
    for start in range(0, upstream_ref.shape[2], HEAD_DIM):
        head = slice(start, start + HEAD_DIM)
        queries, keys, values = stash[0, :, head], stash[1, :, head], stash[2, :, head]
        upstream = upstream_ref[0, :, head]
        probs = probabilities(queries, keys, outside)
        grad_value = product(probs.astype(jnp.bfloat16), upstream, TN)
        grad_probs = product(upstream, values, NT)
        center = jnp.sum(probs * grad_probs, axis=1, keepdims=True)
        grad_logits = (probs * (grad_probs - center) * SCALE).astype(jnp.bfloat16)
        out_ref[0, 0, :, head] = (product(grad_logits, keys, NN) * factor).astype(jnp.bfloat16)
        out_ref[1, 0, :, head] = (product(grad_logits, queries, TN) * factor).astype(jnp.bfloat16)
        out_ref[2, 0, :, head] = (grad_value * factor).astype(jnp.bfloat16)


def backward(chunk, pieces, upstream, row, column, factor, earlier):
    _, length, width = upstream.shape
    step = width // CHUNKS
    parts = len(pieces)
    whole = pl.BlockSpec(memory_space=pltpu.VMEM)
    operands = [*pieces, upstream, row, column, factor]
    in_specs = [whole] * parts + [
        pl.BlockSpec((1, length, step), lambda i: (0, 0, chunk)),
        pl.BlockSpec((1, length), lambda i: (0, 0)),
        pl.BlockSpec((length, 1), lambda i: (0, 0)),
        pl.BlockSpec(memory_space=pltpu.SMEM),
    ]
    aliases = {}
    if earlier is not None:
        aliases = {len(operands): 0}
        operands.append(earlier)
        in_specs.append(pl.BlockSpec(memory_space=pl.ANY))
    return pl.pallas_call(
        functools.partial(backward_kernel, parts),
        grid=(1,),
        in_specs=in_specs,
        out_specs=pl.BlockSpec((3, 1, length, step), lambda i: (0, 0, 0, chunk)),
        out_shape=jax.ShapeDtypeStruct((3, 1, length, width), jnp.bfloat16),
        scratch_shapes=[pltpu.VMEM((3, length, step), jnp.bfloat16)],
        input_output_aliases=aliases,
        compiler_params=pltpu.CompilerParams(vmem_limit_bytes=32 * 1024 * 1024),
        cost_estimate=pl.CostEstimate(
            flops=10 * length * length * step,
            bytes_accessed=14 * length * step,
            transcendentals=length * length * step // HEAD_DIM,
        ),
    )(*operands)


def shifted(array, by):
    sections = lax.axis_size("pipe")
    return lax.ppermute(array, "pipe", [(i, (i + by) % sections) for i in range(sections)])


def fetched(piece, k):
    sections, tensors = lax.axis_size("pipe"), lax.axis_size("tensor")
    pairs = [
        (p * tensors + t, (sections - 1 - p) * tensors + (t ^ k))
        for p in range(sections)
        for t in range(tensors)
    ]
    return lax.ppermute(piece, ("pipe", "tensor"), pairs)


def on_device(fwd_qkv, fwd_segments, parked, bwd_segments, grad_out, loss_tokens):
    length, width = grad_out.shape[1:]
    tensors = lax.axis_size("tensor")
    mine = lax.axis_index("tensor")
    step = width // CHUNKS
    pieces = []
    for chunk in range(CHUNKS):
        pieces.append([])
        for k in range(tensors):
            start = (mine ^ k) * width + chunk * step
            piece = lax.dynamic_slice_in_dim(parked, start, step, axis=3)
            pieces[-1].append(fetched(piece, k))
    upstream = shifted(grad_out, -1)
    token_total = lax.psum(loss_tokens.astype(jnp.float32), "dp")
    factor = jnp.float32(lax.axis_size("dp") * length) / token_total
    forward_out = forward(fwd_qkv, fwd_segments, fwd_segments.reshape(length, 1))
    received = shifted(forward_out, 1)
    column = bwd_segments.reshape(length, 1)
    grads = None
    for chunk in range(CHUNKS):
        grads = backward(chunk, pieces[chunk], upstream, bwd_segments, column, factor, grads)
    return (received, grads)


def solution(mesh):
    placed = (
        P(None, ("pipe", "dp"), None, "tensor"),
        P(("pipe", "dp"), None),
        P(None, ("pipe", "dp"), "tensor", None),
        P(("pipe", "dp"), None),
        P(("pipe", "dp"), None, "tensor"),
        P(("pipe", "dp")),
    )
    return jax.shard_map(
        on_device,
        mesh=mesh,
        in_specs=placed,
        out_specs=(P(("pipe", "dp"), None, "tensor"), P(None, ("pipe", "dp"), None, "tensor")),
        check_vma=False,
    )
```

time: 354 us -> 196 us (0.55)
  blocking collectives: 169 us -> 9.81 us
  starting transfers between devices: 10.1 us -> 105 us
  local copies, waits for them, and re-layouts: 89.4 us -> 11.6 us
  matrix products: 38.1 us -> 0 us
  Pallas kernels: 0 us -> 21.2 us
  waiting for transfers between devices: 39.1 us -> 45.4 us
  other arithmetic: 3.84 us -> 0 us
    all_to_all x2 -> x0, blocking collectives: 158 us -> none  [the longest x1 81.6 us: fetch(): lax.all_to_all(pieces, 'pipe', split_axis=1, concat_axis=1, tiled=True)]
    ppermute x2 -> x18, starting transfers between devices: 3.57 us -> 105 us  [the longest x16 98 us: fetched(): return lax.ppermute(piece, ('pipe', 'tensor'), pairs)]
    dot_general x5 -> x0, matrix products: 29.7 us -> none  [the longest x1 8.63 us: attend_backward(): jnp.einsum('hqk,qhd->khd', grad_logits, query_heads, preferred_element_ty...]
    pallas_call x0 -> x5, Pallas kernels: none -> 21.2 us  [the longest x4 16.3 us: backward(): pl.pallas_call(functools.partial(backward_kernel, parts), grid=(1,), in_s...]
    reshape x4 -> x2, local copies, waits for them, and re-layouts: 19.5 us -> 0.94 us  [the longest x1 0.8 us: on_device(): fwd_segments.reshape(length, 1)]
    unnamed x15 -> x23, local copies, waits for them, and re-layouts: 24.4 us -> 7.6 us
    another operation x7 -> x0, local copies, waits for them, and re-layouts: 16.3 us -> none  [the longest x4 8.55 us: split_rows(): return matrix.reshape(length, matrix.shape[1] // HEAD_DIM, HEAD_DIM)]
    all_to_all x2 -> x0, local copies, waits for them, and re-layouts: 13.3 us -> none  [the longest x1 12 us: split_heads(): lax.all_to_all(parked_block, 'tensor', split_axis=3, concat_axis=2, tiled...]
  transfers between devices with their start and end apart: 3 -> 18, of which waited for: 1 -> 11; matrix products, arithmetic and copies ran while one was open for 16% -> 2% of each run, Pallas kernels for 0% -> 8%
where the time goes in v1:
time: 196 us
  starting transfers between devices  105 us (54%)
  waiting for transfers between devices  45.4 us (23%)
  Pallas kernels  21.2 us (11%)
  local copies, waits for them, and re-layouts  11.6 us (6%)
  blocking collectives  9.81 us (5%)
  between operations  2.14 us (1%)
    ppermute x16, starting transfers between devices, fetched(): return lax.ppermute(piece, ('pipe', 'tensor'), pairs)  98 us
    ppermute x16, waiting for transfers between devices, fetched(): return lax.ppermute(piece, ('pipe', 'tensor'), pairs)  45.4 us
    pallas_call x4, Pallas kernels, backward(): pl.pallas_call(functools.partial(backward_kernel, parts), grid=(1,), in_s...  16.3 us
    psum x1, blocking collectives, on_device(): token_total = lax.psum(loss_tokens.astype(jnp.float32), 'dp')  9.81 us
    unnamed x23, local copies, waits for them, and re-layouts  7.6 us
    ppermute x2, starting transfers between devices, shifted(): lax.ppermute(array, 'pipe', [(i, (i + by) % sections) for i in range(sect...  7.49 us
    pallas_call x1, Pallas kernels, forward(): pl.pallas_call(forward_kernel, grid=(CHUNKS,), in_specs=[pl.BlockSpec((3,...  4.87 us
  transfers between devices with their start and end apart: 18, of which 11 were waited for; matrix products, arithmetic and copies ran while one was open for 2% of the time, Pallas kernels for 8%

profile of v1, /device:TPU:1, one launch (start us, length us, event | category | flops | bytes accessed | tf_op | source)
XLA Modules:
  0.0 195.5 jit_solution(10743263114752719137)
XLA Ops:
  0.6 7.4 %collective-permute-start.5 = (bf16[1,256,2048]{2,1,0:T(8,128)(2,1)}, bf16[1,256,2048]{2,1,0:T(8,128)(2,1)S(1)}, u32[]{:S(2)}, u32[]{:S(2)}) collective-permute-start(bf16[1,256,2048]{2,1,0:T(8,128)(2,1)} %param.10), channel_id=1, source_target_pairs={{0,240},{16,0},{32,16},{48,32},{64,48},{80,64},{96,80},{112,96},{1... | collective-permute-start | bytes 3145736 | tf_op jit(solution)/shard_map/ppermute | solution.py:127
  8.0 0.8 copy.11.column_ref
  8.9 0.0 copy-start
  8.9 1.9 copy-done
  10.7 0.0 copy-start.10
  10.7 0.7 copy-done.10
  11.4 4.9 %shard_map.77 = bf16[1,256,2048]{2,1,0:T(8,128)(2,1)S(1)} custom-call(bf16[3,1,256,2048]{3,2,1,0:T(8,128)(2,1)S(1)} %copy-done, s32[1,256]{1,0:T(1,128)S(1)} %copy-done.10, s32[256,1]{1,0:T(8,128)S(1)} %copy.11.column_ref), custom_call_target="tpu_custom_call" | custom-call | flops 536870912 | bytes 4194304 | tf_op jit(solution)/shard_map/pallas_call | solution.py:47
  16.3 0.1 collective-permute-start
  16.5 0.0 copy-start.9
  16.5 3.1 %constant_dynamic-slice_fusion = (bf16[3,1,64,512]{3,2,1,0:T(8,128)(2,1)S(1)}, bf16[3,1,64,512]{3,2,1,0:T(8,128)(2,1)S(1)}, bf16[3,1,64,512]{3,2,1,0:T(8,128)(2,...) fusion(bf16[3,1,64,8192]{3,2,1,0:T(8,128)(2,1)} %param.8, ...), kind=kLoop, calls=%fused_computation | loop fusion | bytes 6291520 | tf_op jit(solution)/shard_map/dynamic_slice | solution.py:150
  19.5 3.4 %collective-permute-start.14 = (bf16[3,1,64,512]{3,2,1,0:T(8,128)(2,1)S(1)}, bf16[3,1,64,512]{3,2,1,0:T(8,128)(2,1)S(1)}, u32[]{:S(2)}, u32[]{:S(2)}) collective-permute-start(bf16[3,1,64,512]{3,2,1,0:T(8,128)(2,1)S(1)} %get-tuple-element.4), channel_id=1, source_target_pairs={{0,240},{4,244},{8,248},{12,252},{16,224},{20,228},{24,232},{28,23... | collective-permute-start | bytes 589832 | tf_op jit(solution)/shard_map/ppermute | solution.py:137
  23.0 1.3 collective-permute-start.15
  24.2 5.0 %collective-permute-start.16 = (bf16[3,1,64,512]{3,2,1,0:T(8,128)(2,1)S(1)}, bf16[3,1,64,512]{3,2,1,0:T(8,128)(2,1)S(1)}, u32[]{:S(2)}, u32[]{:S(2)}) collective-permute-start(bf16[3,1,64,512]{3,2,1,0:T(8,128)(2,1)S(1)} %get-tuple-element.17), channel_id=1, source_target_pairs={{0,248},{4,252},{8,240},{12,244},{16,232},{20,236},{24,224},{28,22... | collective-permute-start | bytes 589832 | tf_op jit(solution)/shard_map/ppermute | solution.py:137
  29.2 17.8 %collective-permute-done.14.refs_0_ = bf16[3,1,64,512]{3,2,1,0:T(8,128)(2,1)S(1)} collective-permute-done((bf16[3,1,64,512]{3,2,1,0:T(8,128)(2,1)S(1)}, bf16[3,1,64,512]{3,2,1,0:T(8,128)(2,1)S(1)}, u32[]{:S(2)}, u32[]{:S(2)}) %collective-permute-start.14) | collective-permute-done | bytes 196640 | tf_op jit(solution)/shard_map/ppermute | solution.py:137
  47.0 70.5 %collective-permute-start.17 = (bf16[3,1,64,512]{3,2,1,0:T(8,128)(2,1)S(1)}, bf16[3,1,64,512]{3,2,1,0:T(8,128)(2,1)S(1)}, u32[]{:S(2)}, u32[]{:S(2)}) collective-permute-start(bf16[3,1,64,512]{3,2,1,0:T(8,128)(2,1)S(1)} %get-tuple-element.2), channel_id=1, source_target_pairs={{0,252},{4,248},{8,244},{12,240},{16,236},{20,232},{24,228},{28,22... | collective-permute-start | bytes 589832 | tf_op jit(solution)/shard_map/ppermute | solution.py:137
  117.5 3.3 %collective-permute-done.15.refs_1_ = bf16[3,1,64,512]{3,2,1,0:T(8,128)(2,1)S(1)} collective-permute-done((bf16[3,1,64,512]{3,2,1,0:T(8,128)(2,1)S(1)}, bf16[3,1,64,512]{3,2,1,0:T(8,128)(2,1)S(1)}, u32[]{:S(2)}, u32[]{:S(2)}) %collective-permute-start.15) | collective-permute-done | bytes 196640 | tf_op jit(solution)/shard_map/ppermute | solution.py:137
  120.7 0.6 collective-permute-start.10
  121.3 2.2 %collective-permute-done.16.refs_2_ = bf16[3,1,64,512]{3,2,1,0:T(8,128)(2,1)S(1)} collective-permute-done((bf16[3,1,64,512]{3,2,1,0:T(8,128)(2,1)S(1)}, bf16[3,1,64,512]{3,2,1,0:T(8,128)(2,1)S(1)}, u32[]{:S(2)}, u32[]{:S(2)}) %collective-permute-start.16) | collective-permute-done | bytes 196640 | tf_op jit(solution)/shard_map/ppermute | solution.py:137
  123.6 0.9 collective-permute-start.11
  124.4 6.0 %collective-permute-done.17.refs_3_ = bf16[3,1,64,512]{3,2,1,0:T(8,128)(2,1)S(1)} collective-permute-done((bf16[3,1,64,512]{3,2,1,0:T(8,128)(2,1)S(1)}, bf16[3,1,64,512]{3,2,1,0:T(8,128)(2,1)S(1)}, u32[]{:S(2)}, u32[]{:S(2)}) %collective-permute-start.17) | collective-permute-done | bytes 196640 | tf_op jit(solution)/shard_map/ppermute | solution.py:137
  130.4 0.0 collective-permute-start.12
  130.4 0.6 collective-permute-done.10.refs_0_
  131.1 3.4 %collective-permute-start.13 = (bf16[3,1,64,512]{3,2,1,0:T(8,128)(2,1)S(1)}, bf16[3,1,64,512]{3,2,1,0:T(8,128)(2,1)S(1)}, u32[]{:S(2)}, u32[]{:S(2)}) collective-permute-start(bf16[3,1,64,512]{3,2,1,0:T(8,128)(2,1)S(1)} %get-tuple-element.5), channel_id=1, source_target_pairs={{0,252},{4,248},{8,244},{12,240},{16,236},{20,232},{24,228},{28,22... | collective-permute-start | bytes 589832 | tf_op jit(solution)/shard_map/ppermute | solution.py:137
  134.5 2.2 %collective-permute-done.11.refs_1_ = bf16[3,1,64,512]{3,2,1,0:T(8,128)(2,1)S(1)} collective-permute-done((bf16[3,1,64,512]{3,2,1,0:T(8,128)(2,1)S(1)}, bf16[3,1,64,512]{3,2,1,0:T(8,128)(2,1)S(1)}, u32[]{:S(2)}, u32[]{:S(2)}) %collective-permute-start.11) | collective-permute-done | bytes 196640 | tf_op jit(solution)/shard_map/ppermute | solution.py:137
  136.6 1.5 collective-permute-start.6
  138.2 2.5 %collective-permute-done.12.refs_2_ = bf16[3,1,64,512]{3,2,1,0:T(8,128)(2,1)S(1)} collective-permute-done((bf16[3,1,64,512]{3,2,1,0:T(8,128)(2,1)S(1)}, bf16[3,1,64,512]{3,2,1,0:T(8,128)(2,1)S(1)}, u32[]{:S(2)}, u32[]{:S(2)}) %collective-permute-start.12) | collective-permute-done | bytes 196640 | tf_op jit(solution)/shard_map/ppermute | solution.py:137
  140.7 0.0 collective-permute-start.7
  140.7 6.2 %collective-permute-done.13.refs_3_ = bf16[3,1,64,512]{3,2,1,0:T(8,128)(2,1)S(1)} collective-permute-done((bf16[3,1,64,512]{3,2,1,0:T(8,128)(2,1)S(1)}, bf16[3,1,64,512]{3,2,1,0:T(8,128)(2,1)S(1)}, u32[]{:S(2)}, u32[]{:S(2)}) %collective-permute-start.13) | collective-permute-done | bytes 196640 | tf_op jit(solution)/shard_map/ppermute | solution.py:137
  147.0 0.0 copy-start.1
  147.0 0.7 copy-done.1
  147.6 0.0 collective-permute-start.8
  147.6 0.9 collective-permute-done.6.refs_0_
  148.5 0.0 copy-start.3
  148.5 0.7 copy-done.3
  149.2 2.5 %collective-permute-start.9 = (bf16[3,1,64,512]{3,2,1,0:T(8,128)(2,1)}, bf16[3,1,64,512]{3,2,1,0:T(8,128)(2,1)}, u32[]{:S(2)}, u32[]{:S(2)}) collective-permute-start(bf16[3,1,64,512]{3,2,1,0:T(8,128)(2,1)} %get-tuple-element.9), channel_id=1, source_target_pairs={{0,252},{4,248},{8,244},{12,240},{16,236},{20,232},{24,228},{28,22... | collective-permute-start | bytes 589832 | tf_op jit(solution)/shard_map/ppermute | solution.py:137
  151.7 1.8 collective-permute-done.7.refs_1_
  153.5 0.0 copy-start.5
  153.5 0.7 copy-done.5
  154.2 1.9 collective-permute-start.1
  156.1 1.9 collective-permute-done.8.refs_2_
  157.9 0.0 copy-start.7
  157.9 0.7 copy-done.7
  158.6 0.0 collective-permute-start.2
  158.6 0.0 collective-permute-done.5.refs_4_
  158.6 4.5 %collective-permute-start.3 = (bf16[3,1,64,512]{3,2,1,0:T(8,128)(2,1)}, bf16[3,1,64,512]{3,2,1,0:T(8,128)(2,1)}, u32[]{:S(2)}, u32[]{:S(2)}) collective-permute-start(bf16[3,1,64,512]{3,2,1,0:T(8,128)(2,1)} %get-tuple-element.14), channel_id=1, source_target_pairs={{0,248},{4,252},{8,240},{12,244},{16,232},{20,236},{24,224},{28,22... | collective-permute-start | bytes 589832 | tf_op jit(solution)/shard_map/ppermute | solution.py:137
  163.2 0.0 collective-permute-done
  163.2 2.4 %collective-permute-start.4 = (bf16[3,1,64,512]{3,2,1,0:T(8,128)(2,1)}, bf16[3,1,64,512]{3,2,1,0:T(8,128)(2,1)S(1)}, u32[]{:S(2)}, u32[]{:S(2)}) collective-permute-start(bf16[3,1,64,512]{3,2,1,0:T(8,128)(2,1)} %get-tuple-element.13), channel_id=1, source_target_pairs={{0,252},{4,248},{8,244},{12,240},{16,236},{20,232},{24,228},{28,22... | collective-permute-start | bytes 589832 | tf_op jit(solution)/shard_map/ppermute | solution.py:137
  166.2 9.8 %psum.7 = f32[1]{0:T(128)} all-reduce(f32[1]{0:T(128)S(6)} %convert_element_type.3), channel_id=1, replica_groups=mesh['pipe'=16,'tensor'=4,'dp'=4] {'dp'}, use_global_device_ids=true, to_apply=%region_0.0 | all-reduce | flops 1 | bytes 8 | tf_op jit(solution)/shard_map/psum | solution.py:153
  176.1 0.0 copy-done.9
  176.1 0.1 copy.15.refs_6_
  176.9 3.6 %shard_map.78.refs_8_ = bf16[3,1,256,2048]{3,2,1,0:T(8,128)(2,1)} custom-call(bf16[3,1,64,512]{3,2,1,0:T(8,128)(2,1)S(1)} %collective-permute-done.14.refs_0_, bf16[3,1,64,512]{3,2,1,0:T(8,128)(2,1)S(1)} %collective-permute-done.15.refs_1_, bf16[3,1,64,512]{3,2,1,0:T(8,128)(2,1)S(1)} %collective-permute-done.16.refs_2_, ...), custom_call_target="tpu_custom_call" | custom-call | flops 335544320 | bytes 1835008 | tf_op jit(solution)/shard_map/pallas_call | solution.py:108
  180.5 0.0 copy-done.2
  180.5 3.6 %shard_map.79.refs_8_ = bf16[3,1,256,2048]{3,2,1,0:T(8,128)(2,1)} custom-call(bf16[3,1,64,512]{3,2,1,0:T(8,128)(2,1)S(1)} %collective-permute-done.10.refs_0_, bf16[3,1,64,512]{3,2,1,0:T(8,128)(2,1)S(1)} %collective-permute-done.11.refs_1_, bf16[3,1,64,512]{3,2,1,0:T(8,128)(2,1)S(1)} %collective-permute-done.12.refs_2_, ...), custom_call_target="tpu_custom_call", output_to_operand_aliasing={{}: (8, {})} | custom-call | flops 335544320 | bytes 1835008 | tf_op jit(solution)/shard_map/pallas_call | solution.py:108
  184.0 0.0 collective-permute-done.9.refs_3_
  184.1 0.0 copy-done.4
  184.1 0.0 copy-done.6
  184.1 0.0 copy-done.8
  184.1 4.5 %shard_map.80.refs_8_ = bf16[3,1,256,2048]{3,2,1,0:T(8,128)(2,1)} custom-call(bf16[3,1,64,512]{3,2,1,0:T(8,128)(2,1)S(1)} %copy-done.4, bf16[3,1,64,512]{3,2,1,0:T(8,128)(2,1)S(1)} %copy-done.6, bf16[3,1,64,512]{3,2,1,0:T(8,128)(2,1)S(1)} %copy-done.8, bf16[3,1,64,512]{3,2,1,0:T(8,128)(2,1)} %collective-permute-done.9.refs_3_, ...), custom_call_target="tpu_custom_call", output_to_operand_aliasing={{}: (8, {})} | custom-call | flops 335544320 | bytes 1835008 | tf_op jit(solution)/shard_map/pallas_call | solution.py:108
  188.5 0.0 collective-permute-done.1.refs_0_
  188.6 0.0 collective-permute-done.2.refs_1_
  188.6 0.0 collective-permute-done.3.refs_2_
  188.6 0.0 collective-permute-done.4.refs_3_
  188.6 4.7 %shard_map.81 = bf16[3,1,256,2048]{3,2,1,0:T(8,128)(2,1)} custom-call(bf16[3,1,64,512]{3,2,1,0:T(8,128)(2,1)} %collective-permute-done.1.refs_0_, bf16[3,1,64,512]{3,2,1,0:T(8,128)(2,1)} %collective-permute-done.2.refs_1_, bf16[3,1,64,512]{3,2,1,0:T(8,128)(2,1)} %collective-permute-done.3.refs_2_, ...), custom_call_target="tpu_custom_call", output_to_operand_aliasing={{}: (8, {})} | custom-call | flops 335544320 | bytes 1835008 | tf_op jit(solution)/shard_map/pallas_call | solution.py:108
  193.2 2.3 %copy.21 = bf16[1,256,2048]{2,1,0:T(8,128)(2,1)} copy(bf16[1,256,2048]{2,1,0:T(8,128)(2,1)} %collective-permute-done) | data formatting | bytes 2097152
  (4 shorter events, 0.0 us)
Async XLA Ops:
  0.6 158.0 %collective-permute-start.5 = (bf16[1,256,2048]{2,1,0:T(8,128)(2,1)}, bf16[1,256,2048]{2,1,0:T(8,128)(2,1)S(1)}, u32[]{:S(2)}, u32[]{:S(2)}) collective-permute-start(bf16[1,256,2048]{2,1,0:T(8,128)(2,1)} %param.10), channel_id=1, source_target_pairs={{0,240},{16,0},{32,16},{48,32},{64,48},{80,64},{96,80},{112,96},{1... | collective-permute-start | bytes 3145736 | tf_op jit(solution)/shard_map/ppermute | solution.py:127
  8.9 1.9 copy-start
  10.7 0.7 copy-start.10
  16.3 146.9 %collective-permute-start = (bf16[1,256,2048]{2,1,0:T(8,128)(2,1)S(1)}, bf16[1,256,2048]{2,1,0:T(8,128)(2,1)}, u32[]{:S(2)}, u32[]{:S(2)}) collective-permute-start(bf16[1,256,2048]{2,1,0:T(8,128)(2,1)S(1)} %shard_map.77), channel_id=1, source_target_pairs={{0,16},{16,32},{32,48},{48,64},{64,80},{80,96},{96,112},{112,128},... | collective-permute-start | bytes 3145736 | tf_op jit(solution)/shard_map/ppermute | solution.py:127
  16.5 159.6 %copy-start.9 = (s32[1,256]{1,0:T(1,128)S(1)}, s32[1,256]{1,0:T(1,128)}, u32[]{:S(2)}) copy-start(s32[1,256]{1,0:T(1,128)} %refs_5_.7) | copy-start | bytes 3076
  19.5 27.5 %collective-permute-start.14 = (bf16[3,1,64,512]{3,2,1,0:T(8,128)(2,1)S(1)}, bf16[3,1,64,512]{3,2,1,0:T(8,128)(2,1)S(1)}, u32[]{:S(2)}, u32[]{:S(2)}) collective-permute-start(bf16[3,1,64,512]{3,2,1,0:T(8,128)(2,1)S(1)} %get-tuple-element.4), channel_id=1, source_target_pairs={{0,240},{4,244},{8,248},{12,252},{16,224},{20,228},{24,232},{28,23... | collective-permute-start | bytes 589832 | tf_op jit(solution)/shard_map/ppermute | solution.py:137
  23.0 97.8 %collective-permute-start.15 = (bf16[3,1,64,512]{3,2,1,0:T(8,128)(2,1)S(1)}, bf16[3,1,64,512]{3,2,1,0:T(8,128)(2,1)S(1)}, u32[]{:S(2)}, u32[]{:S(2)}) collective-permute-start(bf16[3,1,64,512]{3,2,1,0:T(8,128)(2,1)S(1)} %get-tuple-element.3), channel_id=1, source_target_pairs={{0,244},{4,240},{8,252},{12,248},{16,228},{20,224},{24,236},{28,23... | collective-permute-start | bytes 589832 | tf_op jit(solution)/shard_map/ppermute | solution.py:137
  24.2 99.3 %collective-permute-start.16 = (bf16[3,1,64,512]{3,2,1,0:T(8,128)(2,1)S(1)}, bf16[3,1,64,512]{3,2,1,0:T(8,128)(2,1)S(1)}, u32[]{:S(2)}, u32[]{:S(2)}) collective-permute-start(bf16[3,1,64,512]{3,2,1,0:T(8,128)(2,1)S(1)} %get-tuple-element.17), channel_id=1, source_target_pairs={{0,248},{4,252},{8,240},{12,244},{16,232},{20,236},{24,224},{28,22... | collective-permute-start | bytes 589832 | tf_op jit(solution)/shard_map/ppermute | solution.py:137
  47.0 83.4 %collective-permute-start.17 = (bf16[3,1,64,512]{3,2,1,0:T(8,128)(2,1)S(1)}, bf16[3,1,64,512]{3,2,1,0:T(8,128)(2,1)S(1)}, u32[]{:S(2)}, u32[]{:S(2)}) collective-permute-start(bf16[3,1,64,512]{3,2,1,0:T(8,128)(2,1)S(1)} %get-tuple-element.2), channel_id=1, source_target_pairs={{0,252},{4,248},{8,244},{12,240},{16,236},{20,232},{24,228},{28,22... | collective-permute-start | bytes 589832 | tf_op jit(solution)/shard_map/ppermute | solution.py:137
  120.7 10.3 %collective-permute-start.10 = (bf16[3,1,64,512]{3,2,1,0:T(8,128)(2,1)S(1)}, bf16[3,1,64,512]{3,2,1,0:T(8,128)(2,1)S(1)}, u32[]{:S(2)}, u32[]{:S(2)}) collective-permute-start(bf16[3,1,64,512]{3,2,1,0:T(8,128)(2,1)S(1)} %get-tuple-element.8), channel_id=1, source_target_pairs={{0,240},{4,244},{8,248},{12,252},{16,224},{20,228},{24,232},{28,23... | collective-permute-start | bytes 589832 | tf_op jit(solution)/shard_map/ppermute | solution.py:137
  123.6 13.1 %collective-permute-start.11 = (bf16[3,1,64,512]{3,2,1,0:T(8,128)(2,1)S(1)}, bf16[3,1,64,512]{3,2,1,0:T(8,128)(2,1)S(1)}, u32[]{:S(2)}, u32[]{:S(2)}) collective-permute-start(bf16[3,1,64,512]{3,2,1,0:T(8,128)(2,1)S(1)} %get-tuple-element.7), channel_id=1, source_target_pairs={{0,244},{4,240},{8,252},{12,248},{16,228},{20,224},{24,236},{28,23... | collective-permute-start | bytes 589832 | tf_op jit(solution)/shard_map/ppermute | solution.py:137
  130.4 10.3 %collective-permute-start.12 = (bf16[3,1,64,512]{3,2,1,0:T(8,128)(2,1)S(1)}, bf16[3,1,64,512]{3,2,1,0:T(8,128)(2,1)S(1)}, u32[]{:S(2)}, u32[]{:S(2)}) collective-permute-start(bf16[3,1,64,512]{3,2,1,0:T(8,128)(2,1)S(1)} %get-tuple-element.6), channel_id=1, source_target_pairs={{0,248},{4,252},{8,240},{12,244},{16,232},{20,236},{24,224},{28,22... | collective-permute-start | bytes 589832 | tf_op jit(solution)/shard_map/ppermute | solution.py:137
  131.1 15.9 %collective-permute-start.13 = (bf16[3,1,64,512]{3,2,1,0:T(8,128)(2,1)S(1)}, bf16[3,1,64,512]{3,2,1,0:T(8,128)(2,1)S(1)}, u32[]{:S(2)}, u32[]{:S(2)}) collective-permute-start(bf16[3,1,64,512]{3,2,1,0:T(8,128)(2,1)S(1)} %get-tuple-element.5), channel_id=1, source_target_pairs={{0,252},{4,248},{8,244},{12,240},{16,236},{20,232},{24,228},{28,22... | collective-permute-start | bytes 589832 | tf_op jit(solution)/shard_map/ppermute | solution.py:137
  136.6 11.9 %collective-permute-start.6 = (bf16[3,1,64,512]{3,2,1,0:T(8,128)(2,1)S(1)}, bf16[3,1,64,512]{3,2,1,0:T(8,128)(2,1)S(1)}, u32[]{:S(2)}, u32[]{:S(2)}) collective-permute-start(bf16[3,1,64,512]{3,2,1,0:T(8,128)(2,1)S(1)} %get-tuple-element.12), channel_id=1, source_target_pairs={{0,240},{4,244},{8,248},{12,252},{16,224},{20,228},{24,232},{28,23... | collective-permute-start | bytes 589832 | tf_op jit(solution)/shard_map/ppermute | solution.py:137
  140.7 12.8 %collective-permute-start.7 = (bf16[3,1,64,512]{3,2,1,0:T(8,128)(2,1)S(1)}, bf16[3,1,64,512]{3,2,1,0:T(8,128)(2,1)S(1)}, u32[]{:S(2)}, u32[]{:S(2)}) collective-permute-start(bf16[3,1,64,512]{3,2,1,0:T(8,128)(2,1)S(1)} %get-tuple-element.11), channel_id=1, source_target_pairs={{0,244},{4,240},{8,252},{12,248},{16,228},{20,224},{24,236},{28,23... | collective-permute-start | bytes 589832 | tf_op jit(solution)/shard_map/ppermute | solution.py:137
  147.0 0.7 copy-start.1
  147.6 10.3 %collective-permute-start.8 = (bf16[3,1,64,512]{3,2,1,0:T(8,128)(2,1)S(1)}, bf16[3,1,64,512]{3,2,1,0:T(8,128)(2,1)S(1)}, u32[]{:S(2)}, u32[]{:S(2)}) collective-permute-start(bf16[3,1,64,512]{3,2,1,0:T(8,128)(2,1)S(1)} %get-tuple-element.10), channel_id=1, source_target_pairs={{0,248},{4,252},{8,240},{12,244},{16,232},{20,236},{24,224},{28,22... | collective-permute-start | bytes 589832 | tf_op jit(solution)/shard_map/ppermute | solution.py:137
  148.5 0.7 copy-start.3
  149.2 34.8 %collective-permute-start.9 = (bf16[3,1,64,512]{3,2,1,0:T(8,128)(2,1)}, bf16[3,1,64,512]{3,2,1,0:T(8,128)(2,1)}, u32[]{:S(2)}, u32[]{:S(2)}) collective-permute-start(bf16[3,1,64,512]{3,2,1,0:T(8,128)(2,1)} %get-tuple-element.9), channel_id=1, source_target_pairs={{0,252},{4,248},{8,244},{12,240},{16,236},{20,232},{24,228},{28,22... | collective-permute-start | bytes 589832 | tf_op jit(solution)/shard_map/ppermute | solution.py:137
  153.5 0.7 copy-start.5
  154.2 34.4 %collective-permute-start.1 = (bf16[3,1,64,512]{3,2,1,0:T(8,128)(2,1)}, bf16[3,1,64,512]{3,2,1,0:T(8,128)(2,1)}, u32[]{:S(2)}, u32[]{:S(2)}) collective-permute-start(bf16[3,1,64,512]{3,2,1,0:T(8,128)(2,1)} %get-tuple-element.16), channel_id=1, source_target_pairs={{0,240},{4,244},{8,248},{12,252},{16,224},{20,228},{24,232},{28,23... | collective-permute-start | bytes 589832 | tf_op jit(solution)/shard_map/ppermute | solution.py:137
  157.9 0.7 copy-start.7
  158.6 29.9 %collective-permute-start.2 = (bf16[3,1,64,512]{3,2,1,0:T(8,128)(2,1)}, bf16[3,1,64,512]{3,2,1,0:T(8,128)(2,1)}, u32[]{:S(2)}, u32[]{:S(2)}) collective-permute-start(bf16[3,1,64,512]{3,2,1,0:T(8,128)(2,1)} %get-tuple-element.15), channel_id=1, source_target_pairs={{0,244},{4,240},{8,252},{12,248},{16,228},{20,224},{24,236},{28,23... | collective-permute-start | bytes 589832 | tf_op jit(solution)/shard_map/ppermute | solution.py:137
  158.6 29.9 %collective-permute-start.3 = (bf16[3,1,64,512]{3,2,1,0:T(8,128)(2,1)}, bf16[3,1,64,512]{3,2,1,0:T(8,128)(2,1)}, u32[]{:S(2)}, u32[]{:S(2)}) collective-permute-start(bf16[3,1,64,512]{3,2,1,0:T(8,128)(2,1)} %get-tuple-element.14), channel_id=1, source_target_pairs={{0,248},{4,252},{8,240},{12,244},{16,232},{20,236},{24,224},{28,22... | collective-permute-start | bytes 589832 | tf_op jit(solution)/shard_map/ppermute | solution.py:137
  163.2 17.3 %copy-start.2 = (bf16[3,1,64,512]{3,2,1,0:T(8,128)(2,1)S(1)}, bf16[3,1,64,512]{3,2,1,0:T(8,128)(2,1)}, u32[]{:S(2)}) copy-start(bf16[3,1,64,512]{3,2,1,0:T(8,128)(2,1)} %copy-done.1) | copy-start | bytes 589828
  163.2 25.4 %collective-permute-start.4 = (bf16[3,1,64,512]{3,2,1,0:T(8,128)(2,1)}, bf16[3,1,64,512]{3,2,1,0:T(8,128)(2,1)S(1)}, u32[]{:S(2)}, u32[]{:S(2)}) collective-permute-start(bf16[3,1,64,512]{3,2,1,0:T(8,128)(2,1)} %get-tuple-element.13), channel_id=1, source_target_pairs={{0,252},{4,248},{8,244},{12,240},{16,236},{20,232},{24,228},{28,22... | collective-permute-start | bytes 589832 | tf_op jit(solution)/shard_map/ppermute | solution.py:137
  180.5 3.6 %copy-start.4 = (bf16[3,1,64,512]{3,2,1,0:T(8,128)(2,1)S(1)}, bf16[3,1,64,512]{3,2,1,0:T(8,128)(2,1)}, u32[]{:S(2)}) copy-start(bf16[3,1,64,512]{3,2,1,0:T(8,128)(2,1)} %copy-done.3) | copy-start | bytes 589828
  180.5 3.6 %copy-start.6 = (bf16[3,1,64,512]{3,2,1,0:T(8,128)(2,1)S(1)}, bf16[3,1,64,512]{3,2,1,0:T(8,128)(2,1)}, u32[]{:S(2)}) copy-start(bf16[3,1,64,512]{3,2,1,0:T(8,128)(2,1)} %copy-done.5) | copy-start | bytes 589828
  180.5 3.6 %copy-start.8 = (bf16[3,1,64,512]{3,2,1,0:T(8,128)(2,1)S(1)}, bf16[3,1,64,512]{3,2,1,0:T(8,128)(2,1)}, u32[]{:S(2)}) copy-start(bf16[3,1,64,512]{3,2,1,0:T(8,128)(2,1)} %copy-done.7) | copy-start | bytes 589828

commit v2 on v1

--- a/solution.py
+++ b/solution.py
@@ -122,19 +122,34 @@
     )(*operands)
 
 
-def shifted(array, by):
-    sections = lax.axis_size("pipe")
-    return lax.ppermute(array, "pipe", [(i, (i + by) % sections) for i in range(sections)])
+def moved(array, target):
+    sections, tensors = lax.axis_size("pipe"), lax.axis_size("tensor")
+    pairs = []
+    for p in range(sections):
+        for t in range(tensors):
+            section, tensor = target(p, t)
+            pairs.append((p * tensors + t, section % sections * tensors + tensor))
+    return lax.ppermute(array, ("pipe", "tensor"), pairs)
 
 
 def fetched(piece, k):
-    sections, tensors = lax.axis_size("pipe"), lax.axis_size("tensor")
-    pairs = [
-        (p * tensors + t, (sections - 1 - p) * tensors + (t ^ k))
-        for p in range(sections)
-        for t in range(tensors)
-    ]
-    return lax.ppermute(piece, ("pipe", "tensor"), pairs)
+    last = lax.axis_size("pipe") - 1
+    return moved(piece, lambda p, t: (last - p, t ^ k))
+
+
+def swapped(array):
+    return moved(array, lambda p, t: (p ^ (t & 1), t))
+
+
+def stepped(array, by):
+    kept = 1 if by > 0 else 0
+
+    def target(p, t):
+        if t & 1 == 0:
+            return p + by, t
+        return (p if p & 1 == kept else p + 2 * by), t
+
+    return moved(array, target)
 
 
 def on_device(fwd_qkv, fwd_segments, parked, bwd_segments, grad_out, loss_tokens):
@@ -142,22 +157,42 @@
     tensors = lax.axis_size("tensor")
     mine = lax.axis_index("tensor")
     step = width // CHUNKS
-    pieces = []
-    for chunk in range(CHUNKS):
-        pieces.append([])
-        for k in range(tensors):
-            start = (mine ^ k) * width + chunk * step
-            piece = lax.dynamic_slice_in_dim(parked, start, step, axis=3)
-            pieces[-1].append(fetched(piece, k))
-    upstream = shifted(grad_out, -1)
+    def fetched_chunk(whole, chunk):
+        starts = [(mine ^ k) * width + chunk * step for k in range(tensors)]
+        cut = [lax.dynamic_slice_in_dim(whole, start, step, axis=3) for start in starts]
+        fetches = []
+        for k, piece in enumerate(cut):
+            with jax.named_scope(f"stash_{chunk}_{k}"):
+                fetches.append(fetched(piece, k))
+        return fetches
+
+    pieces = [fetched_chunk(parked, chunk) for chunk in range(3)]
+    with jax.named_scope("swap_grad"):
+        swapped_grad = swapped(grad_out)
     token_total = lax.psum(loss_tokens.astype(jnp.float32), "dp")
+    with jax.named_scope("forward_heads"):
+        forward_out = forward(fwd_qkv, fwd_segments, fwd_segments.reshape(length, 1))
+    pieces[0], swapped_grad, token_total, forward_out = lax.optimization_barrier(
+        (pieces[0], swapped_grad, token_total, forward_out)
+    )
+    with jax.named_scope("step_grad"):
+        upstream = stepped(swapped_grad, -1)
     factor = jnp.float32(lax.axis_size("dp") * length) / token_total
-    forward_out = forward(fwd_qkv, fwd_segments, fwd_segments.reshape(length, 1))
-    received = shifted(forward_out, 1)
+    with jax.named_scope("swap_out"):
+        swapped_out = swapped(forward_out)
+    pieces[1], swapped_out = lax.optimization_barrier((pieces[1], swapped_out))
     column = bwd_segments.reshape(length, 1)
     grads = None
     for chunk in range(CHUNKS):
-        grads = backward(chunk, pieces[chunk], upstream, bwd_segments, column, factor, grads)
+        with jax.named_scope(f"backward_{chunk}"):
+            grads = backward(
+                chunk, pieces[chunk], upstream, bwd_segments, column, factor, grads
+            )
+        if len(pieces) < CHUNKS:
+            parked, grads = lax.optimization_barrier((parked, grads))
+            pieces.append(fetched_chunk(parked, len(pieces)))
+    with jax.named_scope("step_out"):
+        received = stepped(swapped_out, 1)
     return (received, grads)
 
 

time: 196 us -> 197 us (level)
  waiting for transfers between devices: 45.4 us -> 80.4 us
  starting transfers between devices: 105 us -> 76.7 us
  local copies, waits for them, and re-layouts: 11.6 us -> 7.04 us
    ppermute x18 -> x20, waiting for transfers between devices: 45.4 us -> 80.4 us  [moved(): return lax.ppermute(array, ('pipe', 'tensor'), pairs)]
    ppermute x18 -> x20, starting transfers between devices: 105 us -> 76.7 us  [moved(): return lax.ppermute(array, ('pipe', 'tensor'), pairs)]
    unnamed x23 -> x15, local copies, waits for them, and re-layouts: 7.6 us -> 2.33 us
    dynamic_slice x1 -> x2, local copies, waits for them, and re-layouts: 3.05 us -> 4.44 us  [fetched_chunk(): lax.dynamic_slice_in_dim(whole, start, step, axis=3)]
  transfers between devices with their start and end apart: 18 -> 20, of which waited for: 11 -> 9; matrix products, arithmetic and copies ran while one was open for 2% -> 2% of each run, Pallas kernels for 8% -> 10%
where the time goes in v2:
time: 197 us; the launch traced here: 196 us
  waiting for transfers between devices  80.4 us (41%)
  starting transfers between devices  76.7 us (39%)
  Pallas kernels  20.2 us (10%)
  blocking collectives  10 us (5%)
  local copies, waits for them, and re-layouts  7.04 us (4%)
  between operations  2.11 us (1%)
    ppermute x20, waiting for transfers between devices, moved(): return lax.ppermute(array, ('pipe', 'tensor'), pairs)  80.4 us
    ppermute x20, starting transfers between devices, moved(): return lax.ppermute(array, ('pipe', 'tensor'), pairs)  76.7 us
    pallas_call x4, Pallas kernels, backward(): pl.pallas_call(functools.partial(backward_kernel, parts), grid=(1,), in_s...  15.3 us
    psum x1, blocking collectives, on_device(): token_total = lax.psum(loss_tokens.astype(jnp.float32), 'dp')  10 us
    pallas_call x1, Pallas kernels, forward(): pl.pallas_call(forward_kernel, grid=(CHUNKS,), in_specs=[pl.BlockSpec((3,...  4.88 us
    dynamic_slice x2, local copies, waits for them, and re-layouts, fetched_chunk(): lax.dynamic_slice_in_dim(whole, start, step, axis=3)  4.44 us
  transfers between devices with their start and end apart: 20, of which 9 were waited for; matrix products, arithmetic and copies ran while one was open for 2% of the time, Pallas kernels for 10%

profile of v2, /device:TPU:1, one launch (start us, length us, event | category | flops | bytes accessed | tf_op | source)
XLA Modules:
  0.0 196.5 jit_solution(15717968142746530875)
XLA Ops:
  0.6 0.0 copy-start.2
  0.6 0.0 copy-start
  0.6 4.2 %collective-permute-start.8 = (bf16[1,256,2048]{2,1,0:T(8,128)(2,1)}, bf16[1,256,2048]{2,1,0:T(8,128)(2,1)}, u32[]{:S(2)}, u32[]{:S(2)}) collective-permute-start(bf16[1,256,2048]{2,1,0:T(8,128)(2,1)} %param.10), channel_id=1, source_target_pairs={{0,0},{4,20},{8,8},{12,28},{16,16},{20,4},{24,24},{28,12},{32,32},... | collective-permute-start | bytes 3145736 | tf_op jit(solution)/shard_map/swap_grad/ppermute | solution.py:132
  4.9 3.2 %constant_dynamic-slice_fusion = (bf16[3,1,64,512]{3,2,1,0:T(8,128)(2,1)}, bf16[3,1,64,512]{3,2,1,0:T(8,128)(2,1)}, bf16[3,1,64,512]{3,2,1,0:T(8,128)(2,1)}, bf1...) fusion(bf16[3,1,64,8192]{3,2,1,0:T(8,128)(2,1)} %param.8, ...), kind=kLoop, calls=%fused_computation | loop fusion | bytes 4718640 | tf_op jit(solution)/shard_map/dynamic_slice | solution.py:162
  8.1 5.6 %collective-permute-start.4 = (bf16[3,1,64,512]{3,2,1,0:T(8,128)(2,1)}, bf16[3,1,64,512]{3,2,1,0:T(8,128)(2,1)S(1)}, u32[]{:S(2)}, u32[]{:S(2)}) collective-permute-start(bf16[3,1,64,512]{3,2,1,0:T(8,128)(2,1)} %get-tuple-element.36), channel_id=1, source_target_pairs={{0,240},{4,244},{8,248},{12,252},{16,224},{20,228},{24,232},{28,23... | collective-permute-start | bytes 589832 | tf_op jit(solution)/shard_map/stash_0_0/ppermute | solution.py:132
  13.7 7.9 %collective-permute-start.5 = (bf16[3,1,64,512]{3,2,1,0:T(8,128)(2,1)}, bf16[3,1,64,512]{3,2,1,0:T(8,128)(2,1)}, u32[]{:S(2)}, u32[]{:S(2)}) collective-permute-start(bf16[3,1,64,512]{3,2,1,0:T(8,128)(2,1)} %get-tuple-element.35), channel_id=1, source_target_pairs={{0,244},{4,240},{8,252},{12,248},{16,228},{20,224},{24,236},{28,23... | collective-permute-start | bytes 589832 | tf_op jit(solution)/shard_map/stash_0_1/ppermute | solution.py:132
  21.7 5.0 %collective-permute-start.6 = (bf16[3,1,64,512]{3,2,1,0:T(8,128)(2,1)}, bf16[3,1,64,512]{3,2,1,0:T(8,128)(2,1)}, u32[]{:S(2)}, u32[]{:S(2)}) collective-permute-start(bf16[3,1,64,512]{3,2,1,0:T(8,128)(2,1)} %get-tuple-element.34), channel_id=1, source_target_pairs={{0,248},{4,252},{8,240},{12,244},{16,232},{20,236},{24,224},{28,22... | collective-permute-start | bytes 589832 | tf_op jit(solution)/shard_map/stash_0_2/ppermute | solution.py:132
  26.7 0.2 collective-permute-start.7
  27.6 10.0 %psum.7 = f32[1]{0:T(128)} all-reduce(f32[1]{0:T(128)S(6)} %convert_element_type.3), channel_id=1, replica_groups=mesh['pipe'=16,'tensor'=4,'dp'=4] {'dp'}, use_global_device_ids=true, to_apply=%region_0.0 | all-reduce | flops 1 | bytes 8 | tf_op jit(solution)/shard_map/psum | solution.py:172
  37.6 0.0 copy-done.2
  37.6 0.1 copy.11.column_ref
  37.7 0.0 copy-done
  37.8 0.0 copy-start.6
  37.8 0.0 copy-start.5
  37.8 0.0 copy-start.4
  37.8 0.0 copy-start.3
  37.8 4.9 %forward_heads.1 = bf16[1,256,2048]{2,1,0:T(8,128)(2,1)S(1)} custom-call(bf16[3,1,256,2048]{3,2,1,0:T(8,128)(2,1)S(1)} %copy-done, s32[1,256]{1,0:T(1,128)S(1)} %copy-done.2, s32[256,1]{1,0:T(8,128)S(1)} %copy.11.column_ref), custom_call_target="tpu_custom_call" | custom-call | flops 536870912 | bytes 4194304 | tf_op jit(solution)/shard_map/forward_heads/pallas_call | solution.py:47
  42.7 0.0 collective-permute-done.4.refs_0_
  42.7 3.0 %collective-permute-done.5.refs_1_ = bf16[3,1,64,512]{3,2,1,0:T(8,128)(2,1)} collective-permute-done((bf16[3,1,64,512]{3,2,1,0:T(8,128)(2,1)}, bf16[3,1,64,512]{3,2,1,0:T(8,128)(2,1)}, u32[]{:S(2)}, u32[]{:S(2)}) %collective-permute-start.5) | collective-permute-done | bytes 196640 | tf_op jit(solution)/shard_map/stash_0_1/ppermute | solution.py:132
  45.7 2.8 %collective-permute-done.6.refs_2_ = bf16[3,1,64,512]{3,2,1,0:T(8,128)(2,1)} collective-permute-done((bf16[3,1,64,512]{3,2,1,0:T(8,128)(2,1)}, bf16[3,1,64,512]{3,2,1,0:T(8,128)(2,1)}, u32[]{:S(2)}, u32[]{:S(2)}) %collective-permute-start.6) | collective-permute-done | bytes 196640 | tf_op jit(solution)/shard_map/stash_0_2/ppermute | solution.py:132
  48.5 5.4 %collective-permute-done.7.refs_3_ = bf16[3,1,64,512]{3,2,1,0:T(8,128)(2,1)} collective-permute-done((bf16[3,1,64,512]{3,2,1,0:T(8,128)(2,1)}, bf16[3,1,64,512]{3,2,1,0:T(8,128)(2,1)}, u32[]{:S(2)}, u32[]{:S(2)}) %collective-permute-start.7) | collective-permute-done | bytes 196640 | tf_op jit(solution)/shard_map/stash_0_3/ppermute | solution.py:132
  53.9 0.0 collective-permute-done.8
  53.9 1.9 collective-permute-start.9
  55.8 1.9 collective-permute-start.11
  57.7 0.0 copy-done.6
  57.7 5.0 %collective-permute-start = (bf16[3,1,64,512]{3,2,1,0:T(8,128)(2,1)S(1)}, bf16[3,1,64,512]{3,2,1,0:T(8,128)(2,1)S(1)}, u32[]{:S(2)}, u32[]{:S(2)}) collective-permute-start(bf16[3,1,64,512]{3,2,1,0:T(8,128)(2,1)S(1)} %copy-done.6), channel_id=1, source_target_pairs={{0,240},{4,244},{8,248},{12,252},{16,224},{20,228},{24,232},{28,23... | collective-permute-start | bytes 589832 | tf_op jit(solution)/shard_map/stash_1_0/ppermute | solution.py:132
  62.7 0.0 copy-done.5
  62.7 0.2 collective-permute-start.1
  62.9 0.0 copy-done.4
  62.9 0.4 collective-permute-start.2
  63.3 15.0 %collective-permute-done.refs_0_ = bf16[3,1,64,512]{3,2,1,0:T(8,128)(2,1)S(1)} collective-permute-done((bf16[3,1,64,512]{3,2,1,0:T(8,128)(2,1)S(1)}, bf16[3,1,64,512]{3,2,1,0:T(8,128)(2,1)S(1)}, u32[]{:S(2)}, u32[]{:S(2)}) %collective-permute-start) | collective-permute-done | bytes 196640 | tf_op jit(solution)/shard_map/stash_1_0/ppermute | solution.py:132
  78.3 0.0 copy-done.3
  78.3 21.2 %collective-permute-start.3 = (bf16[3,1,64,512]{3,2,1,0:T(8,128)(2,1)S(1)}, bf16[3,1,64,512]{3,2,1,0:T(8,128)(2,1)S(1)}, u32[]{:S(2)}, u32[]{:S(2)}) collective-permute-start(bf16[3,1,64,512]{3,2,1,0:T(8,128)(2,1)S(1)} %copy-done.3), channel_id=1, source_target_pairs={{0,252},{4,248},{8,244},{12,240},{16,236},{20,232},{24,228},{28,22... | collective-permute-start | bytes 589832 | tf_op jit(solution)/shard_map/stash_1_3/ppermute | solution.py:132
  99.5 0.0 collective-permute-done.1.refs_1_
  99.5 0.0 collective-permute-done.2.refs_2_
  99.5 7.2 %collective-permute-done.3.refs_3_ = bf16[3,1,64,512]{3,2,1,0:T(8,128)(2,1)S(1)} collective-permute-done((bf16[3,1,64,512]{3,2,1,0:T(8,128)(2,1)S(1)}, bf16[3,1,64,512]{3,2,1,0:T(8,128)(2,1)S(1)}, u32[]{:S(2)}, u32[]{:S(2)}) %collective-permute-start.3) | collective-permute-done | bytes 196640 | tf_op jit(solution)/shard_map/stash_1_3/ppermute | solution.py:132
  106.7 0.0 collective-permute-done.9
  106.7 1.9 collective-permute-start.10
  108.6 9.0 %collective-permute-start.16 = (bf16[3,1,64,512]{3,2,1,0:T(8,128)(2,1)}, bf16[3,1,64,512]{3,2,1,0:T(8,128)(2,1)S(1)}, u32[]{:S(2)}, u32[]{:S(2)}) collective-permute-start(bf16[3,1,64,512]{3,2,1,0:T(8,128)(2,1)} %get-tuple-element.32), channel_id=1, source_target_pairs={{0,240},{4,244},{8,248},{12,252},{16,224},{20,228},{24,232},{28,23... | collective-permute-start | bytes 589832 | tf_op jit(solution)/shard_map/stash_2_0/ppermute | solution.py:132
  117.6 0.0 collective-permute-start.17
  117.6 1.3 collective-permute-start.18
  119.0 0.0 collective-permute-done.11.refs_4_
  119.0 4.0 %collective-permute-start.19 = (bf16[3,1,64,512]{3,2,1,0:T(8,128)(2,1)}, bf16[3,1,64,512]{3,2,1,0:T(8,128)(2,1)S(1)}, u32[]{:S(2)}, u32[]{:S(2)}) collective-permute-start(bf16[3,1,64,512]{3,2,1,0:T(8,128)(2,1)} %get-tuple-element.30), channel_id=1, source_target_pairs={{0,252},{4,248},{8,244},{12,240},{16,236},{20,232},{24,228},{28,22... | collective-permute-start | bytes 589832 | tf_op jit(solution)/shard_map/stash_2_3/ppermute | solution.py:132
  123.0 0.0 copy-done.1
  123.0 0.1 copy.12.refs_6_
  123.8 4.7 %backward_0.1.refs_8_ = bf16[3,1,256,2048]{3,2,1,0:T(8,128)(2,1)} custom-call(bf16[3,1,64,512]{3,2,1,0:T(8,128)(2,1)S(1)} %collective-permute-done.4.refs_0_, bf16[3,1,64,512]{3,2,1,0:T(8,128)(2,1)} %collective-permute-done.5.refs_1_, bf16[3,1,64,512]{3,2,1,0:T(8,128)(2,1)} %collective-permute-done.6.refs_2_, ...), custom_call_target="tpu_custom_call" | custom-call | flops 335544320 | bytes 1835008 | tf_op jit(solution)/shard_map/backward_0/pallas_call | solution.py:108
  128.4 1.3 constant_dynamic-slice_fusion.4
  129.7 9.2 %collective-permute-done.16.refs_0_ = bf16[3,1,64,512]{3,2,1,0:T(8,128)(2,1)S(1)} collective-permute-done((bf16[3,1,64,512]{3,2,1,0:T(8,128)(2,1)}, bf16[3,1,64,512]{3,2,1,0:T(8,128)(2,1)S(1)}, u32[]{:S(2)}, u32[]{:S(2)}) %collective-permute-start.16) | collective-permute-done | bytes 196640 | tf_op jit(solution)/shard_map/stash_2_0/ppermute | solution.py:132
  138.9 4.2 %collective-permute-start.12 = (bf16[3,1,64,512]{3,2,1,0:T(8,128)(2,1)S(1)}, bf16[3,1,64,512]{3,2,1,0:T(8,128)(2,1)S(1)}, u32[]{:S(2)}, u32[]{:S(2)}) collective-permute-start(bf16[3,1,64,512]{3,2,1,0:T(8,128)(2,1)S(1)} %get-tuple-element.45), channel_id=1, source_target_pairs={{0,240},{4,244},{8,248},{12,252},{16,224},{20,228},{24,232},{28,23... | collective-permute-start | bytes 589832 | tf_op jit(solution)/shard_map/stash_3_0/ppermute | solution.py:132
  143.1 29.0 %collective-permute-done.17.refs_1_ = bf16[3,1,64,512]{3,2,1,0:T(8,128)(2,1)S(1)} collective-permute-done((bf16[3,1,64,512]{3,2,1,0:T(8,128)(2,1)}, bf16[3,1,64,512]{3,2,1,0:T(8,128)(2,1)S(1)}, u32[]{:S(2)}, u32[]{:S(2)}) %collective-permute-start.17) | collective-permute-done | bytes 196640 | tf_op jit(solution)/shard_map/stash_2_1/ppermute | solution.py:132
  172.1 0.2 collective-permute-start.13
  172.3 0.0 collective-permute-done.18.refs_2_
  172.3 0.0 collective-permute-start.14
  172.3 5.7 %collective-permute-done.19.refs_3_ = bf16[3,1,64,512]{3,2,1,0:T(8,128)(2,1)S(1)} collective-permute-done((bf16[3,1,64,512]{3,2,1,0:T(8,128)(2,1)}, bf16[3,1,64,512]{3,2,1,0:T(8,128)(2,1)S(1)}, u32[]{:S(2)}, u32[]{:S(2)}) %collective-permute-start.19) | collective-permute-done | bytes 196640 | tf_op jit(solution)/shard_map/stash_2_3/ppermute | solution.py:132
  178.0 2.4 %collective-permute-start.15 = (bf16[3,1,64,512]{3,2,1,0:T(8,128)(2,1)S(1)}, bf16[3,1,64,512]{3,2,1,0:T(8,128)(2,1)S(1)}, u32[]{:S(2)}, u32[]{:S(2)}) collective-permute-start(bf16[3,1,64,512]{3,2,1,0:T(8,128)(2,1)S(1)} %get-tuple-element.42), channel_id=1, source_target_pairs={{0,252},{4,248},{8,244},{12,240},{16,236},{20,232},{24,228},{28,22... | collective-permute-start | bytes 589832 | tf_op jit(solution)/shard_map/stash_3_3/ppermute | solution.py:132
  180.4 3.6 %backward_1.1.refs_8_ = bf16[3,1,256,2048]{3,2,1,0:T(8,128)(2,1)} custom-call(bf16[3,1,64,512]{3,2,1,0:T(8,128)(2,1)S(1)} %collective-permute-done.refs_0_, bf16[3,1,64,512]{3,2,1,0:T(8,128)(2,1)S(1)} %collective-permute-done.1.refs_1_, bf16[3,1,64,512]{3,2,1,0:T(8,128)(2,1)S(1)} %collective-permute-done.2.refs_2_, ...), custom_call_target="tpu_custom_call", output_to_operand_aliasing={{}: (8, {})} | custom-call | flops 335544320 | bytes 1835008 | tf_op jit(solution)/shard_map/backward_1/pallas_call | solution.py:108
  183.9 3.6 %backward_2.1.refs_8_ = bf16[3,1,256,2048]{3,2,1,0:T(8,128)(2,1)} custom-call(bf16[3,1,64,512]{3,2,1,0:T(8,128)(2,1)S(1)} %collective-permute-done.16.refs_0_, bf16[3,1,64,512]{3,2,1,0:T(8,128)(2,1)S(1)} %collective-permute-done.17.refs_1_, bf16[3,1,64,512]{3,2,1,0:T(8,128)(2,1)S(1)} %collective-permute-done.18.refs_2_, ...), custom_call_target="tpu_custom_call", output_to_operand_aliasing={{}: (8, {})} | custom-call | flops 335544320 | bytes 1835008 | tf_op jit(solution)/shard_map/backward_2/pallas_call | solution.py:108
  187.5 0.0 collective-permute-done.12.refs_0_
  187.5 0.0 collective-permute-done.13.refs_1_
  187.5 0.0 collective-permute-done.14.refs_2_
  187.5 3.1 %collective-permute-done.15.refs_3_ = bf16[3,1,64,512]{3,2,1,0:T(8,128)(2,1)S(1)} collective-permute-done((bf16[3,1,64,512]{3,2,1,0:T(8,128)(2,1)S(1)}, bf16[3,1,64,512]{3,2,1,0:T(8,128)(2,1)S(1)}, u32[]{:S(2)}, u32[]{:S(2)}) %collective-permute-start.15) | collective-permute-done | bytes 196640 | tf_op jit(solution)/shard_map/stash_3_3/ppermute | solution.py:132
  190.6 3.6 %backward_3.1 = bf16[3,1,256,2048]{3,2,1,0:T(8,128)(2,1)} custom-call(bf16[3,1,64,512]{3,2,1,0:T(8,128)(2,1)S(1)} %collective-permute-done.12.refs_0_, bf16[3,1,64,512]{3,2,1,0:T(8,128)(2,1)S(1)} %collective-permute-done.13.refs_1_, bf16[3,1,64,512]{3,2,1,0:T(8,128)(2,1)S(1)} %collective-permute-done.14.refs_2_, ...), custom_call_target="tpu_custom_call", output_to_operand_aliasing={{}: (8, {})} | custom-call | flops 335544320 | bytes 1835008 | tf_op jit(solution)/shard_map/backward_3/pallas_call | solution.py:108
  194.2 0.0 collective-permute-done.10
  194.2 2.3 %copy.21 = bf16[1,256,2048]{2,1,0:T(8,128)(2,1)} copy(bf16[1,256,2048]{2,1,0:T(8,128)(2,1)} %collective-permute-done.10) | data formatting | bytes 2097152
  (1 shorter events, 0.0 us)
Async XLA Ops:
  0.6 37.0 %copy-start.2 = (s32[1,256]{1,0:T(1,128)S(1)}, s32[1,256]{1,0:T(1,128)}, u32[]{:S(2)}) copy-start(s32[1,256]{1,0:T(1,128)} %row_ref.1) | copy-start | bytes 3076
  0.6 37.1 %copy-start = (bf16[3,1,256,2048]{3,2,1,0:T(8,128)(2,1)S(1)}, bf16[3,1,256,2048]{3,2,1,0:T(8,128)(2,1)}, u32[]{:S(2)}) copy-start(bf16[3,1,256,2048]{3,2,1,0:T(8,128)(2,1)} %qkv_ref.1) | copy-start | bytes 9437188
  0.6 53.2 %collective-permute-start.8 = (bf16[1,256,2048]{2,1,0:T(8,128)(2,1)}, bf16[1,256,2048]{2,1,0:T(8,128)(2,1)}, u32[]{:S(2)}, u32[]{:S(2)}) collective-permute-start(bf16[1,256,2048]{2,1,0:T(8,128)(2,1)} %param.10), channel_id=1, source_target_pairs={{0,0},{4,20},{8,8},{12,28},{16,16},{20,4},{24,24},{28,12},{32,32},... | collective-permute-start | bytes 3145736 | tf_op jit(solution)/shard_map/swap_grad/ppermute | solution.py:132
  8.1 114.9 %copy-start.1 = (s32[1,256]{1,0:T(1,128)S(1)}, s32[1,256]{1,0:T(1,128)}, u32[]{:S(2)}) copy-start(s32[1,256]{1,0:T(1,128)} %refs_5_.7) | copy-start | bytes 3076
  8.1 34.6 %collective-permute-start.4 = (bf16[3,1,64,512]{3,2,1,0:T(8,128)(2,1)}, bf16[3,1,64,512]{3,2,1,0:T(8,128)(2,1)S(1)}, u32[]{:S(2)}, u32[]{:S(2)}) collective-permute-start(bf16[3,1,64,512]{3,2,1,0:T(8,128)(2,1)} %get-tuple-element.36), channel_id=1, source_target_pairs={{0,240},{4,244},{8,248},{12,252},{16,224},{20,228},{24,232},{28,23... | collective-permute-start | bytes 589832 | tf_op jit(solution)/shard_map/stash_0_0/ppermute | solution.py:132
  13.7 32.0 %collective-permute-start.5 = (bf16[3,1,64,512]{3,2,1,0:T(8,128)(2,1)}, bf16[3,1,64,512]{3,2,1,0:T(8,128)(2,1)}, u32[]{:S(2)}, u32[]{:S(2)}) collective-permute-start(bf16[3,1,64,512]{3,2,1,0:T(8,128)(2,1)} %get-tuple-element.35), channel_id=1, source_target_pairs={{0,244},{4,240},{8,252},{12,248},{16,228},{20,224},{24,236},{28,23... | collective-permute-start | bytes 589832 | tf_op jit(solution)/shard_map/stash_0_1/ppermute | solution.py:132
  21.7 26.8 %collective-permute-start.6 = (bf16[3,1,64,512]{3,2,1,0:T(8,128)(2,1)}, bf16[3,1,64,512]{3,2,1,0:T(8,128)(2,1)}, u32[]{:S(2)}, u32[]{:S(2)}) collective-permute-start(bf16[3,1,64,512]{3,2,1,0:T(8,128)(2,1)} %get-tuple-element.34), channel_id=1, source_target_pairs={{0,248},{4,252},{8,240},{12,244},{16,232},{20,236},{24,224},{28,22... | collective-permute-start | bytes 589832 | tf_op jit(solution)/shard_map/stash_0_2/ppermute | solution.py:132
  26.7 27.2 %collective-permute-start.7 = (bf16[3,1,64,512]{3,2,1,0:T(8,128)(2,1)}, bf16[3,1,64,512]{3,2,1,0:T(8,128)(2,1)}, u32[]{:S(2)}, u32[]{:S(2)}) collective-permute-start(bf16[3,1,64,512]{3,2,1,0:T(8,128)(2,1)} %get-tuple-element.33), channel_id=1, source_target_pairs={{0,252},{4,248},{8,244},{12,240},{16,236},{20,232},{24,228},{28,22... | collective-permute-start | bytes 589832 | tf_op jit(solution)/shard_map/stash_0_3/ppermute | solution.py:132
  37.8 19.9 %copy-start.6 = (bf16[3,1,64,512]{3,2,1,0:T(8,128)(2,1)S(1)}, bf16[3,1,64,512]{3,2,1,0:T(8,128)(2,1)}, u32[]{:S(2)}) copy-start(bf16[3,1,64,512]{3,2,1,0:T(8,128)(2,1)} %get-tuple-element.40) | copy-start | bytes 589828
  37.8 25.0 %copy-start.5 = (bf16[3,1,64,512]{3,2,1,0:T(8,128)(2,1)S(1)}, bf16[3,1,64,512]{3,2,1,0:T(8,128)(2,1)}, u32[]{:S(2)}) copy-start(bf16[3,1,64,512]{3,2,1,0:T(8,128)(2,1)} %get-tuple-element.39) | copy-start | bytes 589828
  37.8 25.1 %copy-start.4 = (bf16[3,1,64,512]{3,2,1,0:T(8,128)(2,1)S(1)}, bf16[3,1,64,512]{3,2,1,0:T(8,128)(2,1)}, u32[]{:S(2)}) copy-start(bf16[3,1,64,512]{3,2,1,0:T(8,128)(2,1)} %get-tuple-element.38) | copy-start | bytes 589828
  37.8 40.5 %copy-start.3 = (bf16[3,1,64,512]{3,2,1,0:T(8,128)(2,1)S(1)}, bf16[3,1,64,512]{3,2,1,0:T(8,128)(2,1)}, u32[]{:S(2)}) copy-start(bf16[3,1,64,512]{3,2,1,0:T(8,128)(2,1)} %get-tuple-element.37) | copy-start | bytes 589828
  53.9 52.8 %collective-permute-start.9 = (bf16[1,256,2048]{2,1,0:T(8,128)(2,1)S(1)}, bf16[1,256,2048]{2,1,0:T(8,128)(2,1)}, u32[]{:S(2)}, u32[]{:S(2)}) collective-permute-start(bf16[1,256,2048]{2,1,0:T(8,128)(2,1)S(1)} %forward_heads.1), channel_id=1, source_target_pairs={{0,0},{4,20},{8,8},{12,28},{16,16},{20,4},{24,24},{28,12},{32,32},... | collective-permute-start | bytes 3145736 | tf_op jit(solution)/shard_map/swap_out/ppermute | solution.py:132
  55.8 63.1 %collective-permute-start.11 = (bf16[1,256,2048]{2,1,0:T(8,128)(2,1)}, bf16[1,256,2048]{2,1,0:T(8,128)(2,1)S(1)}, u32[]{:S(2)}, u32[]{:S(2)}) collective-permute-start(bf16[1,256,2048]{2,1,0:T(8,128)(2,1)} %collective-permute-done.8), channel_id=1, source_target_pairs={{0,240},{4,4},{8,248},{12,12},{16,0},{20,244},{24,8},{28,252},{32,... | collective-permute-start | bytes 3145736 | tf_op jit(solution)/shard_map/step_grad/ppermute | solution.py:132
  57.7 20.6 %collective-permute-start = (bf16[3,1,64,512]{3,2,1,0:T(8,128)(2,1)S(1)}, bf16[3,1,64,512]{3,2,1,0:T(8,128)(2,1)S(1)}, u32[]{:S(2)}, u32[]{:S(2)}) collective-permute-start(bf16[3,1,64,512]{3,2,1,0:T(8,128)(2,1)S(1)} %copy-done.6), channel_id=1, source_target_pairs={{0,240},{4,244},{8,248},{12,252},{16,224},{20,228},{24,232},{28,23... | collective-permute-start | bytes 589832 | tf_op jit(solution)/shard_map/stash_1_0/ppermute | solution.py:132
  62.7 36.8 %collective-permute-start.1 = (bf16[3,1,64,512]{3,2,1,0:T(8,128)(2,1)S(1)}, bf16[3,1,64,512]{3,2,1,0:T(8,128)(2,1)S(1)}, u32[]{:S(2)}, u32[]{:S(2)}) collective-permute-start(bf16[3,1,64,512]{3,2,1,0:T(8,128)(2,1)S(1)} %copy-done.5), channel_id=1, source_target_pairs={{0,244},{4,240},{8,252},{12,248},{16,228},{20,224},{24,236},{28,23... | collective-permute-start | bytes 589832 | tf_op jit(solution)/shard_map/stash_1_1/ppermute | solution.py:132
  62.9 36.6 %collective-permute-start.2 = (bf16[3,1,64,512]{3,2,1,0:T(8,128)(2,1)S(1)}, bf16[3,1,64,512]{3,2,1,0:T(8,128)(2,1)S(1)}, u32[]{:S(2)}, u32[]{:S(2)}) collective-permute-start(bf16[3,1,64,512]{3,2,1,0:T(8,128)(2,1)S(1)} %copy-done.4), channel_id=1, source_target_pairs={{0,248},{4,252},{8,240},{12,244},{16,232},{20,236},{24,224},{28,22... | collective-permute-start | bytes 589832 | tf_op jit(solution)/shard_map/stash_1_2/ppermute | solution.py:132
  78.3 28.4 %collective-permute-start.3 = (bf16[3,1,64,512]{3,2,1,0:T(8,128)(2,1)S(1)}, bf16[3,1,64,512]{3,2,1,0:T(8,128)(2,1)S(1)}, u32[]{:S(2)}, u32[]{:S(2)}) collective-permute-start(bf16[3,1,64,512]{3,2,1,0:T(8,128)(2,1)S(1)} %copy-done.3), channel_id=1, source_target_pairs={{0,252},{4,248},{8,244},{12,240},{16,236},{20,232},{24,228},{28,22... | collective-permute-start | bytes 589832 | tf_op jit(solution)/shard_map/stash_1_3/ppermute | solution.py:132
  106.7 87.4 %collective-permute-start.10 = (bf16[1,256,2048]{2,1,0:T(8,128)(2,1)}, bf16[1,256,2048]{2,1,0:T(8,128)(2,1)}, u32[]{:S(2)}, u32[]{:S(2)}) collective-permute-start(bf16[1,256,2048]{2,1,0:T(8,128)(2,1)} %collective-permute-done.9), channel_id=1, source_target_pairs={{0,16},{4,36},{8,24},{12,44},{16,32},{20,20},{24,40},{28,28},{32,4... | collective-permute-start | bytes 3145736 | tf_op jit(solution)/shard_map/step_out/ppermute | solution.py:132
  108.6 30.2 %collective-permute-start.16 = (bf16[3,1,64,512]{3,2,1,0:T(8,128)(2,1)}, bf16[3,1,64,512]{3,2,1,0:T(8,128)(2,1)S(1)}, u32[]{:S(2)}, u32[]{:S(2)}) collective-permute-start(bf16[3,1,64,512]{3,2,1,0:T(8,128)(2,1)} %get-tuple-element.32), channel_id=1, source_target_pairs={{0,240},{4,244},{8,248},{12,252},{16,224},{20,228},{24,232},{28,23... | collective-permute-start | bytes 589832 | tf_op jit(solution)/shard_map/stash_2_0/ppermute | solution.py:132
  117.6 54.5 %collective-permute-start.17 = (bf16[3,1,64,512]{3,2,1,0:T(8,128)(2,1)}, bf16[3,1,64,512]{3,2,1,0:T(8,128)(2,1)S(1)}, u32[]{:S(2)}, u32[]{:S(2)}) collective-permute-start(bf16[3,1,64,512]{3,2,1,0:T(8,128)(2,1)} %get-tuple-element.31), channel_id=1, source_target_pairs={{0,244},{4,240},{8,252},{12,248},{16,228},{20,224},{24,236},{28,23... | collective-permute-start | bytes 589832 | tf_op jit(solution)/shard_map/stash_2_1/ppermute | solution.py:132
  117.6 54.6 %collective-permute-start.18 = (bf16[3,1,64,512]{3,2,1,0:T(8,128)(2,1)}, bf16[3,1,64,512]{3,2,1,0:T(8,128)(2,1)S(1)}, u32[]{:S(2)}, u32[]{:S(2)}) collective-permute-start(bf16[3,1,64,512]{3,2,1,0:T(8,128)(2,1)} %get-tuple-element.41), channel_id=1, source_target_pairs={{0,248},{4,252},{8,240},{12,244},{16,232},{20,236},{24,224},{28,22... | collective-permute-start | bytes 589832 | tf_op jit(solution)/shard_map/stash_2_2/ppermute | solution.py:132
  119.0 59.0 %collective-permute-start.19 = (bf16[3,1,64,512]{3,2,1,0:T(8,128)(2,1)}, bf16[3,1,64,512]{3,2,1,0:T(8,128)(2,1)S(1)}, u32[]{:S(2)}, u32[]{:S(2)}) collective-permute-start(bf16[3,1,64,512]{3,2,1,0:T(8,128)(2,1)} %get-tuple-element.30), channel_id=1, source_target_pairs={{0,252},{4,248},{8,244},{12,240},{16,236},{20,232},{24,228},{28,22... | collective-permute-start | bytes 589832 | tf_op jit(solution)/shard_map/stash_2_3/ppermute | solution.py:132
  138.9 48.6 %collective-permute-start.12 = (bf16[3,1,64,512]{3,2,1,0:T(8,128)(2,1)S(1)}, bf16[3,1,64,512]{3,2,1,0:T(8,128)(2,1)S(1)}, u32[]{:S(2)}, u32[]{:S(2)}) collective-permute-start(bf16[3,1,64,512]{3,2,1,0:T(8,128)(2,1)S(1)} %get-tuple-element.45), channel_id=1, source_target_pairs={{0,240},{4,244},{8,248},{12,252},{16,224},{20,228},{24,232},{28,23... | collective-permute-start | bytes 589832 | tf_op jit(solution)/shard_map/stash_3_0/ppermute | solution.py:132
  172.1 15.4 %collective-permute-start.13 = (bf16[3,1,64,512]{3,2,1,0:T(8,128)(2,1)S(1)}, bf16[3,1,64,512]{3,2,1,0:T(8,128)(2,1)S(1)}, u32[]{:S(2)}, u32[]{:S(2)}) collective-permute-start(bf16[3,1,64,512]{3,2,1,0:T(8,128)(2,1)S(1)} %get-tuple-element.44), channel_id=1, source_target_pairs={{0,244},{4,240},{8,252},{12,248},{16,228},{20,224},{24,236},{28,23... | collective-permute-start | bytes 589832 | tf_op jit(solution)/shard_map/stash_3_1/ppermute | solution.py:132
  172.3 15.2 %collective-permute-start.14 = (bf16[3,1,64,512]{3,2,1,0:T(8,128)(2,1)S(1)}, bf16[3,1,64,512]{3,2,1,0:T(8,128)(2,1)S(1)}, u32[]{:S(2)}, u32[]{:S(2)}) collective-permute-start(bf16[3,1,64,512]{3,2,1,0:T(8,128)(2,1)S(1)} %get-tuple-element.43), channel_id=1, source_target_pairs={{0,248},{4,252},{8,240},{12,244},{16,232},{20,236},{24,224},{28,22... | collective-permute-start | bytes 589832 | tf_op jit(solution)/shard_map/stash_3_2/ppermute | solution.py:132
  178.0 12.6 %collective-permute-start.15 = (bf16[3,1,64,512]{3,2,1,0:T(8,128)(2,1)S(1)}, bf16[3,1,64,512]{3,2,1,0:T(8,128)(2,1)S(1)}, u32[]{:S(2)}, u32[]{:S(2)}) collective-permute-start(bf16[3,1,64,512]{3,2,1,0:T(8,128)(2,1)S(1)} %get-tuple-element.42), channel_id=1, source_target_pairs={{0,252},{4,248},{8,244},{12,240},{16,236},{20,232},{24,228},{28,22... | collective-permute-start | bytes 589832 | tf_op jit(solution)/shard_map/stash_3_3/ppermute | solution.py:132

commit v3 on v2

--- a/solution.py
+++ b/solution.py
@@ -65,7 +65,7 @@
 
 def backward_kernel(parts, *refs):
     pieces, refs = refs[:parts], refs[parts:]
-    upstream_ref, row_ref, column_ref, factor_ref = refs[:4]
+    direct_ref, around_ref, row_ref, column_ref, factor_ref = refs[:5]
     out_ref, stash = refs[-2:]
     mine = lax.axis_index("tensor")
     rows = pieces[0].shape[2]
@@ -74,10 +74,11 @@
         stash[:, pl.ds(start, rows), :] = pieces[k][:, 0]
     outside = outside_of(row_ref, column_ref)
     factor = factor_ref[0]
-    for start in range(0, upstream_ref.shape[2], HEAD_DIM):
+    around = took_both(-1)
+    for start in range(0, direct_ref.shape[2], HEAD_DIM):
         head = slice(start, start + HEAD_DIM)
         queries, keys, values = stash[0, :, head], stash[1, :, head], stash[2, :, head]
-        upstream = upstream_ref[0, :, head]
+        upstream = jnp.where(around, around_ref[0, :, head], direct_ref[0, :, head])
         probs = probabilities(queries, keys, outside)
         grad_value = product(probs.astype(jnp.bfloat16), upstream, TN)
         grad_probs = product(upstream, values, NT)
@@ -89,12 +90,16 @@
 
 
 def backward(chunk, pieces, upstream, row, column, factor, earlier):
-    _, length, width = upstream.shape
+    _, length, width = upstream[0].shape
     step = width // CHUNKS
     parts = len(pieces)
-    whole = pl.BlockSpec(memory_space=pltpu.VMEM)
-    operands = [*pieces, upstream, row, column, factor]
-    in_specs = [whole] * parts + [
+    piece_specs = [
+        pl.BlockSpec((3, 1, p.shape[2], step), lambda i, c=chunk if p.shape[3] > step else 0: (0, 0, 0, c))
+        for p in pieces
+    ]
+    operands = [*pieces, *upstream, row, column, factor]
+    in_specs = piece_specs + [
+        pl.BlockSpec((1, length, step), lambda i: (0, 0, chunk)),
         pl.BlockSpec((1, length, step), lambda i: (0, 0, chunk)),
         pl.BlockSpec((1, length), lambda i: (0, 0)),
         pl.BlockSpec((length, 1), lambda i: (0, 0)),
@@ -137,19 +142,34 @@
     return moved(piece, lambda p, t: (last - p, t ^ k))
 
 
-def swapped(array):
-    return moved(array, lambda p, t: (p ^ (t & 1), t))
-
-
-def stepped(array, by):
-    kept = 1 if by > 0 else 0
-
-    def target(p, t):
-        if t & 1 == 0:
-            return p + by, t
-        return (p if p & 1 == kept else p + 2 * by), t
-
-    return moved(array, target)
+def first_hop(array, by):
+    return moved(array, lambda p, t: (p ^ 1 if t & 1 else p + by, t))
+
+
+def second_hop(array, by):
+    sections, tensors = lax.axis_size("pipe"), lax.axis_size("tensor")
+    pairs = []
+    for p in range(0 if by > 0 else 1, sections, 2):
+        for t in range(1, tensors, 2):
+            pairs.append((p * tensors + t, (p + 2 * by) % sections * tensors + t))
+    return lax.ppermute(array, ("pipe", "tensor"), pairs)
+
+
+def took_both(by):
+    kept = 0 if by > 0 else 1
+    return jnp.logical_and(lax.axis_index("pipe") & 1 == kept, lax.axis_index("tensor") & 1 == 1)
+
+
+def odd_pairs(kind):
+    sections, tensors = lax.axis_size("pipe"), lax.axis_size("tensor")
+    pairs = []
+    for p in range(sections):
+        for t in range(tensors):
+            if t & 1 and kind == "swap":
+                pairs.append((p * tensors + t, (p ^ 1) * tensors + t))
+            if kind == "step" and (t & 1 == 0 or p & 1 == 0):
+                pairs.append((p * tensors + t, (p + 1 + (t & 1)) % sections * tensors + t))
+    return pairs
 
 
 def on_device(fwd_qkv, fwd_segments, parked, bwd_segments, grad_out, loss_tokens):
@@ -157,42 +177,47 @@
     tensors = lax.axis_size("tensor")
     mine = lax.axis_index("tensor")
     step = width // CHUNKS
-    def fetched_chunk(whole, chunk):
-        starts = [(mine ^ k) * width + chunk * step for k in range(tensors)]
-        cut = [lax.dynamic_slice_in_dim(whole, start, step, axis=3) for start in starts]
-        fetches = []
-        for k, piece in enumerate(cut):
-            with jax.named_scope(f"stash_{chunk}_{k}"):
-                fetches.append(fetched(piece, k))
-        return fetches
-
-    pieces = [fetched_chunk(parked, chunk) for chunk in range(3)]
-    with jax.named_scope("swap_grad"):
-        swapped_grad = swapped(grad_out)
+
+    def fetched_part(whole, k, first, count):
+        start = (mine ^ k) * width + first * step
+        piece = lax.dynamic_slice_in_dim(whole, start, count * step, axis=3)
+        with jax.named_scope(f"stash_{k}_{first}"):
+            return fetched(piece, k)
+
+    with jax.named_scope("step_grad_1"):
+        upstream_direct = first_hop(grad_out, -1)
+    early = [fetched_part(parked, k, 0, CHUNKS) for k in range(2)]
+    with jax.named_scope("step_grad_2"):
+        upstream_around = second_hop(upstream_direct, -1)
+    early[0], fwd_qkv, loss_tokens, parked = lax.optimization_barrier(
+        (early[0], fwd_qkv, loss_tokens, parked)
+    )
     token_total = lax.psum(loss_tokens.astype(jnp.float32), "dp")
     with jax.named_scope("forward_heads"):
         forward_out = forward(fwd_qkv, fwd_segments, fwd_segments.reshape(length, 1))
-    pieces[0], swapped_grad, token_total, forward_out = lax.optimization_barrier(
-        (pieces[0], swapped_grad, token_total, forward_out)
-    )
-    with jax.named_scope("step_grad"):
-        upstream = stepped(swapped_grad, -1)
+    token_total, forward_out = lax.optimization_barrier((token_total, forward_out))
     factor = jnp.float32(lax.axis_size("dp") * length) / token_total
     with jax.named_scope("swap_out"):
-        swapped_out = swapped(forward_out)
-    pieces[1], swapped_out = lax.optimization_barrier((pieces[1], swapped_out))
+        swapped_out = lax.ppermute(forward_out, ("pipe", "tensor"), odd_pairs("swap"))
+    early[1], upstream_around, parked = lax.optimization_barrier(
+        (early[1], upstream_around, parked)
+    )
+    late = [[fetched_part(parked, k, c, 1) for k in range(2, tensors)] for c in range(4)]
+    upstream = (upstream_direct, upstream_around)
+    odd = lax.axis_index("tensor") & 1 == 1
+    stepping = jnp.where(odd, swapped_out, forward_out)
+    late[:3], stepping = lax.optimization_barrier((late[:3], stepping))
     column = bwd_segments.reshape(length, 1)
     grads = None
     for chunk in range(CHUNKS):
         with jax.named_scope(f"backward_{chunk}"):
             grads = backward(
-                chunk, pieces[chunk], upstream, bwd_segments, column, factor, grads
+                chunk, early + late[chunk], upstream, bwd_segments, column, factor, grads
             )
-        if len(pieces) < CHUNKS:
-            parked, grads = lax.optimization_barrier((parked, grads))
-            pieces.append(fetched_chunk(parked, len(pieces)))
     with jax.named_scope("step_out"):
-        received = stepped(swapped_out, 1)
+        stepped_out = lax.ppermute(stepping, ("pipe", "tensor"), odd_pairs("step"))
+    last = lax.axis_index("pipe") & 1 == 1
+    received = jnp.where(jnp.logical_and(odd, last), swapped_out, stepped_out)
     return (received, grads)
 
 

time: 197 us -> 191 us (0.970)
  waiting for transfers between devices: 80.4 us -> 56.1 us
  local copies, waits for them, and re-layouts: 7.04 us -> 11.9 us
  other arithmetic: 0 us -> 4.61 us
  Pallas kernels: 20.2 us -> 23.7 us
  starting transfers between devices: 76.7 us -> 80.1 us
    ppermute x20 -> x11, waiting for transfers between devices: 80.4 us -> 56 us  [moved(): return lax.ppermute(array, ('pipe', 'tensor'), pairs)]
    select_n x0 -> x2, other arithmetic: none -> 4.61 us  [the longest x1 2.31 us: on_device(): stepping = jnp.where(odd, swapped_out, forward_out)]
    ppermute x0 -> x3, starting transfers between devices: none -> 4.54 us  [the longest x1 1.91 us: on_device(): lax.ppermute(forward_out, ('pipe', 'tensor'), odd_pairs('swap'))]
    unnamed x15 -> x22, local copies, waits for them, and re-layouts: 2.33 us -> 6.44 us
    pallas_call x4, Pallas kernels: 15.3 us -> 18.2 us  [backward(): pl.pallas_call(functools.partial(backward_kernel, parts), grid=(1,), in_s...]
    ppermute x20 -> x11, starting transfers between devices: 76.7 us -> 75.5 us  [moved(): return lax.ppermute(array, ('pipe', 'tensor'), pairs)]
  transfers between devices with their start and end apart: 20 -> 14, of which waited for: 9 -> 7; matrix products, arithmetic and copies ran while one was open for 2% -> 4% of each run, Pallas kernels for 10% -> 13%
where the time goes in v3:
time: 191 us; the launch traced here: 189 us
  starting transfers between devices  80.1 us (42%)
  waiting for transfers between devices  56.1 us (29%)
  Pallas kernels  23.7 us (12%)
  local copies, waits for them, and re-layouts  11.9 us (6%)
  blocking collectives  10.1 us (5%)
  other arithmetic  4.61 us (2%)
  between operations  2.12 us (1%)
    ppermute x11, starting transfers between devices, moved(): return lax.ppermute(array, ('pipe', 'tensor'), pairs)  75.5 us
    ppermute x11, waiting for transfers between devices, moved(): return lax.ppermute(array, ('pipe', 'tensor'), pairs)  56 us
    pallas_call x4, Pallas kernels, backward(): pl.pallas_call(functools.partial(backward_kernel, parts), grid=(1,), in_s...  18.2 us
    psum x1, blocking collectives, on_device(): token_total = lax.psum(loss_tokens.astype(jnp.float32), 'dp')  10.1 us
    unnamed x22, local copies, waits for them, and re-layouts  6.44 us
    pallas_call x1, Pallas kernels, forward(): pl.pallas_call(forward_kernel, grid=(CHUNKS,), in_specs=[pl.BlockSpec((3,...  5.56 us
    dynamic_slice x2, local copies, waits for them, and re-layouts, fetched_part(): piece = lax.dynamic_slice_in_dim(whole, start, count * step, axis=3)  5.23 us
  transfers between devices with their start and end apart: 14, of which 7 were waited for; matrix products, arithmetic and copies ran while one was open for 4% of the time, Pallas kernels for 13%

profile of v3, /device:TPU:1, one launch (start us, length us, event | category | flops | bytes accessed | tf_op | source)
XLA Modules:
  0.0 188.6 jit_solution(16387192723470983160)
XLA Ops:
  0.6 0.0 copy-start.10
  0.6 2.1 %collective-permute-start.3 = (bf16[1,256,2048]{2,1,0:T(8,128)(2,1)}, bf16[1,256,2048]{2,1,0:T(8,128)(2,1)S(1)}, u32[]{:S(2)}, u32[]{:S(2)}) collective-permute-start(bf16[1,256,2048]{2,1,0:T(8,128)(2,1)} %param.10), channel_id=1, source_target_pairs={{0,240},{4,20},{8,248},{12,28},{16,0},{20,4},{24,8},{28,12},{32,16... | collective-permute-start | bytes 3145736 | tf_op jit(solution)/shard_map/step_grad_1/ppermute | solution.py:137
  2.8 2.7 %constant_dynamic-slice_fusion.8 = (bf16[3,1,64,2048]{3,2,1,0:T(8,128)(2,1)}, bf16[3,1,64,2048]{3,2,1,0:T(8,128)(2,1)}) fusion(bf16[3,1,64,8192]{3,2,1,0:T(8,128)(2,1)} %param.8, s32[]{:T(128)S(6)} %select_n.46, s32[]{:T(128)S(6)} %select_n.45), kind=kLoop, calls=%fused_computation.10 | loop fusion | bytes 3145736 | tf_op jit(solution)/shard_map/dynamic_slice | solution.py:183
  5.4 5.5 %collective-permute-start = (bf16[3,1,64,2048]{3,2,1,0:T(8,128)(2,1)}, bf16[3,1,64,2048]{3,2,1,0:T(8,128)(2,1)S(1)}, u32[]{:S(2)}, u32[]{:S(2)}) collective-permute-start(bf16[3,1,64,2048]{3,2,1,0:T(8,128)(2,1)} %get-tuple-element.43), channel_id=1, source_target_pairs={{0,240},{4,244},{8,248},{12,252},{16,224},{20,228},{24,232},{28,23... | collective-permute-start | bytes 2359304 | tf_op jit(solution)/shard_map/stash_0_0/ppermute | solution.py:137
  11.0 20.8 %collective-permute-done.3.refs_4_ = bf16[1,256,2048]{2,1,0:T(8,128)(2,1)S(1)} collective-permute-done((bf16[1,256,2048]{2,1,0:T(8,128)(2,1)}, bf16[1,256,2048]{2,1,0:T(8,128)(2,1)S(1)}, u32[]{:S(2)}, u32[]{:S(2)}) %collective-permute-start.3) | collective-permute-done | bytes 1048608 | tf_op jit(solution)/shard_map/step_grad_1/ppermute | solution.py:137
  31.8 0.7 collective-permute-start.4
  32.5 19.4 %collective-permute-start.2 = (bf16[3,1,64,2048]{3,2,1,0:T(8,128)(2,1)}, bf16[3,1,64,2048]{3,2,1,0:T(8,128)(2,1)}, u32[]{:S(2)}, u32[]{:S(2)}) collective-permute-start(bf16[3,1,64,2048]{3,2,1,0:T(8,128)(2,1)} %get-tuple-element.42), channel_id=1, source_target_pairs={{0,244},{4,240},{8,252},{12,248},{16,228},{20,224},{24,236},{28,23... | collective-permute-start | bytes 2359304 | tf_op jit(solution)/shard_map/stash_1_0/ppermute | solution.py:137
  52.5 10.1 %psum.7 = f32[1]{0:T(128)} all-reduce(f32[1]{0:T(128)S(6)} %convert_element_type.3), channel_id=1, replica_groups=mesh['pipe'=16,'tensor'=4,'dp'=4] {'dp'}, use_global_device_ids=true, to_apply=%region_0.0 | all-reduce | flops 1 | bytes 8 | tf_op jit(solution)/shard_map/psum | solution.py:195
  62.6 0.0 copy-done.10
  62.6 0.1 copy.11.column_ref
  62.7 0.0 collective-permute-done.refs_0_
  62.7 0.0 copy-start
  62.7 1.9 copy-done
  64.6 5.6 %forward_heads.1 = bf16[1,256,2048]{2,1,0:T(8,128)(2,1)} custom-call(bf16[3,1,256,2048]{3,2,1,0:T(8,128)(2,1)S(1)} %copy-done, s32[1,256]{1,0:T(1,128)S(1)} %copy-done.10, s32[256,1]{1,0:T(8,128)S(1)} %copy.11.column_ref), custom_call_target="tpu_custom_call" | custom-call | flops 536870912 | bytes 4194304 | tf_op jit(solution)/shard_map/forward_heads/pallas_call | solution.py:47
  70.2 1.9 %collective-permute-start.1 = (bf16[1,256,2048]{2,1,0:T(8,128)(2,1)}, bf16[1,256,2048]{2,1,0:T(8,128)(2,1)}, u32[]{:S(2)}, u32[]{:S(2)}) collective-permute-start(bf16[1,256,2048]{2,1,0:T(8,128)(2,1)} %forward_heads.1), channel_id=1, source_target_pairs={{4,20},{12,28},{20,4},{28,12},{36,52},{44,60},{52,36},{60,44},{68,... | collective-permute-start | bytes 3145736 | tf_op jit(solution)/shard_map/swap_out/ppermute | solution.py:201
  72.1 0.0 copy-start.9
  72.2 19.7 %collective-permute-done.2.refs_1_ = bf16[3,1,64,2048]{3,2,1,0:T(8,128)(2,1)} collective-permute-done((bf16[3,1,64,2048]{3,2,1,0:T(8,128)(2,1)}, bf16[3,1,64,2048]{3,2,1,0:T(8,128)(2,1)}, u32[]{:S(2)}, u32[]{:S(2)}) %collective-permute-start.2) | collective-permute-done | bytes 786464 | tf_op jit(solution)/shard_map/stash_1_0/ppermute | solution.py:137
  91.9 0.0 collective-permute-done.4.refs_5_
  91.9 2.5 %constant_dynamic-slice_fusion = (bf16[3,1,64,512]{3,2,1,0:T(8,128)(2,1)}, bf16[3,1,64,512]{3,2,1,0:T(8,128)(2,1)}, bf16[3,1,64,512]{3,2,1,0:T(8,128)(2,1)}, bf1...) fusion(bf16[3,1,64,8192]{3,2,1,0:T(8,128)(2,1)} %param.8, ...), kind=kLoop, calls=%fused_computation.2 | loop fusion | bytes 3145760 | tf_op jit(solution)/shard_map/dynamic_slice | solution.py:183
  94.4 25.2 %collective-permute-start.10 = (bf16[3,1,64,512]{3,2,1,0:T(8,128)(2,1)}, bf16[3,1,64,512]{3,2,1,0:T(8,128)(2,1)S(1)}, u32[]{:S(2)}, u32[]{:S(2)}) collective-permute-start(bf16[3,1,64,512]{3,2,1,0:T(8,128)(2,1)} %get-tuple-element.36), channel_id=1, source_target_pairs={{0,252},{4,248},{8,244},{12,240},{16,236},{20,232},{24,228},{28,22... | collective-permute-start | bytes 589832 | tf_op jit(solution)/shard_map/stash_3_2/ppermute | solution.py:137
  119.6 2.3 %collective-permute-start.9 = (bf16[3,1,64,512]{3,2,1,0:T(8,128)(2,1)}, bf16[3,1,64,512]{3,2,1,0:T(8,128)(2,1)S(1)}, u32[]{:S(2)}, u32[]{:S(2)}) collective-permute-start(bf16[3,1,64,512]{3,2,1,0:T(8,128)(2,1)} %get-tuple-element.37), channel_id=1, source_target_pairs={{0,248},{4,252},{8,240},{12,244},{16,232},{20,236},{24,224},{28,22... | collective-permute-start | bytes 589832 | tf_op jit(solution)/shard_map/stash_2_2/ppermute | solution.py:137
  122.0 5.3 %collective-permute-start.8 = (bf16[3,1,64,512]{3,2,1,0:T(8,128)(2,1)}, bf16[3,1,64,512]{3,2,1,0:T(8,128)(2,1)S(1)}, u32[]{:S(2)}, u32[]{:S(2)}) collective-permute-start(bf16[3,1,64,512]{3,2,1,0:T(8,128)(2,1)} %get-tuple-element.38), channel_id=1, source_target_pairs={{0,252},{4,248},{8,244},{12,240},{16,236},{20,232},{24,228},{28,22... | collective-permute-start | bytes 589832 | tf_op jit(solution)/shard_map/stash_3_1/ppermute | solution.py:137
  127.2 0.0 collective-permute-start.7
  127.2 0.0 collective-permute-done.1
  127.2 2.5 %collective-permute-start.6 = (bf16[3,1,64,512]{3,2,1,0:T(8,128)(2,1)}, bf16[3,1,64,512]{3,2,1,0:T(8,128)(2,1)S(1)}, u32[]{:S(2)}, u32[]{:S(2)}) collective-permute-start(bf16[3,1,64,512]{3,2,1,0:T(8,128)(2,1)} %get-tuple-element.40), channel_id=1, source_target_pairs={{0,252},{4,248},{8,244},{12,240},{16,236},{20,232},{24,228},{28,22... | collective-permute-start | bytes 589832 | tf_op jit(solution)/shard_map/stash_3_0/ppermute | solution.py:137
  129.8 0.0 collective-permute-done.10.refs_3_
  129.8 4.6 %collective-permute-start.5 = (bf16[3,1,64,512]{3,2,1,0:T(8,128)(2,1)S(1)}, bf16[3,1,64,512]{3,2,1,0:T(8,128)(2,1)S(1)}, u32[]{:S(2)}, u32[]{:S(2)}) collective-permute-start(bf16[3,1,64,512]{3,2,1,0:T(8,128)(2,1)S(1)} %get-tuple-element.41), channel_id=1, source_target_pairs={{0,248},{4,252},{8,240},{12,244},{16,232},{20,236},{24,224},{28,22... | collective-permute-start | bytes 589832 | tf_op jit(solution)/shard_map/stash_2_0/ppermute | solution.py:137
  134.4 2.3 %broadcast_select_fusion = bf16[1,256,2048]{2,1,0:T(8,128)(2,1)} fusion(bf16[1,256,2048]{2,1,0:T(8,128)(2,1)} %collective-permute-done.1, bf16[1,256,2048]{2,1,0:T(8,128)(2,1)} %forward_heads.1, pred[]{:T(512)S(6)} %eq.6), kind=kLoop, calls=%fused_computation | loop fusion | flops 524288 | bytes 3145729 | tf_op jit(solution)/shard_map/jit(_where)/select_n | solution.py:208
  136.7 0.0 collective-permute-done.9.refs_2_
  136.7 0.5 collective-permute-done.8.refs_3_
  137.2 0.0 copy-start.1
  137.2 0.7 copy-done.1
  137.9 1.1 collective-permute-done.7.refs_2_
  139.0 0.0 copy-start.3
  139.0 0.7 copy-done.3
  139.7 5.9 %collective-permute-done.6.refs_3_ = bf16[3,1,64,512]{3,2,1,0:T(8,128)(2,1)S(1)} collective-permute-done((bf16[3,1,64,512]{3,2,1,0:T(8,128)(2,1)}, bf16[3,1,64,512]{3,2,1,0:T(8,128)(2,1)S(1)}, u32[]{:S(2)}, u32[]{:S(2)}) %collective-permute-start.6) | collective-permute-done | bytes 196640 | tf_op jit(solution)/shard_map/stash_3_0/ppermute | solution.py:137
  145.6 0.0 copy-start.5
  145.6 0.7 copy-done.5
  146.3 1.1 collective-permute-done.5.refs_2_
  147.4 0.0 copy-start.7
  147.4 0.7 copy-done.7
  148.1 1.9 %collective-permute-start.11 = (bf16[1,256,2048]{2,1,0:T(8,128)(2,1)}, bf16[1,256,2048]{2,1,0:T(8,128)(2,1)}, u32[]{:S(2)}, u32[]{:S(2)}) collective-permute-start(bf16[1,256,2048]{2,1,0:T(8,128)(2,1)} %broadcast_select_fusion), channel_id=1, source_target_pairs={{0,16},{4,36},{8,24},{12,44},{16,32},{24,40},{32,48},{36,68},{40,5... | collective-permute-start | bytes 3145736 | tf_op jit(solution)/shard_map/step_out/ppermute | solution.py:218
  150.0 6.3 %collective-permute-start.13 = (bf16[3,1,64,512]{3,2,1,0:T(8,128)(2,1)}, bf16[3,1,64,512]{3,2,1,0:T(8,128)(2,1)}, u32[]{:S(2)}, u32[]{:S(2)}) collective-permute-start(bf16[3,1,64,512]{3,2,1,0:T(8,128)(2,1)} %get-tuple-element.34), channel_id=1, source_target_pairs={{0,252},{4,248},{8,244},{12,240},{16,236},{20,232},{24,228},{28,22... | collective-permute-start | bytes 589832 | tf_op jit(solution)/shard_map/stash_3_3/ppermute | solution.py:137
  156.3 2.3 %collective-permute-start.12 = (bf16[3,1,64,512]{3,2,1,0:T(8,128)(2,1)}, bf16[3,1,64,512]{3,2,1,0:T(8,128)(2,1)}, u32[]{:S(2)}, u32[]{:S(2)}) collective-permute-start(bf16[3,1,64,512]{3,2,1,0:T(8,128)(2,1)} %get-tuple-element.35), channel_id=1, source_target_pairs={{0,248},{4,252},{8,240},{12,244},{16,232},{20,236},{24,224},{28,22... | collective-permute-start | bytes 589832 | tf_op jit(solution)/shard_map/stash_2_3/ppermute | solution.py:137
  158.6 0.0 copy-done.9
  158.6 0.1 copy.15.refs_7_
  159.4 0.0 copy-start.6
  159.4 0.9 copy-done.6
  160.3 0.0 copy-start.8
  160.3 0.9 copy-done.8
  161.2 0.0 copy-start.2
  161.2 0.0 copy-start.4
  161.2 4.5 %backward_0.1.refs_9_ = bf16[3,1,256,2048]{3,2,1,0:T(8,128)(2,1)} custom-call(bf16[3,1,64,2048]{3,2,1,0:T(8,128)(2,1)S(1)} %collective-permute-done.refs_0_, bf16[3,1,64,2048]{3,2,1,0:T(8,128)(2,1)} %collective-permute-done.2.refs_1_, bf16[3,1,64,512]{3,2,1,0:T(8,128)(2,1)S(1)} %copy-done.8, bf16[3,1,64,512]{3,2,1,0:T(8,128)(2,1)S(1)} %copy-done.6, ...), custom_call_target="tpu_custom_call" | custom-call | flops 335544320 | bytes 1835008 | tf_op jit(solution)/shard_map/backward_0/pallas_call | solution.py:113
  165.8 0.0 copy-done.2
  165.8 0.0 copy-done.4
  165.8 4.5 %backward_1.1.refs_9_ = bf16[3,1,256,2048]{3,2,1,0:T(8,128)(2,1)} custom-call(bf16[3,1,64,2048]{3,2,1,0:T(8,128)(2,1)S(1)} %collective-permute-done.refs_0_, bf16[3,1,64,2048]{3,2,1,0:T(8,128)(2,1)} %collective-permute-done.2.refs_1_, bf16[3,1,64,512]{3,2,1,0:T(8,128)(2,1)S(1)} %copy-done.4, ...), custom_call_target="tpu_custom_call", output_to_operand_aliasing={{}: (9, {})} | custom-call | flops 335544320 | bytes 1835008 | tf_op jit(solution)/shard_map/backward_1/pallas_call | solution.py:113
  170.3 4.5 %backward_2.1.refs_9_ = bf16[3,1,256,2048]{3,2,1,0:T(8,128)(2,1)} custom-call(bf16[3,1,64,2048]{3,2,1,0:T(8,128)(2,1)S(1)} %collective-permute-done.refs_0_, bf16[3,1,64,2048]{3,2,1,0:T(8,128)(2,1)} %collective-permute-done.2.refs_1_, bf16[3,1,64,512]{3,2,1,0:T(8,128)(2,1)S(1)} %collective-permute-done.9.refs_2_, ...), custom_call_target="tpu_custom_call", output_to_operand_aliasing={{}: (9, {})} | custom-call | flops 335544320 | bytes 1835008 | tf_op jit(solution)/shard_map/backward_2/pallas_call | solution.py:113
  174.8 6.8 %collective-permute-done.13.refs_3_ = bf16[3,1,64,512]{3,2,1,0:T(8,128)(2,1)} collective-permute-done((bf16[3,1,64,512]{3,2,1,0:T(8,128)(2,1)}, bf16[3,1,64,512]{3,2,1,0:T(8,128)(2,1)}, u32[]{:S(2)}, u32[]{:S(2)}) %collective-permute-start.13) | collective-permute-done | bytes 196640 | tf_op jit(solution)/shard_map/stash_3_3/ppermute | solution.py:137
  181.6 0.0 collective-permute-done.12.refs_2_
  181.6 4.7 %backward_3.1 = bf16[3,1,256,2048]{3,2,1,0:T(8,128)(2,1)} custom-call(bf16[3,1,64,2048]{3,2,1,0:T(8,128)(2,1)S(1)} %collective-permute-done.refs_0_, bf16[3,1,64,2048]{3,2,1,0:T(8,128)(2,1)} %collective-permute-done.2.refs_1_, bf16[3,1,64,512]{3,2,1,0:T(8,128)(2,1)} %collective-permute-done.12.refs_2_, ...), custom_call_target="tpu_custom_call", output_to_operand_aliasing={{}: (9, {})} | custom-call | flops 335544320 | bytes 1835008 | tf_op jit(solution)/shard_map/backward_3/pallas_call | solution.py:113
  186.3 0.0 collective-permute-done.11
  186.3 2.3 %broadcast_select_fusion.1 = bf16[1,256,2048]{2,1,0:T(8,128)(2,1)} fusion(bf16[1,256,2048]{2,1,0:T(8,128)(2,1)} %collective-permute-done.1, bf16[1,256,2048]{2,1,0:T(8,128)(2,1)} %collective-permute-done.11, pred[]{:T(512)S(6)} %and.13), kind=kLoop, calls=%fused_computation.1 | loop fusion | flops 524288 | bytes 3145729 | tf_op jit(solution)/shard_map/jit(_where)/select_n | solution.py:220
Async XLA Ops:
  0.6 61.9 %copy-start.10 = (s32[1,256]{1,0:T(1,128)S(1)}, s32[1,256]{1,0:T(1,128)}, u32[]{:S(2)}) copy-start(s32[1,256]{1,0:T(1,128)} %row_ref.1) | copy-start | bytes 3076
  0.6 31.1 %collective-permute-start.3 = (bf16[1,256,2048]{2,1,0:T(8,128)(2,1)}, bf16[1,256,2048]{2,1,0:T(8,128)(2,1)S(1)}, u32[]{:S(2)}, u32[]{:S(2)}) collective-permute-start(bf16[1,256,2048]{2,1,0:T(8,128)(2,1)} %param.10), channel_id=1, source_target_pairs={{0,240},{4,20},{8,248},{12,28},{16,0},{20,4},{24,8},{28,12},{32,16... | collective-permute-start | bytes 3145736 | tf_op jit(solution)/shard_map/step_grad_1/ppermute | solution.py:137
  5.4 57.3 %collective-permute-start = (bf16[3,1,64,2048]{3,2,1,0:T(8,128)(2,1)}, bf16[3,1,64,2048]{3,2,1,0:T(8,128)(2,1)S(1)}, u32[]{:S(2)}, u32[]{:S(2)}) collective-permute-start(bf16[3,1,64,2048]{3,2,1,0:T(8,128)(2,1)} %get-tuple-element.43), channel_id=1, source_target_pairs={{0,240},{4,244},{8,248},{12,252},{16,224},{20,228},{24,232},{28,23... | collective-permute-start | bytes 2359304 | tf_op jit(solution)/shard_map/stash_0_0/ppermute | solution.py:137
  31.8 60.1 %collective-permute-start.4 = (bf16[1,256,2048]{2,1,0:T(8,128)(2,1)S(1)}, bf16[1,256,2048]{2,1,0:T(8,128)(2,1)S(1)}, u32[]{:S(2)}, u32[]{:S(2)}) collective-permute-start(bf16[1,256,2048]{2,1,0:T(8,128)(2,1)S(1)} %collective-permute-done.3.refs_4_), channel_id=1, source_target_pairs={{20,244},{28,252},{52,20},{60,28},{84,52},{92,60},{116,84},{124,92... | collective-permute-start | bytes 3145736 | tf_op jit(solution)/shard_map/step_grad_2/ppermute | solution.py:155
  32.5 59.4 %collective-permute-start.2 = (bf16[3,1,64,2048]{3,2,1,0:T(8,128)(2,1)}, bf16[3,1,64,2048]{3,2,1,0:T(8,128)(2,1)}, u32[]{:S(2)}, u32[]{:S(2)}) collective-permute-start(bf16[3,1,64,2048]{3,2,1,0:T(8,128)(2,1)} %get-tuple-element.42), channel_id=1, source_target_pairs={{0,244},{4,240},{8,252},{12,248},{16,228},{20,224},{24,236},{28,23... | collective-permute-start | bytes 2359304 | tf_op jit(solution)/shard_map/stash_1_0/ppermute | solution.py:137
  62.7 1.9 %copy-start = (bf16[3,1,256,2048]{3,2,1,0:T(8,128)(2,1)S(1)}, bf16[3,1,256,2048]{3,2,1,0:T(8,128)(2,1)}, u32[]{:S(2)}) copy-start(bf16[3,1,256,2048]{3,2,1,0:T(8,128)(2,1)} %qkv_ref) | copy-start | bytes 9437188
  70.2 57.1 %collective-permute-start.1 = (bf16[1,256,2048]{2,1,0:T(8,128)(2,1)}, bf16[1,256,2048]{2,1,0:T(8,128)(2,1)}, u32[]{:S(2)}, u32[]{:S(2)}) collective-permute-start(bf16[1,256,2048]{2,1,0:T(8,128)(2,1)} %forward_heads.1), channel_id=1, source_target_pairs={{4,20},{12,28},{20,4},{28,12},{36,52},{44,60},{52,36},{60,44},{68,... | collective-permute-start | bytes 3145736 | tf_op jit(solution)/shard_map/swap_out/ppermute | solution.py:201
  72.1 86.4 %copy-start.9 = (s32[1,256]{1,0:T(1,128)S(1)}, s32[1,256]{1,0:T(1,128)}, u32[]{:S(2)}) copy-start(s32[1,256]{1,0:T(1,128)} %refs_6_.7) | copy-start | bytes 3076
  94.4 35.4 %collective-permute-start.10 = (bf16[3,1,64,512]{3,2,1,0:T(8,128)(2,1)}, bf16[3,1,64,512]{3,2,1,0:T(8,128)(2,1)S(1)}, u32[]{:S(2)}, u32[]{:S(2)}) collective-permute-start(bf16[3,1,64,512]{3,2,1,0:T(8,128)(2,1)} %get-tuple-element.36), channel_id=1, source_target_pairs={{0,252},{4,248},{8,244},{12,240},{16,236},{20,232},{24,228},{28,22... | collective-permute-start | bytes 589832 | tf_op jit(solution)/shard_map/stash_3_2/ppermute | solution.py:137
  119.6 17.1 %collective-permute-start.9 = (bf16[3,1,64,512]{3,2,1,0:T(8,128)(2,1)}, bf16[3,1,64,512]{3,2,1,0:T(8,128)(2,1)S(1)}, u32[]{:S(2)}, u32[]{:S(2)}) collective-permute-start(bf16[3,1,64,512]{3,2,1,0:T(8,128)(2,1)} %get-tuple-element.37), channel_id=1, source_target_pairs={{0,248},{4,252},{8,240},{12,244},{16,232},{20,236},{24,224},{28,22... | collective-permute-start | bytes 589832 | tf_op jit(solution)/shard_map/stash_2_2/ppermute | solution.py:137
  122.0 15.2 %collective-permute-start.8 = (bf16[3,1,64,512]{3,2,1,0:T(8,128)(2,1)}, bf16[3,1,64,512]{3,2,1,0:T(8,128)(2,1)S(1)}, u32[]{:S(2)}, u32[]{:S(2)}) collective-permute-start(bf16[3,1,64,512]{3,2,1,0:T(8,128)(2,1)} %get-tuple-element.38), channel_id=1, source_target_pairs={{0,252},{4,248},{8,244},{12,240},{16,236},{20,232},{24,228},{28,22... | collective-permute-start | bytes 589832 | tf_op jit(solution)/shard_map/stash_3_1/ppermute | solution.py:137
  127.2 11.8 %collective-permute-start.7 = (bf16[3,1,64,512]{3,2,1,0:T(8,128)(2,1)}, bf16[3,1,64,512]{3,2,1,0:T(8,128)(2,1)S(1)}, u32[]{:S(2)}, u32[]{:S(2)}) collective-permute-start(bf16[3,1,64,512]{3,2,1,0:T(8,128)(2,1)} %get-tuple-element.39), channel_id=1, source_target_pairs={{0,248},{4,252},{8,240},{12,244},{16,232},{20,236},{24,224},{28,22... | collective-permute-start | bytes 589832 | tf_op jit(solution)/shard_map/stash_2_1/ppermute | solution.py:137
  127.2 18.4 %collective-permute-start.6 = (bf16[3,1,64,512]{3,2,1,0:T(8,128)(2,1)}, bf16[3,1,64,512]{3,2,1,0:T(8,128)(2,1)S(1)}, u32[]{:S(2)}, u32[]{:S(2)}) collective-permute-start(bf16[3,1,64,512]{3,2,1,0:T(8,128)(2,1)} %get-tuple-element.40), channel_id=1, source_target_pairs={{0,252},{4,248},{8,244},{12,240},{16,236},{20,232},{24,228},{28,22... | collective-permute-start | bytes 589832 | tf_op jit(solution)/shard_map/stash_3_0/ppermute | solution.py:137
  129.8 17.6 %collective-permute-start.5 = (bf16[3,1,64,512]{3,2,1,0:T(8,128)(2,1)S(1)}, bf16[3,1,64,512]{3,2,1,0:T(8,128)(2,1)S(1)}, u32[]{:S(2)}, u32[]{:S(2)}) collective-permute-start(bf16[3,1,64,512]{3,2,1,0:T(8,128)(2,1)S(1)} %get-tuple-element.41), channel_id=1, source_target_pairs={{0,248},{4,252},{8,240},{12,244},{16,232},{20,236},{24,224},{28,22... | collective-permute-start | bytes 589832 | tf_op jit(solution)/shard_map/stash_2_0/ppermute | solution.py:137
  137.2 0.7 copy-start.1
  139.0 0.7 copy-start.3
  145.6 0.7 copy-start.5
  147.4 0.7 copy-start.7
  148.1 38.2 %collective-permute-start.11 = (bf16[1,256,2048]{2,1,0:T(8,128)(2,1)}, bf16[1,256,2048]{2,1,0:T(8,128)(2,1)}, u32[]{:S(2)}, u32[]{:S(2)}) collective-permute-start(bf16[1,256,2048]{2,1,0:T(8,128)(2,1)} %broadcast_select_fusion), channel_id=1, source_target_pairs={{0,16},{4,36},{8,24},{12,44},{16,32},{24,40},{32,48},{36,68},{40,5... | collective-permute-start | bytes 3145736 | tf_op jit(solution)/shard_map/step_out/ppermute | solution.py:218
  150.0 31.6 %collective-permute-start.13 = (bf16[3,1,64,512]{3,2,1,0:T(8,128)(2,1)}, bf16[3,1,64,512]{3,2,1,0:T(8,128)(2,1)}, u32[]{:S(2)}, u32[]{:S(2)}) collective-permute-start(bf16[3,1,64,512]{3,2,1,0:T(8,128)(2,1)} %get-tuple-element.34), channel_id=1, source_target_pairs={{0,252},{4,248},{8,244},{12,240},{16,236},{20,232},{24,228},{28,22... | collective-permute-start | bytes 589832 | tf_op jit(solution)/shard_map/stash_3_3/ppermute | solution.py:137
  156.3 25.3 %collective-permute-start.12 = (bf16[3,1,64,512]{3,2,1,0:T(8,128)(2,1)}, bf16[3,1,64,512]{3,2,1,0:T(8,128)(2,1)}, u32[]{:S(2)}, u32[]{:S(2)}) collective-permute-start(bf16[3,1,64,512]{3,2,1,0:T(8,128)(2,1)} %get-tuple-element.35), channel_id=1, source_target_pairs={{0,248},{4,252},{8,240},{12,244},{16,232},{20,236},{24,224},{28,22... | collective-permute-start | bytes 589832 | tf_op jit(solution)/shard_map/stash_2_3/ppermute | solution.py:137
  159.4 0.9 copy-start.6
  160.3 0.9 copy-start.8
  161.2 4.5 %copy-start.2 = (bf16[3,1,64,512]{3,2,1,0:T(8,128)(2,1)S(1)}, bf16[3,1,64,512]{3,2,1,0:T(8,128)(2,1)}, u32[]{:S(2)}) copy-start(bf16[3,1,64,512]{3,2,1,0:T(8,128)(2,1)} %copy-done.1) | copy-start | bytes 589828
  161.2 4.5 %copy-start.4 = (bf16[3,1,64,512]{3,2,1,0:T(8,128)(2,1)S(1)}, bf16[3,1,64,512]{3,2,1,0:T(8,128)(2,1)}, u32[]{:S(2)}) copy-start(bf16[3,1,64,512]{3,2,1,0:T(8,128)(2,1)} %copy-done.3) | copy-start | bytes 589828

commit v4 on v3

--- a/solution.py
+++ b/solution.py
@@ -74,7 +74,7 @@
         stash[:, pl.ds(start, rows), :] = pieces[k][:, 0]
     outside = outside_of(row_ref, column_ref)
     factor = factor_ref[0]
-    around = took_both(-1)
+    around = came_around(-1)
     for start in range(0, direct_ref.shape[2], HEAD_DIM):
         head = slice(start, start + HEAD_DIM)
         queries, keys, values = stash[0, :, head], stash[1, :, head], stash[2, :, head]
@@ -94,7 +94,7 @@
     step = width // CHUNKS
     parts = len(pieces)
     piece_specs = [
-        pl.BlockSpec((3, 1, p.shape[2], step), lambda i, c=chunk if p.shape[3] > step else 0: (0, 0, 0, c))
+        pl.BlockSpec((3, 1, p.shape[2], step), lambda i, c=chunk % (p.shape[3] // step): (0, 0, 0, c))
         for p in pieces
     ]
     operands = [*pieces, *upstream, row, column, factor]
@@ -142,34 +142,36 @@
     return moved(piece, lambda p, t: (last - p, t ^ k))
 
 
-def first_hop(array, by):
-    return moved(array, lambda p, t: (p ^ 1 if t & 1 else p + by, t))
-
-
-def second_hop(array, by):
-    sections, tensors = lax.axis_size("pipe"), lax.axis_size("tensor")
-    pairs = []
-    for p in range(0 if by > 0 else 1, sections, 2):
-        for t in range(1, tensors, 2):
-            pairs.append((p * tensors + t, (p + 2 * by) % sections * tensors + t))
-    return lax.ppermute(array, ("pipe", "tensor"), pairs)
-
-
-def took_both(by):
-    kept = 0 if by > 0 else 1
-    return jnp.logical_and(lax.axis_index("pipe") & 1 == kept, lax.axis_index("tensor") & 1 == 1)
-
-
-def odd_pairs(kind):
+def detoured(p, t, by):
+    half = lax.axis_size("pipe") // 2
+    return (t & 1) * (p % half == (half - 1 if by > 0 else 0))
+
+
+def shift_pairs(by, leg):
     sections, tensors = lax.axis_size("pipe"), lax.axis_size("tensor")
     pairs = []
     for p in range(sections):
         for t in range(tensors):
-            if t & 1 and kind == "swap":
-                pairs.append((p * tensors + t, (p ^ 1) * tensors + t))
-            if kind == "step" and (t & 1 == 0 or p & 1 == 0):
-                pairs.append((p * tensors + t, (p + 1 + (t & 1)) % sections * tensors + t))
+            aside = detoured(p, t, by)
+            start, end = p, p + by
+            if leg == "aside":
+                end = p - by
+            if leg == "onward":
+                start = p - by
+            if aside == (leg != "direct"):
+                pairs.append((start % sections * tensors + t, end % sections * tensors + t))
     return pairs
+
+
+def shifted(array, by, leg):
+    with jax.named_scope(f"{leg}_{'out' if by > 0 else 'grad'}"):
+        return lax.ppermute(array, ("pipe", "tensor"), shift_pairs(by, leg))
+
+
+def came_around(by):
+    sections = lax.axis_size("pipe")
+    source = (lax.axis_index("pipe") + sections - by) % sections
+    return detoured(source, lax.axis_index("tensor"), by) == 1
 
 
 def on_device(fwd_qkv, fwd_segments, parked, bwd_segments, grad_out, loss_tokens):
@@ -184,40 +186,34 @@
         with jax.named_scope(f"stash_{k}_{first}"):
             return fetched(piece, k)
 
-    with jax.named_scope("step_grad_1"):
-        upstream_direct = first_hop(grad_out, -1)
-    early = [fetched_part(parked, k, 0, CHUNKS) for k in range(2)]
-    with jax.named_scope("step_grad_2"):
-        upstream_around = second_hop(upstream_direct, -1)
-    early[0], fwd_qkv, loss_tokens, parked = lax.optimization_barrier(
-        (early[0], fwd_qkv, loss_tokens, parked)
+    upstream_direct = shifted(grad_out, -1, "direct")
+    upstream_aside = shifted(grad_out, -1, "aside")
+    early = [fetched_part(parked, k, 0, CHUNKS) for k in range(3)]
+    upstream_around = shifted(upstream_aside, -1, "onward")
+    early[0], parked, loss_tokens = lax.optimization_barrier((early[0], parked, loss_tokens))
+    token_total = lax.psum(loss_tokens.astype(jnp.float32), "dp")
+    late = [fetched_part(parked, 3, 0, 2)]
+    early[1], parked, token_total = lax.optimization_barrier((early[1], parked, token_total))
+    factor = jnp.float32(lax.axis_size("dp") * length) / token_total
+    early, upstream_direct, upstream_around, fwd_qkv, token_total = lax.optimization_barrier(
+        (early, upstream_direct, upstream_around, fwd_qkv, token_total)
     )
-    token_total = lax.psum(loss_tokens.astype(jnp.float32), "dp")
+    upstream = (upstream_direct, upstream_around)
     with jax.named_scope("forward_heads"):
         forward_out = forward(fwd_qkv, fwd_segments, fwd_segments.reshape(length, 1))
-    token_total, forward_out = lax.optimization_barrier((token_total, forward_out))
-    factor = jnp.float32(lax.axis_size("dp") * length) / token_total
-    with jax.named_scope("swap_out"):
-        swapped_out = lax.ppermute(forward_out, ("pipe", "tensor"), odd_pairs("swap"))
-    early[1], upstream_around, parked = lax.optimization_barrier(
-        (early[1], upstream_around, parked)
-    )
-    late = [[fetched_part(parked, k, c, 1) for k in range(2, tensors)] for c in range(4)]
-    upstream = (upstream_direct, upstream_around)
-    odd = lax.axis_index("tensor") & 1 == 1
-    stepping = jnp.where(odd, swapped_out, forward_out)
-    late[:3], stepping = lax.optimization_barrier((late[:3], stepping))
+    late[0], forward_out = lax.optimization_barrier((late[0], forward_out))
+    late += [late[0], fetched_part(parked, 3, 2, 1), fetched_part(parked, 3, 3, 1)]
+    received = shifted(forward_out, 1, "direct")
+    received_aside = shifted(forward_out, 1, "aside")
+    received_around = shifted(received_aside, 1, "onward")
     column = bwd_segments.reshape(length, 1)
     grads = None
     for chunk in range(CHUNKS):
         with jax.named_scope(f"backward_{chunk}"):
             grads = backward(
-                chunk, early + late[chunk], upstream, bwd_segments, column, factor, grads
+                chunk, early + [late[chunk]], upstream, bwd_segments, column, factor, grads
             )
-    with jax.named_scope("step_out"):
-        stepped_out = lax.ppermute(stepping, ("pipe", "tensor"), odd_pairs("step"))
-    last = lax.axis_index("pipe") & 1 == 1
-    received = jnp.where(jnp.logical_and(odd, last), swapped_out, stepped_out)
+    received = jnp.where(came_around(1), received_around, received)
     return (received, grads)
 
 

time: 191 us -> 225 us (1.18)
  the two profiles are of different devices: /device:TPU:1 before, /device:TPU:22 now
where the time goes in v4:
time: 225 us; the launch traced here: 224 us
  waiting for transfers between devices  98.9 us (44%)
  starting transfers between devices  78.9 us (35%)
  Pallas kernels  24.1 us (11%)
  blocking collectives  8.94 us (4%)
  local copies, waits for them, and re-layouts  8.91 us (4%)
  other arithmetic  2.31 us (1%)
    ppermute x6, waiting for transfers between devices, moved(): return lax.ppermute(array, ('pipe', 'tensor'), pairs)  98.9 us
    ppermute x6, starting transfers between devices, moved(): return lax.ppermute(array, ('pipe', 'tensor'), pairs)  68.2 us
    pallas_call x4, Pallas kernels, backward(): pl.pallas_call(functools.partial(backward_kernel, parts), grid=(1,), in_s...  18.5 us
    ppermute x6, starting transfers between devices, shifted(): return lax.ppermute(array, ('pipe', 'tensor'), shift_pairs(by, leg))  10.7 us
    psum x1, blocking collectives, on_device(): token_total = lax.psum(loss_tokens.astype(jnp.float32), 'dp')  8.94 us
    dynamic_slice x3, local copies, waits for them, and re-layouts, fetched_part(): piece = lax.dynamic_slice_in_dim(whole, start, count * step, axis=3)  6.74 us
    pallas_call x1, Pallas kernels, forward(): pl.pallas_call(forward_kernel, grid=(CHUNKS,), in_specs=[pl.BlockSpec((3,...  5.55 us
  transfers between devices with their start and end apart: 12, of which 5 were waited for; matrix products, arithmetic and copies ran while one was open for 3% of the time, Pallas kernels for 11%

profile of v4, /device:TPU:22, one launch (start us, length us, event | category | flops | bytes accessed | tf_op | source)
XLA Modules:
  0.0 224.1 jit_solution(14746181519469442378)
XLA Ops:
  0.6 0.0 copy-start.2
  0.6 1.7 collective-permute-start.5
  2.3 3.1 %constant_dynamic-slice_fusion.2 = (bf16[3,1,64,2048]{3,2,1,0:T(8,128)(2,1)}, bf16[3,1,64,2048]{3,2,1,0:T(8,128)(2,1)}, bf16[3,1,64,2048]{3,2,1,0:T(8,128)(2,1)}) fusion(bf16[3,1,64,8192]{3,2,1,0:T(8,128)(2,1)} %param.8, s32[]{:T(128)S(6)} %select_n.43, s32[]{:T(128)S(6)} %select_n.40, s32[]{:T(128)S(6)} %select_n.42), kind=kLoop, calls=%fused_computation.3 | loop fusion | bytes 4718604 | tf_op jit(solution)/shard_map/dynamic_slice | solution.py:185
  5.4 0.0 copy-start.1
  5.4 6.1 %collective-permute-start = (bf16[3,1,64,2048]{3,2,1,0:T(8,128)(2,1)}, bf16[3,1,64,2048]{3,2,1,0:T(8,128)(2,1)S(1)}, u32[]{:S(2)}, u32[]{:S(2)}) collective-permute-start(bf16[3,1,64,2048]{3,2,1,0:T(8,128)(2,1)} %get-tuple-element.33), channel_id=1, source_target_pairs={{0,240},{4,244},{8,248},{12,252},{16,224},{20,228},{24,232},{28,23... | collective-permute-start | bytes 2359304 | tf_op jit(solution)/shard_map/stash_0_0/ppermute | solution.py:137
  11.6 3.1 %collective-permute-start.4 = (bf16[1,256,2048]{2,1,0:T(8,128)(2,1)}, bf16[1,256,2048]{2,1,0:T(8,128)(2,1)S(1)}, u32[]{:S(2)}, u32[]{:S(2)}) collective-permute-start(bf16[1,256,2048]{2,1,0:T(8,128)(2,1)} %param.10), channel_id=1, source_target_pairs={{0,240},{8,248},{16,0},{20,4},{24,8},{28,12},{32,16},{36,20},{40,2... | collective-permute-start | bytes 3145736 | tf_op jit(solution)/shard_map/direct_grad/ppermute | solution.py:168
  14.7 0.0 collective-permute-done.5
  14.7 0.7 collective-permute-start.6
  15.4 0.1 collective-permute-start.2
  15.5 6.5 %collective-permute-start.3 = (bf16[3,1,64,2048]{3,2,1,0:T(8,128)(2,1)}, bf16[3,1,64,2048]{3,2,1,0:T(8,128)(2,1)}, u32[]{:S(2)}, u32[]{:S(2)}) collective-permute-start(bf16[3,1,64,2048]{3,2,1,0:T(8,128)(2,1)} %get-tuple-element.32), channel_id=1, source_target_pairs={{0,248},{4,252},{8,240},{12,244},{16,232},{20,236},{24,224},{28,22... | collective-permute-start | bytes 2359304 | tf_op jit(solution)/shard_map/stash_2_0/ppermute | solution.py:137
  22.0 66.8 %collective-permute-done.refs_0_ = bf16[3,1,64,2048]{3,2,1,0:T(8,128)(2,1)S(1)} collective-permute-done((bf16[3,1,64,2048]{3,2,1,0:T(8,128)(2,1)}, bf16[3,1,64,2048]{3,2,1,0:T(8,128)(2,1)S(1)}, u32[]{:S(2)}, u32[]{:S(2)}) %collective-permute-start) | collective-permute-done | bytes 786464 | tf_op jit(solution)/shard_map/stash_0_0/ppermute | solution.py:137
  88.8 1.8 constant_dynamic-slice_fusion.4
  90.6 1.6 collective-permute-start.1
  92.8 8.9 %psum.7 = f32[1]{0:T(128)} all-reduce(f32[1]{0:T(128)S(6)} %convert_element_type.4), channel_id=1, replica_groups=mesh['pipe'=16,'tensor'=4,'dp'=4] {'dp'}, use_global_device_ids=true, to_apply=%region_0.0 | all-reduce | flops 1 | bytes 8 | tf_op jit(solution)/shard_map/psum | solution.py:194
  101.7 0.0 copy-done.2
  101.7 0.1 copy.11.column_ref
  101.9 3.8 %collective-permute-done.2.refs_1_ = bf16[3,1,64,2048]{3,2,1,0:T(8,128)(2,1)} collective-permute-done((bf16[3,1,64,2048]{3,2,1,0:T(8,128)(2,1)}, bf16[3,1,64,2048]{3,2,1,0:T(8,128)(2,1)}, u32[]{:S(2)}, u32[]{:S(2)}) %collective-permute-start.2) | collective-permute-done | bytes 786464 | tf_op jit(solution)/shard_map/stash_1_0/ppermute | solution.py:137
  105.7 25.1 %collective-permute-done.3.refs_2_ = bf16[3,1,64,2048]{3,2,1,0:T(8,128)(2,1)} collective-permute-done((bf16[3,1,64,2048]{3,2,1,0:T(8,128)(2,1)}, bf16[3,1,64,2048]{3,2,1,0:T(8,128)(2,1)}, u32[]{:S(2)}, u32[]{:S(2)}) %collective-permute-start.3) | collective-permute-done | bytes 786464 | tf_op jit(solution)/shard_map/stash_2_0/ppermute | solution.py:137
  130.8 0.0 collective-permute-done.4.refs_4_
  130.8 0.0 collective-permute-done.6.refs_5_
  130.8 0.0 copy-start
  130.8 1.9 copy-done
  132.7 5.6 %forward_heads.1 = bf16[1,256,2048]{2,1,0:T(8,128)(2,1)} custom-call(bf16[3,1,256,2048]{3,2,1,0:T(8,128)(2,1)S(1)} %copy-done, s32[1,256]{1,0:T(1,128)S(1)} %copy-done.2, s32[256,1]{1,0:T(8,128)S(1)} %copy.11.column_ref), custom_call_target="tpu_custom_call" | custom-call | flops 536870912 | bytes 4194304 | tf_op jit(solution)/shard_map/forward_heads/pallas_call | solution.py:47
  138.3 1.1 collective-permute-done.1.refs_3_
  139.4 1.6 collective-permute-start.7
  141.0 1.9 collective-permute-start.9
  142.9 0.0 collective-permute-done.7
  142.9 1.7 collective-permute-start.8
  144.6 1.8 constant_dynamic-slice_fusion
  146.4 53.9 %collective-permute-start.11 = (bf16[3,1,64,512]{3,2,1,0:T(8,128)(2,1)}, bf16[3,1,64,512]{3,2,1,0:T(8,128)(2,1)}, u32[]{:S(2)}, u32[]{:S(2)}) collective-permute-start(bf16[3,1,64,512]{3,2,1,0:T(8,128)(2,1)} %get-tuple-element.30), channel_id=1, source_target_pairs={{0,252},{4,248},{8,244},{12,240},{16,236},{20,232},{24,228},{28,22... | collective-permute-start | bytes 589832 | tf_op jit(solution)/shard_map/stash_3_2/ppermute | solution.py:137
  200.4 0.0 collective-permute-start.10
  200.4 0.0 copy-done.1
  200.4 0.1 copy.15.refs_7_
  201.2 4.6 %backward_0.1.refs_9_ = bf16[3,1,256,2048]{3,2,1,0:T(8,128)(2,1)} custom-call(bf16[3,1,64,2048]{3,2,1,0:T(8,128)(2,1)S(1)} %collective-permute-done.refs_0_, bf16[3,1,64,2048]{3,2,1,0:T(8,128)(2,1)} %collective-permute-done.2.refs_1_, bf16[3,1,64,2048]{3,2,1,0:T(8,128)(2,1)} %collective-permute-done.3.refs_2_, ...), custom_call_target="tpu_custom_call" | custom-call | flops 335544320 | bytes 1835008 | tf_op jit(solution)/shard_map/backward_0/pallas_call | solution.py:113
  205.8 4.6 %backward_1.1.refs_9_ = bf16[3,1,256,2048]{3,2,1,0:T(8,128)(2,1)} custom-call(bf16[3,1,64,2048]{3,2,1,0:T(8,128)(2,1)S(1)} %collective-permute-done.refs_0_, bf16[3,1,64,2048]{3,2,1,0:T(8,128)(2,1)} %collective-permute-done.2.refs_1_, bf16[3,1,64,2048]{3,2,1,0:T(8,128)(2,1)} %collective-permute-done.3.refs_2_, ...), custom_call_target="tpu_custom_call", output_to_operand_aliasing={{}: (9, {})} | custom-call | flops 335544320 | bytes 1835008 | tf_op jit(solution)/shard_map/backward_1/pallas_call | solution.py:113
  210.4 2.0 collective-permute-done.11.refs_3_
  212.4 4.7 %backward_2.1.refs_9_ = bf16[3,1,256,2048]{3,2,1,0:T(8,128)(2,1)} custom-call(bf16[3,1,64,2048]{3,2,1,0:T(8,128)(2,1)S(1)} %collective-permute-done.refs_0_, bf16[3,1,64,2048]{3,2,1,0:T(8,128)(2,1)} %collective-permute-done.2.refs_1_, bf16[3,1,64,2048]{3,2,1,0:T(8,128)(2,1)} %collective-permute-done.3.refs_2_, ...), custom_call_target="tpu_custom_call", output_to_operand_aliasing={{}: (9, {})} | custom-call | flops 335544320 | bytes 1835008 | tf_op jit(solution)/shard_map/backward_2/pallas_call | solution.py:113
  217.1 0.0 collective-permute-done.10.refs_3_
  217.1 4.7 %backward_3.1 = bf16[3,1,256,2048]{3,2,1,0:T(8,128)(2,1)} custom-call(bf16[3,1,64,2048]{3,2,1,0:T(8,128)(2,1)S(1)} %collective-permute-done.refs_0_, bf16[3,1,64,2048]{3,2,1,0:T(8,128)(2,1)} %collective-permute-done.2.refs_1_, bf16[3,1,64,2048]{3,2,1,0:T(8,128)(2,1)} %collective-permute-done.3.refs_2_, ...), custom_call_target="tpu_custom_call", output_to_operand_aliasing={{}: (9, {})} | custom-call | flops 335544320 | bytes 1835008 | tf_op jit(solution)/shard_map/backward_3/pallas_call | solution.py:113
  221.8 0.0 collective-permute-done.9
  221.8 0.0 collective-permute-done.8
  221.8 2.3 %broadcast_select_fusion = bf16[1,256,2048]{2,1,0:T(8,128)(2,1)} fusion(bf16[1,256,2048]{2,1,0:T(8,128)(2,1)} %collective-permute-done.8, bf16[1,256,2048]{2,1,0:T(8,128)(2,1)} %collective-permute-done.9, pred[]{:T(512)S(6)} %eq.10), kind=kLoop, calls=%fused_computation | loop fusion | flops 524288 | bytes 3145729 | tf_op jit(solution)/shard_map/jit(_where)/select_n | solution.py:216
Async XLA Ops:
  0.6 101.1 %copy-start.2 = (s32[1,256]{1,0:T(1,128)S(1)}, s32[1,256]{1,0:T(1,128)}, u32[]{:S(2)}) copy-start(s32[1,256]{1,0:T(1,128)} %row_ref.1) | copy-start | bytes 3076
  0.6 14.0 %collective-permute-start.5 = (bf16[1,256,2048]{2,1,0:T(8,128)(2,1)}, bf16[1,256,2048]{2,1,0:T(8,128)(2,1)}, u32[]{:S(2)}, u32[]{:S(2)}) collective-permute-start(bf16[1,256,2048]{2,1,0:T(8,128)(2,1)} %param.10), channel_id=1, source_target_pairs={{4,20},{12,28},{132,148},{140,156},{5,21},{13,29},{133,149},{141,1... | collective-permute-start | bytes 3145736 | tf_op jit(solution)/shard_map/aside_grad/ppermute | solution.py:168
  5.4 195.0 %copy-start.1 = (s32[1,256]{1,0:T(1,128)S(1)}, s32[1,256]{1,0:T(1,128)}, u32[]{:S(2)}) copy-start(s32[1,256]{1,0:T(1,128)} %refs_6_.7) | copy-start | bytes 3076
  5.4 83.4 %collective-permute-start = (bf16[3,1,64,2048]{3,2,1,0:T(8,128)(2,1)}, bf16[3,1,64,2048]{3,2,1,0:T(8,128)(2,1)S(1)}, u32[]{:S(2)}, u32[]{:S(2)}) collective-permute-start(bf16[3,1,64,2048]{3,2,1,0:T(8,128)(2,1)} %get-tuple-element.33), channel_id=1, source_target_pairs={{0,240},{4,244},{8,248},{12,252},{16,224},{20,228},{24,232},{28,23... | collective-permute-start | bytes 2359304 | tf_op jit(solution)/shard_map/stash_0_0/ppermute | solution.py:137
  11.6 119.2 %collective-permute-start.4 = (bf16[1,256,2048]{2,1,0:T(8,128)(2,1)}, bf16[1,256,2048]{2,1,0:T(8,128)(2,1)S(1)}, u32[]{:S(2)}, u32[]{:S(2)}) collective-permute-start(bf16[1,256,2048]{2,1,0:T(8,128)(2,1)} %param.10), channel_id=1, source_target_pairs={{0,240},{8,248},{16,0},{20,4},{24,8},{28,12},{32,16},{36,20},{40,2... | collective-permute-start | bytes 3145736 | tf_op jit(solution)/shard_map/direct_grad/ppermute | solution.py:168
  14.7 116.1 %collective-permute-start.6 = (bf16[1,256,2048]{2,1,0:T(8,128)(2,1)}, bf16[1,256,2048]{2,1,0:T(8,128)(2,1)S(1)}, u32[]{:S(2)}, u32[]{:S(2)}) collective-permute-start(bf16[1,256,2048]{2,1,0:T(8,128)(2,1)} %collective-permute-done.5), channel_id=1, source_target_pairs={{20,244},{28,252},{148,116},{156,124},{21,245},{29,253},{149,117},... | collective-permute-start | bytes 3145736 | tf_op jit(solution)/shard_map/onward_grad/ppermute | solution.py:168
  15.4 90.3 %collective-permute-start.2 = (bf16[3,1,64,2048]{3,2,1,0:T(8,128)(2,1)}, bf16[3,1,64,2048]{3,2,1,0:T(8,128)(2,1)}, u32[]{:S(2)}, u32[]{:S(2)}) collective-permute-start(bf16[3,1,64,2048]{3,2,1,0:T(8,128)(2,1)} %get-tuple-element.34), channel_id=1, source_target_pairs={{0,244},{4,240},{8,252},{12,248},{16,228},{20,224},{24,236},{28,23... | collective-permute-start | bytes 2359304 | tf_op jit(solution)/shard_map/stash_1_0/ppermute | solution.py:137
  15.5 115.3 %collective-permute-start.3 = (bf16[3,1,64,2048]{3,2,1,0:T(8,128)(2,1)}, bf16[3,1,64,2048]{3,2,1,0:T(8,128)(2,1)}, u32[]{:S(2)}, u32[]{:S(2)}) collective-permute-start(bf16[3,1,64,2048]{3,2,1,0:T(8,128)(2,1)} %get-tuple-element.32), channel_id=1, source_target_pairs={{0,248},{4,252},{8,240},{12,244},{16,232},{20,236},{24,224},{28,22... | collective-permute-start | bytes 2359304 | tf_op jit(solution)/shard_map/stash_2_0/ppermute | solution.py:137
  90.6 48.8 %collective-permute-start.1 = (bf16[3,1,64,1024]{3,2,1,0:T(8,128)(2,1)}, bf16[3,1,64,1024]{3,2,1,0:T(8,128)(2,1)S(1)}, u32[]{:S(2)}, u32[]{:S(2)}) collective-permute-start(bf16[3,1,64,1024]{3,2,1,0:T(8,128)(2,1)} %constant_dynamic-slice_fusion.4), channel_id=1, source_target_pairs={{0,252},{4,248},{8,244},{12,240},{16,236},{20,232},{24,228},{28,22... | collective-permute-start | bytes 1179656 | tf_op jit(solution)/shard_map/stash_3_0/ppermute | solution.py:137
  130.8 1.9 copy-start
  139.4 3.6 %collective-permute-start.7 = (bf16[1,256,2048]{2,1,0:T(8,128)(2,1)}, bf16[1,256,2048]{2,1,0:T(8,128)(2,1)}, u32[]{:S(2)}, u32[]{:S(2)}) collective-permute-start(bf16[1,256,2048]{2,1,0:T(8,128)(2,1)} %forward_heads.1), channel_id=1, source_target_pairs={{116,100},{124,108},{244,228},{252,236},{117,101},{125,109},{245,2... | collective-permute-start | bytes 3145736 | tf_op jit(solution)/shard_map/aside_out/ppermute | solution.py:168
  141.0 80.8 %collective-permute-start.9 = (bf16[1,256,2048]{2,1,0:T(8,128)(2,1)}, bf16[1,256,2048]{2,1,0:T(8,128)(2,1)}, u32[]{:S(2)}, u32[]{:S(2)}) collective-permute-start(bf16[1,256,2048]{2,1,0:T(8,128)(2,1)} %forward_heads.1), channel_id=1, source_target_pairs={{0,16},{4,20},{8,24},{12,28},{16,32},{20,36},{24,40},{28,44},{32,4... | collective-permute-start | bytes 3145736 | tf_op jit(solution)/shard_map/direct_out/ppermute | solution.py:168
  142.9 78.8 %collective-permute-start.8 = (bf16[1,256,2048]{2,1,0:T(8,128)(2,1)}, bf16[1,256,2048]{2,1,0:T(8,128)(2,1)}, u32[]{:S(2)}, u32[]{:S(2)}) collective-permute-start(bf16[1,256,2048]{2,1,0:T(8,128)(2,1)} %collective-permute-done.7), channel_id=1, source_target_pairs={{100,132},{108,140},{228,4},{236,12},{101,133},{109,141},{229,5},{... | collective-permute-start | bytes 3145736 | tf_op jit(solution)/shard_map/onward_out/ppermute | solution.py:168
  146.4 66.0 %collective-permute-start.11 = (bf16[3,1,64,512]{3,2,1,0:T(8,128)(2,1)}, bf16[3,1,64,512]{3,2,1,0:T(8,128)(2,1)}, u32[]{:S(2)}, u32[]{:S(2)}) collective-permute-start(bf16[3,1,64,512]{3,2,1,0:T(8,128)(2,1)} %get-tuple-element.30), channel_id=1, source_target_pairs={{0,252},{4,248},{8,244},{12,240},{16,236},{20,232},{24,228},{28,22... | collective-permute-start | bytes 589832 | tf_op jit(solution)/shard_map/stash_3_2/ppermute | solution.py:137
  200.4 16.7 %collective-permute-start.10 = (bf16[3,1,64,512]{3,2,1,0:T(8,128)(2,1)}, bf16[3,1,64,512]{3,2,1,0:T(8,128)(2,1)}, u32[]{:S(2)}, u32[]{:S(2)}) collective-permute-start(bf16[3,1,64,512]{3,2,1,0:T(8,128)(2,1)} %get-tuple-element.31), channel_id=1, source_target_pairs={{0,252},{4,248},{8,244},{12,240},{16,236},{20,232},{24,228},{28,22... | collective-permute-start | bytes 589832 | tf_op jit(solution)/shard_map/stash_3_3/ppermute | solution.py:137

commit v5 on v1

v5 whole, which is shorter than its diff:
```python
import functools
import math

import jax
import jax.numpy as jnp
from jax import lax
from jax.experimental import pallas as pl
from jax.experimental.pallas import tpu as pltpu
from jax.sharding import PartitionSpec as P

HEAD_DIM = 128
FORWARD_STEPS = 4
CHUNKS = ((0, 8), (8, 4), (12, 4))
SCALE = HEAD_DIM ** (-0.5)
EXPONENT = SCALE * math.log2(math.e)
NT = (((1,), (1,)), ((), ()))
NN = (((1,), (0,)), ((), ()))
TN = (((0,), (0,)), ((), ()))
AXES = ("pipe", "tensor")


def product(left, right, dims):
    return lax.dot_general(left, right, dims, preferred_element_type=jnp.float32)


def probabilities(queries, keys, outside):
    logits = product(queries, keys, NT) + outside
    highest = jnp.max(logits, axis=1, keepdims=True)
    weights = jnp.exp2((logits - highest) * EXPONENT)
    return weights * (1.0 / jnp.sum(weights, axis=1, keepdims=True))


def outside_of(segment_ref):
    length = segment_ref.shape[1]
    across = jnp.broadcast_to(segment_ref[...].astype(jnp.float32), (length, length))
    return jnp.where(across == across.T, 0.0, -1e31).astype(jnp.float32)


def forward_kernel(qkv_ref, grad_ref, segment_ref, out_ref, aside_ref, outside):
    sends_out = detoured(lax.axis_index("pipe"), 1, 1) == 1

    @pl.when(pl.program_id(0) == 0)
    def _():
        outside[...] = outside_of(segment_ref)

    for start in range(0, out_ref.shape[2], HEAD_DIM):
        head = slice(start, start + HEAD_DIM)
        probs = probabilities(qkv_ref[0, 0, :, head], qkv_ref[1, 0, :, head], outside[...])
        mixed = product(probs.astype(jnp.bfloat16), qkv_ref[2, 0, :, head], NN)
        mixed = mixed.astype(jnp.bfloat16)
        out_ref[0, :, head] = mixed
        aside_ref[0, :, head] = jnp.where(sends_out, mixed, grad_ref[0, :, head])


def forward(qkv, grad_out, segment):
    _, _, length, width = qkv.shape
    step = width // FORWARD_STEPS
    columns = pl.BlockSpec((1, length, step), lambda c: (0, 0, c))
    out = jax.ShapeDtypeStruct((1, length, width), jnp.bfloat16)
    return pl.pallas_call(
        forward_kernel,
        grid=(FORWARD_STEPS,),
        in_specs=[
            pl.BlockSpec((3, 1, length, step), lambda c: (0, 0, 0, c)),
            columns,
            pl.BlockSpec((1, length), lambda c: (0, 0)),
        ],
        out_specs=[columns, columns],
        out_shape=[out, out],
        scratch_shapes=[pltpu.VMEM((length, length), jnp.float32)],
        compiler_params=pltpu.CompilerParams(vmem_limit_bytes=56 * 1024 * 1024),
        cost_estimate=pl.CostEstimate(
            flops=4 * length * length * width,
            bytes_accessed=12 * length * width,
            transcendentals=length * length * width // HEAD_DIM,
        ),
    )(qkv, grad_out, segment)


def backward_kernel(parts, *refs):
    pieces, refs = refs[:parts], refs[parts:]
    direct_ref, around_ref, segment_ref, factor_ref = refs[:4]
    out_ref, stash = refs[-2:] if len(refs) < 8 else (refs[-3], refs[-1])
    around = came_around(-1)
    mine = lax.axis_index("tensor")
    rows = pieces[0].shape[2]
    for k in range(parts):
        start = pl.multiple_of((mine ^ k) * rows, rows)
        stash[:, pl.ds(start, rows), :] = pieces[k][:, 0]
    outside = outside_of(segment_ref)
    factor = factor_ref[0]
    for start in range(0, direct_ref.shape[2], HEAD_DIM):
        head = slice(start, start + HEAD_DIM)
        queries, keys, values = stash[0, :, head], stash[1, :, head], stash[2, :, head]
        upstream = jnp.where(around, around_ref[0, :, head], direct_ref[0, :, head])
        probs = probabilities(queries, keys, outside)
        grad_value = product(probs.astype(jnp.bfloat16), upstream, TN)
        grad_probs = product(upstream, values, NT)
        center = jnp.sum(probs * grad_probs, axis=1, keepdims=True)
        grad_logits = (probs * (grad_probs - center) * SCALE).astype(jnp.bfloat16)
        out_ref[0, 0, :, head] = (product(grad_logits, keys, NN) * factor).astype(jnp.bfloat16)
        out_ref[1, 0, :, head] = (product(grad_logits, queries, TN) * factor).astype(jnp.bfloat16)
        out_ref[2, 0, :, head] = (grad_value * factor).astype(jnp.bfloat16)


def backward(chunk, pieces, upstream, segment, factor, earlier, carried=None):
    _, length, width = upstream[0].shape
    first, heads = CHUNKS[chunk]
    step = heads * HEAD_DIM
    place = first // heads
    parts = len(pieces)
    operands = [*pieces, *upstream, segment, factor]
    in_specs = [pl.BlockSpec(memory_space=pltpu.VMEM)] * parts + [
        pl.BlockSpec((1, length, step), lambda i: (0, 0, place)),
        pl.BlockSpec((1, length, step), lambda i: (0, 0, place)),
        pl.BlockSpec((1, length), lambda i: (0, 0)),
        pl.BlockSpec(memory_space=pltpu.SMEM),
    ]
    out_specs = [pl.BlockSpec((3, 1, length, step), lambda i: (0, 0, 0, place))]
    out_shape = [jax.ShapeDtypeStruct((3, 1, length, width), jnp.bfloat16)]
    aliases = {}
    for array in (earlier, carried):
        if array is not None:
            aliases[len(operands)] = len(aliases)
            operands.append(array)
            in_specs.append(pl.BlockSpec(memory_space=pl.ANY))
    if carried is not None:
        out_specs.append(pl.BlockSpec(memory_space=pl.ANY))
        out_shape.append(jax.ShapeDtypeStruct(carried.shape, carried.dtype))
    return pl.pallas_call(
        functools.partial(backward_kernel, parts),
        grid=(1,),
        in_specs=in_specs,
        out_specs=out_specs,
        out_shape=out_shape,
        scratch_shapes=[pltpu.VMEM((3, length, step), jnp.bfloat16)],
        input_output_aliases=aliases,
        compiler_params=pltpu.CompilerParams(vmem_limit_bytes=32 * 1024 * 1024),
        cost_estimate=pl.CostEstimate(
            flops=10 * length * length * step,
            bytes_accessed=14 * length * step,
            transcendentals=length * length * step // HEAD_DIM,
        ),
    )(*operands)


def fetched(piece, k):
    sections, tensors = lax.axis_size("pipe"), lax.axis_size("tensor")
    pairs = [
        (p * tensors + t, (sections - 1 - p) * tensors + (t ^ k))
        for p in range(sections)
        for t in range(tensors)
    ]
    return lax.ppermute(piece, AXES, pairs)


def detoured(p, t, by):
    half = lax.axis_size("pipe") // 2
    return (t & 1) * (p % half == (half - 1 if by > 0 else 0))


def shifted(array, by):
    sections, tensors = lax.axis_size("pipe"), lax.axis_size("tensor")
    pairs = [
        (p * tensors + t, (p + by) % sections * tensors + t)
        for p in range(sections)
        for t in range(tensors)
        if not detoured(p, t, by)
    ]
    with jax.named_scope("direct_out" if by > 0 else "direct_grad"):
        return lax.ppermute(array, AXES, pairs)


def detour(array, leg):
    sections, tensors = lax.axis_size("pipe"), lax.axis_size("tensor")
    pairs = []
    for by in (-1, 1):
        for p in range(sections):
            for t in range(tensors):
                if detoured(p, t, by):
                    start, end = (p, p - by) if leg == "aside" else (p - by, p + by)
                    pairs.append((start % sections * tensors + t, end % sections * tensors + t))
    with jax.named_scope(f"{leg}_both"):
        return lax.ppermute(array, AXES, pairs)


def came_around(by):
    sections = lax.axis_size("pipe")
    source = (lax.axis_index("pipe") + sections - by) % sections
    return detoured(source, lax.axis_index("tensor"), by) == 1


def on_device(fwd_qkv, fwd_segments, parked, bwd_segments, grad_out, loss_tokens):
    length, width = grad_out.shape[1:]
    tensors = lax.axis_size("tensor")
    mine = lax.axis_index("tensor")

    def fetched_chunk(whole, chunk):
        first, heads = CHUNKS[chunk]
        pieces = []
        for k in range(tensors):
            start = (mine ^ k) * width + first * HEAD_DIM
            piece = lax.dynamic_slice_in_dim(whole, start, heads * HEAD_DIM, axis=3)
            with jax.named_scope(f"stash_{k}_{chunk}"):
                pieces.append(fetched(piece, k))
        return pieces

    upstream_direct = shifted(grad_out, -1)
    with jax.named_scope("forward_heads"):
        forward_out, aside = forward(fwd_qkv, grad_out, fwd_segments)
    received_direct = shifted(forward_out, 1)
    around = detour(detour(aside, "aside"), "onward")
    upstream = (upstream_direct, around)
    pieces = [fetched_chunk(parked, 0)]
    tokens = loss_tokens.astype(jnp.float32)
    pieces[0][0], tokens = lax.optimization_barrier((pieces[0][0], tokens))
    token_total = lax.psum(tokens, "dp")
    factor = jnp.float32(lax.axis_size("dp") * length) / token_total
    parked, token_total = lax.optimization_barrier((parked, token_total))
    pieces.append(fetched_chunk(parked, 1))
    received = jnp.where(came_around(1), around, received_direct)
    (grads,) = backward(0, pieces[0], upstream, bwd_segments, factor, None)
    parked, grads = lax.optimization_barrier((parked, grads))
    pieces.append(fetched_chunk(parked, 2))
    (grads,) = backward(1, pieces[1], upstream, bwd_segments, factor, grads)
    grads, received = backward(2, pieces[2], upstream, bwd_segments, factor, grads, received)
    return (received, grads)


def solution(mesh):
    placed = (
        P(None, ("pipe", "dp"), None, "tensor"),
        P(("pipe", "dp"), None),
        P(None, ("pipe", "dp"), "tensor", None),
        P(("pipe", "dp"), None),
        P(("pipe", "dp"), None, "tensor"),
        P(("pipe", "dp")),
    )
    return jax.shard_map(
        on_device,
        mesh=mesh,
        in_specs=placed,
        out_specs=(P(("pipe", "dp"), None, "tensor"), P(None, ("pipe", "dp"), None, "tensor")),
        check_vma=False,
    )
```

time: 196 us -> 209 us (1.066)
  waiting for transfers between devices: 45.4 us -> 122 us
  starting transfers between devices: 105 us -> 43.1 us
  local copies, waits for them, and re-layouts: 11.6 us -> 5.8 us
  blocking collectives: 9.81 us -> 11.9 us
    ppermute x18 -> x16, waiting for transfers between devices: 45.4 us -> 122 us  [the longest x12 80.8 us: fetched(): return lax.ppermute(piece, AXES, pairs)]
    ppermute x18 -> x16, starting transfers between devices: 105 us -> 43.1 us  [the longest x12 30.3 us: fetched(): return lax.ppermute(piece, AXES, pairs)]
    unnamed x23 -> x2, local copies, waits for them, and re-layouts: 7.6 us -> 0.01 us
    dynamic_slice x1 -> x3, local copies, waits for them, and re-layouts: 3.05 us -> 5.79 us  [fetched_chunk(): piece = lax.dynamic_slice_in_dim(whole, start, heads * HEAD_DIM, axis=3)]
    psum x1, blocking collectives: 9.81 us -> 11.9 us  [on_device(): token_total = lax.psum(tokens, 'dp')]
    pallas_call x1, Pallas kernels: 4.87 us -> 6.97 us  [forward(): pl.pallas_call(forward_kernel, grid=(FORWARD_STEPS,), in_specs=[pl.BlockS...]
    pallas_call x4 -> x3, Pallas kernels: 16.3 us -> 15.2 us  [backward(): pl.pallas_call(functools.partial(backward_kernel, parts), grid=(1,), in_s...]
  transfers between devices with their start and end apart: 18 -> 16, of which waited for: 11 -> 6; matrix products, arithmetic and copies ran while one was open for 2% -> 3% of each run, Pallas kernels for 8% -> 6%
where the time goes in v5:
time: 209 us; the launch traced here: 208 us
  waiting for transfers between devices  122 us (58%)
  starting transfers between devices  43.1 us (21%)
  Pallas kernels  22.2 us (11%)
  blocking collectives  11.9 us (6%)
  local copies, waits for them, and re-layouts  5.8 us (3%)
    ppermute x12, waiting for transfers between devices, fetched(): return lax.ppermute(piece, AXES, pairs)  80.8 us
    ppermute x2, waiting for transfers between devices, detour(): return lax.ppermute(array, AXES, pairs)  41.1 us
    ppermute x12, starting transfers between devices, fetched(): return lax.ppermute(piece, AXES, pairs)  30.3 us
    pallas_call x3, Pallas kernels, backward(): pl.pallas_call(functools.partial(backward_kernel, parts), grid=(1,), in_s...  15.2 us
    psum x1, blocking collectives, on_device(): token_total = lax.psum(tokens, 'dp')  11.9 us
    pallas_call x1, Pallas kernels, forward(): pl.pallas_call(forward_kernel, grid=(FORWARD_STEPS,), in_specs=[pl.BlockS...  6.97 us
    ppermute x2, starting transfers between devices, shifted(): return lax.ppermute(array, AXES, pairs)  6.44 us
    ppermute x2, starting transfers between devices, detour(): return lax.ppermute(array, AXES, pairs)  6.34 us
  transfers between devices with their start and end apart: 16, of which 6 were waited for; matrix products, arithmetic and copies ran while one was open for 3% of the time, Pallas kernels for 6%

profile of v5, /device:TPU:1, one launch (start us, length us, event | category | flops | bytes accessed | tf_op | source)
XLA Modules:
  0.0 208.1 jit_solution(14361903891202165792)
XLA Ops:
  0.6 7.0 %forward_heads.1 = (bf16[1,256,2048]{2,1,0:T(8,128)(2,1)}, bf16[1,256,2048]{2,1,0:T(8,128)(2,1)}) custom-call(bf16[3,1,256,2048]{3,2,1,0:T(8,128)(2,1)} %qkv_ref.1, bf16[1,256,2048]{2,1,0:T(8,128)(2,1)} %grad_ref.1, s32[1,256]{1,0:T(1,128)} %segment_ref.1), custom_call_target="tpu_custom_call" | custom-call | flops 536870912 | bytes 6291456 | tf_op jit(solution)/shard_map/forward_heads/pallas_call | solution.py:60
  7.6 0.0 copy-start
  7.6 5.1 %collective-permute-start.5 = (bf16[1,256,2048]{2,1,0:T(8,128)(2,1)}, bf16[1,256,2048]{2,1,0:T(8,128)(2,1)}, u32[]{:S(2)}, u32[]{:S(2)}) collective-permute-start(bf16[1,256,2048]{2,1,0:T(8,128)(2,1)} %get-tuple-element.14), channel_id=1, source_target_pairs={{4,20},{12,28},{132,148},{140,156},{116,100},{124,108},{244,228},{... | collective-permute-start | bytes 3145736 | tf_op jit(solution)/shard_map/aside_both/ppermute | solution.py:184
  12.7 1.3 collective-permute-start.4
  13.9 41.1 %collective-permute-done.5 = bf16[1,256,2048]{2,1,0:T(8,128)(2,1)} collective-permute-done((bf16[1,256,2048]{2,1,0:T(8,128)(2,1)}, bf16[1,256,2048]{2,1,0:T(8,128)(2,1)}, u32[]{:S(2)}, u32[]{:S(2)}) %collective-permute-start.5) | collective-permute-done | bytes 1048608 | tf_op jit(solution)/shard_map/aside_both/ppermute | solution.py:184
  55.1 1.3 collective-permute-start.6
  56.3 5.2 %collective-permute-start.15 = (bf16[1,256,2048]{2,1,0:T(8,128)(2,1)}, bf16[1,256,2048]{2,1,0:T(8,128)(2,1)}, u32[]{:S(2)}, u32[]{:S(2)}) collective-permute-start(bf16[1,256,2048]{2,1,0:T(8,128)(2,1)} %get-tuple-element.17), channel_id=1, source_target_pairs={{0,16},{4,20},{8,24},{12,28},{16,32},{20,36},{24,40},{28,44},{32,4... | collective-permute-start | bytes 3145736 | tf_op jit(solution)/shard_map/direct_out/ppermute | solution.py:171
  61.5 2.4 %constant_dynamic-slice_fusion.8 = (bf16[3,1,64,1024]{3,2,1,0:T(8,128)(2,1)S(1)}, bf16[3,1,64,1024]{3,2,1,0:T(8,128)(2,1)}, bf16[3,1,64,1024]{3,2,1,0:T(8,128)(2,1)S(1)}, bf16[3,1,64,1024]{3,2,1,0:T(8,128)(2,1)}) fusion(bf16[3,1,64,8192]{3,2,1,0:T(8,128)(2,1)} %param.8, s32[]{:T(128)S(6)} %select_n.58, s32[]{:T(128)S(6)} %select_n.56, s32[]{:T(128)S(6)} %select_n.55, ...), kind=kLoop, calls=%fused_computation.9 | loop fusion | bytes 3145744 | tf_op jit(solution)/shard_map/dynamic_slice | solution.py:203
  63.9 0.0 collective-permute-start.3
  63.9 0.0 collective-permute-start
  63.9 44.1 %collective-permute-done.3.refs_3_ = bf16[3,1,64,1024]{3,2,1,0:T(8,128)(2,1)S(1)} collective-permute-done((bf16[3,1,64,1024]{3,2,1,0:T(8,128)(2,1)S(1)}, bf16[3,1,64,1024]{3,2,1,0:T(8,128)(2,1)S(1)}, u32[]{:S(2)}, u32[]{:S(2)}) %collective-permute-start.3) | collective-permute-done | bytes 393248 | tf_op jit(solution)/shard_map/stash_3_0/ppermute | solution.py:154
  108.1 0.0 collective-permute-start.1
  108.1 0.0 collective-permute-done.refs_0_
  108.1 4.8 %collective-permute-start.2 = (bf16[3,1,64,1024]{3,2,1,0:T(8,128)(2,1)}, bf16[3,1,64,1024]{3,2,1,0:T(8,128)(2,1)}, u32[]{:S(2)}, u32[]{:S(2)}) collective-permute-start(bf16[3,1,64,1024]{3,2,1,0:T(8,128)(2,1)} %get-tuple-element.31), channel_id=1, source_target_pairs={{0,248},{4,252},{8,240},{12,244},{16,232},{20,236},{24,224},{28,22... | collective-permute-start | bytes 1179656 | tf_op jit(solution)/shard_map/stash_2_0/ppermute | solution.py:154
  113.5 11.9 %psum.7 = f32[1]{0:T(128)} all-reduce(f32[1]{0:T(128)S(6)} %convert_element_type.4), channel_id=1, replica_groups=mesh['pipe'=16,'tensor'=4,'dp'=4] {'dp'}, use_global_device_ids=true, to_apply=%region_0.0 | all-reduce | flops 1 | bytes 8 | tf_op jit(solution)/shard_map/psum | solution.py:217
  125.4 2.1 %constant_dynamic-slice_fusion = (bf16[3,1,64,512]{3,2,1,0:T(8,128)(2,1)}, bf16[3,1,64,512]{3,2,1,0:T(8,128)(2,1)}, bf16[3,1,64,512]{3,2,1,0:T(8,128)(2,1)}, bf16[3,1,64,512]{3,2,1,0:T(8,128)(2,1)}) fusion(bf16[3,1,64,8192]{3,2,1,0:T(8,128)(2,1)} %param.8, s32[]{:T(128)S(6)} %select_n.66, s32[]{:T(128)S(6)} %select_n.65, s32[]{:T(128)S(6)} %select_n.64, ...), kind=kLoop, calls=%fused_computation.1 | loop fusion | bytes 1572880 | tf_op jit(solution)/shard_map/dynamic_slice | solution.py:203
  127.6 29.4 %collective-permute-done.1.refs_1_ = bf16[3,1,64,1024]{3,2,1,0:T(8,128)(2,1)S(1)} collective-permute-done((bf16[3,1,64,1024]{3,2,1,0:T(8,128)(2,1)}, bf16[3,1,64,1024]{3,2,1,0:T(8,128)(2,1)S(1)}, u32[]{:S(2)}, u32[]{:S(2)}) %collective-permute-start.1) | collective-permute-done | bytes 393248 | tf_op jit(solution)/shard_map/stash_1_0/ppermute | solution.py:154
  156.9 12.5 %collective-permute-start.14 = (bf16[3,1,64,512]{3,2,1,0:T(8,128)(2,1)}, bf16[3,1,64,512]{3,2,1,0:T(8,128)(2,1)S(1)}, u32[]{:S(2)}, u32[]{:S(2)}) collective-permute-start(bf16[3,1,64,512]{3,2,1,0:T(8,128)(2,1)} %get-tuple-element.20), channel_id=1, source_target_pairs={{0,252},{4,248},{8,244},{12,240},{16,236},{20,232},{24,228},{28,22... | collective-permute-start | bytes 589832 | tf_op jit(solution)/shard_map/stash_3_1/ppermute | solution.py:154
  169.4 0.0 collective-permute-done.2.refs_2_
  169.4 0.0 collective-permute-start.13
  169.4 0.0 collective-permute-done.4.refs_4_
  169.4 0.1 collective-permute-start.12
  170.2 0.0 collective-permute-done.6.refs_5_
  170.2 3.9 %collective-permute-start.11 = (bf16[3,1,64,512]{3,2,1,0:T(8,128)(2,1)}, bf16[3,1,64,512]{3,2,1,0:T(8,128)(2,1)S(1)}, u32[]{:S(2)}, u32[]{:S(2)}) collective-permute-start(bf16[3,1,64,512]{3,2,1,0:T(8,128)(2,1)} %get-tuple-element.23), channel_id=1, source_target_pairs={{0,240},{4,244},{8,248},{12,252},{16,224},{20,228},{24,232},{28,23... | collective-permute-start | bytes 589832 | tf_op jit(solution)/shard_map/stash_0_1/ppermute | solution.py:154
  174.1 0.0 copy-done
  174.1 7.1 %shard_map.77.refs_8_ = bf16[3,1,256,2048]{3,2,1,0:T(8,128)(2,1)} custom-call(bf16[3,1,64,1024]{3,2,1,0:T(8,128)(2,1)S(1)} %collective-permute-done.refs_0_, bf16[3,1,64,1024]{3,2,1,0:T(8,128)(2,1)S(1)} %collective-permute-done.1.refs_1_, bf16[3,1,64,1024]{3,2,1,0:T(8,128)(2,1)} %collective-permute-done.2.refs_2_, ...), custom_call_target="tpu_custom_call" | custom-call | flops 671088640 | bytes 3670016 | tf_op jit(solution)/shard_map/pallas_call | solution.py:130
  181.2 1.3 constant_dynamic-slice_fusion.4
  182.5 0.0 collective-permute-done.14.refs_3_
  182.5 5.0 %collective-permute-start.10 = (bf16[3,1,64,512]{3,2,1,0:T(8,128)(2,1)S(1)}, bf16[3,1,64,512]{3,2,1,0:T(8,128)(2,1)S(1)}, u32[]{:S(2)}, u32[]{:S(2)}) collective-permute-start(bf16[3,1,64,512]{3,2,1,0:T(8,128)(2,1)S(1)} %get-tuple-element.24), channel_id=1, source_target_pairs={{0,252},{4,248},{8,244},{12,240},{16,236},{20,232},{24,228},{28,22... | collective-permute-start | bytes 589832 | tf_op jit(solution)/shard_map/stash_3_2/ppermute | solution.py:154
  187.5 0.0 collective-permute-done.13.refs_2_
  187.5 0.1 collective-permute-start.9
  187.6 0.0 collective-permute-done.12.refs_1_
  187.6 0.2 collective-permute-start.8
  187.8 0.0 collective-permute-done.15
  187.8 3.7 %collective-permute-start.7 = (bf16[3,1,64,512]{3,2,1,0:T(8,128)(2,1)S(1)}, bf16[3,1,64,512]{3,2,1,0:T(8,128)(2,1)S(1)}, u32[]{:S(2)}, u32[]{:S(2)}) collective-permute-start(bf16[3,1,64,512]{3,2,1,0:T(8,128)(2,1)S(1)} %get-tuple-element.27), channel_id=1, source_target_pairs={{0,240},{4,244},{8,248},{12,252},{16,224},{20,228},{24,232},{28,23... | collective-permute-start | bytes 589832 | tf_op jit(solution)/shard_map/stash_0_2/ppermute | solution.py:154
  191.5 1.1 broadcast_select_fusion.refs_9_
  192.6 0.0 collective-permute-done.11.refs_0_
  192.6 4.6 %shard_map.78.refs_8_ = bf16[3,1,256,2048]{3,2,1,0:T(8,128)(2,1)} custom-call(bf16[3,1,64,512]{3,2,1,0:T(8,128)(2,1)S(1)} %collective-permute-done.11.refs_0_, bf16[3,1,64,512]{3,2,1,0:T(8,128)(2,1)} %collective-permute-done.12.refs_1_, bf16[3,1,64,512]{3,2,1,0:T(8,128)(2,1)} %collective-permute-done.13.refs_2_, ...), custom_call_target="tpu_custom_call", output_to_operand_aliasing={{}: (8, {})} | custom-call | flops 335544320 | bytes 1835008 | tf_op jit(solution)/shard_map/pallas_call | solution.py:130
  197.2 0.0 collective-permute-done.10.refs_3_
  197.2 0.3 collective-permute-done.9.refs_2_
  197.5 3.0 %collective-permute-done.8.refs_1_ = bf16[3,1,64,512]{3,2,1,0:T(8,128)(2,1)S(1)} collective-permute-done((bf16[3,1,64,512]{3,2,1,0:T(8,128)(2,1)S(1)}, bf16[3,1,64,512]{3,2,1,0:T(8,128)(2,1)S(1)}, u32[]{:S(2)}, u32[]{:S(2)}) %collective-permute-start.8) | collective-permute-done | bytes 196640 | tf_op jit(solution)/shard_map/stash_1_2/ppermute | solution.py:154
  200.5 4.0 %collective-permute-done.7.refs_0_ = bf16[3,1,64,512]{3,2,1,0:T(8,128)(2,1)S(1)} collective-permute-done((bf16[3,1,64,512]{3,2,1,0:T(8,128)(2,1)S(1)}, bf16[3,1,64,512]{3,2,1,0:T(8,128)(2,1)S(1)}, u32[]{:S(2)}, u32[]{:S(2)}) %collective-permute-start.7) | collective-permute-done | bytes 196640 | tf_op jit(solution)/shard_map/stash_0_2/ppermute | solution.py:154
  204.5 3.6 %shard_map.79 = (bf16[3,1,256,2048]{3,2,1,0:T(8,128)(2,1)}, bf16[1,256,2048]{2,1,0:T(8,128)(2,1)}) custom-call(bf16[3,1,64,512]{3,2,1,0:T(8,128)(2,1)S(1)} %collective-permute-done.7.refs_0_, bf16[3,1,64,512]{3,2,1,0:T(8,128)(2,1)S(1)} %collective-permute-done.8.refs_1_, ...), custom_call_target="tpu_custom_call", output_to_operand_aliasing={{0}: (8, {}), {1}: (9, {})} | custom-call | flops 335544320 | bytes 1835008 | tf_op jit(solution)/shard_map/pallas_call | solution.py:130
Async XLA Ops:
  7.6 166.5 %copy-start = (s32[1,256]{1,0:T(1,128)S(1)}, s32[1,256]{1,0:T(1,128)}, u32[]{:S(2)}) copy-start(s32[1,256]{1,0:T(1,128)} %refs_6_.5) | copy-start | bytes 3076
  7.6 47.5 %collective-permute-start.5 = (bf16[1,256,2048]{2,1,0:T(8,128)(2,1)}, bf16[1,256,2048]{2,1,0:T(8,128)(2,1)}, u32[]{:S(2)}, u32[]{:S(2)}) collective-permute-start(bf16[1,256,2048]{2,1,0:T(8,128)(2,1)} %get-tuple-element.14), channel_id=1, source_target_pairs={{4,20},{12,28},{132,148},{140,156},{116,100},{124,108},{244,228},{... | collective-permute-start | bytes 3145736 | tf_op jit(solution)/shard_map/aside_both/ppermute | solution.py:184
  12.7 156.8 %collective-permute-start.4 = (bf16[1,256,2048]{2,1,0:T(8,128)(2,1)}, bf16[1,256,2048]{2,1,0:T(8,128)(2,1)S(1)}, u32[]{:S(2)}, u32[]{:S(2)}) collective-permute-start(bf16[1,256,2048]{2,1,0:T(8,128)(2,1)} %grad_ref.1), channel_id=1, source_target_pairs={{0,240},{8,248},{16,0},{20,4},{24,8},{28,12},{32,16},{36,20},{40,2... | collective-permute-start | bytes 3145736 | tf_op jit(solution)/shard_map/direct_grad/ppermute | solution.py:171
  55.1 115.1 %collective-permute-start.6 = (bf16[1,256,2048]{2,1,0:T(8,128)(2,1)}, bf16[1,256,2048]{2,1,0:T(8,128)(2,1)S(1)}, u32[]{:S(2)}, u32[]{:S(2)}) collective-permute-start(bf16[1,256,2048]{2,1,0:T(8,128)(2,1)} %collective-permute-done.5), channel_id=1, source_target_pairs={{20,244},{28,252},{148,116},{156,124},{100,132},{108,140},{228,4},... | collective-permute-start | bytes 3145736 | tf_op jit(solution)/shard_map/onward_both/ppermute | solution.py:184
  56.3 131.5 %collective-permute-start.15 = (bf16[1,256,2048]{2,1,0:T(8,128)(2,1)}, bf16[1,256,2048]{2,1,0:T(8,128)(2,1)}, u32[]{:S(2)}, u32[]{:S(2)}) collective-permute-start(bf16[1,256,2048]{2,1,0:T(8,128)(2,1)} %get-tuple-element.17), channel_id=1, source_target_pairs={{0,16},{4,20},{8,24},{12,28},{16,32},{20,36},{24,40},{28,44},{32,4... | collective-permute-start | bytes 3145736 | tf_op jit(solution)/shard_map/direct_out/ppermute | solution.py:171
  63.9 44.2 %collective-permute-start.3 = (bf16[3,1,64,1024]{3,2,1,0:T(8,128)(2,1)S(1)}, bf16[3,1,64,1024]{3,2,1,0:T(8,128)(2,1)S(1)}, u32[]{:S(2)}, u32[]{:S(2)}) collective-permute-start(bf16[3,1,64,1024]{3,2,1,0:T(8,128)(2,1)S(1)} %get-tuple-element.28), channel_id=1, source_target_pairs={{0,252},{4,248},{8,244},{12,240},{16,236},{20,232},{24,228},{28,22... | collective-permute-start | bytes 1179656 | tf_op jit(solution)/shard_map/stash_3_0/ppermute | solution.py:154
  63.9 44.2 %collective-permute-start = (bf16[3,1,64,1024]{3,2,1,0:T(8,128)(2,1)S(1)}, bf16[3,1,64,1024]{3,2,1,0:T(8,128)(2,1)S(1)}, u32[]{:S(2)}, u32[]{:S(2)}) collective-permute-start(bf16[3,1,64,1024]{3,2,1,0:T(8,128)(2,1)S(1)} %get-tuple-element.30), channel_id=1, source_target_pairs={{0,240},{4,244},{8,248},{12,252},{16,224},{20,228},{24,232},{28,23... | collective-permute-start | bytes 1179656 | tf_op jit(solution)/shard_map/stash_0_0/ppermute | solution.py:154
  108.1 48.8 %collective-permute-start.1 = (bf16[3,1,64,1024]{3,2,1,0:T(8,128)(2,1)}, bf16[3,1,64,1024]{3,2,1,0:T(8,128)(2,1)S(1)}, u32[]{:S(2)}, u32[]{:S(2)}) collective-permute-start(bf16[3,1,64,1024]{3,2,1,0:T(8,128)(2,1)} %get-tuple-element.29), channel_id=1, source_target_pairs={{0,244},{4,240},{8,252},{12,248},{16,228},{20,224},{24,236},{28,23... | collective-permute-start | bytes 1179656 | tf_op jit(solution)/shard_map/stash_1_0/ppermute | solution.py:154
  108.1 61.4 %collective-permute-start.2 = (bf16[3,1,64,1024]{3,2,1,0:T(8,128)(2,1)}, bf16[3,1,64,1024]{3,2,1,0:T(8,128)(2,1)}, u32[]{:S(2)}, u32[]{:S(2)}) collective-permute-start(bf16[3,1,64,1024]{3,2,1,0:T(8,128)(2,1)} %get-tuple-element.31), channel_id=1, source_target_pairs={{0,248},{4,252},{8,240},{12,244},{16,232},{20,236},{24,224},{28,22... | collective-permute-start | bytes 1179656 | tf_op jit(solution)/shard_map/stash_2_0/ppermute | solution.py:154
  156.9 25.6 %collective-permute-start.14 = (bf16[3,1,64,512]{3,2,1,0:T(8,128)(2,1)}, bf16[3,1,64,512]{3,2,1,0:T(8,128)(2,1)S(1)}, u32[]{:S(2)}, u32[]{:S(2)}) collective-permute-start(bf16[3,1,64,512]{3,2,1,0:T(8,128)(2,1)} %get-tuple-element.20), channel_id=1, source_target_pairs={{0,252},{4,248},{8,244},{12,240},{16,236},{20,232},{24,228},{28,22... | collective-permute-start | bytes 589832 | tf_op jit(solution)/shard_map/stash_3_1/ppermute | solution.py:154
  169.4 18.1 %collective-permute-start.13 = (bf16[3,1,64,512]{3,2,1,0:T(8,128)(2,1)}, bf16[3,1,64,512]{3,2,1,0:T(8,128)(2,1)}, u32[]{:S(2)}, u32[]{:S(2)}) collective-permute-start(bf16[3,1,64,512]{3,2,1,0:T(8,128)(2,1)} %get-tuple-element.21), channel_id=1, source_target_pairs={{0,248},{4,252},{8,240},{12,244},{16,232},{20,236},{24,224},{28,22... | collective-permute-start | bytes 589832 | tf_op jit(solution)/shard_map/stash_2_1/ppermute | solution.py:154
  169.4 18.2 %collective-permute-start.12 = (bf16[3,1,64,512]{3,2,1,0:T(8,128)(2,1)}, bf16[3,1,64,512]{3,2,1,0:T(8,128)(2,1)}, u32[]{:S(2)}, u32[]{:S(2)}) collective-permute-start(bf16[3,1,64,512]{3,2,1,0:T(8,128)(2,1)} %get-tuple-element.22), channel_id=1, source_target_pairs={{0,244},{4,240},{8,252},{12,248},{16,228},{20,224},{24,236},{28,23... | collective-permute-start | bytes 589832 | tf_op jit(solution)/shard_map/stash_1_1/ppermute | solution.py:154
  170.2 22.4 %collective-permute-start.11 = (bf16[3,1,64,512]{3,2,1,0:T(8,128)(2,1)}, bf16[3,1,64,512]{3,2,1,0:T(8,128)(2,1)S(1)}, u32[]{:S(2)}, u32[]{:S(2)}) collective-permute-start(bf16[3,1,64,512]{3,2,1,0:T(8,128)(2,1)} %get-tuple-element.23), channel_id=1, source_target_pairs={{0,240},{4,244},{8,248},{12,252},{16,224},{20,228},{24,232},{28,23... | collective-permute-start | bytes 589832 | tf_op jit(solution)/shard_map/stash_0_1/ppermute | solution.py:154
  182.5 14.7 %collective-permute-start.10 = (bf16[3,1,64,512]{3,2,1,0:T(8,128)(2,1)S(1)}, bf16[3,1,64,512]{3,2,1,0:T(8,128)(2,1)S(1)}, u32[]{:S(2)}, u32[]{:S(2)}) collective-permute-start(bf16[3,1,64,512]{3,2,1,0:T(8,128)(2,1)S(1)} %get-tuple-element.24), channel_id=1, source_target_pairs={{0,252},{4,248},{8,244},{12,240},{16,236},{20,232},{24,228},{28,22... | collective-permute-start | bytes 589832 | tf_op jit(solution)/shard_map/stash_3_2/ppermute | solution.py:154
  187.5 10.0 %collective-permute-start.9 = (bf16[3,1,64,512]{3,2,1,0:T(8,128)(2,1)S(1)}, bf16[3,1,64,512]{3,2,1,0:T(8,128)(2,1)S(1)}, u32[]{:S(2)}, u32[]{:S(2)}) collective-permute-start(bf16[3,1,64,512]{3,2,1,0:T(8,128)(2,1)S(1)} %get-tuple-element.25), channel_id=1, source_target_pairs={{0,248},{4,252},{8,240},{12,244},{16,232},{20,236},{24,224},{28,22... | collective-permute-start | bytes 589832 | tf_op jit(solution)/shard_map/stash_2_2/ppermute | solution.py:154
  187.6 12.9 %collective-permute-start.8 = (bf16[3,1,64,512]{3,2,1,0:T(8,128)(2,1)S(1)}, bf16[3,1,64,512]{3,2,1,0:T(8,128)(2,1)S(1)}, u32[]{:S(2)}, u32[]{:S(2)}) collective-permute-start(bf16[3,1,64,512]{3,2,1,0:T(8,128)(2,1)S(1)} %get-tuple-element.26), channel_id=1, source_target_pairs={{0,244},{4,240},{8,252},{12,248},{16,228},{20,224},{24,236},{28,23... | collective-permute-start | bytes 589832 | tf_op jit(solution)/shard_map/stash_1_2/ppermute | solution.py:154
  187.8 16.6 %collective-permute-start.7 = (bf16[3,1,64,512]{3,2,1,0:T(8,128)(2,1)S(1)}, bf16[3,1,64,512]{3,2,1,0:T(8,128)(2,1)S(1)}, u32[]{:S(2)}, u32[]{:S(2)}) collective-permute-start(bf16[3,1,64,512]{3,2,1,0:T(8,128)(2,1)S(1)} %get-tuple-element.27), channel_id=1, source_target_pairs={{0,240},{4,244},{8,248},{12,252},{16,224},{20,228},{24,232},{28,23... | collective-permute-start | bytes 589832 | tf_op jit(solution)/shard_map/stash_0_2/ppermute | solution.py:154

commit v6 on v5

--- a/solution.py
+++ b/solution.py
@@ -36,9 +36,7 @@
     return jnp.where(across == across.T, 0.0, -1e31).astype(jnp.float32)
 
 
-def forward_kernel(qkv_ref, grad_ref, segment_ref, out_ref, aside_ref, outside):
-    sends_out = detoured(lax.axis_index("pipe"), 1, 1) == 1
-
+def forward_kernel(qkv_ref, segment_ref, out_ref, outside):
     @pl.when(pl.program_id(0) == 0)
     def _():
         outside[...] = outside_of(segment_ref)
@@ -47,41 +45,35 @@
         head = slice(start, start + HEAD_DIM)
         probs = probabilities(qkv_ref[0, 0, :, head], qkv_ref[1, 0, :, head], outside[...])
         mixed = product(probs.astype(jnp.bfloat16), qkv_ref[2, 0, :, head], NN)
-        mixed = mixed.astype(jnp.bfloat16)
-        out_ref[0, :, head] = mixed
-        aside_ref[0, :, head] = jnp.where(sends_out, mixed, grad_ref[0, :, head])
-
-
-def forward(qkv, grad_out, segment):
+        out_ref[0, :, head] = mixed.astype(jnp.bfloat16)
+
+
+def forward(qkv, segment):
     _, _, length, width = qkv.shape
     step = width // FORWARD_STEPS
-    columns = pl.BlockSpec((1, length, step), lambda c: (0, 0, c))
-    out = jax.ShapeDtypeStruct((1, length, width), jnp.bfloat16)
     return pl.pallas_call(
         forward_kernel,
         grid=(FORWARD_STEPS,),
         in_specs=[
             pl.BlockSpec((3, 1, length, step), lambda c: (0, 0, 0, c)),
-            columns,
             pl.BlockSpec((1, length), lambda c: (0, 0)),
         ],
-        out_specs=[columns, columns],
-        out_shape=[out, out],
+        out_specs=pl.BlockSpec((1, length, step), lambda c: (0, 0, c)),
+        out_shape=jax.ShapeDtypeStruct((1, length, width), jnp.bfloat16),
         scratch_shapes=[pltpu.VMEM((length, length), jnp.float32)],
         compiler_params=pltpu.CompilerParams(vmem_limit_bytes=56 * 1024 * 1024),
         cost_estimate=pl.CostEstimate(
             flops=4 * length * length * width,
-            bytes_accessed=12 * length * width,
+            bytes_accessed=8 * length * width,
             transcendentals=length * length * width // HEAD_DIM,
         ),
-    )(qkv, grad_out, segment)
+    )(qkv, segment)
 
 
 def backward_kernel(parts, *refs):
     pieces, refs = refs[:parts], refs[parts:]
-    direct_ref, around_ref, segment_ref, factor_ref = refs[:4]
-    out_ref, stash = refs[-2:] if len(refs) < 8 else (refs[-3], refs[-1])
-    around = came_around(-1)
+    upstream_ref, segment_ref, factor_ref = refs[:3]
+    out_ref, stash = refs[-2:] if len(refs) < 7 else (refs[-3], refs[-1])
     mine = lax.axis_index("tensor")
     rows = pieces[0].shape[2]
     for k in range(parts):
@@ -89,10 +81,10 @@
         stash[:, pl.ds(start, rows), :] = pieces[k][:, 0]
     outside = outside_of(segment_ref)
     factor = factor_ref[0]
-    for start in range(0, direct_ref.shape[2], HEAD_DIM):
+    for start in range(0, upstream_ref.shape[2], HEAD_DIM):
         head = slice(start, start + HEAD_DIM)
         queries, keys, values = stash[0, :, head], stash[1, :, head], stash[2, :, head]
-        upstream = jnp.where(around, around_ref[0, :, head], direct_ref[0, :, head])
+        upstream = upstream_ref[0, :, head]
         probs = probabilities(queries, keys, outside)
         grad_value = product(probs.astype(jnp.bfloat16), upstream, TN)
         grad_probs = product(upstream, values, NT)
@@ -104,14 +96,13 @@
 
 
 def backward(chunk, pieces, upstream, segment, factor, earlier, carried=None):
-    _, length, width = upstream[0].shape
+    _, length, width = upstream.shape
     first, heads = CHUNKS[chunk]
     step = heads * HEAD_DIM
     place = first // heads
     parts = len(pieces)
-    operands = [*pieces, *upstream, segment, factor]
+    operands = [*pieces, upstream, segment, factor]
     in_specs = [pl.BlockSpec(memory_space=pltpu.VMEM)] * parts + [
-        pl.BlockSpec((1, length, step), lambda i: (0, 0, place)),
         pl.BlockSpec((1, length, step), lambda i: (0, 0, place)),
         pl.BlockSpec((1, length), lambda i: (0, 0)),
         pl.BlockSpec(memory_space=pltpu.SMEM),
@@ -159,29 +150,25 @@
     return (t & 1) * (p % half == (half - 1 if by > 0 else 0))
 
 
-def shifted(array, by):
-    sections, tensors = lax.axis_size("pipe"), lax.axis_size("tensor")
-    pairs = [
-        (p * tensors + t, (p + by) % sections * tensors + t)
-        for p in range(sections)
-        for t in range(tensors)
-        if not detoured(p, t, by)
-    ]
-    with jax.named_scope("direct_out" if by > 0 else "direct_grad"):
-        return lax.ppermute(array, AXES, pairs)
-
-
-def detour(array, leg):
+def shift_pairs(by, leg):
     sections, tensors = lax.axis_size("pipe"), lax.axis_size("tensor")
     pairs = []
-    for by in (-1, 1):
-        for p in range(sections):
-            for t in range(tensors):
-                if detoured(p, t, by):
-                    start, end = (p, p - by) if leg == "aside" else (p - by, p + by)
-                    pairs.append((start % sections * tensors + t, end % sections * tensors + t))
-    with jax.named_scope(f"{leg}_both"):
-        return lax.ppermute(array, AXES, pairs)
+    for p in range(sections):
+        for t in range(tensors):
+            aside = detoured(p, t, by)
+            start, end = p, p + by
+            if leg == "aside":
+                end = p - by
+            if leg == "onward":
+                start = p - by
+            if leg == "whole" or aside == (leg != "direct"):
+                pairs.append((start % sections * tensors + t, end % sections * tensors + t))
+    return pairs
+
+
+def shifted(array, by, leg):
+    with jax.named_scope(f"{leg}_{'out' if by > 0 else 'grad'}"):
+        return lax.ppermute(array, AXES, shift_pairs(by, leg))
 
 
 def came_around(by):
@@ -205,12 +192,12 @@
                 pieces.append(fetched(piece, k))
         return pieces
 
-    upstream_direct = shifted(grad_out, -1)
+    upstream = shifted(grad_out, -1, "whole")
     with jax.named_scope("forward_heads"):
-        forward_out, aside = forward(fwd_qkv, grad_out, fwd_segments)
-    received_direct = shifted(forward_out, 1)
-    around = detour(detour(aside, "aside"), "onward")
-    upstream = (upstream_direct, around)
+        forward_out = forward(fwd_qkv, fwd_segments)
+    received_direct = shifted(forward_out, 1, "whole")
+    received_aside = shifted(forward_out, 1, "aside")
+    received_around = shifted(received_aside, 1, "onward")
     pieces = [fetched_chunk(parked, 0)]
     tokens = loss_tokens.astype(jnp.float32)
     pieces[0][0], tokens = lax.optimization_barrier((pieces[0][0], tokens))
@@ -218,7 +205,7 @@
     factor = jnp.float32(lax.axis_size("dp") * length) / token_total
     parked, token_total = lax.optimization_barrier((parked, token_total))
     pieces.append(fetched_chunk(parked, 1))
-    received = jnp.where(came_around(1), around, received_direct)
+    received = received_direct
     (grads,) = backward(0, pieces[0], upstream, bwd_segments, factor, None)
     parked, grads = lax.optimization_barrier((parked, grads))
     pieces.append(fetched_chunk(parked, 2))

time: 209 us -> 176 us (0.84)
  waiting for transfers between devices: 122 us -> 98.4 us
  starting transfers between devices: 43.1 us -> 36.1 us
    ppermute x4 -> x2, waiting for transfers between devices: 41.1 us -> 0.01 us  [shifted(): return lax.ppermute(array, AXES, shift_pairs(by, leg))]
    ppermute x12, waiting for transfers between devices: 80.8 us -> 98.4 us  [fetched(): return lax.ppermute(piece, AXES, pairs)]
    ppermute x4 -> x2, starting transfers between devices: 12.8 us -> 9.07 us  [shifted(): return lax.ppermute(array, AXES, shift_pairs(by, leg))]
    ppermute x12, starting transfers between devices: 30.3 us -> 27.1 us  [fetched(): return lax.ppermute(piece, AXES, pairs)]
  transfers between devices with their start and end apart: 16 -> 14, of which waited for: 6 -> 7; matrix products, arithmetic and copies ran while one was open for 3% -> 3% of each run, Pallas kernels for 6% -> 10%
where the time goes in v6:
time: 176 us; the launch traced here: 175 us
  waiting for transfers between devices  98.4 us (56%)
  starting transfers between devices  36.1 us (21%)
  Pallas kernels  21.9 us (12%)
  blocking collectives  9.89 us (6%)
  local copies, waits for them, and re-layouts  6.77 us (4%)
  between operations  2.02 us (1%)
    ppermute x12, waiting for transfers between devices, fetched(): return lax.ppermute(piece, AXES, pairs)  98.4 us
    ppermute x12, starting transfers between devices, fetched(): return lax.ppermute(piece, AXES, pairs)  27.1 us
    pallas_call x3, Pallas kernels, backward(): pl.pallas_call(functools.partial(backward_kernel, parts), grid=(1,), in_s...  15.3 us
    psum x1, blocking collectives, on_device(): token_total = lax.psum(tokens, 'dp')  9.89 us
    ppermute x2, starting transfers between devices, shifted(): return lax.ppermute(array, AXES, shift_pairs(by, leg))  9.07 us
    pallas_call x1, Pallas kernels, forward(): pl.pallas_call(forward_kernel, grid=(FORWARD_STEPS,), in_specs=[pl.BlockS...  6.59 us
    dynamic_slice x3, local copies, waits for them, and re-layouts, fetched_chunk(): piece = lax.dynamic_slice_in_dim(whole, start, heads * HEAD_DIM, axis=3)  5.8 us
  transfers between devices with their start and end apart: 14, of which 7 were waited for; matrix products, arithmetic and copies ran while one was open for 3% of the time, Pallas kernels for 10%

profile of v6, /device:TPU:1, one launch (start us, length us, event | category | flops | bytes accessed | tf_op | source)
XLA Modules:
  0.0 175.1 jit_solution(8561536655262256571)
XLA Ops:
  0.6 7.4 %collective-permute-start.4 = (bf16[1,256,2048]{2,1,0:T(8,128)(2,1)}, bf16[1,256,2048]{2,1,0:T(8,128)(2,1)S(1)}, u32[]{:S(2)}, u32[]{:S(2)}) collective-permute-start(bf16[1,256,2048]{2,1,0:T(8,128)(2,1)} %param.10), channel_id=1, source_target_pairs={{0,240},{4,244},{8,248},{12,252},{16,0},{20,4},{24,8},{28,12},{32,... | collective-permute-start | bytes 3145736 | tf_op jit(solution)/shard_map/whole_grad/ppermute | solution.py:171
  8.0 2.4 %constant_dynamic-slice_fusion.8 = (bf16[3,1,64,1024]{3,2,1,0:T(8,128)(2,1)}, bf16[3,1,64,1024]{3,2,1,0:T(8,128)(2,1)}, bf16[3,1,64,1024]{3,2,1,0:T(8,128)(2,1)S(1)}, bf16[3,1,64,1024]{3,2,1,0:T(8,128)(2,1)}) fusion(bf16[3,1,64,8192]{3,2,1,0:T(8,128)(2,1)} %param.8, s32[]{:T(128)S(6)} %select_n.39, s32[]{:T(128)S(6)} %select_n.37, s32[]{:T(128)S(6)} %select_n.36, ...), kind=kLoop, calls=%fused_computation.8 | loop fusion | bytes 3145744 | tf_op jit(solution)/shard_map/dynamic_slice | solution.py:190
  10.4 0.0 copy-start
  10.4 0.3 collective-permute-start
  10.7 6.6 %forward_heads.1 = bf16[1,256,2048]{2,1,0:T(8,128)(2,1)} custom-call(bf16[3,1,256,2048]{3,2,1,0:T(8,128)(2,1)} %qkv_ref.1, s32[1,256]{1,0:T(1,128)} %segment_ref.1), custom_call_target="tpu_custom_call" | custom-call | flops 536870912 | bytes 4194304 | tf_op jit(solution)/shard_map/forward_heads/pallas_call | solution.py:54
  17.3 1.7 collective-permute-start.13
  18.9 4.9 %collective-permute-start.3 = (bf16[3,1,64,1024]{3,2,1,0:T(8,128)(2,1)}, bf16[3,1,64,1024]{3,2,1,0:T(8,128)(2,1)S(1)}, u32[]{:S(2)}, u32[]{:S(2)}) collective-permute-start(bf16[3,1,64,1024]{3,2,1,0:T(8,128)(2,1)} %get-tuple-element.24), channel_id=1, source_target_pairs={{0,252},{4,248},{8,244},{12,240},{16,236},{20,232},{24,228},{28,22... | collective-permute-start | bytes 1179656 | tf_op jit(solution)/shard_map/stash_3_0/ppermute | solution.py:145
  23.8 0.0 collective-permute-start.1
  23.8 65.3 %collective-permute-done.refs_0_ = bf16[3,1,64,1024]{3,2,1,0:T(8,128)(2,1)S(1)} collective-permute-done((bf16[3,1,64,1024]{3,2,1,0:T(8,128)(2,1)S(1)}, bf16[3,1,64,1024]{3,2,1,0:T(8,128)(2,1)S(1)}, u32[]{:S(2)}, u32[]{:S(2)}) %collective-permute-start) | collective-permute-done | bytes 393248 | tf_op jit(solution)/shard_map/stash_0_0/ppermute | solution.py:145
  89.1 5.6 %collective-permute-start.2 = (bf16[3,1,64,1024]{3,2,1,0:T(8,128)(2,1)}, bf16[3,1,64,1024]{3,2,1,0:T(8,128)(2,1)}, u32[]{:S(2)}, u32[]{:S(2)}) collective-permute-start(bf16[3,1,64,1024]{3,2,1,0:T(8,128)(2,1)} %get-tuple-element.27), channel_id=1, source_target_pairs={{0,248},{4,252},{8,240},{12,244},{16,232},{20,236},{24,224},{28,22... | collective-permute-start | bytes 1179656 | tf_op jit(solution)/shard_map/stash_2_0/ppermute | solution.py:145
  95.3 9.9 %psum.7 = f32[1]{0:T(128)} all-reduce(f32[1]{0:T(128)S(6)} %convert_element_type.3), channel_id=1, replica_groups=mesh['pipe'=16,'tensor'=4,'dp'=4] {'dp'}, use_global_device_ids=true, to_apply=%region_0.0 | all-reduce | flops 1 | bytes 8 | tf_op jit(solution)/shard_map/psum | solution.py:204
  105.2 2.1 %constant_dynamic-slice_fusion = (bf16[3,1,64,512]{3,2,1,0:T(8,128)(2,1)}, bf16[3,1,64,512]{3,2,1,0:T(8,128)(2,1)}, bf16[3,1,64,512]{3,2,1,0:T(8,128)(2,1)}, bf16[3,1,64,512]{3,2,1,0:T(8,128)(2,1)}) fusion(bf16[3,1,64,8192]{3,2,1,0:T(8,128)(2,1)} %param.8, s32[]{:T(128)S(6)} %select_n.47, s32[]{:T(128)S(6)} %select_n.46, s32[]{:T(128)S(6)} %select_n.45, ...), kind=kLoop, calls=%fused_computation | loop fusion | bytes 1572880 | tf_op jit(solution)/shard_map/dynamic_slice | solution.py:190
  107.4 13.3 %collective-permute-done.3.refs_3_ = bf16[3,1,64,1024]{3,2,1,0:T(8,128)(2,1)S(1)} collective-permute-done((bf16[3,1,64,1024]{3,2,1,0:T(8,128)(2,1)}, bf16[3,1,64,1024]{3,2,1,0:T(8,128)(2,1)S(1)}, u32[]{:S(2)}, u32[]{:S(2)}) %collective-permute-start.3) | collective-permute-done | bytes 393248 | tf_op jit(solution)/shard_map/stash_3_0/ppermute | solution.py:145
  120.6 0.0 collective-permute-start.12
  120.6 6.9 %collective-permute-done.1.refs_1_ = bf16[3,1,64,1024]{3,2,1,0:T(8,128)(2,1)S(1)} collective-permute-done((bf16[3,1,64,1024]{3,2,1,0:T(8,128)(2,1)}, bf16[3,1,64,1024]{3,2,1,0:T(8,128)(2,1)S(1)}, u32[]{:S(2)}, u32[]{:S(2)}) %collective-permute-start.1) | collective-permute-done | bytes 393248 | tf_op jit(solution)/shard_map/stash_1_0/ppermute | solution.py:145
  127.5 3.3 %collective-permute-start.11 = (bf16[3,1,64,512]{3,2,1,0:T(8,128)(2,1)}, bf16[3,1,64,512]{3,2,1,0:T(8,128)(2,1)}, u32[]{:S(2)}, u32[]{:S(2)}) collective-permute-start(bf16[3,1,64,512]{3,2,1,0:T(8,128)(2,1)} %get-tuple-element.17), channel_id=1, source_target_pairs={{0,248},{4,252},{8,240},{12,244},{16,232},{20,236},{24,224},{28,22... | collective-permute-start | bytes 589832 | tf_op jit(solution)/shard_map/stash_2_1/ppermute | solution.py:145
  130.8 6.8 %collective-permute-done.2.refs_2_ = bf16[3,1,64,1024]{3,2,1,0:T(8,128)(2,1)} collective-permute-done((bf16[3,1,64,1024]{3,2,1,0:T(8,128)(2,1)}, bf16[3,1,64,1024]{3,2,1,0:T(8,128)(2,1)}, u32[]{:S(2)}, u32[]{:S(2)}) %collective-permute-start.2) | collective-permute-done | bytes 393248 | tf_op jit(solution)/shard_map/stash_2_0/ppermute | solution.py:145
  137.6 1.3 collective-permute-start.10
  138.9 0.0 collective-permute-done.4.refs_4_
  138.9 2.7 %collective-permute-start.9 = (bf16[3,1,64,512]{3,2,1,0:T(8,128)(2,1)}, bf16[3,1,64,512]{3,2,1,0:T(8,128)(2,1)}, u32[]{:S(2)}, u32[]{:S(2)}) collective-permute-start(bf16[3,1,64,512]{3,2,1,0:T(8,128)(2,1)} %get-tuple-element.19), channel_id=1, source_target_pairs={{0,240},{4,244},{8,248},{12,252},{16,224},{20,228},{24,232},{28,23... | collective-permute-start | bytes 589832 | tf_op jit(solution)/shard_map/stash_0_1/ppermute | solution.py:145
  142.3 0.0 copy-done
  142.3 7.1 %shard_map.77.refs_7_ = bf16[3,1,256,2048]{3,2,1,0:T(8,128)(2,1)} custom-call(bf16[3,1,64,1024]{3,2,1,0:T(8,128)(2,1)S(1)} %collective-permute-done.refs_0_, bf16[3,1,64,1024]{3,2,1,0:T(8,128)(2,1)S(1)} %collective-permute-done.1.refs_1_, bf16[3,1,64,1024]{3,2,1,0:T(8,128)(2,1)} %collective-permute-done.2.refs_2_, ...), custom_call_target="tpu_custom_call" | custom-call | flops 671088640 | bytes 3670016 | tf_op jit(solution)/shard_map/pallas_call | solution.py:121
  149.4 1.3 constant_dynamic-slice_fusion.4
  150.7 0.0 collective-permute-done.12.refs_3_
  150.7 0.1 collective-permute-start.8
  150.8 0.0 collective-permute-done.11.refs_2_
  150.8 4.9 %collective-permute-start.7 = (bf16[3,1,64,512]{3,2,1,0:T(8,128)(2,1)S(1)}, bf16[3,1,64,512]{3,2,1,0:T(8,128)(2,1)S(1)}, u32[]{:S(2)}, u32[]{:S(2)}) collective-permute-start(bf16[3,1,64,512]{3,2,1,0:T(8,128)(2,1)S(1)} %get-tuple-element.21), channel_id=1, source_target_pairs={{0,248},{4,252},{8,240},{12,244},{16,232},{20,236},{24,224},{28,22... | collective-permute-start | bytes 589832 | tf_op jit(solution)/shard_map/stash_2_2/ppermute | solution.py:145
  155.6 0.0 collective-permute-done.10.refs_1_
  155.6 0.1 collective-permute-start.6
  155.7 0.0 collective-permute-done.9.refs_0_
  155.7 4.0 %collective-permute-start.5 = (bf16[3,1,64,512]{3,2,1,0:T(8,128)(2,1)S(1)}, bf16[3,1,64,512]{3,2,1,0:T(8,128)(2,1)S(1)}, u32[]{:S(2)}, u32[]{:S(2)}) collective-permute-start(bf16[3,1,64,512]{3,2,1,0:T(8,128)(2,1)S(1)} %get-tuple-element.23), channel_id=1, source_target_pairs={{0,240},{4,244},{8,248},{12,252},{16,224},{20,228},{24,232},{28,23... | collective-permute-start | bytes 589832 | tf_op jit(solution)/shard_map/stash_0_2/ppermute | solution.py:145
  159.7 4.7 %shard_map.78.refs_7_ = bf16[3,1,256,2048]{3,2,1,0:T(8,128)(2,1)} custom-call(bf16[3,1,64,512]{3,2,1,0:T(8,128)(2,1)} %collective-permute-done.9.refs_0_, bf16[3,1,64,512]{3,2,1,0:T(8,128)(2,1)} %collective-permute-done.10.refs_1_, bf16[3,1,64,512]{3,2,1,0:T(8,128)(2,1)} %collective-permute-done.11.refs_2_, ...), custom_call_target="tpu_custom_call", output_to_operand_aliasing={{}: (7, {})} | custom-call | flops 335544320 | bytes 1835008 | tf_op jit(solution)/shard_map/pallas_call | solution.py:121
  164.4 0.0 collective-permute-done.13.refs_8_
  164.4 0.0 collective-permute-done.8.refs_3_
  164.4 0.5 collective-permute-done.7.refs_2_
  164.9 2.0 %collective-permute-done.6.refs_1_ = bf16[3,1,64,512]{3,2,1,0:T(8,128)(2,1)S(1)} collective-permute-done((bf16[3,1,64,512]{3,2,1,0:T(8,128)(2,1)S(1)}, bf16[3,1,64,512]{3,2,1,0:T(8,128)(2,1)S(1)}, u32[]{:S(2)}, u32[]{:S(2)}) %collective-permute-start.6) | collective-permute-done | bytes 196640 | tf_op jit(solution)/shard_map/stash_1_2/ppermute | solution.py:145
  166.9 3.7 %collective-permute-done.5.refs_0_ = bf16[3,1,64,512]{3,2,1,0:T(8,128)(2,1)S(1)} collective-permute-done((bf16[3,1,64,512]{3,2,1,0:T(8,128)(2,1)S(1)}, bf16[3,1,64,512]{3,2,1,0:T(8,128)(2,1)S(1)}, u32[]{:S(2)}, u32[]{:S(2)}) %collective-permute-start.5) | collective-permute-done | bytes 196640 | tf_op jit(solution)/shard_map/stash_0_2/ppermute | solution.py:145
  170.5 3.6 %shard_map.79 = (bf16[3,1,256,2048]{3,2,1,0:T(8,128)(2,1)}, bf16[1,256,2048]{2,1,0:T(8,128)(2,1)S(1)}) custom-call(bf16[3,1,64,512]{3,2,1,0:T(8,128)(2,1)S(1)} %collective-permute-done.5.refs_0_, bf16[3,1,64,512]{3,2,1,0:T(8,128)(2,1)S(1)} %collective-permute-done.6.refs_1_, ...), custom_call_target="tpu_custom_call", output_to_operand_aliasing={{0}: (7, {}), {1}: (8, {})} | custom-call | flops 335544320 | bytes 1835008 | tf_op jit(solution)/shard_map/pallas_call | solution.py:121
  174.1 1.0 copy.16
Async XLA Ops:
  0.6 138.3 %collective-permute-start.4 = (bf16[1,256,2048]{2,1,0:T(8,128)(2,1)}, bf16[1,256,2048]{2,1,0:T(8,128)(2,1)S(1)}, u32[]{:S(2)}, u32[]{:S(2)}) collective-permute-start(bf16[1,256,2048]{2,1,0:T(8,128)(2,1)} %param.10), channel_id=1, source_target_pairs={{0,240},{4,244},{8,248},{12,252},{16,0},{20,4},{24,8},{28,12},{32,... | collective-permute-start | bytes 3145736 | tf_op jit(solution)/shard_map/whole_grad/ppermute | solution.py:171
  10.4 131.9 %copy-start = (s32[1,256]{1,0:T(1,128)S(1)}, s32[1,256]{1,0:T(1,128)}, u32[]{:S(2)}) copy-start(s32[1,256]{1,0:T(1,128)} %refs_5_.5) | copy-start | bytes 3076
  10.4 78.7 %collective-permute-start = (bf16[3,1,64,1024]{3,2,1,0:T(8,128)(2,1)S(1)}, bf16[3,1,64,1024]{3,2,1,0:T(8,128)(2,1)S(1)}, u32[]{:S(2)}, u32[]{:S(2)}) collective-permute-start(bf16[3,1,64,1024]{3,2,1,0:T(8,128)(2,1)S(1)} %get-tuple-element.26), channel_id=1, source_target_pairs={{0,240},{4,244},{8,248},{12,252},{16,224},{20,228},{24,232},{28,23... | collective-permute-start | bytes 1179656 | tf_op jit(solution)/shard_map/stash_0_0/ppermute | solution.py:145
  17.3 147.1 %collective-permute-start.13 = (bf16[1,256,2048]{2,1,0:T(8,128)(2,1)}, bf16[1,256,2048]{2,1,0:T(8,128)(2,1)S(1)}, u32[]{:S(2)}, u32[]{:S(2)}) collective-permute-start(bf16[1,256,2048]{2,1,0:T(8,128)(2,1)} %forward_heads.1), channel_id=1, source_target_pairs={{0,16},{4,20},{8,24},{12,28},{16,32},{20,36},{24,40},{28,44},{32,4... | collective-permute-start | bytes 3145736 | tf_op jit(solution)/shard_map/whole_out/ppermute | solution.py:171
  18.9 101.7 %collective-permute-start.3 = (bf16[3,1,64,1024]{3,2,1,0:T(8,128)(2,1)}, bf16[3,1,64,1024]{3,2,1,0:T(8,128)(2,1)S(1)}, u32[]{:S(2)}, u32[]{:S(2)}) collective-permute-start(bf16[3,1,64,1024]{3,2,1,0:T(8,128)(2,1)} %get-tuple-element.24), channel_id=1, source_target_pairs={{0,252},{4,248},{8,244},{12,240},{16,236},{20,232},{24,228},{28,22... | collective-permute-start | bytes 1179656 | tf_op jit(solution)/shard_map/stash_3_0/ppermute | solution.py:145
  23.8 103.7 %collective-permute-start.1 = (bf16[3,1,64,1024]{3,2,1,0:T(8,128)(2,1)}, bf16[3,1,64,1024]{3,2,1,0:T(8,128)(2,1)S(1)}, u32[]{:S(2)}, u32[]{:S(2)}) collective-permute-start(bf16[3,1,64,1024]{3,2,1,0:T(8,128)(2,1)} %get-tuple-element.25), channel_id=1, source_target_pairs={{0,244},{4,240},{8,252},{12,248},{16,228},{20,224},{24,236},{28,23... | collective-permute-start | bytes 1179656 | tf_op jit(solution)/shard_map/stash_1_0/ppermute | solution.py:145
  89.1 48.5 %collective-permute-start.2 = (bf16[3,1,64,1024]{3,2,1,0:T(8,128)(2,1)}, bf16[3,1,64,1024]{3,2,1,0:T(8,128)(2,1)}, u32[]{:S(2)}, u32[]{:S(2)}) collective-permute-start(bf16[3,1,64,1024]{3,2,1,0:T(8,128)(2,1)} %get-tuple-element.27), channel_id=1, source_target_pairs={{0,248},{4,252},{8,240},{12,244},{16,232},{20,236},{24,224},{28,22... | collective-permute-start | bytes 1179656 | tf_op jit(solution)/shard_map/stash_2_0/ppermute | solution.py:145
  120.6 30.0 %collective-permute-start.12 = (bf16[3,1,64,512]{3,2,1,0:T(8,128)(2,1)}, bf16[3,1,64,512]{3,2,1,0:T(8,128)(2,1)S(1)}, u32[]{:S(2)}, u32[]{:S(2)}) collective-permute-start(bf16[3,1,64,512]{3,2,1,0:T(8,128)(2,1)} %get-tuple-element.16), channel_id=1, source_target_pairs={{0,252},{4,248},{8,244},{12,240},{16,236},{20,232},{24,228},{28,22... | collective-permute-start | bytes 589832 | tf_op jit(solution)/shard_map/stash_3_1/ppermute | solution.py:145
  127.5 23.3 %collective-permute-start.11 = (bf16[3,1,64,512]{3,2,1,0:T(8,128)(2,1)}, bf16[3,1,64,512]{3,2,1,0:T(8,128)(2,1)}, u32[]{:S(2)}, u32[]{:S(2)}) collective-permute-start(bf16[3,1,64,512]{3,2,1,0:T(8,128)(2,1)} %get-tuple-element.17), channel_id=1, source_target_pairs={{0,248},{4,252},{8,240},{12,244},{16,232},{20,236},{24,224},{28,22... | collective-permute-start | bytes 589832 | tf_op jit(solution)/shard_map/stash_2_1/ppermute | solution.py:145
  137.6 18.1 %collective-permute-start.10 = (bf16[3,1,64,512]{3,2,1,0:T(8,128)(2,1)}, bf16[3,1,64,512]{3,2,1,0:T(8,128)(2,1)}, u32[]{:S(2)}, u32[]{:S(2)}) collective-permute-start(bf16[3,1,64,512]{3,2,1,0:T(8,128)(2,1)} %get-tuple-element.18), channel_id=1, source_target_pairs={{0,244},{4,240},{8,252},{12,248},{16,228},{20,224},{24,236},{28,23... | collective-permute-start | bytes 589832 | tf_op jit(solution)/shard_map/stash_1_1/ppermute | solution.py:145
  138.9 16.8 %collective-permute-start.9 = (bf16[3,1,64,512]{3,2,1,0:T(8,128)(2,1)}, bf16[3,1,64,512]{3,2,1,0:T(8,128)(2,1)}, u32[]{:S(2)}, u32[]{:S(2)}) collective-permute-start(bf16[3,1,64,512]{3,2,1,0:T(8,128)(2,1)} %get-tuple-element.19), channel_id=1, source_target_pairs={{0,240},{4,244},{8,248},{12,252},{16,224},{20,228},{24,232},{28,23... | collective-permute-start | bytes 589832 | tf_op jit(solution)/shard_map/stash_0_1/ppermute | solution.py:145
  150.7 13.7 %collective-permute-start.8 = (bf16[3,1,64,512]{3,2,1,0:T(8,128)(2,1)S(1)}, bf16[3,1,64,512]{3,2,1,0:T(8,128)(2,1)S(1)}, u32[]{:S(2)}, u32[]{:S(2)}) collective-permute-start(bf16[3,1,64,512]{3,2,1,0:T(8,128)(2,1)S(1)} %get-tuple-element.20), channel_id=1, source_target_pairs={{0,252},{4,248},{8,244},{12,240},{16,236},{20,232},{24,228},{28,22... | collective-permute-start | bytes 589832 | tf_op jit(solution)/shard_map/stash_3_2/ppermute | solution.py:145
  150.8 14.1 %collective-permute-start.7 = (bf16[3,1,64,512]{3,2,1,0:T(8,128)(2,1)S(1)}, bf16[3,1,64,512]{3,2,1,0:T(8,128)(2,1)S(1)}, u32[]{:S(2)}, u32[]{:S(2)}) collective-permute-start(bf16[3,1,64,512]{3,2,1,0:T(8,128)(2,1)S(1)} %get-tuple-element.21), channel_id=1, source_target_pairs={{0,248},{4,252},{8,240},{12,244},{16,232},{20,236},{24,224},{28,22... | collective-permute-start | bytes 589832 | tf_op jit(solution)/shard_map/stash_2_2/ppermute | solution.py:145
  155.6 11.2 %collective-permute-start.6 = (bf16[3,1,64,512]{3,2,1,0:T(8,128)(2,1)S(1)}, bf16[3,1,64,512]{3,2,1,0:T(8,128)(2,1)S(1)}, u32[]{:S(2)}, u32[]{:S(2)}) collective-permute-start(bf16[3,1,64,512]{3,2,1,0:T(8,128)(2,1)S(1)} %get-tuple-element.22), channel_id=1, source_target_pairs={{0,244},{4,240},{8,252},{12,248},{16,228},{20,224},{24,236},{28,23... | collective-permute-start | bytes 589832 | tf_op jit(solution)/shard_map/stash_1_2/ppermute | solution.py:145
  155.7 14.8 %collective-permute-start.5 = (bf16[3,1,64,512]{3,2,1,0:T(8,128)(2,1)S(1)}, bf16[3,1,64,512]{3,2,1,0:T(8,128)(2,1)S(1)}, u32[]{:S(2)}, u32[]{:S(2)}) collective-permute-start(bf16[3,1,64,512]{3,2,1,0:T(8,128)(2,1)S(1)} %get-tuple-element.23), channel_id=1, source_target_pairs={{0,240},{4,244},{8,248},{12,252},{16,224},{20,228},{24,232},{28,23... | collective-permute-start | bytes 589832 | tf_op jit(solution)/shard_map/stash_0_2/ppermute | solution.py:145

commit v7 on v6

--- a/solution.py
+++ b/solution.py
@@ -70,15 +70,22 @@
     )(qkv, segment)
 
 
-def backward_kernel(parts, *refs):
+def backward_kernel(parts, carries, *refs):
     pieces, refs = refs[:parts], refs[parts:]
     upstream_ref, segment_ref, factor_ref = refs[:3]
-    out_ref, stash = refs[-2:] if len(refs) < 7 else (refs[-3], refs[-1])
+    out_ref, stash = refs[-2:]
+    if carries:
+        out_ref = refs[-3]
+        refs[-2][...] = refs[3][...]
     mine = lax.axis_index("tensor")
     rows = pieces[0].shape[2]
-    for k in range(parts):
+    found = [piece[:, 0] for piece in pieces]
+    if parts > 4:
+        around = found.pop(1)
+        found[0] = jnp.where(detoured(lax.axis_index("pipe")), around, found[0])
+    for k, piece in enumerate(found):
         start = pl.multiple_of((mine ^ k) * rows, rows)
-        stash[:, pl.ds(start, rows), :] = pieces[k][:, 0]
+        stash[:, pl.ds(start, rows), :] = piece
     outside = outside_of(segment_ref)
     factor = factor_ref[0]
     for start in range(0, upstream_ref.shape[2], HEAD_DIM):
@@ -109,17 +116,19 @@
     ]
     out_specs = [pl.BlockSpec((3, 1, length, step), lambda i: (0, 0, 0, place))]
     out_shape = [jax.ShapeDtypeStruct((3, 1, length, width), jnp.bfloat16)]
+    if carried is not None:
+        whole = pl.BlockSpec(carried.shape, lambda i: (0, 0, 0))
+        operands.append(carried)
+        in_specs.append(whole)
+        out_specs.append(whole)
+        out_shape.append(jax.ShapeDtypeStruct(carried.shape, carried.dtype))
     aliases = {}
-    for array in (earlier, carried):
-        if array is not None:
-            aliases[len(operands)] = len(aliases)
-            operands.append(array)
-            in_specs.append(pl.BlockSpec(memory_space=pl.ANY))
-    if carried is not None:
-        out_specs.append(pl.BlockSpec(memory_space=pl.ANY))
-        out_shape.append(jax.ShapeDtypeStruct(carried.shape, carried.dtype))
+    if earlier is not None:
+        aliases = {len(operands): 0}
+        operands.append(earlier)
+        in_specs.append(pl.BlockSpec(memory_space=pl.ANY))
     return pl.pallas_call(
-        functools.partial(backward_kernel, parts),
+        functools.partial(backward_kernel, parts, carried is not None),
         grid=(1,),
         in_specs=in_specs,
         out_specs=out_specs,
@@ -135,46 +144,31 @@
     )(*operands)
 
 
-def fetched(piece, k):
-    sections, tensors = lax.axis_size("pipe"), lax.axis_size("tensor")
-    pairs = [
-        (p * tensors + t, (sections - 1 - p) * tensors + (t ^ k))
-        for p in range(sections)
-        for t in range(tensors)
-    ]
-    return lax.ppermute(piece, AXES, pairs)
-
-
-def detoured(p, t, by):
-    half = lax.axis_size("pipe") // 2
-    return (t & 1) * (p % half == (half - 1 if by > 0 else 0))
-
-
-def shift_pairs(by, leg):
+def fetched(piece, k, leg="direct"):
     sections, tensors = lax.axis_size("pipe"), lax.axis_size("tensor")
     pairs = []
     for p in range(sections):
         for t in range(tensors):
-            aside = detoured(p, t, by)
-            start, end = p, p + by
+            start, end = p, sections - 1 - p
             if leg == "aside":
-                end = p - by
+                end = p ^ 1
             if leg == "onward":
-                start = p - by
-            if leg == "whole" or aside == (leg != "direct"):
-                pairs.append((start % sections * tensors + t, end % sections * tensors + t))
-    return pairs
-
-
-def shifted(array, by, leg):
-    with jax.named_scope(f"{leg}_{'out' if by > 0 else 'grad'}"):
-        return lax.ppermute(array, AXES, shift_pairs(by, leg))
-
-
-def came_around(by):
+                start = p ^ 1
+            if leg == "all" or (leg == "direct") != detoured(p):
+                pairs.append((start * tensors + t, end * tensors + (t ^ k)))
+    return lax.ppermute(piece, AXES, pairs)
+
+
+def detoured(section):
+    half = lax.axis_size("pipe") // 2
+    place = section % half
+    return (place == 2) | (place == half - 3)
+
+
+def shifted(array, by):
     sections = lax.axis_size("pipe")
-    source = (lax.axis_index("pipe") + sections - by) % sections
-    return detoured(source, lax.axis_index("tensor"), by) == 1
+    with jax.named_scope("direct_out" if by > 0 else "direct_grad"):
+        return lax.ppermute(array, "pipe", [(p, (p + by) % sections) for p in range(sections)])
 
 
 def on_device(fwd_qkv, fwd_segments, parked, bwd_segments, grad_out, loss_tokens):
@@ -188,29 +182,32 @@
         for k in range(tensors):
             start = (mine ^ k) * width + first * HEAD_DIM
             piece = lax.dynamic_slice_in_dim(whole, start, heads * HEAD_DIM, axis=3)
+            around = chunk == 0 and k == 0
             with jax.named_scope(f"stash_{k}_{chunk}"):
-                pieces.append(fetched(piece, k))
+                pieces.append(fetched(piece, k, "direct" if around else "all"))
+            if around:
+                with jax.named_scope("aside_0"):
+                    piece = fetched(piece, k, "aside")
+                with jax.named_scope("onward_0"):
+                    pieces.append(fetched(piece, k, "onward"))
         return pieces
 
-    upstream = shifted(grad_out, -1, "whole")
+    upstream = shifted(grad_out, -1)
+    pieces = [fetched_chunk(parked, 0)]
     with jax.named_scope("forward_heads"):
         forward_out = forward(fwd_qkv, fwd_segments)
-    received_direct = shifted(forward_out, 1, "whole")
-    received_aside = shifted(forward_out, 1, "aside")
-    received_around = shifted(received_aside, 1, "onward")
-    pieces = [fetched_chunk(parked, 0)]
+    received = shifted(forward_out, 1)
     tokens = loss_tokens.astype(jnp.float32)
     pieces[0][0], tokens = lax.optimization_barrier((pieces[0][0], tokens))
     token_total = lax.psum(tokens, "dp")
     factor = jnp.float32(lax.axis_size("dp") * length) / token_total
     parked, token_total = lax.optimization_barrier((parked, token_total))
     pieces.append(fetched_chunk(parked, 1))
-    received = received_direct
     (grads,) = backward(0, pieces[0], upstream, bwd_segments, factor, None)
     parked, grads = lax.optimization_barrier((parked, grads))
     pieces.append(fetched_chunk(parked, 2))
-    (grads,) = backward(1, pieces[1], upstream, bwd_segments, factor, grads)
-    grads, received = backward(2, pieces[2], upstream, bwd_segments, factor, grads, received)
+    grads, received = backward(1, pieces[1], upstream, bwd_segments, factor, grads, received)
+    (grads,) = backward(2, pieces[2], upstream, bwd_segments, factor, grads)
     return (received, grads)
 
 

time: 176 us -> 167 us (0.949)
  waiting for transfers between devices: 98.4 us -> 83 us
  starting transfers between devices: 36.1 us -> 43.3 us
    ppermute x12 -> x14, waiting for transfers between devices: 98.4 us -> 83 us  [fetched(): return lax.ppermute(piece, AXES, pairs)]
    ppermute x12 -> x14, starting transfers between devices: 27.1 us -> 35.9 us  [fetched(): return lax.ppermute(piece, AXES, pairs)]
  transfers between devices with their start and end apart: 14 -> 16, of which waited for: 7 -> 10; matrix products, arithmetic and copies ran while one was open for 3% -> 3% of each run, Pallas kernels for 10% -> 11%
where the time goes in v7:
time: 167 us; the launch traced here: 166 us
  waiting for transfers between devices  83 us (50%)
  starting transfers between devices  43.3 us (26%)
  Pallas kernels  22.4 us (13%)
  blocking collectives  9.88 us (6%)
  local copies, waits for them, and re-layouts  5.78 us (3%)
  between operations  2.05 us (1%)
    ppermute x14, waiting for transfers between devices, fetched(): return lax.ppermute(piece, AXES, pairs)  83 us
    ppermute x14, starting transfers between devices, fetched(): return lax.ppermute(piece, AXES, pairs)  35.9 us
    pallas_call x3, Pallas kernels, backward(): pl.pallas_call(functools.partial(backward_kernel, parts, carried is not N...  15.8 us
    psum x1, blocking collectives, on_device(): token_total = lax.psum(tokens, 'dp')  9.88 us
    ppermute x2, starting transfers between devices, shifted(): lax.ppermute(array, 'pipe', [(p, (p + by) % sections) for p in range(sect...  7.41 us
    pallas_call x1, Pallas kernels, forward(): pl.pallas_call(forward_kernel, grid=(FORWARD_STEPS,), in_specs=[pl.BlockS...  6.6 us
    dynamic_slice x3, local copies, waits for them, and re-layouts, fetched_chunk(): piece = lax.dynamic_slice_in_dim(whole, start, heads * HEAD_DIM, axis=3)  5.78 us
  transfers between devices with their start and end apart: 16, of which 10 were waited for; matrix products, arithmetic and copies ran while one was open for 3% of the time, Pallas kernels for 11%

profile of v7, /device:TPU:1, one launch (start us, length us, event | category | flops | bytes accessed | tf_op | source)
XLA Modules:
  0.0 166.4 jit_solution(3707174457299807111)
XLA Ops:
  0.6 7.4 %collective-permute-start.5 = (bf16[1,256,2048]{2,1,0:T(8,128)(2,1)}, bf16[1,256,2048]{2,1,0:T(8,128)(2,1)S(1)}, u32[]{:S(2)}, u32[]{:S(2)}) collective-permute-start(bf16[1,256,2048]{2,1,0:T(8,128)(2,1)} %param.10), channel_id=1, source_target_pairs={{0,240},{16,0},{32,16},{48,32},{64,48},{80,64},{96,80},{112,96},{1... | collective-permute-start | bytes 3145736 | tf_op jit(solution)/shard_map/direct_grad/ppermute | solution.py:171
  8.0 2.4 %constant_dynamic-slice_fusion.4 = (bf16[3,1,64,1024]{3,2,1,0:T(8,128)(2,1)S(1)}, bf16[3,1,64,1024]{3,2,1,0:T(8,128)(2,1)}, bf16[3,1,64,1024]{3,2,1,0:T(8,128)(2,1)S(1)}, bf16[3,1,64,1024]{3,2,1,0:T(8,128)(2,1)}) fusion(bf16[3,1,64,8192]{3,2,1,0:T(8,128)(2,1)} %param.8, s32[]{:T(128)S(6)} %select_n.43, s32[]{:T(128)S(6)} %select_n.41, s32[]{:T(128)S(6)} %select_n.36, ...), kind=kLoop, calls=%fused_computation.4 | loop fusion | bytes 3145744 | tf_op jit(solution)/shard_map/dynamic_slice | solution.py:184
  10.4 0.0 copy-start
  10.4 2.7 %collective-permute-start.11 = (bf16[3,1,64,1024]{3,2,1,0:T(8,128)(2,1)S(1)}, bf16[3,1,64,1024]{3,2,1,0:T(8,128)(2,1)S(1)}, u32[]{:S(2)}, u32[]{:S(2)}) collective-permute-start(bf16[3,1,64,1024]{3,2,1,0:T(8,128)(2,1)S(1)} %get-tuple-element.20), channel_id=1, source_target_pairs={{0,252},{4,248},{8,244},{12,240},{16,236},{20,232},{24,228},{28,22... | collective-permute-start | bytes 1179656 | tf_op jit(solution)/shard_map/stash_3_0/ppermute | solution.py:159
  13.0 1.4 collective-permute-start.7
  14.5 4.3 %collective-permute-start = (bf16[3,1,64,1024]{3,2,1,0:T(8,128)(2,1)S(1)}, bf16[3,1,64,1024]{3,2,1,0:T(8,128)(2,1)S(1)}, u32[]{:S(2)}, u32[]{:S(2)}) collective-permute-start(bf16[3,1,64,1024]{3,2,1,0:T(8,128)(2,1)S(1)} %get-tuple-element.22), channel_id=1, source_target_pairs={{0,240},{4,244},{8,248},{12,252},{16,224},{20,228},{24,232},{28,23... | collective-permute-start | bytes 1179656 | tf_op jit(solution)/shard_map/stash_0_0/ppermute | solution.py:159
  18.8 6.6 %forward_heads.1 = bf16[1,256,2048]{2,1,0:T(8,128)(2,1)} custom-call(bf16[3,1,256,2048]{3,2,1,0:T(8,128)(2,1)} %qkv_ref.1, s32[1,256]{1,0:T(1,128)} %segment_ref.1), custom_call_target="tpu_custom_call" | custom-call | flops 536870912 | bytes 4194304 | tf_op jit(solution)/shard_map/forward_heads/pallas_call | solution.py:54
  25.4 0.0 collective-permute-start.6
  25.4 30.0 %collective-permute-done.11.refs_4_ = bf16[3,1,64,1024]{3,2,1,0:T(8,128)(2,1)S(1)} collective-permute-done((bf16[3,1,64,1024]{3,2,1,0:T(8,128)(2,1)S(1)}, bf16[3,1,64,1024]{3,2,1,0:T(8,128)(2,1)S(1)}, u32[]{:S(2)}, u32[]{:S(2)}) %collective-permute-start.11) | collective-permute-done | bytes 393248 | tf_op jit(solution)/shard_map/stash_3_0/ppermute | solution.py:159
  55.4 5.3 %collective-permute-start.9 = (bf16[3,1,64,1024]{3,2,1,0:T(8,128)(2,1)}, bf16[3,1,64,1024]{3,2,1,0:T(8,128)(2,1)S(1)}, u32[]{:S(2)}, u32[]{:S(2)}) collective-permute-start(bf16[3,1,64,1024]{3,2,1,0:T(8,128)(2,1)} %get-tuple-element.21), channel_id=1, source_target_pairs={{0,244},{4,240},{8,252},{12,248},{16,228},{20,224},{24,236},{28,23... | collective-permute-start | bytes 1179656 | tf_op jit(solution)/shard_map/stash_1_0/ppermute | solution.py:159
  60.6 0.0 collective-permute-done.7
  60.7 2.3 %collective-permute-start.10 = (bf16[3,1,64,1024]{3,2,1,0:T(8,128)(2,1)}, bf16[3,1,64,1024]{3,2,1,0:T(8,128)(2,1)}, u32[]{:S(2)}, u32[]{:S(2)}) collective-permute-start(bf16[3,1,64,1024]{3,2,1,0:T(8,128)(2,1)} %get-tuple-element.23), channel_id=1, source_target_pairs={{0,248},{4,252},{8,240},{12,244},{16,232},{20,236},{24,224},{28,22... | collective-permute-start | bytes 1179656 | tf_op jit(solution)/shard_map/stash_2_0/ppermute | solution.py:159
  62.9 0.9 collective-permute-done.refs_0_
  63.8 1.4 collective-permute-start.8
  65.9 9.9 %psum.7 = f32[1]{0:T(128)} all-reduce(f32[1]{0:T(128)S(6)} %convert_element_type.3), channel_id=1, replica_groups=mesh['pipe'=16,'tensor'=4,'dp'=4] {'dp'}, use_global_device_ids=true, to_apply=%region_0.0 | all-reduce | flops 1 | bytes 8 | tf_op jit(solution)/shard_map/psum | solution.py:202
  75.8 2.2 %constant_dynamic-slice_fusion.7 = (bf16[3,1,64,512]{3,2,1,0:T(8,128)(2,1)}, bf16[3,1,64,512]{3,2,1,0:T(8,128)(2,1)}, bf16[3,1,64,512]{3,2,1,0:T(8,128)(2,1)}, bf16[3,1,64,512]{3,2,1,0:T(8,128)(2,1)}) fusion(bf16[3,1,64,8192]{3,2,1,0:T(8,128)(2,1)} %param.8, s32[]{:T(128)S(6)} %select_n.40, s32[]{:T(128)S(6)} %select_n.39, s32[]{:T(128)S(6)} %select_n.38, ...), kind=kLoop, calls=%fused_computation.7 | loop fusion | bytes 1572880 | tf_op jit(solution)/shard_map/dynamic_slice | solution.py:184
  77.9 0.0 collective-permute-done.9.refs_2_
  77.9 9.6 %collective-permute-start.4 = (bf16[3,1,64,512]{3,2,1,0:T(8,128)(2,1)}, bf16[3,1,64,512]{3,2,1,0:T(8,128)(2,1)S(1)}, u32[]{:S(2)}, u32[]{:S(2)}) collective-permute-start(bf16[3,1,64,512]{3,2,1,0:T(8,128)(2,1)} %get-tuple-element.24), channel_id=1, source_target_pairs={{0,252},{4,248},{8,244},{12,240},{16,236},{20,232},{24,228},{28,22... | collective-permute-start | bytes 589832 | tf_op jit(solution)/shard_map/stash_3_1/ppermute | solution.py:159
  87.5 7.9 %collective-permute-done.10.refs_3_ = bf16[3,1,64,1024]{3,2,1,0:T(8,128)(2,1)} collective-permute-done((bf16[3,1,64,1024]{3,2,1,0:T(8,128)(2,1)}, bf16[3,1,64,1024]{3,2,1,0:T(8,128)(2,1)}, u32[]{:S(2)}, u32[]{:S(2)}) %collective-permute-start.10) | collective-permute-done | bytes 393248 | tf_op jit(solution)/shard_map/stash_2_0/ppermute | solution.py:159
  95.4 0.0 collective-permute-start.3
  95.4 0.0 collective-permute-done.8.refs_1_
  95.4 3.5 %collective-permute-start.2 = (bf16[3,1,64,512]{3,2,1,0:T(8,128)(2,1)}, bf16[3,1,64,512]{3,2,1,0:T(8,128)(2,1)}, u32[]{:S(2)}, u32[]{:S(2)}) collective-permute-start(bf16[3,1,64,512]{3,2,1,0:T(8,128)(2,1)} %get-tuple-element.26), channel_id=1, source_target_pairs={{0,244},{4,240},{8,252},{12,248},{16,228},{20,224},{24,236},{28,23... | collective-permute-start | bytes 589832 | tf_op jit(solution)/shard_map/stash_1_1/ppermute | solution.py:159
  98.9 0.0 collective-permute-done.5.refs_5_.refs_4_
  98.9 1.1 collective-permute-start.1
  100.7 0.0 copy-done
  100.8 7.2 %shard_map.77.refs_8_ = bf16[3,1,256,2048]{3,2,1,0:T(8,128)(2,1)} custom-call(bf16[3,1,64,1024]{3,2,1,0:T(8,128)(2,1)S(1)} %collective-permute-done.refs_0_, bf16[3,1,64,1024]{3,2,1,0:T(8,128)(2,1)} %collective-permute-done.8.refs_1_, bf16[3,1,64,1024]{3,2,1,0:T(8,128)(2,1)S(1)} %collective-permute-done.9.refs_2_, ...), custom_call_target="tpu_custom_call" | custom-call | flops 671088640 | bytes 3670016 | tf_op jit(solution)/shard_map/pallas_call | solution.py:130
  108.0 1.3 constant_dynamic-slice_fusion
  109.2 0.0 collective-permute-done.4.refs_3_
  109.2 4.4 %collective-permute-start.15 = (bf16[3,1,64,512]{3,2,1,0:T(8,128)(2,1)S(1)}, bf16[3,1,64,512]{3,2,1,0:T(8,128)(2,1)S(1)}, u32[]{:S(2)}, u32[]{:S(2)}) collective-permute-start(bf16[3,1,64,512]{3,2,1,0:T(8,128)(2,1)S(1)} %get-tuple-element.16), channel_id=1, source_target_pairs={{0,252},{4,248},{8,244},{12,240},{16,236},{20,232},{24,228},{28,22... | collective-permute-start | bytes 589832 | tf_op jit(solution)/shard_map/stash_3_2/ppermute | solution.py:159
  113.7 8.4 %collective-permute-done.3.refs_2_ = bf16[3,1,64,512]{3,2,1,0:T(8,128)(2,1)} collective-permute-done((bf16[3,1,64,512]{3,2,1,0:T(8,128)(2,1)}, bf16[3,1,64,512]{3,2,1,0:T(8,128)(2,1)}, u32[]{:S(2)}, u32[]{:S(2)}) %collective-permute-start.3) | collective-permute-done | bytes 196640 | tf_op jit(solution)/shard_map/stash_2_1/ppermute | solution.py:159
  122.0 0.0 collective-permute-start.14
  122.0 19.9 %collective-permute-done.2.refs_1_ = bf16[3,1,64,512]{3,2,1,0:T(8,128)(2,1)} collective-permute-done((bf16[3,1,64,512]{3,2,1,0:T(8,128)(2,1)}, bf16[3,1,64,512]{3,2,1,0:T(8,128)(2,1)}, u32[]{:S(2)}, u32[]{:S(2)}) %collective-permute-start.2) | collective-permute-done | bytes 196640 | tf_op jit(solution)/shard_map/stash_1_1/ppermute | solution.py:159
  141.9 0.0 collective-permute-start.13
  141.9 4.2 %collective-permute-done.1.refs_0_ = bf16[3,1,64,512]{3,2,1,0:T(8,128)(2,1)} collective-permute-done((bf16[3,1,64,512]{3,2,1,0:T(8,128)(2,1)}, bf16[3,1,64,512]{3,2,1,0:T(8,128)(2,1)}, u32[]{:S(2)}, u32[]{:S(2)}) %collective-permute-start.1) | collective-permute-done | bytes 196640 | tf_op jit(solution)/shard_map/stash_0_1/ppermute | solution.py:159
  146.1 0.0 collective-permute-start.12
  146.1 0.0 collective-permute-done.6.refs_7_
  146.1 5.0 %shard_map.78 = (bf16[3,1,256,2048]{3,2,1,0:T(8,128)(2,1)}, bf16[1,256,2048]{2,1,0:T(8,128)(2,1)}) custom-call(bf16[3,1,64,512]{3,2,1,0:T(8,128)(2,1)} %collective-permute-done.1.refs_0_, bf16[3,1,64,512]{3,2,1,0:T(8,128)(2,1)} %collective-permute-done.2.refs_1_, ...), custom_call_target="tpu_custom_call", output_to_operand_aliasing={{0}: (8, {})} | custom-call | flops 335544320 | bytes 1835008 | tf_op jit(solution)/shard_map/pallas_call | solution.py:130
  151.1 1.6 collective-permute-done.15.refs_3_
  152.8 2.8 %collective-permute-done.14.refs_2_ = bf16[3,1,64,512]{3,2,1,0:T(8,128)(2,1)S(1)} collective-permute-done((bf16[3,1,64,512]{3,2,1,0:T(8,128)(2,1)S(1)}, bf16[3,1,64,512]{3,2,1,0:T(8,128)(2,1)S(1)}, u32[]{:S(2)}, u32[]{:S(2)}) %collective-permute-start.14) | collective-permute-done | bytes 196640 | tf_op jit(solution)/shard_map/stash_2_2/ppermute | solution.py:159
  155.6 3.0 %collective-permute-done.13.refs_1_ = bf16[3,1,64,512]{3,2,1,0:T(8,128)(2,1)S(1)} collective-permute-done((bf16[3,1,64,512]{3,2,1,0:T(8,128)(2,1)S(1)}, bf16[3,1,64,512]{3,2,1,0:T(8,128)(2,1)S(1)}, u32[]{:S(2)}, u32[]{:S(2)}) %collective-permute-start.13) | collective-permute-done | bytes 196640 | tf_op jit(solution)/shard_map/stash_1_2/ppermute | solution.py:159
  158.7 4.2 %collective-permute-done.12.refs_0_ = bf16[3,1,64,512]{3,2,1,0:T(8,128)(2,1)S(1)} collective-permute-done((bf16[3,1,64,512]{3,2,1,0:T(8,128)(2,1)S(1)}, bf16[3,1,64,512]{3,2,1,0:T(8,128)(2,1)S(1)}, u32[]{:S(2)}, u32[]{:S(2)}) %collective-permute-start.12) | collective-permute-done | bytes 196640 | tf_op jit(solution)/shard_map/stash_0_2/ppermute | solution.py:159
  162.9 3.6 %shard_map.79 = bf16[3,1,256,2048]{3,2,1,0:T(8,128)(2,1)} custom-call(bf16[3,1,64,512]{3,2,1,0:T(8,128)(2,1)S(1)} %collective-permute-done.12.refs_0_, bf16[3,1,64,512]{3,2,1,0:T(8,128)(2,1)S(1)} %collective-permute-done.13.refs_1_, bf16[3,1,64,512]{3,2,1,0:T(8,128)(2,1)S(1)} %collective-permute-done.14.refs_2_, ...), custom_call_target="tpu_custom_call", output_to_operand_aliasing={{}: (7, {})} | custom-call | flops 335544320 | bytes 1835008 | tf_op jit(solution)/shard_map/pallas_call | solution.py:130
Async XLA Ops:
  0.6 98.3 %collective-permute-start.5 = (bf16[1,256,2048]{2,1,0:T(8,128)(2,1)}, bf16[1,256,2048]{2,1,0:T(8,128)(2,1)S(1)}, u32[]{:S(2)}, u32[]{:S(2)}) collective-permute-start(bf16[1,256,2048]{2,1,0:T(8,128)(2,1)} %param.10), channel_id=1, source_target_pairs={{0,240},{16,0},{32,16},{48,32},{64,48},{80,64},{96,80},{112,96},{1... | collective-permute-start | bytes 3145736 | tf_op jit(solution)/shard_map/direct_grad/ppermute | solution.py:171
  10.4 90.4 %copy-start = (s32[1,256]{1,0:T(1,128)S(1)}, s32[1,256]{1,0:T(1,128)}, u32[]{:S(2)}) copy-start(s32[1,256]{1,0:T(1,128)} %refs_5_.3) | copy-start | bytes 3076
  10.4 45.0 %collective-permute-start.11 = (bf16[3,1,64,1024]{3,2,1,0:T(8,128)(2,1)S(1)}, bf16[3,1,64,1024]{3,2,1,0:T(8,128)(2,1)S(1)}, u32[]{:S(2)}, u32[]{:S(2)}) collective-permute-start(bf16[3,1,64,1024]{3,2,1,0:T(8,128)(2,1)S(1)} %get-tuple-element.20), channel_id=1, source_target_pairs={{0,252},{4,248},{8,244},{12,240},{16,236},{20,232},{24,228},{28,22... | collective-permute-start | bytes 1179656 | tf_op jit(solution)/shard_map/stash_3_0/ppermute | solution.py:159
  13.0 47.6 %collective-permute-start.7 = (bf16[3,1,64,1024]{3,2,1,0:T(8,128)(2,1)S(1)}, bf16[3,1,64,1024]{3,2,1,0:T(8,128)(2,1)}, u32[]{:S(2)}, u32[]{:S(2)}) collective-permute-start(bf16[3,1,64,1024]{3,2,1,0:T(8,128)(2,1)S(1)} %get-tuple-element.22), channel_id=1, source_target_pairs={{32,48},{36,52},{40,56},{44,60},{80,64},{84,68},{88,72},{92,76},{1... | collective-permute-start | bytes 1179656 | tf_op jit(solution)/shard_map/aside_0/ppermute | solution.py:159
  14.5 49.4 %collective-permute-start = (bf16[3,1,64,1024]{3,2,1,0:T(8,128)(2,1)S(1)}, bf16[3,1,64,1024]{3,2,1,0:T(8,128)(2,1)S(1)}, u32[]{:S(2)}, u32[]{:S(2)}) collective-permute-start(bf16[3,1,64,1024]{3,2,1,0:T(8,128)(2,1)S(1)} %get-tuple-element.22), channel_id=1, source_target_pairs={{0,240},{4,244},{8,248},{12,252},{16,224},{20,228},{24,232},{28,23... | collective-permute-start | bytes 1179656 | tf_op jit(solution)/shard_map/stash_0_0/ppermute | solution.py:159
  25.4 120.7 %collective-permute-start.6 = (bf16[1,256,2048]{2,1,0:T(8,128)(2,1)}, bf16[1,256,2048]{2,1,0:T(8,128)(2,1)S(1)}, u32[]{:S(2)}, u32[]{:S(2)}) collective-permute-start(bf16[1,256,2048]{2,1,0:T(8,128)(2,1)} %forward_heads.1), channel_id=1, source_target_pairs={{0,16},{16,32},{32,48},{48,64},{64,80},{80,96},{96,112},{112,128},... | collective-permute-start | bytes 3145736 | tf_op jit(solution)/shard_map/direct_out/ppermute | solution.py:171
  55.4 22.5 %collective-permute-start.9 = (bf16[3,1,64,1024]{3,2,1,0:T(8,128)(2,1)}, bf16[3,1,64,1024]{3,2,1,0:T(8,128)(2,1)S(1)}, u32[]{:S(2)}, u32[]{:S(2)}) collective-permute-start(bf16[3,1,64,1024]{3,2,1,0:T(8,128)(2,1)} %get-tuple-element.21), channel_id=1, source_target_pairs={{0,244},{4,240},{8,252},{12,248},{16,228},{20,224},{24,236},{28,23... | collective-permute-start | bytes 1179656 | tf_op jit(solution)/shard_map/stash_1_0/ppermute | solution.py:159
  60.7 34.8 %collective-permute-start.10 = (bf16[3,1,64,1024]{3,2,1,0:T(8,128)(2,1)}, bf16[3,1,64,1024]{3,2,1,0:T(8,128)(2,1)}, u32[]{:S(2)}, u32[]{:S(2)}) collective-permute-start(bf16[3,1,64,1024]{3,2,1,0:T(8,128)(2,1)} %get-tuple-element.23), channel_id=1, source_target_pairs={{0,248},{4,252},{8,240},{12,244},{16,232},{20,236},{24,224},{28,22... | collective-permute-start | bytes 1179656 | tf_op jit(solution)/shard_map/stash_2_0/ppermute | solution.py:159
  63.8 31.6 %collective-permute-start.8 = (bf16[3,1,64,1024]{3,2,1,0:T(8,128)(2,1)}, bf16[3,1,64,1024]{3,2,1,0:T(8,128)(2,1)}, u32[]{:S(2)}, u32[]{:S(2)}) collective-permute-start(bf16[3,1,64,1024]{3,2,1,0:T(8,128)(2,1)} %collective-permute-done.7), channel_id=1, source_target_pairs={{48,208},{52,212},{56,216},{60,220},{64,160},{68,164},{72,168},{76... | collective-permute-start | bytes 1179656 | tf_op jit(solution)/shard_map/onward_0/ppermute | solution.py:159
  77.9 31.3 %collective-permute-start.4 = (bf16[3,1,64,512]{3,2,1,0:T(8,128)(2,1)}, bf16[3,1,64,512]{3,2,1,0:T(8,128)(2,1)S(1)}, u32[]{:S(2)}, u32[]{:S(2)}) collective-permute-start(bf16[3,1,64,512]{3,2,1,0:T(8,128)(2,1)} %get-tuple-element.24), channel_id=1, source_target_pairs={{0,252},{4,248},{8,244},{12,240},{16,236},{20,232},{24,228},{28,22... | collective-permute-start | bytes 589832 | tf_op jit(solution)/shard_map/stash_3_1/ppermute | solution.py:159
  95.4 26.6 %collective-permute-start.3 = (bf16[3,1,64,512]{3,2,1,0:T(8,128)(2,1)}, bf16[3,1,64,512]{3,2,1,0:T(8,128)(2,1)}, u32[]{:S(2)}, u32[]{:S(2)}) collective-permute-start(bf16[3,1,64,512]{3,2,1,0:T(8,128)(2,1)} %get-tuple-element.25), channel_id=1, source_target_pairs={{0,248},{4,252},{8,240},{12,244},{16,232},{20,236},{24,224},{28,22... | collective-permute-start | bytes 589832 | tf_op jit(solution)/shard_map/stash_2_1/ppermute | solution.py:159
  95.4 46.5 %collective-permute-start.2 = (bf16[3,1,64,512]{3,2,1,0:T(8,128)(2,1)}, bf16[3,1,64,512]{3,2,1,0:T(8,128)(2,1)}, u32[]{:S(2)}, u32[]{:S(2)}) collective-permute-start(bf16[3,1,64,512]{3,2,1,0:T(8,128)(2,1)} %get-tuple-element.26), channel_id=1, source_target_pairs={{0,244},{4,240},{8,252},{12,248},{16,228},{20,224},{24,236},{28,23... | collective-permute-start | bytes 589832 | tf_op jit(solution)/shard_map/stash_1_1/ppermute | solution.py:159
  98.9 47.2 %collective-permute-start.1 = (bf16[3,1,64,512]{3,2,1,0:T(8,128)(2,1)}, bf16[3,1,64,512]{3,2,1,0:T(8,128)(2,1)}, u32[]{:S(2)}, u32[]{:S(2)}) collective-permute-start(bf16[3,1,64,512]{3,2,1,0:T(8,128)(2,1)} %get-tuple-element.27), channel_id=1, source_target_pairs={{0,240},{4,244},{8,248},{12,252},{16,224},{20,228},{24,232},{28,23... | collective-permute-start | bytes 589832 | tf_op jit(solution)/shard_map/stash_0_1/ppermute | solution.py:159
  109.2 43.5 %collective-permute-start.15 = (bf16[3,1,64,512]{3,2,1,0:T(8,128)(2,1)S(1)}, bf16[3,1,64,512]{3,2,1,0:T(8,128)(2,1)S(1)}, u32[]{:S(2)}, u32[]{:S(2)}) collective-permute-start(bf16[3,1,64,512]{3,2,1,0:T(8,128)(2,1)S(1)} %get-tuple-element.16), channel_id=1, source_target_pairs={{0,252},{4,248},{8,244},{12,240},{16,236},{20,232},{24,228},{28,22... | collective-permute-start | bytes 589832 | tf_op jit(solution)/shard_map/stash_3_2/ppermute | solution.py:159
  122.0 33.6 %collective-permute-start.14 = (bf16[3,1,64,512]{3,2,1,0:T(8,128)(2,1)S(1)}, bf16[3,1,64,512]{3,2,1,0:T(8,128)(2,1)S(1)}, u32[]{:S(2)}, u32[]{:S(2)}) collective-permute-start(bf16[3,1,64,512]{3,2,1,0:T(8,128)(2,1)S(1)} %get-tuple-element.17), channel_id=1, source_target_pairs={{0,248},{4,252},{8,240},{12,244},{16,232},{20,236},{24,224},{28,22... | collective-permute-start | bytes 589832 | tf_op jit(solution)/shard_map/stash_2_2/ppermute | solution.py:159
  141.9 16.7 %collective-permute-start.13 = (bf16[3,1,64,512]{3,2,1,0:T(8,128)(2,1)S(1)}, bf16[3,1,64,512]{3,2,1,0:T(8,128)(2,1)S(1)}, u32[]{:S(2)}, u32[]{:S(2)}) collective-permute-start(bf16[3,1,64,512]{3,2,1,0:T(8,128)(2,1)S(1)} %get-tuple-element.18), channel_id=1, source_target_pairs={{0,244},{4,240},{8,252},{12,248},{16,228},{20,224},{24,236},{28,23... | collective-permute-start | bytes 589832 | tf_op jit(solution)/shard_map/stash_1_2/ppermute | solution.py:159
  146.1 16.7 %collective-permute-start.12 = (bf16[3,1,64,512]{3,2,1,0:T(8,128)(2,1)S(1)}, bf16[3,1,64,512]{3,2,1,0:T(8,128)(2,1)S(1)}, u32[]{:S(2)}, u32[]{:S(2)}) collective-permute-start(bf16[3,1,64,512]{3,2,1,0:T(8,128)(2,1)S(1)} %get-tuple-element.19), channel_id=1, source_target_pairs={{0,240},{4,244},{8,248},{12,252},{16,224},{20,228},{24,232},{28,23... | collective-permute-start | bytes 589832 | tf_op jit(solution)/shard_map/stash_0_2/ppermute | solution.py:159

commit v8 on v7

--- a/solution.py
+++ b/solution.py
@@ -9,8 +9,8 @@
 from jax.sharding import PartitionSpec as P
 
 HEAD_DIM = 128
-FORWARD_STEPS = 4
-CHUNKS = ((0, 8), (8, 4), (12, 4))
+FORWARD_STEPS = 2
+CHUNKS = ((8, 8), (0, 6), (6, 2))
 SCALE = HEAD_DIM ** (-0.5)
 EXPONENT = SCALE * math.log2(math.e)
 NT = (((1,), (1,)), ((), ()))
@@ -24,10 +24,10 @@
 
 
 def probabilities(queries, keys, outside):
-    logits = product(queries, keys, NT) + outside
-    highest = jnp.max(logits, axis=1, keepdims=True)
+    logits = product(keys, queries, NT) + outside
+    highest = jnp.max(logits, axis=0, keepdims=True)
     weights = jnp.exp2((logits - highest) * EXPONENT)
-    return weights * (1.0 / jnp.sum(weights, axis=1, keepdims=True))
+    return weights * (1.0 / jnp.sum(weights, axis=0, keepdims=True))
 
 
 def outside_of(segment_ref):
@@ -44,7 +44,7 @@
     for start in range(0, out_ref.shape[2], HEAD_DIM):
         head = slice(start, start + HEAD_DIM)
         probs = probabilities(qkv_ref[0, 0, :, head], qkv_ref[1, 0, :, head], outside[...])
-        mixed = product(probs.astype(jnp.bfloat16), qkv_ref[2, 0, :, head], NN)
+        mixed = product(probs.astype(jnp.bfloat16), qkv_ref[2, 0, :, head], TN)
         out_ref[0, :, head] = mixed.astype(jnp.bfloat16)
 
 
@@ -93,12 +93,12 @@
         queries, keys, values = stash[0, :, head], stash[1, :, head], stash[2, :, head]
         upstream = upstream_ref[0, :, head]
         probs = probabilities(queries, keys, outside)
-        grad_value = product(probs.astype(jnp.bfloat16), upstream, TN)
-        grad_probs = product(upstream, values, NT)
-        center = jnp.sum(probs * grad_probs, axis=1, keepdims=True)
-        grad_logits = (probs * (grad_probs - center) * SCALE).astype(jnp.bfloat16)
-        out_ref[0, 0, :, head] = (product(grad_logits, keys, NN) * factor).astype(jnp.bfloat16)
-        out_ref[1, 0, :, head] = (product(grad_logits, queries, TN) * factor).astype(jnp.bfloat16)
+        grad_value = product(probs.astype(jnp.bfloat16), upstream, NN)
+        grad_probs = product(values, upstream, NT)
+        center = jnp.sum(probs * grad_probs, axis=0, keepdims=True)
+        grad_logits = (probs * ((grad_probs - center) * SCALE)).astype(jnp.bfloat16)
+        out_ref[0, 0, :, head] = (product(grad_logits, keys, TN) * factor).astype(jnp.bfloat16)
+        out_ref[1, 0, :, head] = (product(grad_logits, queries, NN) * factor).astype(jnp.bfloat16)
         out_ref[2, 0, :, head] = (grad_value * factor).astype(jnp.bfloat16)
 
 

time: 167 us -> 164 us (0.982)
  Pallas kernels: 22.4 us -> 19.3 us
  transfers between devices with their start and end apart: 16 -> 16, of which waited for: 10 -> 8; matrix products, arithmetic and copies ran while one was open for 3% -> 3% of each run, Pallas kernels for 11% -> 11%
where the time goes in v8:
time: 164 us
  waiting for transfers between devices  83.3 us (51%)
  starting transfers between devices  43.8 us (27%)
  Pallas kernels  19.3 us (12%)
  blocking collectives  9.9 us (6%)
  local copies, waits for them, and re-layouts  5.69 us (3%)
  between operations  2.07 us (1%)
    ppermute x14, waiting for transfers between devices, fetched(): return lax.ppermute(piece, AXES, pairs)  83.3 us
    ppermute x14, starting transfers between devices, fetched(): return lax.ppermute(piece, AXES, pairs)  36.4 us
    pallas_call x3, Pallas kernels, backward(): pl.pallas_call(functools.partial(backward_kernel, parts, carried is not N...  14.1 us
    psum x1, blocking collectives, on_device(): token_total = lax.psum(tokens, 'dp')  9.9 us
    ppermute x2, starting transfers between devices, shifted(): lax.ppermute(array, 'pipe', [(p, (p + by) % sections) for p in range(sect...  7.41 us
    dynamic_slice x3, local copies, waits for them, and re-layouts, fetched_chunk(): piece = lax.dynamic_slice_in_dim(whole, start, heads * HEAD_DIM, axis=3)  5.68 us
    pallas_call x1, Pallas kernels, forward(): pl.pallas_call(forward_kernel, grid=(FORWARD_STEPS,), in_specs=[pl.BlockS...  5.2 us
  transfers between devices with their start and end apart: 16, of which 8 were waited for; matrix products, arithmetic and copies ran while one was open for 3% of the time, Pallas kernels for 11%

profile of v8, /device:TPU:1, one launch (start us, length us, event | category | flops | bytes accessed | tf_op | source)
XLA Modules:
  0.0 164.1 jit_solution(14011555539405229735)
XLA Ops:
  0.6 7.4 %collective-permute-start.5 = (bf16[1,256,2048]{2,1,0:T(8,128)(2,1)}, bf16[1,256,2048]{2,1,0:T(8,128)(2,1)S(1)}, u32[]{:S(2)}, u32[]{:S(2)}) collective-permute-start(bf16[1,256,2048]{2,1,0:T(8,128)(2,1)} %param.10), channel_id=1, source_target_pairs={{0,240},{16,0},{32,16},{48,32},{64,48},{80,64},{96,80},{112,96},{1... | collective-permute-start | bytes 3145736 | tf_op jit(solution)/shard_map/direct_grad/ppermute | solution.py:171
  8.0 2.4 %constant_dynamic-slice_fusion.4 = (bf16[3,1,64,1024]{3,2,1,0:T(8,128)(2,1)S(1)}, bf16[3,1,64,1024]{3,2,1,0:T(8,128)(2,1)}, bf16[3,1,64,1024]{3,2,1,0:T(8,128)(2,1)S(1)}, bf16[3,1,64,1024]{3,2,1,0:T(8,128)(2,1)}) fusion(bf16[3,1,64,8192]{3,2,1,0:T(8,128)(2,1)} %param.8, s32[]{:T(128)S(6)} %select_n.43, s32[]{:T(128)S(6)} %select_n.41, s32[]{:T(128)S(6)} %select_n.36, ...), kind=kLoop, calls=%fused_computation.4 | loop fusion | bytes 3145744 | tf_op jit(solution)/shard_map/dynamic_slice | solution.py:184
  10.4 2.7 %collective-permute-start.11 = (bf16[3,1,64,1024]{3,2,1,0:T(8,128)(2,1)S(1)}, bf16[3,1,64,1024]{3,2,1,0:T(8,128)(2,1)S(1)}, u32[]{:S(2)}, u32[]{:S(2)}) collective-permute-start(bf16[3,1,64,1024]{3,2,1,0:T(8,128)(2,1)S(1)} %get-tuple-element.20), channel_id=1, source_target_pairs={{0,252},{4,248},{8,244},{12,240},{16,236},{20,232},{24,228},{28,22... | collective-permute-start | bytes 1179656 | tf_op jit(solution)/shard_map/stash_3_0/ppermute | solution.py:159
  13.0 0.0 copy-start
  13.0 1.5 collective-permute-start.7
  14.6 4.3 %collective-permute-start = (bf16[3,1,64,1024]{3,2,1,0:T(8,128)(2,1)S(1)}, bf16[3,1,64,1024]{3,2,1,0:T(8,128)(2,1)S(1)}, u32[]{:S(2)}, u32[]{:S(2)}) collective-permute-start(bf16[3,1,64,1024]{3,2,1,0:T(8,128)(2,1)S(1)} %get-tuple-element.22), channel_id=1, source_target_pairs={{0,240},{4,244},{8,248},{12,252},{16,224},{20,228},{24,232},{28,23... | collective-permute-start | bytes 1179656 | tf_op jit(solution)/shard_map/stash_0_0/ppermute | solution.py:159
  18.9 5.2 %forward_heads.1 = bf16[1,256,2048]{2,1,0:T(8,128)(2,1)} custom-call(bf16[3,1,256,2048]{3,2,1,0:T(8,128)(2,1)} %qkv_ref.1, s32[1,256]{1,0:T(1,128)} %segment_ref.1), custom_call_target="tpu_custom_call" | custom-call | flops 536870912 | bytes 4194304 | tf_op jit(solution)/shard_map/forward_heads/pallas_call | solution.py:54
  24.1 0.0 collective-permute-start.6
  24.1 31.3 %collective-permute-done.11.refs_4_ = bf16[3,1,64,1024]{3,2,1,0:T(8,128)(2,1)S(1)} collective-permute-done((bf16[3,1,64,1024]{3,2,1,0:T(8,128)(2,1)S(1)}, bf16[3,1,64,1024]{3,2,1,0:T(8,128)(2,1)S(1)}, u32[]{:S(2)}, u32[]{:S(2)}) %collective-permute-start.11) | collective-permute-done | bytes 393248 | tf_op jit(solution)/shard_map/stash_3_0/ppermute | solution.py:159
  55.4 5.3 %collective-permute-start.9 = (bf16[3,1,64,1024]{3,2,1,0:T(8,128)(2,1)}, bf16[3,1,64,1024]{3,2,1,0:T(8,128)(2,1)S(1)}, u32[]{:S(2)}, u32[]{:S(2)}) collective-permute-start(bf16[3,1,64,1024]{3,2,1,0:T(8,128)(2,1)} %get-tuple-element.21), channel_id=1, source_target_pairs={{0,244},{4,240},{8,252},{12,248},{16,228},{20,224},{24,236},{28,23... | collective-permute-start | bytes 1179656 | tf_op jit(solution)/shard_map/stash_1_0/ppermute | solution.py:159
  60.7 0.0 collective-permute-done.7
  60.7 2.2 %collective-permute-start.10 = (bf16[3,1,64,1024]{3,2,1,0:T(8,128)(2,1)}, bf16[3,1,64,1024]{3,2,1,0:T(8,128)(2,1)}, u32[]{:S(2)}, u32[]{:S(2)}) collective-permute-start(bf16[3,1,64,1024]{3,2,1,0:T(8,128)(2,1)} %get-tuple-element.23), channel_id=1, source_target_pairs={{0,248},{4,252},{8,240},{12,244},{16,232},{20,236},{24,224},{28,22... | collective-permute-start | bytes 1179656 | tf_op jit(solution)/shard_map/stash_2_0/ppermute | solution.py:159
  62.9 0.9 collective-permute-done.refs_0_
  63.8 1.4 collective-permute-start.8
  65.9 9.9 %psum.7 = f32[1]{0:T(128)} all-reduce(f32[1]{0:T(128)S(6)} %convert_element_type.3), channel_id=1, replica_groups=mesh['pipe'=16,'tensor'=4,'dp'=4] {'dp'}, use_global_device_ids=true, to_apply=%region_0.0 | all-reduce | flops 1 | bytes 8 | tf_op jit(solution)/shard_map/psum | solution.py:202
  75.8 2.3 %constant_dynamic-slice_fusion.7 = (bf16[3,1,64,768]{3,2,1,0:T(8,128)(2,1)}, bf16[3,1,64,768]{3,2,1,0:T(8,128)(2,1)}, bf16[3,1,64,768]{3,2,1,0:T(8,128)(2,1)}, bf16[3,1,64,768]{3,2,1,0:T(8,128)(2,1)}) fusion(bf16[3,1,64,8192]{3,2,1,0:T(8,128)(2,1)} %param.8, s32[]{:T(128)S(6)} %select_n.40, s32[]{:T(128)S(6)} %select_n.39, s32[]{:T(128)S(6)} %select_n.38, ...), kind=kLoop, calls=%fused_computation.7 | loop fusion | bytes 2359312 | tf_op jit(solution)/shard_map/dynamic_slice | solution.py:184
  78.1 0.0 collective-permute-done.9.refs_2_
  78.1 9.6 %collective-permute-start.4 = (bf16[3,1,64,768]{3,2,1,0:T(8,128)(2,1)}, bf16[3,1,64,768]{3,2,1,0:T(8,128)(2,1)}, u32[]{:S(2)}, u32[]{:S(2)}) collective-permute-start(bf16[3,1,64,768]{3,2,1,0:T(8,128)(2,1)} %get-tuple-element.24), channel_id=1, source_target_pairs={{0,252},{4,248},{8,244},{12,240},{16,236},{20,232},{24,228},{28,22... | collective-permute-start | bytes 884744 | tf_op jit(solution)/shard_map/stash_3_1/ppermute | solution.py:159
  87.7 7.7 %collective-permute-done.10.refs_3_ = bf16[3,1,64,1024]{3,2,1,0:T(8,128)(2,1)} collective-permute-done((bf16[3,1,64,1024]{3,2,1,0:T(8,128)(2,1)}, bf16[3,1,64,1024]{3,2,1,0:T(8,128)(2,1)}, u32[]{:S(2)}, u32[]{:S(2)}) %collective-permute-start.10) | collective-permute-done | bytes 393248 | tf_op jit(solution)/shard_map/stash_2_0/ppermute | solution.py:159
  95.4 0.0 collective-permute-start.3
  95.4 0.0 collective-permute-done.8.refs_1_
  95.4 3.5 %collective-permute-start.2 = (bf16[3,1,64,768]{3,2,1,0:T(8,128)(2,1)}, bf16[3,1,64,768]{3,2,1,0:T(8,128)(2,1)}, u32[]{:S(2)}, u32[]{:S(2)}) collective-permute-start(bf16[3,1,64,768]{3,2,1,0:T(8,128)(2,1)} %get-tuple-element.26), channel_id=1, source_target_pairs={{0,244},{4,240},{8,252},{12,248},{16,228},{20,224},{24,236},{28,23... | collective-permute-start | bytes 884744 | tf_op jit(solution)/shard_map/stash_1_1/ppermute | solution.py:159
  98.9 0.0 collective-permute-done.5.refs_5_.refs_4_
  98.9 1.1 collective-permute-start.1
  100.8 0.0 copy-done
  100.8 6.3 %shard_map.77.refs_8_ = bf16[3,1,256,2048]{3,2,1,0:T(8,128)(2,1)} custom-call(bf16[3,1,64,1024]{3,2,1,0:T(8,128)(2,1)S(1)} %collective-permute-done.refs_0_, bf16[3,1,64,1024]{3,2,1,0:T(8,128)(2,1)} %collective-permute-done.8.refs_1_, bf16[3,1,64,1024]{3,2,1,0:T(8,128)(2,1)S(1)} %collective-permute-done.9.refs_2_, ...), custom_call_target="tpu_custom_call" | custom-call | flops 671088640 | bytes 3670016 | tf_op jit(solution)/shard_map/pallas_call | solution.py:130
  107.1 1.1 constant_dynamic-slice_fusion
  108.2 0.0 collective-permute-done.4.refs_3_
  108.2 4.4 %collective-permute-start.15 = (bf16[3,1,64,256]{3,2,1,0:T(8,128)(2,1)S(1)}, bf16[3,1,64,256]{3,2,1,0:T(8,128)(2,1)S(1)}, u32[]{:S(2)}, u32[]{:S(2)}) collective-permute-start(bf16[3,1,64,256]{3,2,1,0:T(8,128)(2,1)S(1)} %get-tuple-element.16), channel_id=1, source_target_pairs={{0,252},{4,248},{8,244},{12,240},{16,236},{20,232},{24,228},{28,22... | collective-permute-start | bytes 294920 | tf_op jit(solution)/shard_map/stash_3_2/ppermute | solution.py:159
  112.6 28.4 %collective-permute-done.3.refs_2_ = bf16[3,1,64,768]{3,2,1,0:T(8,128)(2,1)} collective-permute-done((bf16[3,1,64,768]{3,2,1,0:T(8,128)(2,1)}, bf16[3,1,64,768]{3,2,1,0:T(8,128)(2,1)}, u32[]{:S(2)}, u32[]{:S(2)}) %collective-permute-start.3) | collective-permute-done | bytes 294944 | tf_op jit(solution)/shard_map/stash_2_1/ppermute | solution.py:159
  141.0 0.3 collective-permute-start.14
  141.3 6.1 %collective-permute-done.2.refs_1_ = bf16[3,1,64,768]{3,2,1,0:T(8,128)(2,1)} collective-permute-done((bf16[3,1,64,768]{3,2,1,0:T(8,128)(2,1)}, bf16[3,1,64,768]{3,2,1,0:T(8,128)(2,1)}, u32[]{:S(2)}, u32[]{:S(2)}) %collective-permute-start.2) | collective-permute-done | bytes 294944 | tf_op jit(solution)/shard_map/stash_1_1/ppermute | solution.py:159
  147.4 0.0 collective-permute-start.13
  147.4 6.3 %collective-permute-done.1.refs_0_ = bf16[3,1,64,768]{3,2,1,0:T(8,128)(2,1)} collective-permute-done((bf16[3,1,64,768]{3,2,1,0:T(8,128)(2,1)}, bf16[3,1,64,768]{3,2,1,0:T(8,128)(2,1)}, u32[]{:S(2)}, u32[]{:S(2)}) %collective-permute-start.1) | collective-permute-done | bytes 294944 | tf_op jit(solution)/shard_map/stash_0_1/ppermute | solution.py:159
  153.7 0.0 collective-permute-start.12
  153.7 0.0 collective-permute-done.6.refs_7_
  153.7 5.7 %shard_map.78 = (bf16[3,1,256,2048]{3,2,1,0:T(8,128)(2,1)}, bf16[1,256,2048]{2,1,0:T(8,128)(2,1)}) custom-call(bf16[3,1,64,768]{3,2,1,0:T(8,128)(2,1)} %collective-permute-done.1.refs_0_, bf16[3,1,64,768]{3,2,1,0:T(8,128)(2,1)} %collective-permute-done.2.refs_1_, ...), custom_call_target="tpu_custom_call", output_to_operand_aliasing={{0}: (8, {})} | custom-call | flops 503316480 | bytes 2752512 | tf_op jit(solution)/shard_map/pallas_call | solution.py:130
  159.5 0.0 collective-permute-done.15.refs_3_
  159.5 0.0 collective-permute-done.14.refs_2_
  159.5 0.5 collective-permute-done.13.refs_1_
  160.0 2.1 %collective-permute-done.12.refs_0_ = bf16[3,1,64,256]{3,2,1,0:T(8,128)(2,1)S(1)} collective-permute-done((bf16[3,1,64,256]{3,2,1,0:T(8,128)(2,1)S(1)}, bf16[3,1,64,256]{3,2,1,0:T(8,128)(2,1)S(1)}, u32[]{:S(2)}, u32[]{:S(2)}) %collective-permute-start.12) | collective-permute-done | bytes 98336 | tf_op jit(solution)/shard_map/stash_0_2/ppermute | solution.py:159
  162.1 2.1 %shard_map.79 = bf16[3,1,256,2048]{3,2,1,0:T(8,128)(2,1)} custom-call(bf16[3,1,64,256]{3,2,1,0:T(8,128)(2,1)S(1)} %collective-permute-done.12.refs_0_, bf16[3,1,64,256]{3,2,1,0:T(8,128)(2,1)S(1)} %collective-permute-done.13.refs_1_, bf16[3,1,64,256]{3,2,1,0:T(8,128)(2,1)S(1)} %collective-permute-done.14.refs_2_, ...), custom_call_target="tpu_custom_call", output_to_operand_aliasing={{}: (7, {})} | custom-call | flops 167772160 | bytes 917504 | tf_op jit(solution)/shard_map/pallas_call | solution.py:130
Async XLA Ops:
  0.6 98.3 %collective-permute-start.5 = (bf16[1,256,2048]{2,1,0:T(8,128)(2,1)}, bf16[1,256,2048]{2,1,0:T(8,128)(2,1)S(1)}, u32[]{:S(2)}, u32[]{:S(2)}) collective-permute-start(bf16[1,256,2048]{2,1,0:T(8,128)(2,1)} %param.10), channel_id=1, source_target_pairs={{0,240},{16,0},{32,16},{48,32},{64,48},{80,64},{96,80},{112,96},{1... | collective-permute-start | bytes 3145736 | tf_op jit(solution)/shard_map/direct_grad/ppermute | solution.py:171
  10.4 45.0 %collective-permute-start.11 = (bf16[3,1,64,1024]{3,2,1,0:T(8,128)(2,1)S(1)}, bf16[3,1,64,1024]{3,2,1,0:T(8,128)(2,1)S(1)}, u32[]{:S(2)}, u32[]{:S(2)}) collective-permute-start(bf16[3,1,64,1024]{3,2,1,0:T(8,128)(2,1)S(1)} %get-tuple-element.20), channel_id=1, source_target_pairs={{0,252},{4,248},{8,244},{12,240},{16,236},{20,232},{24,228},{28,22... | collective-permute-start | bytes 1179656 | tf_op jit(solution)/shard_map/stash_3_0/ppermute | solution.py:159
  13.0 87.7 %copy-start = (s32[1,256]{1,0:T(1,128)S(1)}, s32[1,256]{1,0:T(1,128)}, u32[]{:S(2)}) copy-start(s32[1,256]{1,0:T(1,128)} %refs_5_.3) | copy-start | bytes 3076
  13.0 47.6 %collective-permute-start.7 = (bf16[3,1,64,1024]{3,2,1,0:T(8,128)(2,1)S(1)}, bf16[3,1,64,1024]{3,2,1,0:T(8,128)(2,1)}, u32[]{:S(2)}, u32[]{:S(2)}) collective-permute-start(bf16[3,1,64,1024]{3,2,1,0:T(8,128)(2,1)S(1)} %get-tuple-element.22), channel_id=1, source_target_pairs={{32,48},{36,52},{40,56},{44,60},{80,64},{84,68},{88,72},{92,76},{1... | collective-permute-start | bytes 1179656 | tf_op jit(solution)/shard_map/aside_0/ppermute | solution.py:159
  14.6 49.2 %collective-permute-start = (bf16[3,1,64,1024]{3,2,1,0:T(8,128)(2,1)S(1)}, bf16[3,1,64,1024]{3,2,1,0:T(8,128)(2,1)S(1)}, u32[]{:S(2)}, u32[]{:S(2)}) collective-permute-start(bf16[3,1,64,1024]{3,2,1,0:T(8,128)(2,1)S(1)} %get-tuple-element.22), channel_id=1, source_target_pairs={{0,240},{4,244},{8,248},{12,252},{16,224},{20,228},{24,232},{28,23... | collective-permute-start | bytes 1179656 | tf_op jit(solution)/shard_map/stash_0_0/ppermute | solution.py:159
  24.1 129.6 %collective-permute-start.6 = (bf16[1,256,2048]{2,1,0:T(8,128)(2,1)}, bf16[1,256,2048]{2,1,0:T(8,128)(2,1)S(1)}, u32[]{:S(2)}, u32[]{:S(2)}) collective-permute-start(bf16[1,256,2048]{2,1,0:T(8,128)(2,1)} %forward_heads.1), channel_id=1, source_target_pairs={{0,16},{16,32},{32,48},{48,64},{64,80},{80,96},{96,112},{112,128},... | collective-permute-start | bytes 3145736 | tf_op jit(solution)/shard_map/direct_out/ppermute | solution.py:171
  55.4 22.7 %collective-permute-start.9 = (bf16[3,1,64,1024]{3,2,1,0:T(8,128)(2,1)}, bf16[3,1,64,1024]{3,2,1,0:T(8,128)(2,1)S(1)}, u32[]{:S(2)}, u32[]{:S(2)}) collective-permute-start(bf16[3,1,64,1024]{3,2,1,0:T(8,128)(2,1)} %get-tuple-element.21), channel_id=1, source_target_pairs={{0,244},{4,240},{8,252},{12,248},{16,228},{20,224},{24,236},{28,23... | collective-permute-start | bytes 1179656 | tf_op jit(solution)/shard_map/stash_1_0/ppermute | solution.py:159
  60.7 34.7 %collective-permute-start.10 = (bf16[3,1,64,1024]{3,2,1,0:T(8,128)(2,1)}, bf16[3,1,64,1024]{3,2,1,0:T(8,128)(2,1)}, u32[]{:S(2)}, u32[]{:S(2)}) collective-permute-start(bf16[3,1,64,1024]{3,2,1,0:T(8,128)(2,1)} %get-tuple-element.23), channel_id=1, source_target_pairs={{0,248},{4,252},{8,240},{12,244},{16,232},{20,236},{24,224},{28,22... | collective-permute-start | bytes 1179656 | tf_op jit(solution)/shard_map/stash_2_0/ppermute | solution.py:159
  63.8 31.6 %collective-permute-start.8 = (bf16[3,1,64,1024]{3,2,1,0:T(8,128)(2,1)}, bf16[3,1,64,1024]{3,2,1,0:T(8,128)(2,1)}, u32[]{:S(2)}, u32[]{:S(2)}) collective-permute-start(bf16[3,1,64,1024]{3,2,1,0:T(8,128)(2,1)} %collective-permute-done.7), channel_id=1, source_target_pairs={{48,208},{52,212},{56,216},{60,220},{64,160},{68,164},{72,168},{76... | collective-permute-start | bytes 1179656 | tf_op jit(solution)/shard_map/onward_0/ppermute | solution.py:159
  78.1 30.1 %collective-permute-start.4 = (bf16[3,1,64,768]{3,2,1,0:T(8,128)(2,1)}, bf16[3,1,64,768]{3,2,1,0:T(8,128)(2,1)}, u32[]{:S(2)}, u32[]{:S(2)}) collective-permute-start(bf16[3,1,64,768]{3,2,1,0:T(8,128)(2,1)} %get-tuple-element.24), channel_id=1, source_target_pairs={{0,252},{4,248},{8,244},{12,240},{16,236},{20,232},{24,228},{28,22... | collective-permute-start | bytes 884744 | tf_op jit(solution)/shard_map/stash_3_1/ppermute | solution.py:159
  95.4 45.5 %collective-permute-start.3 = (bf16[3,1,64,768]{3,2,1,0:T(8,128)(2,1)}, bf16[3,1,64,768]{3,2,1,0:T(8,128)(2,1)}, u32[]{:S(2)}, u32[]{:S(2)}) collective-permute-start(bf16[3,1,64,768]{3,2,1,0:T(8,128)(2,1)} %get-tuple-element.25), channel_id=1, source_target_pairs={{0,248},{4,252},{8,240},{12,244},{16,232},{20,236},{24,224},{28,22... | collective-permute-start | bytes 884744 | tf_op jit(solution)/shard_map/stash_2_1/ppermute | solution.py:159
  95.4 52.0 %collective-permute-start.2 = (bf16[3,1,64,768]{3,2,1,0:T(8,128)(2,1)}, bf16[3,1,64,768]{3,2,1,0:T(8,128)(2,1)}, u32[]{:S(2)}, u32[]{:S(2)}) collective-permute-start(bf16[3,1,64,768]{3,2,1,0:T(8,128)(2,1)} %get-tuple-element.26), channel_id=1, source_target_pairs={{0,244},{4,240},{8,252},{12,248},{16,228},{20,224},{24,236},{28,23... | collective-permute-start | bytes 884744 | tf_op jit(solution)/shard_map/stash_1_1/ppermute | solution.py:159
  98.9 54.8 %collective-permute-start.1 = (bf16[3,1,64,768]{3,2,1,0:T(8,128)(2,1)}, bf16[3,1,64,768]{3,2,1,0:T(8,128)(2,1)}, u32[]{:S(2)}, u32[]{:S(2)}) collective-permute-start(bf16[3,1,64,768]{3,2,1,0:T(8,128)(2,1)} %get-tuple-element.27), channel_id=1, source_target_pairs={{0,240},{4,244},{8,248},{12,252},{16,224},{20,228},{24,232},{28,23... | collective-permute-start | bytes 884744 | tf_op jit(solution)/shard_map/stash_0_1/ppermute | solution.py:159
  108.2 51.3 %collective-permute-start.15 = (bf16[3,1,64,256]{3,2,1,0:T(8,128)(2,1)S(1)}, bf16[3,1,64,256]{3,2,1,0:T(8,128)(2,1)S(1)}, u32[]{:S(2)}, u32[]{:S(2)}) collective-permute-start(bf16[3,1,64,256]{3,2,1,0:T(8,128)(2,1)S(1)} %get-tuple-element.16), channel_id=1, source_target_pairs={{0,252},{4,248},{8,244},{12,240},{16,236},{20,232},{24,228},{28,22... | collective-permute-start | bytes 294920 | tf_op jit(solution)/shard_map/stash_3_2/ppermute | solution.py:159
  141.0 18.5 %collective-permute-start.14 = (bf16[3,1,64,256]{3,2,1,0:T(8,128)(2,1)S(1)}, bf16[3,1,64,256]{3,2,1,0:T(8,128)(2,1)S(1)}, u32[]{:S(2)}, u32[]{:S(2)}) collective-permute-start(bf16[3,1,64,256]{3,2,1,0:T(8,128)(2,1)S(1)} %get-tuple-element.17), channel_id=1, source_target_pairs={{0,248},{4,252},{8,240},{12,244},{16,232},{20,236},{24,224},{28,22... | collective-permute-start | bytes 294920 | tf_op jit(solution)/shard_map/stash_2_2/ppermute | solution.py:159
  147.4 12.5 %collective-permute-start.13 = (bf16[3,1,64,256]{3,2,1,0:T(8,128)(2,1)S(1)}, bf16[3,1,64,256]{3,2,1,0:T(8,128)(2,1)S(1)}, u32[]{:S(2)}, u32[]{:S(2)}) collective-permute-start(bf16[3,1,64,256]{3,2,1,0:T(8,128)(2,1)S(1)} %get-tuple-element.18), channel_id=1, source_target_pairs={{0,244},{4,240},{8,252},{12,248},{16,228},{20,224},{24,236},{28,23... | collective-permute-start | bytes 294920 | tf_op jit(solution)/shard_map/stash_1_2/ppermute | solution.py:159
  153.7 8.3 %collective-permute-start.12 = (bf16[3,1,64,256]{3,2,1,0:T(8,128)(2,1)S(1)}, bf16[3,1,64,256]{3,2,1,0:T(8,128)(2,1)S(1)}, u32[]{:S(2)}, u32[]{:S(2)}) collective-permute-start(bf16[3,1,64,256]{3,2,1,0:T(8,128)(2,1)S(1)} %get-tuple-element.19), channel_id=1, source_target_pairs={{0,240},{4,244},{8,248},{12,252},{16,224},{20,228},{24,232},{28,23... | collective-permute-start | bytes 294920 | tf_op jit(solution)/shard_map/stash_0_2/ppermute | solution.py:159

commit v9 on v8

--- a/solution.py
+++ b/solution.py
@@ -10,7 +10,8 @@
 
 HEAD_DIM = 128
 FORWARD_STEPS = 2
-CHUNKS = ((8, 8), (0, 6), (6, 2))
+CHUNKS = ((0, 10), (12, 4), (10, 2))
+DETOUR = (0, 10)
 SCALE = HEAD_DIM ** (-0.5)
 EXPONENT = SCALE * math.log2(math.e)
 NT = (((1,), (1,)), ((), ()))
@@ -70,7 +71,7 @@
     )(qkv, segment)
 
 
-def backward_kernel(parts, carries, *refs):
+def backward_kernel(parts, around_from, carries, *refs):
     pieces, refs = refs[:parts], refs[parts:]
     upstream_ref, segment_ref, factor_ref = refs[:3]
     out_ref, stash = refs[-2:]
@@ -79,9 +80,12 @@
         refs[-2][...] = refs[3][...]
     mine = lax.axis_index("tensor")
     rows = pieces[0].shape[2]
+    if around_from is not None:
+        columns = slice(around_from, around_from + pieces[0].shape[3])
+        around = pieces[-1][:, 0, :, columns]
+        pieces = pieces[:-1]
     found = [piece[:, 0] for piece in pieces]
-    if parts > 4:
-        around = found.pop(1)
+    if around_from is not None:
         found[0] = jnp.where(detoured(lax.axis_index("pipe")), around, found[0])
     for k, piece in enumerate(found):
         start = pl.multiple_of((mine ^ k) * rows, rows)
@@ -102,11 +106,15 @@
         out_ref[2, 0, :, head] = (grad_value * factor).astype(jnp.bfloat16)
 
 
-def backward(chunk, pieces, upstream, segment, factor, earlier, carried=None):
+def backward(chunk, pieces, around, upstream, segment, factor, earlier, carried=None):
     _, length, width = upstream.shape
     first, heads = CHUNKS[chunk]
     step = heads * HEAD_DIM
     place = first // heads
+    around_from = None
+    if DETOUR[0] <= first and first + heads <= sum(DETOUR):
+        around_from = (first - DETOUR[0]) * HEAD_DIM
+        pieces = [*pieces, around]
     parts = len(pieces)
     operands = [*pieces, upstream, segment, factor]
     in_specs = [pl.BlockSpec(memory_space=pltpu.VMEM)] * parts + [
@@ -128,7 +136,7 @@
         operands.append(earlier)
         in_specs.append(pl.BlockSpec(memory_space=pl.ANY))
     return pl.pallas_call(
-        functools.partial(backward_kernel, parts, carried is not None),
+        functools.partial(backward_kernel, parts, around_from, carried is not None),
         grid=(1,),
         in_specs=in_specs,
         out_specs=out_specs,
@@ -176,23 +184,25 @@
     tensors = lax.axis_size("tensor")
     mine = lax.axis_index("tensor")
 
+    def cut(whole, k, first, heads):
+        start = (mine ^ k) * width + first * HEAD_DIM
+        return lax.dynamic_slice_in_dim(whole, start, heads * HEAD_DIM, axis=3)
+
     def fetched_chunk(whole, chunk):
         first, heads = CHUNKS[chunk]
         pieces = []
         for k in range(tensors):
-            start = (mine ^ k) * width + first * HEAD_DIM
-            piece = lax.dynamic_slice_in_dim(whole, start, heads * HEAD_DIM, axis=3)
-            around = chunk == 0 and k == 0
+            goes_around = k == 0 and DETOUR[0] <= first and first + heads <= sum(DETOUR)
             with jax.named_scope(f"stash_{k}_{chunk}"):
-                pieces.append(fetched(piece, k, "direct" if around else "all"))
-            if around:
-                with jax.named_scope("aside_0"):
-                    piece = fetched(piece, k, "aside")
-                with jax.named_scope("onward_0"):
-                    pieces.append(fetched(piece, k, "onward"))
+                piece = cut(whole, k, first, heads)
+                pieces.append(fetched(piece, k, "direct" if goes_around else "all"))
         return pieces
 
     upstream = shifted(grad_out, -1)
+    with jax.named_scope("aside_0"):
+        around = fetched(cut(parked, 0, *DETOUR), 0, "aside")
+    with jax.named_scope("onward_0"):
+        around = fetched(around, 0, "onward")
     pieces = [fetched_chunk(parked, 0)]
     with jax.named_scope("forward_heads"):
         forward_out = forward(fwd_qkv, fwd_segments)
@@ -203,11 +213,13 @@
     factor = jnp.float32(lax.axis_size("dp") * length) / token_total
     parked, token_total = lax.optimization_barrier((parked, token_total))
     pieces.append(fetched_chunk(parked, 1))
-    (grads,) = backward(0, pieces[0], upstream, bwd_segments, factor, None)
+    (grads,) = backward(0, pieces[0], around, upstream, bwd_segments, factor, None)
     parked, grads = lax.optimization_barrier((parked, grads))
     pieces.append(fetched_chunk(parked, 2))
-    grads, received = backward(1, pieces[1], upstream, bwd_segments, factor, grads, received)
-    (grads,) = backward(2, pieces[2], upstream, bwd_segments, factor, grads)
+    grads, received = backward(
+        1, pieces[1], around, upstream, bwd_segments, factor, grads, received
+    )
+    (grads,) = backward(2, pieces[2], around, upstream, bwd_segments, factor, grads)
     return (received, grads)
 
 

time: 164 us -> 173 us (1.055)
  the two profiles are of different devices: /device:TPU:1 before, /device:TPU:23 now
where the time goes in v9:
time: 173 us
  waiting for transfers between devices  77 us (45%)
  starting transfers between devices  63 us (36%)
  Pallas kernels  18.3 us (11%)
  blocking collectives  7.7 us (4%)
  local copies, waits for them, and re-layouts  4.94 us (3%)
  between operations  1.99 us (1%)
    ppermute x14, waiting for transfers between devices, fetched(): return lax.ppermute(piece, AXES, pairs)  77 us
    ppermute x14, starting transfers between devices, fetched(): return lax.ppermute(piece, AXES, pairs)  58 us
    pallas_call x3, Pallas kernels, backward(): pl.pallas_call(functools.partial(backward_kernel, parts, around_from, car...  13.1 us
    psum x1, blocking collectives, on_device(): token_total = lax.psum(tokens, 'dp')  7.7 us
    pallas_call x1, Pallas kernels, forward(): pl.pallas_call(forward_kernel, grid=(FORWARD_STEPS,), in_specs=[pl.BlockS...  5.18 us
    ppermute x2, starting transfers between devices, shifted(): lax.ppermute(array, 'pipe', [(p, (p + by) % sections) for p in range(sect...  4.96 us
    dynamic_slice x3, local copies, waits for them, and re-layouts, cut(): return lax.dynamic_slice_in_dim(whole, start, heads * HEAD_DIM, axis=3)  4.93 us
  transfers between devices with their start and end apart: 16, of which 4 were waited for; matrix products, arithmetic and copies ran while one was open for 3% of the time, Pallas kernels for 9%

profile of v9, /device:TPU:23, one launch (start us, length us, event | category | flops | bytes accessed | tf_op | source)
XLA Modules:
  0.0 173.0 jit_solution(15739301963482702647)
XLA Ops:
  0.6 0.6 collective-permute-start.5
  1.3 2.6 %constant_dynamic-slice_fusion.4 = (bf16[3,1,64,1280]{3,2,1,0:T(8,128)(2,1)}, bf16[3,1,64,1280]{3,2,1,0:T(8,128)(2,1)S(1)}, bf16[3,1,64,1280]{3,2,1,0:T(8,128)(2,1)S(1)}, bf16[3,1,64,1280]{3,2,1,0:T(8,128)(2,1)}) fusion(bf16[3,1,64,8192]{3,2,1,0:T(8,128)(2,1)} %param.8, s32[]{:T(128)S(6)} %select_n.44, s32[]{:T(128)S(6)} %select_n.42, s32[]{:T(128)S(6)} %select_n.37, ...), kind=kLoop, calls=%fused_computation.4 | loop fusion | bytes 3932176 | tf_op jit(solution)/shard_map/stash_3_0/dynamic_slice | solution.py:189
  3.8 0.0 copy-start
  3.8 8.7 %collective-permute-start = (bf16[3,1,64,1280]{3,2,1,0:T(8,128)(2,1)S(1)}, bf16[3,1,64,1280]{3,2,1,0:T(8,128)(2,1)S(1)}, u32[]{:S(2)}, u32[]{:S(2)}) collective-permute-start(bf16[3,1,64,1280]{3,2,1,0:T(8,128)(2,1)S(1)} %get-tuple-element.22), channel_id=1, source_target_pairs={{0,240},{4,244},{8,248},{12,252},{16,224},{20,228},{24,232},{28,23... | collective-permute-start | bytes 1474568 | tf_op jit(solution)/shard_map/stash_0_0/ppermute | solution.py:167
  12.5 1.5 collective-permute-start.10
  14.0 0.9 collective-permute-start.7
  14.8 5.2 %forward_heads.1 = bf16[1,256,2048]{2,1,0:T(8,128)(2,1)} custom-call(bf16[3,1,256,2048]{3,2,1,0:T(8,128)(2,1)} %qkv_ref.1, s32[1,256]{1,0:T(1,128)} %segment_ref.1), custom_call_target="tpu_custom_call" | custom-call | flops 536870912 | bytes 4194304 | tf_op jit(solution)/shard_map/forward_heads/pallas_call | solution.py:55
  20.0 4.3 %collective-permute-start.6 = (bf16[1,256,2048]{2,1,0:T(8,128)(2,1)}, bf16[1,256,2048]{2,1,0:T(8,128)(2,1)S(1)}, u32[]{:S(2)}, u32[]{:S(2)}) collective-permute-start(bf16[1,256,2048]{2,1,0:T(8,128)(2,1)} %forward_heads.1), channel_id=1, source_target_pairs={{0,16},{16,32},{32,48},{48,64},{64,80},{80,96},{96,112},{112,128},... | collective-permute-start | bytes 3145736 | tf_op jit(solution)/shard_map/direct_out/ppermute | solution.py:179
  24.4 29.3 %collective-permute-done.refs_0_ = bf16[3,1,64,1280]{3,2,1,0:T(8,128)(2,1)S(1)} collective-permute-done((bf16[3,1,64,1280]{3,2,1,0:T(8,128)(2,1)S(1)}, bf16[3,1,64,1280]{3,2,1,0:T(8,128)(2,1)S(1)}, u32[]{:S(2)}, u32[]{:S(2)}) %collective-permute-start) | collective-permute-done | bytes 491552 | tf_op jit(solution)/shard_map/stash_0_0/ppermute | solution.py:167
  53.7 5.5 %collective-permute-start.8 = (bf16[3,1,64,1280]{3,2,1,0:T(8,128)(2,1)}, bf16[3,1,64,1280]{3,2,1,0:T(8,128)(2,1)}, u32[]{:S(2)}, u32[]{:S(2)}) collective-permute-start(bf16[3,1,64,1280]{3,2,1,0:T(8,128)(2,1)} %get-tuple-element.23), channel_id=1, source_target_pairs={{0,248},{4,252},{8,240},{12,244},{16,232},{20,236},{24,224},{28,22... | collective-permute-start | bytes 1474568 | tf_op jit(solution)/shard_map/stash_2_0/ppermute | solution.py:167
  59.2 0.0 collective-permute-done.10
  59.2 5.5 %collective-permute-start.9 = (bf16[3,1,64,1280]{3,2,1,0:T(8,128)(2,1)}, bf16[3,1,64,1280]{3,2,1,0:T(8,128)(2,1)}, u32[]{:S(2)}, u32[]{:S(2)}) collective-permute-start(bf16[3,1,64,1280]{3,2,1,0:T(8,128)(2,1)} %get-tuple-element.20), channel_id=1, source_target_pairs={{0,252},{4,248},{8,244},{12,240},{16,236},{20,232},{24,228},{28,22... | collective-permute-start | bytes 1474568 | tf_op jit(solution)/shard_map/stash_3_0/ppermute | solution.py:167
  64.7 4.8 %collective-permute-done.7.refs_1_ = bf16[3,1,64,1280]{3,2,1,0:T(8,128)(2,1)S(1)} collective-permute-done((bf16[3,1,64,1280]{3,2,1,0:T(8,128)(2,1)S(1)}, bf16[3,1,64,1280]{3,2,1,0:T(8,128)(2,1)S(1)}, u32[]{:S(2)}, u32[]{:S(2)}) %collective-permute-start.7) | collective-permute-done | bytes 491552 | tf_op jit(solution)/shard_map/stash_1_0/ppermute | solution.py:167
  69.5 1.5 collective-permute-start.11
  71.6 7.7 %psum.7 = f32[1]{0:T(128)} all-reduce(f32[1]{0:T(128)S(6)} %convert_element_type.3), channel_id=1, replica_groups=mesh['pipe'=16,'tensor'=4,'dp'=4] {'dp'}, use_global_device_ids=true, to_apply=%region_0.0 | all-reduce | flops 1 | bytes 8 | tf_op jit(solution)/shard_map/psum | solution.py:212
  80.0 1.3 constant_dynamic-slice_fusion.7
  81.3 0.0 collective-permute-done.8.refs_2_
  81.3 7.4 %collective-permute-start.1 = (bf16[3,1,64,512]{3,2,1,0:T(8,128)(2,1)S(1)}, bf16[3,1,64,512]{3,2,1,0:T(8,128)(2,1)S(1)}, u32[]{:S(2)}, u32[]{:S(2)}) collective-permute-start(bf16[3,1,64,512]{3,2,1,0:T(8,128)(2,1)S(1)} %get-tuple-element.27), channel_id=1, source_target_pairs={{0,240},{4,244},{8,248},{12,252},{16,224},{20,228},{24,232},{28,23... | collective-permute-start | bytes 589832 | tf_op jit(solution)/shard_map/stash_0_1/ppermute | solution.py:167
  88.7 41.9 %collective-permute-done.9.refs_3_ = bf16[3,1,64,1280]{3,2,1,0:T(8,128)(2,1)} collective-permute-done((bf16[3,1,64,1280]{3,2,1,0:T(8,128)(2,1)}, bf16[3,1,64,1280]{3,2,1,0:T(8,128)(2,1)}, u32[]{:S(2)}, u32[]{:S(2)}) %collective-permute-start.9) | collective-permute-done | bytes 491552 | tf_op jit(solution)/shard_map/stash_3_0/ppermute | solution.py:167
  130.6 8.2 %collective-permute-start.2 = (bf16[3,1,64,512]{3,2,1,0:T(8,128)(2,1)S(1)}, bf16[3,1,64,512]{3,2,1,0:T(8,128)(2,1)S(1)}, u32[]{:S(2)}, u32[]{:S(2)}) collective-permute-start(bf16[3,1,64,512]{3,2,1,0:T(8,128)(2,1)S(1)} %get-tuple-element.26), channel_id=1, source_target_pairs={{0,244},{4,240},{8,252},{12,248},{16,228},{20,224},{24,236},{28,23... | collective-permute-start | bytes 589832 | tf_op jit(solution)/shard_map/stash_1_1/ppermute | solution.py:167
  138.8 0.0 collective-permute-done.11.refs_4_
  138.8 6.4 %collective-permute-start.3 = (bf16[3,1,64,512]{3,2,1,0:T(8,128)(2,1)S(1)}, bf16[3,1,64,512]{3,2,1,0:T(8,128)(2,1)S(1)}, u32[]{:S(2)}, u32[]{:S(2)}) collective-permute-start(bf16[3,1,64,512]{3,2,1,0:T(8,128)(2,1)S(1)} %get-tuple-element.25), channel_id=1, source_target_pairs={{0,248},{4,252},{8,240},{12,244},{16,232},{20,236},{24,224},{28,22... | collective-permute-start | bytes 589832 | tf_op jit(solution)/shard_map/stash_2_1/ppermute | solution.py:167
  145.2 0.0 collective-permute-done.5.refs_5_.refs_4_
  145.2 3.4 %collective-permute-start.4 = (bf16[3,1,64,512]{3,2,1,0:T(8,128)(2,1)S(1)}, bf16[3,1,64,512]{3,2,1,0:T(8,128)(2,1)S(1)}, u32[]{:S(2)}, u32[]{:S(2)}) collective-permute-start(bf16[3,1,64,512]{3,2,1,0:T(8,128)(2,1)S(1)} %get-tuple-element.24), channel_id=1, source_target_pairs={{0,252},{4,248},{8,244},{12,240},{16,236},{20,232},{24,228},{28,22... | collective-permute-start | bytes 589832 | tf_op jit(solution)/shard_map/stash_3_1/ppermute | solution.py:167
  148.6 0.0 copy-done
  148.6 7.6 %shard_map.77.refs_8_ = bf16[3,1,256,2048]{3,2,1,0:T(8,128)(2,1)} custom-call(bf16[3,1,64,1280]{3,2,1,0:T(8,128)(2,1)S(1)} %collective-permute-done.refs_0_, bf16[3,1,64,1280]{3,2,1,0:T(8,128)(2,1)S(1)} %collective-permute-done.7.refs_1_, bf16[3,1,64,1280]{3,2,1,0:T(8,128)(2,1)} %collective-permute-done.8.refs_2_, ...), custom_call_target="tpu_custom_call" | custom-call | flops 838860800 | bytes 4587520 | tf_op jit(solution)/shard_map/pallas_call | solution.py:138
  156.2 1.1 constant_dynamic-slice_fusion
  157.3 0.0 collective-permute-done.1.refs_0_
  157.3 0.3 collective-permute-start.12
  157.6 0.0 collective-permute-done.2.refs_1_
  157.6 0.8 collective-permute-start.13
  158.3 0.0 collective-permute-done.3.refs_2_
  158.4 4.7 %collective-permute-start.14 = (bf16[3,1,64,256]{3,2,1,0:T(8,128)(2,1)S(1)}, bf16[3,1,64,256]{3,2,1,0:T(8,128)(2,1)S(1)}, u32[]{:S(2)}, u32[]{:S(2)}) collective-permute-start(bf16[3,1,64,256]{3,2,1,0:T(8,128)(2,1)S(1)} %get-tuple-element.17), channel_id=1, source_target_pairs={{0,248},{4,252},{8,240},{12,244},{16,232},{20,236},{24,224},{28,22... | collective-permute-start | bytes 294920 | tf_op jit(solution)/shard_map/stash_2_2/ppermute | solution.py:167
  163.0 0.0 collective-permute-done.4.refs_3_
  163.0 3.4 %collective-permute-start.15 = (bf16[3,1,64,256]{3,2,1,0:T(8,128)(2,1)S(1)}, bf16[3,1,64,256]{3,2,1,0:T(8,128)(2,1)S(1)}, u32[]{:S(2)}, u32[]{:S(2)}) collective-permute-start(bf16[3,1,64,256]{3,2,1,0:T(8,128)(2,1)S(1)} %get-tuple-element.16), channel_id=1, source_target_pairs={{0,252},{4,248},{8,244},{12,240},{16,236},{20,232},{24,228},{28,22... | collective-permute-start | bytes 294920 | tf_op jit(solution)/shard_map/stash_3_2/ppermute | solution.py:167
  166.5 0.0 collective-permute-done.6.refs_7_
  166.5 3.5 %shard_map.78 = (bf16[3,1,256,2048]{3,2,1,0:T(8,128)(2,1)}, bf16[1,256,2048]{2,1,0:T(8,128)(2,1)}) custom-call(bf16[3,1,64,512]{3,2,1,0:T(8,128)(2,1)S(1)} %collective-permute-done.1.refs_0_, bf16[3,1,64,512]{3,2,1,0:T(8,128)(2,1)S(1)} %collective-permute-done.2.refs_1_, ...), custom_call_target="tpu_custom_call", output_to_operand_aliasing={{0}: (8, {})} | custom-call | flops 335544320 | bytes 1835008 | tf_op jit(solution)/shard_map/pallas_call | solution.py:138
  170.0 0.0 collective-permute-done.12.refs_0_
  170.0 0.0 collective-permute-done.13.refs_1_
  170.0 0.0 collective-permute-done.14.refs_2_
  170.0 0.9 collective-permute-done.15.refs_3_
  170.9 2.1 %shard_map.79 = bf16[3,1,256,2048]{3,2,1,0:T(8,128)(2,1)} custom-call(bf16[3,1,64,256]{3,2,1,0:T(8,128)(2,1)S(1)} %collective-permute-done.12.refs_0_, bf16[3,1,64,256]{3,2,1,0:T(8,128)(2,1)S(1)} %collective-permute-done.13.refs_1_, bf16[3,1,64,256]{3,2,1,0:T(8,128)(2,1)S(1)} %collective-permute-done.14.refs_2_, ...), custom_call_target="tpu_custom_call", output_to_operand_aliasing={{}: (7, {})} | custom-call | flops 167772160 | bytes 917504 | tf_op jit(solution)/shard_map/pallas_call | solution.py:138
Async XLA Ops:
  0.6 144.5 %collective-permute-start.5 = (bf16[1,256,2048]{2,1,0:T(8,128)(2,1)}, bf16[1,256,2048]{2,1,0:T(8,128)(2,1)S(1)}, u32[]{:S(2)}, u32[]{:S(2)}) collective-permute-start(bf16[1,256,2048]{2,1,0:T(8,128)(2,1)} %param.10), channel_id=1, source_target_pairs={{0,240},{16,0},{32,16},{48,32},{64,48},{80,64},{96,80},{112,96},{1... | collective-permute-start | bytes 3145736 | tf_op jit(solution)/shard_map/direct_grad/ppermute | solution.py:179
  3.8 144.8 %copy-start = (s32[1,256]{1,0:T(1,128)S(1)}, s32[1,256]{1,0:T(1,128)}, u32[]{:S(2)}) copy-start(s32[1,256]{1,0:T(1,128)} %refs_5_.3) | copy-start | bytes 3076
  3.8 49.8 %collective-permute-start = (bf16[3,1,64,1280]{3,2,1,0:T(8,128)(2,1)S(1)}, bf16[3,1,64,1280]{3,2,1,0:T(8,128)(2,1)S(1)}, u32[]{:S(2)}, u32[]{:S(2)}) collective-permute-start(bf16[3,1,64,1280]{3,2,1,0:T(8,128)(2,1)S(1)} %get-tuple-element.22), channel_id=1, source_target_pairs={{0,240},{4,244},{8,248},{12,252},{16,224},{20,228},{24,232},{28,23... | collective-permute-start | bytes 1474568 | tf_op jit(solution)/shard_map/stash_0_0/ppermute | solution.py:167
  12.5 46.6 %collective-permute-start.10 = (bf16[3,1,64,1280]{3,2,1,0:T(8,128)(2,1)S(1)}, bf16[3,1,64,1280]{3,2,1,0:T(8,128)(2,1)}, u32[]{:S(2)}, u32[]{:S(2)}) collective-permute-start(bf16[3,1,64,1280]{3,2,1,0:T(8,128)(2,1)S(1)} %get-tuple-element.22), channel_id=1, source_target_pairs={{32,48},{36,52},{40,56},{44,60},{80,64},{84,68},{88,72},{92,76},{1... | collective-permute-start | bytes 1474568 | tf_op jit(solution)/shard_map/aside_0/ppermute | solution.py:167
  14.0 55.5 %collective-permute-start.7 = (bf16[3,1,64,1280]{3,2,1,0:T(8,128)(2,1)S(1)}, bf16[3,1,64,1280]{3,2,1,0:T(8,128)(2,1)S(1)}, u32[]{:S(2)}, u32[]{:S(2)}) collective-permute-start(bf16[3,1,64,1280]{3,2,1,0:T(8,128)(2,1)S(1)} %get-tuple-element.21), channel_id=1, source_target_pairs={{0,244},{4,240},{8,252},{12,248},{16,228},{20,224},{24,236},{28,23... | collective-permute-start | bytes 1474568 | tf_op jit(solution)/shard_map/stash_1_0/ppermute | solution.py:167
  20.0 146.5 %collective-permute-start.6 = (bf16[1,256,2048]{2,1,0:T(8,128)(2,1)}, bf16[1,256,2048]{2,1,0:T(8,128)(2,1)S(1)}, u32[]{:S(2)}, u32[]{:S(2)}) collective-permute-start(bf16[1,256,2048]{2,1,0:T(8,128)(2,1)} %forward_heads.1), channel_id=1, source_target_pairs={{0,16},{16,32},{32,48},{48,64},{64,80},{80,96},{96,112},{112,128},... | collective-permute-start | bytes 3145736 | tf_op jit(solution)/shard_map/direct_out/ppermute | solution.py:179
  53.7 27.6 %collective-permute-start.8 = (bf16[3,1,64,1280]{3,2,1,0:T(8,128)(2,1)}, bf16[3,1,64,1280]{3,2,1,0:T(8,128)(2,1)}, u32[]{:S(2)}, u32[]{:S(2)}) collective-permute-start(bf16[3,1,64,1280]{3,2,1,0:T(8,128)(2,1)} %get-tuple-element.23), channel_id=1, source_target_pairs={{0,248},{4,252},{8,240},{12,244},{16,232},{20,236},{24,224},{28,22... | collective-permute-start | bytes 1474568 | tf_op jit(solution)/shard_map/stash_2_0/ppermute | solution.py:167
  59.2 71.4 %collective-permute-start.9 = (bf16[3,1,64,1280]{3,2,1,0:T(8,128)(2,1)}, bf16[3,1,64,1280]{3,2,1,0:T(8,128)(2,1)}, u32[]{:S(2)}, u32[]{:S(2)}) collective-permute-start(bf16[3,1,64,1280]{3,2,1,0:T(8,128)(2,1)} %get-tuple-element.20), channel_id=1, source_target_pairs={{0,252},{4,248},{8,244},{12,240},{16,236},{20,232},{24,228},{28,22... | collective-permute-start | bytes 1474568 | tf_op jit(solution)/shard_map/stash_3_0/ppermute | solution.py:167
  69.5 69.3 %collective-permute-start.11 = (bf16[3,1,64,1280]{3,2,1,0:T(8,128)(2,1)}, bf16[3,1,64,1280]{3,2,1,0:T(8,128)(2,1)}, u32[]{:S(2)}, u32[]{:S(2)}) collective-permute-start(bf16[3,1,64,1280]{3,2,1,0:T(8,128)(2,1)} %collective-permute-done.10), channel_id=1, source_target_pairs={{48,208},{52,212},{56,216},{60,220},{64,160},{68,164},{72,168},{76... | collective-permute-start | bytes 1474568 | tf_op jit(solution)/shard_map/onward_0/ppermute | solution.py:167
  81.3 76.0 %collective-permute-start.1 = (bf16[3,1,64,512]{3,2,1,0:T(8,128)(2,1)S(1)}, bf16[3,1,64,512]{3,2,1,0:T(8,128)(2,1)S(1)}, u32[]{:S(2)}, u32[]{:S(2)}) collective-permute-start(bf16[3,1,64,512]{3,2,1,0:T(8,128)(2,1)S(1)} %get-tuple-element.27), channel_id=1, source_target_pairs={{0,240},{4,244},{8,248},{12,252},{16,224},{20,228},{24,232},{28,23... | collective-permute-start | bytes 589832 | tf_op jit(solution)/shard_map/stash_0_1/ppermute | solution.py:167
  130.6 27.0 %collective-permute-start.2 = (bf16[3,1,64,512]{3,2,1,0:T(8,128)(2,1)S(1)}, bf16[3,1,64,512]{3,2,1,0:T(8,128)(2,1)S(1)}, u32[]{:S(2)}, u32[]{:S(2)}) collective-permute-start(bf16[3,1,64,512]{3,2,1,0:T(8,128)(2,1)S(1)} %get-tuple-element.26), channel_id=1, source_target_pairs={{0,244},{4,240},{8,252},{12,248},{16,228},{20,224},{24,236},{28,23... | collective-permute-start | bytes 589832 | tf_op jit(solution)/shard_map/stash_1_1/ppermute | solution.py:167
  138.8 19.5 %collective-permute-start.3 = (bf16[3,1,64,512]{3,2,1,0:T(8,128)(2,1)S(1)}, bf16[3,1,64,512]{3,2,1,0:T(8,128)(2,1)S(1)}, u32[]{:S(2)}, u32[]{:S(2)}) collective-permute-start(bf16[3,1,64,512]{3,2,1,0:T(8,128)(2,1)S(1)} %get-tuple-element.25), channel_id=1, source_target_pairs={{0,248},{4,252},{8,240},{12,244},{16,232},{20,236},{24,224},{28,22... | collective-permute-start | bytes 589832 | tf_op jit(solution)/shard_map/stash_2_1/ppermute | solution.py:167
  145.2 17.9 %collective-permute-start.4 = (bf16[3,1,64,512]{3,2,1,0:T(8,128)(2,1)S(1)}, bf16[3,1,64,512]{3,2,1,0:T(8,128)(2,1)S(1)}, u32[]{:S(2)}, u32[]{:S(2)}) collective-permute-start(bf16[3,1,64,512]{3,2,1,0:T(8,128)(2,1)S(1)} %get-tuple-element.24), channel_id=1, source_target_pairs={{0,252},{4,248},{8,244},{12,240},{16,236},{20,232},{24,228},{28,22... | collective-permute-start | bytes 589832 | tf_op jit(solution)/shard_map/stash_3_1/ppermute | solution.py:167
  157.3 12.7 %collective-permute-start.12 = (bf16[3,1,64,256]{3,2,1,0:T(8,128)(2,1)S(1)}, bf16[3,1,64,256]{3,2,1,0:T(8,128)(2,1)S(1)}, u32[]{:S(2)}, u32[]{:S(2)}) collective-permute-start(bf16[3,1,64,256]{3,2,1,0:T(8,128)(2,1)S(1)} %get-tuple-element.19), channel_id=1, source_target_pairs={{0,240},{4,244},{8,248},{12,252},{16,224},{20,228},{24,232},{28,23... | collective-permute-start | bytes 294920 | tf_op jit(solution)/shard_map/stash_0_2/ppermute | solution.py:167
  157.6 12.4 %collective-permute-start.13 = (bf16[3,1,64,256]{3,2,1,0:T(8,128)(2,1)S(1)}, bf16[3,1,64,256]{3,2,1,0:T(8,128)(2,1)S(1)}, u32[]{:S(2)}, u32[]{:S(2)}) collective-permute-start(bf16[3,1,64,256]{3,2,1,0:T(8,128)(2,1)S(1)} %get-tuple-element.18), channel_id=1, source_target_pairs={{0,244},{4,240},{8,252},{12,248},{16,228},{20,224},{24,236},{28,23... | collective-permute-start | bytes 294920 | tf_op jit(solution)/shard_map/stash_1_2/ppermute | solution.py:167
  158.4 11.6 %collective-permute-start.14 = (bf16[3,1,64,256]{3,2,1,0:T(8,128)(2,1)S(1)}, bf16[3,1,64,256]{3,2,1,0:T(8,128)(2,1)S(1)}, u32[]{:S(2)}, u32[]{:S(2)}) collective-permute-start(bf16[3,1,64,256]{3,2,1,0:T(8,128)(2,1)S(1)} %get-tuple-element.17), channel_id=1, source_target_pairs={{0,248},{4,252},{8,240},{12,244},{16,232},{20,236},{24,224},{28,22... | collective-permute-start | bytes 294920 | tf_op jit(solution)/shard_map/stash_2_2/ppermute | solution.py:167
  163.0 7.8 %collective-permute-start.15 = (bf16[3,1,64,256]{3,2,1,0:T(8,128)(2,1)S(1)}, bf16[3,1,64,256]{3,2,1,0:T(8,128)(2,1)S(1)}, u32[]{:S(2)}, u32[]{:S(2)}) collective-permute-start(bf16[3,1,64,256]{3,2,1,0:T(8,128)(2,1)S(1)} %get-tuple-element.16), channel_id=1, source_target_pairs={{0,252},{4,248},{8,244},{12,240},{16,236},{20,232},{24,228},{28,22... | collective-permute-start | bytes 294920 | tf_op jit(solution)/shard_map/stash_3_2/ppermute | solution.py:167

commit v10 on v9

--- a/solution.py
+++ b/solution.py
@@ -10,8 +10,8 @@
 
 HEAD_DIM = 128
 FORWARD_STEPS = 2
-CHUNKS = ((0, 10), (12, 4), (10, 2))
-DETOUR = (0, 10)
+CHUNKS = ((0, 8), (8, 4), (12, 4))
+DETOUR = (0, 8)
 SCALE = HEAD_DIM ** (-0.5)
 EXPONENT = SCALE * math.log2(math.e)
 NT = (((1,), (1,)), ((), ()))
@@ -208,7 +208,7 @@
         forward_out = forward(fwd_qkv, fwd_segments)
     received = shifted(forward_out, 1)
     tokens = loss_tokens.astype(jnp.float32)
-    pieces[0][0], tokens = lax.optimization_barrier((pieces[0][0], tokens))
+    pieces[0][3], tokens = lax.optimization_barrier((pieces[0][3], tokens))
     token_total = lax.psum(tokens, "dp")
     factor = jnp.float32(lax.axis_size("dp") * length) / token_total
     parked, token_total = lax.optimization_barrier((parked, token_total))

time: 173 us -> 167 us (0.965)
  the two profiles are of different devices: /device:TPU:23 before, /device:TPU:1 now
where the time goes in v10:
time: 167 us
  starting transfers between devices  73.4 us (44%)
  waiting for transfers between devices  56.3 us (34%)
  Pallas kernels  19.2 us (11%)
  blocking collectives  10.1 us (6%)
  local copies, waits for them, and re-layouts  5.78 us (3%)
  between operations  2.06 us (1%)
    ppermute x14, starting transfers between devices, fetched(): return lax.ppermute(piece, AXES, pairs)  66 us
    ppermute x14, waiting for transfers between devices, fetched(): return lax.ppermute(piece, AXES, pairs)  56.3 us
    pallas_call x3, Pallas kernels, backward(): pl.pallas_call(functools.partial(backward_kernel, parts, around_from, car...  14 us
    psum x1, blocking collectives, on_device(): token_total = lax.psum(tokens, 'dp')  10.1 us
    ppermute x2, starting transfers between devices, shifted(): lax.ppermute(array, 'pipe', [(p, (p + by) % sections) for p in range(sect...  7.41 us
    dynamic_slice x3, local copies, waits for them, and re-layouts, cut(): return lax.dynamic_slice_in_dim(whole, start, heads * HEAD_DIM, axis=3)  5.78 us
    pallas_call x1, Pallas kernels, forward(): pl.pallas_call(forward_kernel, grid=(FORWARD_STEPS,), in_specs=[pl.BlockS...  5.18 us
  transfers between devices with their start and end apart: 16, of which 5 were waited for; matrix products, arithmetic and copies ran while one was open for 3% of the time, Pallas kernels for 10%

profile of v10, /device:TPU:1, one launch (start us, length us, event | category | flops | bytes accessed | tf_op | source)
XLA Modules:
  0.0 166.8 jit_solution(12244693951179810025)
XLA Ops:
  0.6 7.4 %collective-permute-start.5 = (bf16[1,256,2048]{2,1,0:T(8,128)(2,1)}, bf16[1,256,2048]{2,1,0:T(8,128)(2,1)S(1)}, u32[]{:S(2)}, u32[]{:S(2)}) collective-permute-start(bf16[1,256,2048]{2,1,0:T(8,128)(2,1)} %param.10), channel_id=1, source_target_pairs={{0,240},{16,0},{32,16},{48,32},{64,48},{80,64},{96,80},{112,96},{1... | collective-permute-start | bytes 3145736 | tf_op jit(solution)/shard_map/direct_grad/ppermute | solution.py:179
  8.0 2.4 %constant_dynamic-slice_fusion.4 = (bf16[3,1,64,1024]{3,2,1,0:T(8,128)(2,1)S(1)}, bf16[3,1,64,1024]{3,2,1,0:T(8,128)(2,1)}, bf16[3,1,64,1024]{3,2,1,0:T(8,128)(2,1)S(1)}, bf16[3,1,64,1024]{3,2,1,0:T(8,128)(2,1)}) fusion(bf16[3,1,64,8192]{3,2,1,0:T(8,128)(2,1)} %param.8, s32[]{:T(128)S(6)} %select_n.44, s32[]{:T(128)S(6)} %select_n.42, s32[]{:T(128)S(6)} %select_n.37, ...), kind=kLoop, calls=%fused_computation.4 | loop fusion | bytes 3145744 | tf_op jit(solution)/shard_map/stash_2_0/dynamic_slice | solution.py:189
  10.4 0.0 copy-start
  10.4 1.8 %collective-permute-start.9 = (bf16[3,1,64,1024]{3,2,1,0:T(8,128)(2,1)S(1)}, bf16[3,1,64,1024]{3,2,1,0:T(8,128)(2,1)S(1)}, u32[]{:S(2)}, u32[]{:S(2)}) collective-permute-start(bf16[3,1,64,1024]{3,2,1,0:T(8,128)(2,1)S(1)} %get-tuple-element.20), channel_id=1, source_target_pairs={{0,248},{4,252},{8,240},{12,244},{16,232},{20,236},{24,224},{28,22... | collective-permute-start | bytes 1179656 | tf_op jit(solution)/shard_map/stash_2_0/ppermute | solution.py:167
  12.2 4.1 %collective-permute-start = (bf16[3,1,64,1024]{3,2,1,0:T(8,128)(2,1)S(1)}, bf16[3,1,64,1024]{3,2,1,0:T(8,128)(2,1)S(1)}, u32[]{:S(2)}, u32[]{:S(2)}) collective-permute-start(bf16[3,1,64,1024]{3,2,1,0:T(8,128)(2,1)S(1)} %get-tuple-element.22), channel_id=1, source_target_pairs={{0,252},{4,248},{8,244},{12,240},{16,236},{20,232},{24,228},{28,22... | collective-permute-start | bytes 1179656 | tf_op jit(solution)/shard_map/stash_3_0/ppermute | solution.py:167
  16.3 1.4 collective-permute-start.10
  17.7 5.2 %forward_heads.1 = bf16[1,256,2048]{2,1,0:T(8,128)(2,1)} custom-call(bf16[3,1,256,2048]{3,2,1,0:T(8,128)(2,1)} %qkv_ref.1, s32[1,256]{1,0:T(1,128)} %segment_ref.1), custom_call_target="tpu_custom_call" | custom-call | flops 536870912 | bytes 4194304 | tf_op jit(solution)/shard_map/forward_heads/pallas_call | solution.py:55
  22.9 0.0 collective-permute-start.6
  22.9 40.9 %collective-permute-done.9.refs_2_ = bf16[3,1,64,1024]{3,2,1,0:T(8,128)(2,1)S(1)} collective-permute-done((bf16[3,1,64,1024]{3,2,1,0:T(8,128)(2,1)S(1)}, bf16[3,1,64,1024]{3,2,1,0:T(8,128)(2,1)S(1)}, u32[]{:S(2)}, u32[]{:S(2)}) %collective-permute-start.9) | collective-permute-done | bytes 393248 | tf_op jit(solution)/shard_map/stash_2_0/ppermute | solution.py:167
  63.8 7.6 %collective-permute-start.8 = (bf16[3,1,64,1024]{3,2,1,0:T(8,128)(2,1)}, bf16[3,1,64,1024]{3,2,1,0:T(8,128)(2,1)S(1)}, u32[]{:S(2)}, u32[]{:S(2)}) collective-permute-start(bf16[3,1,64,1024]{3,2,1,0:T(8,128)(2,1)} %get-tuple-element.23), channel_id=1, source_target_pairs={{0,244},{4,240},{8,252},{12,248},{16,228},{20,224},{24,236},{28,23... | collective-permute-start | bytes 1179656 | tf_op jit(solution)/shard_map/stash_1_0/ppermute | solution.py:167
  71.4 0.9 collective-permute-done.refs_3_
  72.3 9.2 %collective-permute-start.7 = (bf16[3,1,64,1024]{3,2,1,0:T(8,128)(2,1)}, bf16[3,1,64,1024]{3,2,1,0:T(8,128)(2,1)}, u32[]{:S(2)}, u32[]{:S(2)}) collective-permute-start(bf16[3,1,64,1024]{3,2,1,0:T(8,128)(2,1)} %get-tuple-element.21), channel_id=1, source_target_pairs={{0,240},{4,244},{8,248},{12,252},{16,224},{20,228},{24,232},{28,23... | collective-permute-start | bytes 1179656 | tf_op jit(solution)/shard_map/stash_0_0/ppermute | solution.py:167
  81.4 0.0 collective-permute-done.10
  81.4 1.4 collective-permute-start.11
  83.5 10.1 %psum.7 = f32[1]{0:T(128)} all-reduce(f32[1]{0:T(128)S(6)} %convert_element_type.3), channel_id=1, replica_groups=mesh['pipe'=16,'tensor'=4,'dp'=4] {'dp'}, use_global_device_ids=true, to_apply=%region_0.0 | all-reduce | flops 1 | bytes 8 | tf_op jit(solution)/shard_map/psum | solution.py:212
  93.6 2.2 %constant_dynamic-slice_fusion.7 = (bf16[3,1,64,512]{3,2,1,0:T(8,128)(2,1)}, bf16[3,1,64,512]{3,2,1,0:T(8,128)(2,1)}, bf16[3,1,64,512]{3,2,1,0:T(8,128)(2,1)}, bf16[3,1,64,512]{3,2,1,0:T(8,128)(2,1)}) fusion(bf16[3,1,64,8192]{3,2,1,0:T(8,128)(2,1)} %param.8, s32[]{:T(128)S(6)} %select_n.41, s32[]{:T(128)S(6)} %select_n.40, s32[]{:T(128)S(6)} %select_n.39, ...), kind=kLoop, calls=%fused_computation.7 | loop fusion | bytes 1572880 | tf_op jit(solution)/shard_map/stash_3_1/dynamic_slice | solution.py:189
  95.8 0.0 collective-permute-done.8.refs_1_
  95.8 1.6 collective-permute-start.4
  97.4 0.0 collective-permute-done.7.refs_0_
  97.4 2.6 %collective-permute-start.3 = (bf16[3,1,64,512]{3,2,1,0:T(8,128)(2,1)}, bf16[3,1,64,512]{3,2,1,0:T(8,128)(2,1)}, u32[]{:S(2)}, u32[]{:S(2)}) collective-permute-start(bf16[3,1,64,512]{3,2,1,0:T(8,128)(2,1)} %get-tuple-element.25), channel_id=1, source_target_pairs={{0,248},{4,252},{8,240},{12,244},{16,232},{20,236},{24,224},{28,22... | collective-permute-start | bytes 589832 | tf_op jit(solution)/shard_map/stash_2_1/ppermute | solution.py:167
  100.0 0.0 collective-permute-done.11.refs_4_
  100.0 0.0 collective-permute-start.2
  100.0 0.0 collective-permute-done.5.refs_5_.refs_4_
  100.0 4.7 %collective-permute-start.1 = (bf16[3,1,64,512]{3,2,1,0:T(8,128)(2,1)}, bf16[3,1,64,512]{3,2,1,0:T(8,128)(2,1)}, u32[]{:S(2)}, u32[]{:S(2)}) collective-permute-start(bf16[3,1,64,512]{3,2,1,0:T(8,128)(2,1)} %get-tuple-element.27), channel_id=1, source_target_pairs={{0,240},{4,244},{8,248},{12,252},{16,224},{20,228},{24,232},{28,23... | collective-permute-start | bytes 589832 | tf_op jit(solution)/shard_map/stash_0_1/ppermute | solution.py:167
  105.4 0.0 copy-done
  105.4 6.3 %shard_map.77.refs_8_ = bf16[3,1,256,2048]{3,2,1,0:T(8,128)(2,1)} custom-call(bf16[3,1,64,1024]{3,2,1,0:T(8,128)(2,1)} %collective-permute-done.7.refs_0_, bf16[3,1,64,1024]{3,2,1,0:T(8,128)(2,1)S(1)} %collective-permute-done.8.refs_1_, bf16[3,1,64,1024]{3,2,1,0:T(8,128)(2,1)S(1)} %collective-permute-done.9.refs_2_, ...), custom_call_target="tpu_custom_call" | custom-call | flops 671088640 | bytes 3670016 | tf_op jit(solution)/shard_map/pallas_call | solution.py:138
  111.8 1.3 constant_dynamic-slice_fusion
  113.0 6.5 %collective-permute-done.4.refs_3_ = bf16[3,1,64,512]{3,2,1,0:T(8,128)(2,1)S(1)} collective-permute-done((bf16[3,1,64,512]{3,2,1,0:T(8,128)(2,1)}, bf16[3,1,64,512]{3,2,1,0:T(8,128)(2,1)S(1)}, u32[]{:S(2)}, u32[]{:S(2)}) %collective-permute-start.4) | collective-permute-done | bytes 196640 | tf_op jit(solution)/shard_map/stash_3_1/ppermute | solution.py:167
  119.5 20.5 %collective-permute-start.15 = (bf16[3,1,64,512]{3,2,1,0:T(8,128)(2,1)S(1)}, bf16[3,1,64,512]{3,2,1,0:T(8,128)(2,1)S(1)}, u32[]{:S(2)}, u32[]{:S(2)}) collective-permute-start(bf16[3,1,64,512]{3,2,1,0:T(8,128)(2,1)S(1)} %get-tuple-element.16), channel_id=1, source_target_pairs={{0,252},{4,248},{8,244},{12,240},{16,236},{20,232},{24,228},{28,22... | collective-permute-start | bytes 589832 | tf_op jit(solution)/shard_map/stash_3_2/ppermute | solution.py:167
  140.0 0.0 collective-permute-done.3.refs_2_
  140.0 3.9 %collective-permute-start.14 = (bf16[3,1,64,512]{3,2,1,0:T(8,128)(2,1)S(1)}, bf16[3,1,64,512]{3,2,1,0:T(8,128)(2,1)S(1)}, u32[]{:S(2)}, u32[]{:S(2)}) collective-permute-start(bf16[3,1,64,512]{3,2,1,0:T(8,128)(2,1)S(1)} %get-tuple-element.17), channel_id=1, source_target_pairs={{0,248},{4,252},{8,240},{12,244},{16,232},{20,236},{24,224},{28,22... | collective-permute-start | bytes 589832 | tf_op jit(solution)/shard_map/stash_2_2/ppermute | solution.py:167
  143.9 0.0 collective-permute-done.2.refs_1_
  143.9 3.4 %collective-permute-start.13 = (bf16[3,1,64,512]{3,2,1,0:T(8,128)(2,1)S(1)}, bf16[3,1,64,512]{3,2,1,0:T(8,128)(2,1)S(1)}, u32[]{:S(2)}, u32[]{:S(2)}) collective-permute-start(bf16[3,1,64,512]{3,2,1,0:T(8,128)(2,1)S(1)} %get-tuple-element.18), channel_id=1, source_target_pairs={{0,244},{4,240},{8,252},{12,248},{16,228},{20,224},{24,236},{28,23... | collective-permute-start | bytes 589832 | tf_op jit(solution)/shard_map/stash_1_2/ppermute | solution.py:167
  147.3 0.0 collective-permute-done.1.refs_0_
  147.3 3.8 %collective-permute-start.12 = (bf16[3,1,64,512]{3,2,1,0:T(8,128)(2,1)S(1)}, bf16[3,1,64,512]{3,2,1,0:T(8,128)(2,1)S(1)}, u32[]{:S(2)}, u32[]{:S(2)}) collective-permute-start(bf16[3,1,64,512]{3,2,1,0:T(8,128)(2,1)S(1)} %get-tuple-element.19), channel_id=1, source_target_pairs={{0,240},{4,244},{8,248},{12,252},{16,224},{20,228},{24,232},{28,23... | collective-permute-start | bytes 589832 | tf_op jit(solution)/shard_map/stash_0_2/ppermute | solution.py:167
  151.1 0.0 collective-permute-done.6.refs_7_
  151.1 4.6 %shard_map.78 = (bf16[3,1,256,2048]{3,2,1,0:T(8,128)(2,1)}, bf16[1,256,2048]{2,1,0:T(8,128)(2,1)}) custom-call(bf16[3,1,64,512]{3,2,1,0:T(8,128)(2,1)} %collective-permute-done.1.refs_0_, bf16[3,1,64,512]{3,2,1,0:T(8,128)(2,1)} %collective-permute-done.2.refs_1_, ...), custom_call_target="tpu_custom_call", output_to_operand_aliasing={{0}: (8, {})} | custom-call | flops 335544320 | bytes 1835008 | tf_op jit(solution)/shard_map/pallas_call | solution.py:138
  155.7 0.0 collective-permute-done.15.refs_3_
  155.7 0.0 collective-permute-done.14.refs_2_
  155.7 3.7 %collective-permute-done.13.refs_1_ = bf16[3,1,64,512]{3,2,1,0:T(8,128)(2,1)S(1)} collective-permute-done((bf16[3,1,64,512]{3,2,1,0:T(8,128)(2,1)S(1)}, bf16[3,1,64,512]{3,2,1,0:T(8,128)(2,1)S(1)}, u32[]{:S(2)}, u32[]{:S(2)}) %collective-permute-start.13) | collective-permute-done | bytes 196640 | tf_op jit(solution)/shard_map/stash_1_2/ppermute | solution.py:167
  159.5 4.2 %collective-permute-done.12.refs_0_ = bf16[3,1,64,512]{3,2,1,0:T(8,128)(2,1)S(1)} collective-permute-done((bf16[3,1,64,512]{3,2,1,0:T(8,128)(2,1)S(1)}, bf16[3,1,64,512]{3,2,1,0:T(8,128)(2,1)S(1)}, u32[]{:S(2)}, u32[]{:S(2)}) %collective-permute-start.12) | collective-permute-done | bytes 196640 | tf_op jit(solution)/shard_map/stash_0_2/ppermute | solution.py:167
  163.7 3.1 %shard_map.79 = bf16[3,1,256,2048]{3,2,1,0:T(8,128)(2,1)} custom-call(bf16[3,1,64,512]{3,2,1,0:T(8,128)(2,1)S(1)} %collective-permute-done.12.refs_0_, bf16[3,1,64,512]{3,2,1,0:T(8,128)(2,1)S(1)} %collective-permute-done.13.refs_1_, bf16[3,1,64,512]{3,2,1,0:T(8,128)(2,1)S(1)} %collective-permute-done.14.refs_2_, ...), custom_call_target="tpu_custom_call", output_to_operand_aliasing={{}: (7, {})} | custom-call | flops 335544320 | bytes 1835008 | tf_op jit(solution)/shard_map/pallas_call | solution.py:138
Async XLA Ops:
  0.6 99.4 %collective-permute-start.5 = (bf16[1,256,2048]{2,1,0:T(8,128)(2,1)}, bf16[1,256,2048]{2,1,0:T(8,128)(2,1)S(1)}, u32[]{:S(2)}, u32[]{:S(2)}) collective-permute-start(bf16[1,256,2048]{2,1,0:T(8,128)(2,1)} %param.10), channel_id=1, source_target_pairs={{0,240},{16,0},{32,16},{48,32},{64,48},{80,64},{96,80},{112,96},{1... | collective-permute-start | bytes 3145736 | tf_op jit(solution)/shard_map/direct_grad/ppermute | solution.py:179
  10.4 95.0 %copy-start = (s32[1,256]{1,0:T(1,128)S(1)}, s32[1,256]{1,0:T(1,128)}, u32[]{:S(2)}) copy-start(s32[1,256]{1,0:T(1,128)} %refs_5_.3) | copy-start | bytes 3076
  10.4 53.4 %collective-permute-start.9 = (bf16[3,1,64,1024]{3,2,1,0:T(8,128)(2,1)S(1)}, bf16[3,1,64,1024]{3,2,1,0:T(8,128)(2,1)S(1)}, u32[]{:S(2)}, u32[]{:S(2)}) collective-permute-start(bf16[3,1,64,1024]{3,2,1,0:T(8,128)(2,1)S(1)} %get-tuple-element.20), channel_id=1, source_target_pairs={{0,248},{4,252},{8,240},{12,244},{16,232},{20,236},{24,224},{28,22... | collective-permute-start | bytes 1179656 | tf_op jit(solution)/shard_map/stash_2_0/ppermute | solution.py:167
  12.2 60.0 %collective-permute-start = (bf16[3,1,64,1024]{3,2,1,0:T(8,128)(2,1)S(1)}, bf16[3,1,64,1024]{3,2,1,0:T(8,128)(2,1)S(1)}, u32[]{:S(2)}, u32[]{:S(2)}) collective-permute-start(bf16[3,1,64,1024]{3,2,1,0:T(8,128)(2,1)S(1)} %get-tuple-element.22), channel_id=1, source_target_pairs={{0,252},{4,248},{8,244},{12,240},{16,236},{20,232},{24,228},{28,22... | collective-permute-start | bytes 1179656 | tf_op jit(solution)/shard_map/stash_3_0/ppermute | solution.py:167
  16.3 65.1 %collective-permute-start.10 = (bf16[3,1,64,1024]{3,2,1,0:T(8,128)(2,1)}, bf16[3,1,64,1024]{3,2,1,0:T(8,128)(2,1)}, u32[]{:S(2)}, u32[]{:S(2)}) collective-permute-start(bf16[3,1,64,1024]{3,2,1,0:T(8,128)(2,1)} %get-tuple-element.21), channel_id=1, source_target_pairs={{32,48},{36,52},{40,56},{44,60},{80,64},{84,68},{88,72},{92,76},{1... | collective-permute-start | bytes 1179656 | tf_op jit(solution)/shard_map/aside_0/ppermute | solution.py:167
  22.9 128.2 %collective-permute-start.6 = (bf16[1,256,2048]{2,1,0:T(8,128)(2,1)}, bf16[1,256,2048]{2,1,0:T(8,128)(2,1)S(1)}, u32[]{:S(2)}, u32[]{:S(2)}) collective-permute-start(bf16[1,256,2048]{2,1,0:T(8,128)(2,1)} %forward_heads.1), channel_id=1, source_target_pairs={{0,16},{16,32},{32,48},{48,64},{64,80},{80,96},{96,112},{112,128},... | collective-permute-start | bytes 3145736 | tf_op jit(solution)/shard_map/direct_out/ppermute | solution.py:179
  63.8 31.9 %collective-permute-start.8 = (bf16[3,1,64,1024]{3,2,1,0:T(8,128)(2,1)}, bf16[3,1,64,1024]{3,2,1,0:T(8,128)(2,1)S(1)}, u32[]{:S(2)}, u32[]{:S(2)}) collective-permute-start(bf16[3,1,64,1024]{3,2,1,0:T(8,128)(2,1)} %get-tuple-element.23), channel_id=1, source_target_pairs={{0,244},{4,240},{8,252},{12,248},{16,228},{20,224},{24,236},{28,23... | collective-permute-start | bytes 1179656 | tf_op jit(solution)/shard_map/stash_1_0/ppermute | solution.py:167
  72.3 25.2 %collective-permute-start.7 = (bf16[3,1,64,1024]{3,2,1,0:T(8,128)(2,1)}, bf16[3,1,64,1024]{3,2,1,0:T(8,128)(2,1)}, u32[]{:S(2)}, u32[]{:S(2)}) collective-permute-start(bf16[3,1,64,1024]{3,2,1,0:T(8,128)(2,1)} %get-tuple-element.21), channel_id=1, source_target_pairs={{0,240},{4,244},{8,248},{12,252},{16,224},{20,228},{24,232},{28,23... | collective-permute-start | bytes 1179656 | tf_op jit(solution)/shard_map/stash_0_0/ppermute | solution.py:167
  81.4 18.6 %collective-permute-start.11 = (bf16[3,1,64,1024]{3,2,1,0:T(8,128)(2,1)}, bf16[3,1,64,1024]{3,2,1,0:T(8,128)(2,1)}, u32[]{:S(2)}, u32[]{:S(2)}) collective-permute-start(bf16[3,1,64,1024]{3,2,1,0:T(8,128)(2,1)} %collective-permute-done.10), channel_id=1, source_target_pairs={{48,208},{52,212},{56,216},{60,220},{64,160},{68,164},{72,168},{76... | collective-permute-start | bytes 1179656 | tf_op jit(solution)/shard_map/onward_0/ppermute | solution.py:167
  95.8 23.7 %collective-permute-start.4 = (bf16[3,1,64,512]{3,2,1,0:T(8,128)(2,1)}, bf16[3,1,64,512]{3,2,1,0:T(8,128)(2,1)S(1)}, u32[]{:S(2)}, u32[]{:S(2)}) collective-permute-start(bf16[3,1,64,512]{3,2,1,0:T(8,128)(2,1)} %get-tuple-element.24), channel_id=1, source_target_pairs={{0,252},{4,248},{8,244},{12,240},{16,236},{20,232},{24,228},{28,22... | collective-permute-start | bytes 589832 | tf_op jit(solution)/shard_map/stash_3_1/ppermute | solution.py:167
  97.4 42.6 %collective-permute-start.3 = (bf16[3,1,64,512]{3,2,1,0:T(8,128)(2,1)}, bf16[3,1,64,512]{3,2,1,0:T(8,128)(2,1)}, u32[]{:S(2)}, u32[]{:S(2)}) collective-permute-start(bf16[3,1,64,512]{3,2,1,0:T(8,128)(2,1)} %get-tuple-element.25), channel_id=1, source_target_pairs={{0,248},{4,252},{8,240},{12,244},{16,232},{20,236},{24,224},{28,22... | collective-permute-start | bytes 589832 | tf_op jit(solution)/shard_map/stash_2_1/ppermute | solution.py:167
  100.0 43.8 %collective-permute-start.2 = (bf16[3,1,64,512]{3,2,1,0:T(8,128)(2,1)}, bf16[3,1,64,512]{3,2,1,0:T(8,128)(2,1)}, u32[]{:S(2)}, u32[]{:S(2)}) collective-permute-start(bf16[3,1,64,512]{3,2,1,0:T(8,128)(2,1)} %get-tuple-element.26), channel_id=1, source_target_pairs={{0,244},{4,240},{8,252},{12,248},{16,228},{20,224},{24,236},{28,23... | collective-permute-start | bytes 589832 | tf_op jit(solution)/shard_map/stash_1_1/ppermute | solution.py:167
  100.0 47.3 %collective-permute-start.1 = (bf16[3,1,64,512]{3,2,1,0:T(8,128)(2,1)}, bf16[3,1,64,512]{3,2,1,0:T(8,128)(2,1)}, u32[]{:S(2)}, u32[]{:S(2)}) collective-permute-start(bf16[3,1,64,512]{3,2,1,0:T(8,128)(2,1)} %get-tuple-element.27), channel_id=1, source_target_pairs={{0,240},{4,244},{8,248},{12,252},{16,224},{20,228},{24,232},{28,23... | collective-permute-start | bytes 589832 | tf_op jit(solution)/shard_map/stash_0_1/ppermute | solution.py:167
  119.5 36.2 %collective-permute-start.15 = (bf16[3,1,64,512]{3,2,1,0:T(8,128)(2,1)S(1)}, bf16[3,1,64,512]{3,2,1,0:T(8,128)(2,1)S(1)}, u32[]{:S(2)}, u32[]{:S(2)}) collective-permute-start(bf16[3,1,64,512]{3,2,1,0:T(8,128)(2,1)S(1)} %get-tuple-element.16), channel_id=1, source_target_pairs={{0,252},{4,248},{8,244},{12,240},{16,236},{20,232},{24,228},{28,22... | collective-permute-start | bytes 589832 | tf_op jit(solution)/shard_map/stash_3_2/ppermute | solution.py:167
  140.0 15.7 %collective-permute-start.14 = (bf16[3,1,64,512]{3,2,1,0:T(8,128)(2,1)S(1)}, bf16[3,1,64,512]{3,2,1,0:T(8,128)(2,1)S(1)}, u32[]{:S(2)}, u32[]{:S(2)}) collective-permute-start(bf16[3,1,64,512]{3,2,1,0:T(8,128)(2,1)S(1)} %get-tuple-element.17), channel_id=1, source_target_pairs={{0,248},{4,252},{8,240},{12,244},{16,232},{20,236},{24,224},{28,22... | collective-permute-start | bytes 589832 | tf_op jit(solution)/shard_map/stash_2_2/ppermute | solution.py:167
  143.9 15.6 %collective-permute-start.13 = (bf16[3,1,64,512]{3,2,1,0:T(8,128)(2,1)S(1)}, bf16[3,1,64,512]{3,2,1,0:T(8,128)(2,1)S(1)}, u32[]{:S(2)}, u32[]{:S(2)}) collective-permute-start(bf16[3,1,64,512]{3,2,1,0:T(8,128)(2,1)S(1)} %get-tuple-element.18), channel_id=1, source_target_pairs={{0,244},{4,240},{8,252},{12,248},{16,228},{20,224},{24,236},{28,23... | collective-permute-start | bytes 589832 | tf_op jit(solution)/shard_map/stash_1_2/ppermute | solution.py:167
  147.3 16.4 %collective-permute-start.12 = (bf16[3,1,64,512]{3,2,1,0:T(8,128)(2,1)S(1)}, bf16[3,1,64,512]{3,2,1,0:T(8,128)(2,1)S(1)}, u32[]{:S(2)}, u32[]{:S(2)}) collective-permute-start(bf16[3,1,64,512]{3,2,1,0:T(8,128)(2,1)S(1)} %get-tuple-element.19), channel_id=1, source_target_pairs={{0,240},{4,244},{8,248},{12,252},{16,224},{20,228},{24,232},{28,23... | collective-permute-start | bytes 589832 | tf_op jit(solution)/shard_map/stash_0_2/ppermute | solution.py:167

commit v11 on v9

--- a/solution.py
+++ b/solution.py
@@ -208,7 +208,7 @@
         forward_out = forward(fwd_qkv, fwd_segments)
     received = shifted(forward_out, 1)
     tokens = loss_tokens.astype(jnp.float32)
-    pieces[0][0], tokens = lax.optimization_barrier((pieces[0][0], tokens))
+    pieces[0][3], tokens = lax.optimization_barrier((pieces[0][3], tokens))
     token_total = lax.psum(tokens, "dp")
     factor = jnp.float32(lax.axis_size("dp") * length) / token_total
     parked, token_total = lax.optimization_barrier((parked, token_total))

time: 173 us -> 164 us (0.948)
  the two profiles are of different devices: /device:TPU:23 before, /device:TPU:1 now
where the time goes in v11:
time: 164 us
  waiting for transfers between devices  91.5 us (56%)
  starting transfers between devices  36.8 us (22%)
  Pallas kernels  18.3 us (11%)
  blocking collectives  10 us (6%)
  local copies, waits for them, and re-layouts  4.94 us (3%)
  between operations  1.97 us (1%)
    ppermute x14, waiting for transfers between devices, fetched(): return lax.ppermute(piece, AXES, pairs)  91.5 us
    ppermute x14, starting transfers between devices, fetched(): return lax.ppermute(piece, AXES, pairs)  29.4 us
    pallas_call x3, Pallas kernels, backward(): pl.pallas_call(functools.partial(backward_kernel, parts, around_from, car...  13.1 us
    psum x1, blocking collectives, on_device(): token_total = lax.psum(tokens, 'dp')  10 us
    ppermute x2, starting transfers between devices, shifted(): lax.ppermute(array, 'pipe', [(p, (p + by) % sections) for p in range(sect...  7.41 us
    pallas_call x1, Pallas kernels, forward(): pl.pallas_call(forward_kernel, grid=(FORWARD_STEPS,), in_specs=[pl.BlockS...  5.19 us
    dynamic_slice x3, local copies, waits for them, and re-layouts, cut(): return lax.dynamic_slice_in_dim(whole, start, heads * HEAD_DIM, axis=3)  4.93 us
  transfers between devices with their start and end apart: 16, of which 8 were waited for; matrix products, arithmetic and copies ran while one was open for 3% of the time, Pallas kernels for 10%

profile of v11, /device:TPU:1, one launch (start us, length us, event | category | flops | bytes accessed | tf_op | source)
XLA Modules:
  0.0 163.6 jit_solution(4933392890430799046)
XLA Ops:
  0.6 7.4 %collective-permute-start.5 = (bf16[1,256,2048]{2,1,0:T(8,128)(2,1)}, bf16[1,256,2048]{2,1,0:T(8,128)(2,1)S(1)}, u32[]{:S(2)}, u32[]{:S(2)}) collective-permute-start(bf16[1,256,2048]{2,1,0:T(8,128)(2,1)} %param.10), channel_id=1, source_target_pairs={{0,240},{16,0},{32,16},{48,32},{64,48},{80,64},{96,80},{112,96},{1... | collective-permute-start | bytes 3145736 | tf_op jit(solution)/shard_map/direct_grad/ppermute | solution.py:179
  8.0 2.6 %constant_dynamic-slice_fusion.4 = (bf16[3,1,64,1280]{3,2,1,0:T(8,128)(2,1)}, bf16[3,1,64,1280]{3,2,1,0:T(8,128)(2,1)S(1)}, bf16[3,1,64,1280]{3,2,1,0:T(8,128)(2,1)S(1)}, bf16[3,1,64,1280]{3,2,1,0:T(8,128)(2,1)}) fusion(bf16[3,1,64,8192]{3,2,1,0:T(8,128)(2,1)} %param.8, s32[]{:T(128)S(6)} %select_n.44, s32[]{:T(128)S(6)} %select_n.42, s32[]{:T(128)S(6)} %select_n.37, ...), kind=kLoop, calls=%fused_computation.4 | loop fusion | bytes 3932176 | tf_op jit(solution)/shard_map/stash_2_0/dynamic_slice | solution.py:189
  10.6 0.0 copy-start
  10.6 2.7 %collective-permute-start = (bf16[3,1,64,1280]{3,2,1,0:T(8,128)(2,1)S(1)}, bf16[3,1,64,1280]{3,2,1,0:T(8,128)(2,1)S(1)}, u32[]{:S(2)}, u32[]{:S(2)}) collective-permute-start(bf16[3,1,64,1280]{3,2,1,0:T(8,128)(2,1)S(1)} %get-tuple-element.22), channel_id=1, source_target_pairs={{0,252},{4,248},{8,244},{12,240},{16,236},{20,232},{24,228},{28,22... | collective-permute-start | bytes 1474568 | tf_op jit(solution)/shard_map/stash_3_0/ppermute | solution.py:167
  13.3 1.4 collective-permute-start.10
  14.7 4.3 %collective-permute-start.7 = (bf16[3,1,64,1280]{3,2,1,0:T(8,128)(2,1)S(1)}, bf16[3,1,64,1280]{3,2,1,0:T(8,128)(2,1)S(1)}, u32[]{:S(2)}, u32[]{:S(2)}) collective-permute-start(bf16[3,1,64,1280]{3,2,1,0:T(8,128)(2,1)S(1)} %get-tuple-element.21), channel_id=1, source_target_pairs={{0,240},{4,244},{8,248},{12,252},{16,224},{20,228},{24,232},{28,23... | collective-permute-start | bytes 1474568 | tf_op jit(solution)/shard_map/stash_0_0/ppermute | solution.py:167
  19.1 5.2 %forward_heads.1 = bf16[1,256,2048]{2,1,0:T(8,128)(2,1)} custom-call(bf16[3,1,256,2048]{3,2,1,0:T(8,128)(2,1)} %qkv_ref.1, s32[1,256]{1,0:T(1,128)} %segment_ref.1), custom_call_target="tpu_custom_call" | custom-call | flops 536870912 | bytes 4194304 | tf_op jit(solution)/shard_map/forward_heads/pallas_call | solution.py:55
  24.2 0.0 collective-permute-start.6
  24.3 37.5 %collective-permute-done.refs_3_ = bf16[3,1,64,1280]{3,2,1,0:T(8,128)(2,1)S(1)} collective-permute-done((bf16[3,1,64,1280]{3,2,1,0:T(8,128)(2,1)S(1)}, bf16[3,1,64,1280]{3,2,1,0:T(8,128)(2,1)S(1)}, u32[]{:S(2)}, u32[]{:S(2)}) %collective-permute-start) | collective-permute-done | bytes 491552 | tf_op jit(solution)/shard_map/stash_3_0/ppermute | solution.py:167
  61.7 5.3 %collective-permute-start.8 = (bf16[3,1,64,1280]{3,2,1,0:T(8,128)(2,1)}, bf16[3,1,64,1280]{3,2,1,0:T(8,128)(2,1)}, u32[]{:S(2)}, u32[]{:S(2)}) collective-permute-start(bf16[3,1,64,1280]{3,2,1,0:T(8,128)(2,1)} %get-tuple-element.23), channel_id=1, source_target_pairs={{0,244},{4,240},{8,252},{12,248},{16,228},{20,224},{24,236},{28,23... | collective-permute-start | bytes 1474568 | tf_op jit(solution)/shard_map/stash_1_0/ppermute | solution.py:167
  67.0 0.0 collective-permute-done.10
  67.0 2.2 %collective-permute-start.9 = (bf16[3,1,64,1280]{3,2,1,0:T(8,128)(2,1)}, bf16[3,1,64,1280]{3,2,1,0:T(8,128)(2,1)}, u32[]{:S(2)}, u32[]{:S(2)}) collective-permute-start(bf16[3,1,64,1280]{3,2,1,0:T(8,128)(2,1)} %get-tuple-element.20), channel_id=1, source_target_pairs={{0,248},{4,252},{8,240},{12,244},{16,232},{20,236},{24,224},{28,22... | collective-permute-start | bytes 1474568 | tf_op jit(solution)/shard_map/stash_2_0/ppermute | solution.py:167
  69.2 3.0 %collective-permute-done.7.refs_0_ = bf16[3,1,64,1280]{3,2,1,0:T(8,128)(2,1)S(1)} collective-permute-done((bf16[3,1,64,1280]{3,2,1,0:T(8,128)(2,1)S(1)}, bf16[3,1,64,1280]{3,2,1,0:T(8,128)(2,1)S(1)}, u32[]{:S(2)}, u32[]{:S(2)}) %collective-permute-start.7) | collective-permute-done | bytes 491552 | tf_op jit(solution)/shard_map/stash_0_0/ppermute | solution.py:167
  72.3 1.5 collective-permute-start.11
  74.4 10.0 %psum.7 = f32[1]{0:T(128)} all-reduce(f32[1]{0:T(128)S(6)} %convert_element_type.3), channel_id=1, replica_groups=mesh['pipe'=16,'tensor'=4,'dp'=4] {'dp'}, use_global_device_ids=true, to_apply=%region_0.0 | all-reduce | flops 1 | bytes 8 | tf_op jit(solution)/shard_map/psum | solution.py:212
  85.1 1.3 constant_dynamic-slice_fusion.7
  86.3 12.9 %collective-permute-done.8.refs_1_ = bf16[3,1,64,1280]{3,2,1,0:T(8,128)(2,1)} collective-permute-done((bf16[3,1,64,1280]{3,2,1,0:T(8,128)(2,1)}, bf16[3,1,64,1280]{3,2,1,0:T(8,128)(2,1)}, u32[]{:S(2)}, u32[]{:S(2)}) %collective-permute-start.8) | collective-permute-done | bytes 491552 | tf_op jit(solution)/shard_map/stash_1_0/ppermute | solution.py:167
  99.2 0.0 collective-permute-start.1
  99.2 26.0 %collective-permute-done.9.refs_2_ = bf16[3,1,64,1280]{3,2,1,0:T(8,128)(2,1)} collective-permute-done((bf16[3,1,64,1280]{3,2,1,0:T(8,128)(2,1)}, bf16[3,1,64,1280]{3,2,1,0:T(8,128)(2,1)}, u32[]{:S(2)}, u32[]{:S(2)}) %collective-permute-start.9) | collective-permute-done | bytes 491552 | tf_op jit(solution)/shard_map/stash_2_0/ppermute | solution.py:167
  125.2 1.0 collective-permute-start.2
  126.2 0.0 collective-permute-done.11.refs_4_
  126.2 4.9 %collective-permute-start.3 = (bf16[3,1,64,512]{3,2,1,0:T(8,128)(2,1)S(1)}, bf16[3,1,64,512]{3,2,1,0:T(8,128)(2,1)S(1)}, u32[]{:S(2)}, u32[]{:S(2)}) collective-permute-start(bf16[3,1,64,512]{3,2,1,0:T(8,128)(2,1)S(1)} %get-tuple-element.25), channel_id=1, source_target_pairs={{0,248},{4,252},{8,240},{12,244},{16,232},{20,236},{24,224},{28,22... | collective-permute-start | bytes 589832 | tf_op jit(solution)/shard_map/stash_2_1/ppermute | solution.py:167
  131.1 0.0 collective-permute-done.5.refs_5_.refs_4_
  131.1 0.1 collective-permute-start.4
  131.1 0.0 copy-done
  131.2 7.6 %shard_map.77.refs_8_ = bf16[3,1,256,2048]{3,2,1,0:T(8,128)(2,1)} custom-call(bf16[3,1,64,1280]{3,2,1,0:T(8,128)(2,1)S(1)} %collective-permute-done.7.refs_0_, bf16[3,1,64,1280]{3,2,1,0:T(8,128)(2,1)} %collective-permute-done.8.refs_1_, bf16[3,1,64,1280]{3,2,1,0:T(8,128)(2,1)} %collective-permute-done.9.refs_2_, ...), custom_call_target="tpu_custom_call" | custom-call | flops 838860800 | bytes 4587520 | tf_op jit(solution)/shard_map/pallas_call | solution.py:138
  138.7 1.1 constant_dynamic-slice_fusion
  139.8 0.0 collective-permute-done.1.refs_0_
  139.8 2.0 %collective-permute-start.12 = (bf16[3,1,64,256]{3,2,1,0:T(8,128)(2,1)S(1)}, bf16[3,1,64,256]{3,2,1,0:T(8,128)(2,1)S(1)}, u32[]{:S(2)}, u32[]{:S(2)}) collective-permute-start(bf16[3,1,64,256]{3,2,1,0:T(8,128)(2,1)S(1)} %get-tuple-element.19), channel_id=1, source_target_pairs={{0,240},{4,244},{8,248},{12,252},{16,224},{20,228},{24,232},{28,23... | collective-permute-start | bytes 294920 | tf_op jit(solution)/shard_map/stash_0_2/ppermute | solution.py:167
  141.8 0.0 collective-permute-done.2.refs_1_
  141.8 2.4 %collective-permute-start.13 = (bf16[3,1,64,256]{3,2,1,0:T(8,128)(2,1)S(1)}, bf16[3,1,64,256]{3,2,1,0:T(8,128)(2,1)S(1)}, u32[]{:S(2)}, u32[]{:S(2)}) collective-permute-start(bf16[3,1,64,256]{3,2,1,0:T(8,128)(2,1)S(1)} %get-tuple-element.18), channel_id=1, source_target_pairs={{0,244},{4,240},{8,252},{12,248},{16,228},{20,224},{24,236},{28,23... | collective-permute-start | bytes 294920 | tf_op jit(solution)/shard_map/stash_1_2/ppermute | solution.py:167
  144.3 4.6 %collective-permute-done.3.refs_2_ = bf16[3,1,64,512]{3,2,1,0:T(8,128)(2,1)S(1)} collective-permute-done((bf16[3,1,64,512]{3,2,1,0:T(8,128)(2,1)S(1)}, bf16[3,1,64,512]{3,2,1,0:T(8,128)(2,1)S(1)}, u32[]{:S(2)}, u32[]{:S(2)}) %collective-permute-start.3) | collective-permute-done | bytes 196640 | tf_op jit(solution)/shard_map/stash_2_1/ppermute | solution.py:167
  148.8 0.1 collective-permute-start.14
  149.0 4.4 %collective-permute-done.4.refs_3_ = bf16[3,1,64,512]{3,2,1,0:T(8,128)(2,1)S(1)} collective-permute-done((bf16[3,1,64,512]{3,2,1,0:T(8,128)(2,1)S(1)}, bf16[3,1,64,512]{3,2,1,0:T(8,128)(2,1)S(1)}, u32[]{:S(2)}, u32[]{:S(2)}) %collective-permute-start.4) | collective-permute-done | bytes 196640 | tf_op jit(solution)/shard_map/stash_3_1/ppermute | solution.py:167
  153.4 1.4 collective-permute-start.15
  154.8 0.0 collective-permute-done.6.refs_7_
  154.8 3.5 %shard_map.78 = (bf16[3,1,256,2048]{3,2,1,0:T(8,128)(2,1)}, bf16[1,256,2048]{2,1,0:T(8,128)(2,1)}) custom-call(bf16[3,1,64,512]{3,2,1,0:T(8,128)(2,1)S(1)} %collective-permute-done.1.refs_0_, bf16[3,1,64,512]{3,2,1,0:T(8,128)(2,1)S(1)} %collective-permute-done.2.refs_1_, ...), custom_call_target="tpu_custom_call", output_to_operand_aliasing={{0}: (8, {})} | custom-call | flops 335544320 | bytes 1835008 | tf_op jit(solution)/shard_map/pallas_call | solution.py:138
  158.3 0.0 collective-permute-done.12.refs_0_
  158.3 0.0 collective-permute-done.13.refs_1_
  158.3 1.1 collective-permute-done.14.refs_2_
  159.4 2.1 %collective-permute-done.15.refs_3_ = bf16[3,1,64,256]{3,2,1,0:T(8,128)(2,1)S(1)} collective-permute-done((bf16[3,1,64,256]{3,2,1,0:T(8,128)(2,1)S(1)}, bf16[3,1,64,256]{3,2,1,0:T(8,128)(2,1)S(1)}, u32[]{:S(2)}, u32[]{:S(2)}) %collective-permute-start.15) | collective-permute-done | bytes 98336 | tf_op jit(solution)/shard_map/stash_3_2/ppermute | solution.py:167
  161.5 2.1 %shard_map.79 = bf16[3,1,256,2048]{3,2,1,0:T(8,128)(2,1)} custom-call(bf16[3,1,64,256]{3,2,1,0:T(8,128)(2,1)S(1)} %collective-permute-done.12.refs_0_, bf16[3,1,64,256]{3,2,1,0:T(8,128)(2,1)S(1)} %collective-permute-done.13.refs_1_, bf16[3,1,64,256]{3,2,1,0:T(8,128)(2,1)S(1)} %collective-permute-done.14.refs_2_, ...), custom_call_target="tpu_custom_call", output_to_operand_aliasing={{}: (7, {})} | custom-call | flops 167772160 | bytes 917504 | tf_op jit(solution)/shard_map/pallas_call | solution.py:138
Async XLA Ops:
  0.6 130.5 %collective-permute-start.5 = (bf16[1,256,2048]{2,1,0:T(8,128)(2,1)}, bf16[1,256,2048]{2,1,0:T(8,128)(2,1)S(1)}, u32[]{:S(2)}, u32[]{:S(2)}) collective-permute-start(bf16[1,256,2048]{2,1,0:T(8,128)(2,1)} %param.10), channel_id=1, source_target_pairs={{0,240},{16,0},{32,16},{48,32},{64,48},{80,64},{96,80},{112,96},{1... | collective-permute-start | bytes 3145736 | tf_op jit(solution)/shard_map/direct_grad/ppermute | solution.py:179
  10.6 120.5 %copy-start = (s32[1,256]{1,0:T(1,128)S(1)}, s32[1,256]{1,0:T(1,128)}, u32[]{:S(2)}) copy-start(s32[1,256]{1,0:T(1,128)} %refs_5_.3) | copy-start | bytes 3076
  10.6 51.1 %collective-permute-start = (bf16[3,1,64,1280]{3,2,1,0:T(8,128)(2,1)S(1)}, bf16[3,1,64,1280]{3,2,1,0:T(8,128)(2,1)S(1)}, u32[]{:S(2)}, u32[]{:S(2)}) collective-permute-start(bf16[3,1,64,1280]{3,2,1,0:T(8,128)(2,1)S(1)} %get-tuple-element.22), channel_id=1, source_target_pairs={{0,252},{4,248},{8,244},{12,240},{16,236},{20,232},{24,228},{28,22... | collective-permute-start | bytes 1474568 | tf_op jit(solution)/shard_map/stash_3_0/ppermute | solution.py:167
  13.3 53.7 %collective-permute-start.10 = (bf16[3,1,64,1280]{3,2,1,0:T(8,128)(2,1)S(1)}, bf16[3,1,64,1280]{3,2,1,0:T(8,128)(2,1)}, u32[]{:S(2)}, u32[]{:S(2)}) collective-permute-start(bf16[3,1,64,1280]{3,2,1,0:T(8,128)(2,1)S(1)} %get-tuple-element.21), channel_id=1, source_target_pairs={{32,48},{36,52},{40,56},{44,60},{80,64},{84,68},{88,72},{92,76},{1... | collective-permute-start | bytes 1474568 | tf_op jit(solution)/shard_map/aside_0/ppermute | solution.py:167
  14.7 57.5 %collective-permute-start.7 = (bf16[3,1,64,1280]{3,2,1,0:T(8,128)(2,1)S(1)}, bf16[3,1,64,1280]{3,2,1,0:T(8,128)(2,1)S(1)}, u32[]{:S(2)}, u32[]{:S(2)}) collective-permute-start(bf16[3,1,64,1280]{3,2,1,0:T(8,128)(2,1)S(1)} %get-tuple-element.21), channel_id=1, source_target_pairs={{0,240},{4,244},{8,248},{12,252},{16,224},{20,228},{24,232},{28,23... | collective-permute-start | bytes 1474568 | tf_op jit(solution)/shard_map/stash_0_0/ppermute | solution.py:167
  24.2 130.5 %collective-permute-start.6 = (bf16[1,256,2048]{2,1,0:T(8,128)(2,1)}, bf16[1,256,2048]{2,1,0:T(8,128)(2,1)S(1)}, u32[]{:S(2)}, u32[]{:S(2)}) collective-permute-start(bf16[1,256,2048]{2,1,0:T(8,128)(2,1)} %forward_heads.1), channel_id=1, source_target_pairs={{0,16},{16,32},{32,48},{48,64},{64,80},{80,96},{96,112},{112,128},... | collective-permute-start | bytes 3145736 | tf_op jit(solution)/shard_map/direct_out/ppermute | solution.py:179
  61.7 37.5 %collective-permute-start.8 = (bf16[3,1,64,1280]{3,2,1,0:T(8,128)(2,1)}, bf16[3,1,64,1280]{3,2,1,0:T(8,128)(2,1)}, u32[]{:S(2)}, u32[]{:S(2)}) collective-permute-start(bf16[3,1,64,1280]{3,2,1,0:T(8,128)(2,1)} %get-tuple-element.23), channel_id=1, source_target_pairs={{0,244},{4,240},{8,252},{12,248},{16,228},{20,224},{24,236},{28,23... | collective-permute-start | bytes 1474568 | tf_op jit(solution)/shard_map/stash_1_0/ppermute | solution.py:167
  67.0 58.1 %collective-permute-start.9 = (bf16[3,1,64,1280]{3,2,1,0:T(8,128)(2,1)}, bf16[3,1,64,1280]{3,2,1,0:T(8,128)(2,1)}, u32[]{:S(2)}, u32[]{:S(2)}) collective-permute-start(bf16[3,1,64,1280]{3,2,1,0:T(8,128)(2,1)} %get-tuple-element.20), channel_id=1, source_target_pairs={{0,248},{4,252},{8,240},{12,244},{16,232},{20,236},{24,224},{28,22... | collective-permute-start | bytes 1474568 | tf_op jit(solution)/shard_map/stash_2_0/ppermute | solution.py:167
  72.3 53.9 %collective-permute-start.11 = (bf16[3,1,64,1280]{3,2,1,0:T(8,128)(2,1)}, bf16[3,1,64,1280]{3,2,1,0:T(8,128)(2,1)}, u32[]{:S(2)}, u32[]{:S(2)}) collective-permute-start(bf16[3,1,64,1280]{3,2,1,0:T(8,128)(2,1)} %collective-permute-done.10), channel_id=1, source_target_pairs={{48,208},{52,212},{56,216},{60,220},{64,160},{68,164},{72,168},{76... | collective-permute-start | bytes 1474568 | tf_op jit(solution)/shard_map/onward_0/ppermute | solution.py:167
  99.2 40.6 %collective-permute-start.1 = (bf16[3,1,64,512]{3,2,1,0:T(8,128)(2,1)S(1)}, bf16[3,1,64,512]{3,2,1,0:T(8,128)(2,1)S(1)}, u32[]{:S(2)}, u32[]{:S(2)}) collective-permute-start(bf16[3,1,64,512]{3,2,1,0:T(8,128)(2,1)S(1)} %get-tuple-element.27), channel_id=1, source_target_pairs={{0,240},{4,244},{8,248},{12,252},{16,224},{20,228},{24,232},{28,23... | collective-permute-start | bytes 589832 | tf_op jit(solution)/shard_map/stash_0_1/ppermute | solution.py:167
  125.2 16.7 %collective-permute-start.2 = (bf16[3,1,64,512]{3,2,1,0:T(8,128)(2,1)S(1)}, bf16[3,1,64,512]{3,2,1,0:T(8,128)(2,1)S(1)}, u32[]{:S(2)}, u32[]{:S(2)}) collective-permute-start(bf16[3,1,64,512]{3,2,1,0:T(8,128)(2,1)S(1)} %get-tuple-element.26), channel_id=1, source_target_pairs={{0,244},{4,240},{8,252},{12,248},{16,228},{20,224},{24,236},{28,23... | collective-permute-start | bytes 589832 | tf_op jit(solution)/shard_map/stash_1_1/ppermute | solution.py:167
  126.2 22.7 %collective-permute-start.3 = (bf16[3,1,64,512]{3,2,1,0:T(8,128)(2,1)S(1)}, bf16[3,1,64,512]{3,2,1,0:T(8,128)(2,1)S(1)}, u32[]{:S(2)}, u32[]{:S(2)}) collective-permute-start(bf16[3,1,64,512]{3,2,1,0:T(8,128)(2,1)S(1)} %get-tuple-element.25), channel_id=1, source_target_pairs={{0,248},{4,252},{8,240},{12,244},{16,232},{20,236},{24,224},{28,22... | collective-permute-start | bytes 589832 | tf_op jit(solution)/shard_map/stash_2_1/ppermute | solution.py:167
  131.1 22.3 %collective-permute-start.4 = (bf16[3,1,64,512]{3,2,1,0:T(8,128)(2,1)S(1)}, bf16[3,1,64,512]{3,2,1,0:T(8,128)(2,1)S(1)}, u32[]{:S(2)}, u32[]{:S(2)}) collective-permute-start(bf16[3,1,64,512]{3,2,1,0:T(8,128)(2,1)S(1)} %get-tuple-element.24), channel_id=1, source_target_pairs={{0,252},{4,248},{8,244},{12,240},{16,236},{20,232},{24,228},{28,22... | collective-permute-start | bytes 589832 | tf_op jit(solution)/shard_map/stash_3_1/ppermute | solution.py:167
  139.8 18.4 %collective-permute-start.12 = (bf16[3,1,64,256]{3,2,1,0:T(8,128)(2,1)S(1)}, bf16[3,1,64,256]{3,2,1,0:T(8,128)(2,1)S(1)}, u32[]{:S(2)}, u32[]{:S(2)}) collective-permute-start(bf16[3,1,64,256]{3,2,1,0:T(8,128)(2,1)S(1)} %get-tuple-element.19), channel_id=1, source_target_pairs={{0,240},{4,244},{8,248},{12,252},{16,224},{20,228},{24,232},{28,23... | collective-permute-start | bytes 294920 | tf_op jit(solution)/shard_map/stash_0_2/ppermute | solution.py:167
  141.8 16.4 %collective-permute-start.13 = (bf16[3,1,64,256]{3,2,1,0:T(8,128)(2,1)S(1)}, bf16[3,1,64,256]{3,2,1,0:T(8,128)(2,1)S(1)}, u32[]{:S(2)}, u32[]{:S(2)}) collective-permute-start(bf16[3,1,64,256]{3,2,1,0:T(8,128)(2,1)S(1)} %get-tuple-element.18), channel_id=1, source_target_pairs={{0,244},{4,240},{8,252},{12,248},{16,228},{20,224},{24,236},{28,23... | collective-permute-start | bytes 294920 | tf_op jit(solution)/shard_map/stash_1_2/ppermute | solution.py:167
  148.8 10.5 %collective-permute-start.14 = (bf16[3,1,64,256]{3,2,1,0:T(8,128)(2,1)S(1)}, bf16[3,1,64,256]{3,2,1,0:T(8,128)(2,1)S(1)}, u32[]{:S(2)}, u32[]{:S(2)}) collective-permute-start(bf16[3,1,64,256]{3,2,1,0:T(8,128)(2,1)S(1)} %get-tuple-element.17), channel_id=1, source_target_pairs={{0,248},{4,252},{8,240},{12,244},{16,232},{20,236},{24,224},{28,22... | collective-permute-start | bytes 294920 | tf_op jit(solution)/shard_map/stash_2_2/ppermute | solution.py:167
  153.4 8.1 %collective-permute-start.15 = (bf16[3,1,64,256]{3,2,1,0:T(8,128)(2,1)S(1)}, bf16[3,1,64,256]{3,2,1,0:T(8,128)(2,1)S(1)}, u32[]{:S(2)}, u32[]{:S(2)}) collective-permute-start(bf16[3,1,64,256]{3,2,1,0:T(8,128)(2,1)S(1)} %get-tuple-element.16), channel_id=1, source_target_pairs={{0,252},{4,248},{8,244},{12,240},{16,236},{20,232},{24,228},{28,22... | collective-permute-start | bytes 294920 | tf_op jit(solution)/shard_map/stash_3_2/ppermute | solution.py:167

commit v12 on v11

--- a/solution.py
+++ b/solution.py
@@ -188,10 +188,10 @@
         start = (mine ^ k) * width + first * HEAD_DIM
         return lax.dynamic_slice_in_dim(whole, start, heads * HEAD_DIM, axis=3)
 
-    def fetched_chunk(whole, chunk):
+    def fetched_chunk(whole, chunk, partners):
         first, heads = CHUNKS[chunk]
         pieces = []
-        for k in range(tensors):
+        for k in partners:
             goes_around = k == 0 and DETOUR[0] <= first and first + heads <= sum(DETOUR)
             with jax.named_scope(f"stash_{k}_{chunk}"):
                 piece = cut(whole, k, first, heads)
@@ -199,11 +199,15 @@
         return pieces
 
     upstream = shifted(grad_out, -1)
+    leading = cut(parked, 3, *CHUNKS[0])
+    leading, parked = lax.optimization_barrier((leading, parked))
+    with jax.named_scope("stash_3_0"):
+        leading = fetched(leading, 3, "all")
     with jax.named_scope("aside_0"):
         around = fetched(cut(parked, 0, *DETOUR), 0, "aside")
     with jax.named_scope("onward_0"):
         around = fetched(around, 0, "onward")
-    pieces = [fetched_chunk(parked, 0)]
+    pieces = [[*fetched_chunk(parked, 0, range(3)), leading]]
     with jax.named_scope("forward_heads"):
         forward_out = forward(fwd_qkv, fwd_segments)
     received = shifted(forward_out, 1)
@@ -212,10 +216,10 @@
     token_total = lax.psum(tokens, "dp")
     factor = jnp.float32(lax.axis_size("dp") * length) / token_total
     parked, token_total = lax.optimization_barrier((parked, token_total))
-    pieces.append(fetched_chunk(parked, 1))
+    pieces.append(fetched_chunk(parked, 1, range(tensors)))
     (grads,) = backward(0, pieces[0], around, upstream, bwd_segments, factor, None)
     parked, grads = lax.optimization_barrier((parked, grads))
-    pieces.append(fetched_chunk(parked, 2))
+    pieces.append(fetched_chunk(parked, 2, range(tensors)))
     grads, received = backward(
         1, pieces[1], around, upstream, bwd_segments, factor, grads, received
     )

time: 164 us -> 164 us (level); the launches traced: 164 us -> 161 us
  waiting for transfers between devices: 91.5 us -> 80.8 us
  starting transfers between devices: 36.8 us -> 43.5 us
  local copies, waits for them, and re-layouts: 4.94 us -> 6.62 us
    ppermute x14, starting transfers between devices: 29.4 us -> 42.1 us  [fetched(): return lax.ppermute(piece, AXES, pairs)]
    ppermute x14, waiting for transfers between devices: 91.5 us -> 80.8 us  [fetched(): return lax.ppermute(piece, AXES, pairs)]
    ppermute x2, starting transfers between devices: 7.41 us -> 1.46 us  [shifted(): lax.ppermute(array, 'pipe', [(p, (p + by) % sections) for p in range(sect...]
    dynamic_slice x3 -> x4, local copies, waits for them, and re-layouts: 4.93 us -> 6.61 us  [cut(): return lax.dynamic_slice_in_dim(whole, start, heads * HEAD_DIM, axis=3)]
  transfers between devices with their start and end apart: 16 -> 16, of which waited for: 8 -> 4; matrix products, arithmetic and copies ran while one was open for 3% -> 3% of each run, Pallas kernels for 10% -> 10%
where the time goes in v12:
time: 164 us; the launch traced here: 161 us
  waiting for transfers between devices  80.8 us (49%)
  starting transfers between devices  43.5 us (27%)
  Pallas kernels  18.3 us (11%)
  blocking collectives  10 us (6%)
  local copies, waits for them, and re-layouts  6.62 us (4%)
  between operations  1.99 us (1%)
    ppermute x14, waiting for transfers between devices, fetched(): return lax.ppermute(piece, AXES, pairs)  80.8 us
    ppermute x14, starting transfers between devices, fetched(): return lax.ppermute(piece, AXES, pairs)  42.1 us
    pallas_call x3, Pallas kernels, backward(): pl.pallas_call(functools.partial(backward_kernel, parts, around_from, car...  13.1 us
    psum x1, blocking collectives, on_device(): token_total = lax.psum(tokens, 'dp')  10 us
    dynamic_slice x4, local copies, waits for them, and re-layouts, cut(): return lax.dynamic_slice_in_dim(whole, start, heads * HEAD_DIM, axis=3)  6.61 us
    pallas_call x1, Pallas kernels, forward(): pl.pallas_call(forward_kernel, grid=(FORWARD_STEPS,), in_specs=[pl.BlockS...  5.18 us
  transfers between devices with their start and end apart: 16, of which 4 were waited for; matrix products, arithmetic and copies ran while one was open for 3% of the time, Pallas kernels for 10%

profile of v12, /device:TPU:1, one launch (start us, length us, event | category | flops | bytes accessed | tf_op | source)
XLA Modules:
  0.0 161.3 jit_solution(684144144630535930)
XLA Ops:
  0.6 1.9 %constant_dynamic-slice_fusion.11 = bf16[3,1,64,1280]{3,2,1,0:T(8,128)(2,1)} fusion(bf16[3,1,64,8192]{3,2,1,0:T(8,128)(2,1)} %param.8, s32[]{:T(128)S(6)} %select_n.37), kind=kLoop, calls=%fused_computation.11 | loop fusion | bytes 983044 | tf_op jit(solution)/shard_map/dynamic_slice | solution.py:189
  2.5 9.2 %collective-permute-start = (bf16[3,1,64,1280]{3,2,1,0:T(8,128)(2,1)}, bf16[3,1,64,1280]{3,2,1,0:T(8,128)(2,1)S(1)}, u32[]{:S(2)}, u32[]{:S(2)}) collective-permute-start(bf16[3,1,64,1280]{3,2,1,0:T(8,128)(2,1)} %constant_dynamic-slice_fusion.11), channel_id=1, source_target_pairs={{0,252},{4,248},{8,244},{12,240},{16,236},{20,232},{24,228},{28,22... | collective-permute-start | bytes 1474568 | tf_op jit(solution)/shard_map/stash_3_0/ppermute | solution.py:167
  11.7 0.0 collective-permute-start.5
  11.7 2.4 %constant_dynamic-slice_fusion.4 = (bf16[3,1,64,1280]{3,2,1,0:T(8,128)(2,1)S(1)}, bf16[3,1,64,1280]{3,2,1,0:T(8,128)(2,1)}, bf16[3,1,64,1280]{3,2,1,0:T(8,128)(2,1)}) fusion(bf16[3,1,64,8192]{3,2,1,0:T(8,128)(2,1)} %param.8, s32[]{:T(128)S(6)} %select_n.44, s32[]{:T(128)S(6)} %select_n.43, s32[]{:T(128)S(6)} %select_n.42), kind=kLoop, calls=%fused_computation.4 | loop fusion | bytes 2949132 | tf_op jit(solution)/shard_map/stash_2_0/dynamic_slice | solution.py:189
  14.1 0.0 copy-start
  14.1 0.0 collective-permute-start.9
  14.1 1.6 collective-permute-start.10
  15.7 5.2 %forward_heads.1 = bf16[1,256,2048]{2,1,0:T(8,128)(2,1)} custom-call(bf16[3,1,256,2048]{3,2,1,0:T(8,128)(2,1)} %qkv_ref.1, s32[1,256]{1,0:T(1,128)} %segment_ref.1), custom_call_target="tpu_custom_call" | custom-call | flops 536870912 | bytes 4194304 | tf_op jit(solution)/shard_map/forward_heads/pallas_call | solution.py:55
  20.8 1.5 collective-permute-start.6
  22.3 22.1 %collective-permute-done.refs_3_ = bf16[3,1,64,1280]{3,2,1,0:T(8,128)(2,1)S(1)} collective-permute-done((bf16[3,1,64,1280]{3,2,1,0:T(8,128)(2,1)}, bf16[3,1,64,1280]{3,2,1,0:T(8,128)(2,1)S(1)}, u32[]{:S(2)}, u32[]{:S(2)}) %collective-permute-start) | collective-permute-done | bytes 491552 | tf_op jit(solution)/shard_map/stash_3_0/ppermute | solution.py:167
  44.4 0.0 collective-permute-start.8
  44.4 43.2 %collective-permute-done.9.refs_2_ = bf16[3,1,64,1280]{3,2,1,0:T(8,128)(2,1)S(1)} collective-permute-done((bf16[3,1,64,1280]{3,2,1,0:T(8,128)(2,1)S(1)}, bf16[3,1,64,1280]{3,2,1,0:T(8,128)(2,1)S(1)}, u32[]{:S(2)}, u32[]{:S(2)}) %collective-permute-start.9) | collective-permute-done | bytes 491552 | tf_op jit(solution)/shard_map/stash_2_0/ppermute | solution.py:167
  87.6 4.9 %collective-permute-start.7 = (bf16[3,1,64,1280]{3,2,1,0:T(8,128)(2,1)}, bf16[3,1,64,1280]{3,2,1,0:T(8,128)(2,1)}, u32[]{:S(2)}, u32[]{:S(2)}) collective-permute-start(bf16[3,1,64,1280]{3,2,1,0:T(8,128)(2,1)} %get-tuple-element.26), channel_id=1, source_target_pairs={{0,240},{4,244},{8,248},{12,252},{16,224},{20,228},{24,232},{28,23... | collective-permute-start | bytes 1474568 | tf_op jit(solution)/shard_map/stash_0_0/ppermute | solution.py:167
  92.5 0.0 collective-permute-done.10
  92.5 1.5 collective-permute-start.11
  94.7 10.0 %psum.7 = f32[1]{0:T(128)} all-reduce(f32[1]{0:T(128)S(6)} %convert_element_type.3), channel_id=1, replica_groups=mesh['pipe'=16,'tensor'=4,'dp'=4] {'dp'}, use_global_device_ids=true, to_apply=%region_0.0 | all-reduce | flops 1 | bytes 8 | tf_op jit(solution)/shard_map/psum | solution.py:216
  105.3 1.3 constant_dynamic-slice_fusion.7
  106.6 0.0 collective-permute-done.8.refs_1_
  106.6 4.1 %collective-permute-start.4 = (bf16[3,1,64,512]{3,2,1,0:T(8,128)(2,1)S(1)}, bf16[3,1,64,512]{3,2,1,0:T(8,128)(2,1)S(1)}, u32[]{:S(2)}, u32[]{:S(2)}) collective-permute-start(bf16[3,1,64,512]{3,2,1,0:T(8,128)(2,1)S(1)} %get-tuple-element.27), channel_id=1, source_target_pairs={{0,252},{4,248},{8,244},{12,240},{16,236},{20,232},{24,228},{28,22... | collective-permute-start | bytes 589832 | tf_op jit(solution)/shard_map/stash_3_1/ppermute | solution.py:167
  110.7 14.9 %collective-permute-done.7.refs_0_ = bf16[3,1,64,1280]{3,2,1,0:T(8,128)(2,1)} collective-permute-done((bf16[3,1,64,1280]{3,2,1,0:T(8,128)(2,1)}, bf16[3,1,64,1280]{3,2,1,0:T(8,128)(2,1)}, u32[]{:S(2)}, u32[]{:S(2)}) %collective-permute-start.7) | collective-permute-done | bytes 491552 | tf_op jit(solution)/shard_map/stash_0_0/ppermute | solution.py:167
  125.6 3.6 %collective-permute-start.3 = (bf16[3,1,64,512]{3,2,1,0:T(8,128)(2,1)S(1)}, bf16[3,1,64,512]{3,2,1,0:T(8,128)(2,1)S(1)}, u32[]{:S(2)}, u32[]{:S(2)}) collective-permute-start(bf16[3,1,64,512]{3,2,1,0:T(8,128)(2,1)S(1)} %get-tuple-element.28), channel_id=1, source_target_pairs={{0,248},{4,252},{8,240},{12,244},{16,232},{20,236},{24,224},{28,22... | collective-permute-start | bytes 589832 | tf_op jit(solution)/shard_map/stash_2_1/ppermute | solution.py:167
  129.2 0.0 collective-permute-done.11.refs_4_
  129.2 2.0 %collective-permute-start.2 = (bf16[3,1,64,512]{3,2,1,0:T(8,128)(2,1)S(1)}, bf16[3,1,64,512]{3,2,1,0:T(8,128)(2,1)S(1)}, u32[]{:S(2)}, u32[]{:S(2)}) collective-permute-start(bf16[3,1,64,512]{3,2,1,0:T(8,128)(2,1)S(1)} %get-tuple-element.29), channel_id=1, source_target_pairs={{0,244},{4,240},{8,252},{12,248},{16,228},{20,224},{24,236},{28,23... | collective-permute-start | bytes 589832 | tf_op jit(solution)/shard_map/stash_1_1/ppermute | solution.py:167
  131.3 0.0 collective-permute-done.5.refs_5_.refs_4_
  131.3 2.1 %collective-permute-start.1 = (bf16[3,1,64,512]{3,2,1,0:T(8,128)(2,1)S(1)}, bf16[3,1,64,512]{3,2,1,0:T(8,128)(2,1)S(1)}, u32[]{:S(2)}, u32[]{:S(2)}) collective-permute-start(bf16[3,1,64,512]{3,2,1,0:T(8,128)(2,1)S(1)} %get-tuple-element.30), channel_id=1, source_target_pairs={{0,240},{4,244},{8,248},{12,252},{16,224},{20,228},{24,232},{28,23... | collective-permute-start | bytes 589832 | tf_op jit(solution)/shard_map/stash_0_1/ppermute | solution.py:167
  133.4 0.0 copy-done
  133.4 7.6 %shard_map.77.refs_8_ = bf16[3,1,256,2048]{3,2,1,0:T(8,128)(2,1)} custom-call(bf16[3,1,64,1280]{3,2,1,0:T(8,128)(2,1)} %collective-permute-done.7.refs_0_, bf16[3,1,64,1280]{3,2,1,0:T(8,128)(2,1)} %collective-permute-done.8.refs_1_, bf16[3,1,64,1280]{3,2,1,0:T(8,128)(2,1)S(1)} %collective-permute-done.9.refs_2_, ...), custom_call_target="tpu_custom_call" | custom-call | flops 838860800 | bytes 4587520 | tf_op jit(solution)/shard_map/pallas_call | solution.py:138
  141.0 1.1 constant_dynamic-slice_fusion
  142.1 0.0 collective-permute-done.4.refs_3_
  142.1 3.0 %collective-permute-start.15 = (bf16[3,1,64,256]{3,2,1,0:T(8,128)(2,1)S(1)}, bf16[3,1,64,256]{3,2,1,0:T(8,128)(2,1)S(1)}, u32[]{:S(2)}, u32[]{:S(2)}) collective-permute-start(bf16[3,1,64,256]{3,2,1,0:T(8,128)(2,1)S(1)} %get-tuple-element.20), channel_id=1, source_target_pairs={{0,252},{4,248},{8,244},{12,240},{16,236},{20,232},{24,228},{28,22... | collective-permute-start | bytes 294920 | tf_op jit(solution)/shard_map/stash_3_2/ppermute | solution.py:167
  145.0 0.0 collective-permute-done.3.refs_2_
  145.0 2.8 %collective-permute-start.14 = (bf16[3,1,64,256]{3,2,1,0:T(8,128)(2,1)S(1)}, bf16[3,1,64,256]{3,2,1,0:T(8,128)(2,1)S(1)}, u32[]{:S(2)}, u32[]{:S(2)}) collective-permute-start(bf16[3,1,64,256]{3,2,1,0:T(8,128)(2,1)S(1)} %get-tuple-element.21), channel_id=1, source_target_pairs={{0,248},{4,252},{8,240},{12,244},{16,232},{20,236},{24,224},{28,22... | collective-permute-start | bytes 294920 | tf_op jit(solution)/shard_map/stash_2_2/ppermute | solution.py:167
  147.9 0.0 collective-permute-done.2.refs_1_
  147.9 3.3 %collective-permute-start.13 = (bf16[3,1,64,256]{3,2,1,0:T(8,128)(2,1)S(1)}, bf16[3,1,64,256]{3,2,1,0:T(8,128)(2,1)S(1)}, u32[]{:S(2)}, u32[]{:S(2)}) collective-permute-start(bf16[3,1,64,256]{3,2,1,0:T(8,128)(2,1)S(1)} %get-tuple-element.22), channel_id=1, source_target_pairs={{0,244},{4,240},{8,252},{12,248},{16,228},{20,224},{24,236},{28,23... | collective-permute-start | bytes 294920 | tf_op jit(solution)/shard_map/stash_1_2/ppermute | solution.py:167
  151.1 0.0 collective-permute-done.1.refs_0_
  151.1 3.9 %collective-permute-start.12 = (bf16[3,1,64,256]{3,2,1,0:T(8,128)(2,1)S(1)}, bf16[3,1,64,256]{3,2,1,0:T(8,128)(2,1)S(1)}, u32[]{:S(2)}, u32[]{:S(2)}) collective-permute-start(bf16[3,1,64,256]{3,2,1,0:T(8,128)(2,1)S(1)} %get-tuple-element.23), channel_id=1, source_target_pairs={{0,240},{4,244},{8,248},{12,252},{16,224},{20,228},{24,232},{28,23... | collective-permute-start | bytes 294920 | tf_op jit(solution)/shard_map/stash_0_2/ppermute | solution.py:167
  155.1 0.0 collective-permute-done.6.refs_7_
  155.1 3.5 %shard_map.78 = (bf16[3,1,256,2048]{3,2,1,0:T(8,128)(2,1)}, bf16[1,256,2048]{2,1,0:T(8,128)(2,1)}) custom-call(bf16[3,1,64,512]{3,2,1,0:T(8,128)(2,1)S(1)} %collective-permute-done.1.refs_0_, bf16[3,1,64,512]{3,2,1,0:T(8,128)(2,1)S(1)} %collective-permute-done.2.refs_1_, ...), custom_call_target="tpu_custom_call", output_to_operand_aliasing={{0}: (8, {})} | custom-call | flops 335544320 | bytes 1835008 | tf_op jit(solution)/shard_map/pallas_call | solution.py:138
  158.5 0.0 collective-permute-done.15.refs_3_
  158.5 0.0 collective-permute-done.14.refs_2_
  158.6 0.0 collective-permute-done.13.refs_1_
  158.6 0.6 collective-permute-done.12.refs_0_
  159.2 2.1 %shard_map.79 = bf16[3,1,256,2048]{3,2,1,0:T(8,128)(2,1)} custom-call(bf16[3,1,64,256]{3,2,1,0:T(8,128)(2,1)S(1)} %collective-permute-done.12.refs_0_, bf16[3,1,64,256]{3,2,1,0:T(8,128)(2,1)S(1)} %collective-permute-done.13.refs_1_, bf16[3,1,64,256]{3,2,1,0:T(8,128)(2,1)S(1)} %collective-permute-done.14.refs_2_, ...), custom_call_target="tpu_custom_call", output_to_operand_aliasing={{}: (7, {})} | custom-call | flops 167772160 | bytes 917504 | tf_op jit(solution)/shard_map/pallas_call | solution.py:138
Async XLA Ops:
  2.5 41.9 %collective-permute-start = (bf16[3,1,64,1280]{3,2,1,0:T(8,128)(2,1)}, bf16[3,1,64,1280]{3,2,1,0:T(8,128)(2,1)S(1)}, u32[]{:S(2)}, u32[]{:S(2)}) collective-permute-start(bf16[3,1,64,1280]{3,2,1,0:T(8,128)(2,1)} %constant_dynamic-slice_fusion.11), channel_id=1, source_target_pairs={{0,252},{4,248},{8,244},{12,240},{16,236},{20,232},{24,228},{28,22... | collective-permute-start | bytes 1474568 | tf_op jit(solution)/shard_map/stash_3_0/ppermute | solution.py:167
  11.7 119.6 %collective-permute-start.5 = (bf16[1,256,2048]{2,1,0:T(8,128)(2,1)}, bf16[1,256,2048]{2,1,0:T(8,128)(2,1)S(1)}, u32[]{:S(2)}, u32[]{:S(2)}) collective-permute-start(bf16[1,256,2048]{2,1,0:T(8,128)(2,1)} %param.10), channel_id=1, source_target_pairs={{0,240},{16,0},{32,16},{48,32},{64,48},{80,64},{96,80},{112,96},{1... | collective-permute-start | bytes 3145736 | tf_op jit(solution)/shard_map/direct_grad/ppermute | solution.py:179
  14.1 119.3 %copy-start = (s32[1,256]{1,0:T(1,128)S(1)}, s32[1,256]{1,0:T(1,128)}, u32[]{:S(2)}) copy-start(s32[1,256]{1,0:T(1,128)} %refs_5_.3) | copy-start | bytes 3076
  14.1 73.5 %collective-permute-start.9 = (bf16[3,1,64,1280]{3,2,1,0:T(8,128)(2,1)S(1)}, bf16[3,1,64,1280]{3,2,1,0:T(8,128)(2,1)S(1)}, u32[]{:S(2)}, u32[]{:S(2)}) collective-permute-start(bf16[3,1,64,1280]{3,2,1,0:T(8,128)(2,1)S(1)} %get-tuple-element.24), channel_id=1, source_target_pairs={{0,248},{4,252},{8,240},{12,244},{16,232},{20,236},{24,224},{28,22... | collective-permute-start | bytes 1474568 | tf_op jit(solution)/shard_map/stash_2_0/ppermute | solution.py:167
  14.1 78.4 %collective-permute-start.10 = (bf16[3,1,64,1280]{3,2,1,0:T(8,128)(2,1)}, bf16[3,1,64,1280]{3,2,1,0:T(8,128)(2,1)}, u32[]{:S(2)}, u32[]{:S(2)}) collective-permute-start(bf16[3,1,64,1280]{3,2,1,0:T(8,128)(2,1)} %get-tuple-element.26), channel_id=1, source_target_pairs={{32,48},{36,52},{40,56},{44,60},{80,64},{84,68},{88,72},{92,76},{1... | collective-permute-start | bytes 1474568 | tf_op jit(solution)/shard_map/aside_0/ppermute | solution.py:167
  20.8 134.2 %collective-permute-start.6 = (bf16[1,256,2048]{2,1,0:T(8,128)(2,1)}, bf16[1,256,2048]{2,1,0:T(8,128)(2,1)S(1)}, u32[]{:S(2)}, u32[]{:S(2)}) collective-permute-start(bf16[1,256,2048]{2,1,0:T(8,128)(2,1)} %forward_heads.1), channel_id=1, source_target_pairs={{0,16},{16,32},{32,48},{48,64},{64,80},{80,96},{96,112},{112,128},... | collective-permute-start | bytes 3145736 | tf_op jit(solution)/shard_map/direct_out/ppermute | solution.py:179
  44.4 62.2 %collective-permute-start.8 = (bf16[3,1,64,1280]{3,2,1,0:T(8,128)(2,1)}, bf16[3,1,64,1280]{3,2,1,0:T(8,128)(2,1)}, u32[]{:S(2)}, u32[]{:S(2)}) collective-permute-start(bf16[3,1,64,1280]{3,2,1,0:T(8,128)(2,1)} %get-tuple-element.25), channel_id=1, source_target_pairs={{0,244},{4,240},{8,252},{12,248},{16,228},{20,224},{24,236},{28,23... | collective-permute-start | bytes 1474568 | tf_op jit(solution)/shard_map/stash_1_0/ppermute | solution.py:167
  87.6 38.0 %collective-permute-start.7 = (bf16[3,1,64,1280]{3,2,1,0:T(8,128)(2,1)}, bf16[3,1,64,1280]{3,2,1,0:T(8,128)(2,1)}, u32[]{:S(2)}, u32[]{:S(2)}) collective-permute-start(bf16[3,1,64,1280]{3,2,1,0:T(8,128)(2,1)} %get-tuple-element.26), channel_id=1, source_target_pairs={{0,240},{4,244},{8,248},{12,252},{16,224},{20,228},{24,232},{28,23... | collective-permute-start | bytes 1474568 | tf_op jit(solution)/shard_map/stash_0_0/ppermute | solution.py:167
  92.5 36.7 %collective-permute-start.11 = (bf16[3,1,64,1280]{3,2,1,0:T(8,128)(2,1)}, bf16[3,1,64,1280]{3,2,1,0:T(8,128)(2,1)}, u32[]{:S(2)}, u32[]{:S(2)}) collective-permute-start(bf16[3,1,64,1280]{3,2,1,0:T(8,128)(2,1)} %collective-permute-done.10), channel_id=1, source_target_pairs={{48,208},{52,212},{56,216},{60,220},{64,160},{68,164},{72,168},{76... | collective-permute-start | bytes 1474568 | tf_op jit(solution)/shard_map/onward_0/ppermute | solution.py:167
  106.6 35.5 %collective-permute-start.4 = (bf16[3,1,64,512]{3,2,1,0:T(8,128)(2,1)S(1)}, bf16[3,1,64,512]{3,2,1,0:T(8,128)(2,1)S(1)}, u32[]{:S(2)}, u32[]{:S(2)}) collective-permute-start(bf16[3,1,64,512]{3,2,1,0:T(8,128)(2,1)S(1)} %get-tuple-element.27), channel_id=1, source_target_pairs={{0,252},{4,248},{8,244},{12,240},{16,236},{20,232},{24,228},{28,22... | collective-permute-start | bytes 589832 | tf_op jit(solution)/shard_map/stash_3_1/ppermute | solution.py:167
  125.6 19.4 %collective-permute-start.3 = (bf16[3,1,64,512]{3,2,1,0:T(8,128)(2,1)S(1)}, bf16[3,1,64,512]{3,2,1,0:T(8,128)(2,1)S(1)}, u32[]{:S(2)}, u32[]{:S(2)}) collective-permute-start(bf16[3,1,64,512]{3,2,1,0:T(8,128)(2,1)S(1)} %get-tuple-element.28), channel_id=1, source_target_pairs={{0,248},{4,252},{8,240},{12,244},{16,232},{20,236},{24,224},{28,22... | collective-permute-start | bytes 589832 | tf_op jit(solution)/shard_map/stash_2_1/ppermute | solution.py:167
  129.2 18.6 %collective-permute-start.2 = (bf16[3,1,64,512]{3,2,1,0:T(8,128)(2,1)S(1)}, bf16[3,1,64,512]{3,2,1,0:T(8,128)(2,1)S(1)}, u32[]{:S(2)}, u32[]{:S(2)}) collective-permute-start(bf16[3,1,64,512]{3,2,1,0:T(8,128)(2,1)S(1)} %get-tuple-element.29), channel_id=1, source_target_pairs={{0,244},{4,240},{8,252},{12,248},{16,228},{20,224},{24,236},{28,23... | collective-permute-start | bytes 589832 | tf_op jit(solution)/shard_map/stash_1_1/ppermute | solution.py:167
  131.3 19.9 %collective-permute-start.1 = (bf16[3,1,64,512]{3,2,1,0:T(8,128)(2,1)S(1)}, bf16[3,1,64,512]{3,2,1,0:T(8,128)(2,1)S(1)}, u32[]{:S(2)}, u32[]{:S(2)}) collective-permute-start(bf16[3,1,64,512]{3,2,1,0:T(8,128)(2,1)S(1)} %get-tuple-element.30), channel_id=1, source_target_pairs={{0,240},{4,244},{8,248},{12,252},{16,224},{20,228},{24,232},{28,23... | collective-permute-start | bytes 589832 | tf_op jit(solution)/shard_map/stash_0_1/ppermute | solution.py:167
  142.1 16.5 %collective-permute-start.15 = (bf16[3,1,64,256]{3,2,1,0:T(8,128)(2,1)S(1)}, bf16[3,1,64,256]{3,2,1,0:T(8,128)(2,1)S(1)}, u32[]{:S(2)}, u32[]{:S(2)}) collective-permute-start(bf16[3,1,64,256]{3,2,1,0:T(8,128)(2,1)S(1)} %get-tuple-element.20), channel_id=1, source_target_pairs={{0,252},{4,248},{8,244},{12,240},{16,236},{20,232},{24,228},{28,22... | collective-permute-start | bytes 294920 | tf_op jit(solution)/shard_map/stash_3_2/ppermute | solution.py:167
  145.0 13.5 %collective-permute-start.14 = (bf16[3,1,64,256]{3,2,1,0:T(8,128)(2,1)S(1)}, bf16[3,1,64,256]{3,2,1,0:T(8,128)(2,1)S(1)}, u32[]{:S(2)}, u32[]{:S(2)}) collective-permute-start(bf16[3,1,64,256]{3,2,1,0:T(8,128)(2,1)S(1)} %get-tuple-element.21), channel_id=1, source_target_pairs={{0,248},{4,252},{8,240},{12,244},{16,232},{20,236},{24,224},{28,22... | collective-permute-start | bytes 294920 | tf_op jit(solution)/shard_map/stash_2_2/ppermute | solution.py:167
  147.9 10.7 %collective-permute-start.13 = (bf16[3,1,64,256]{3,2,1,0:T(8,128)(2,1)S(1)}, bf16[3,1,64,256]{3,2,1,0:T(8,128)(2,1)S(1)}, u32[]{:S(2)}, u32[]{:S(2)}) collective-permute-start(bf16[3,1,64,256]{3,2,1,0:T(8,128)(2,1)S(1)} %get-tuple-element.22), channel_id=1, source_target_pairs={{0,244},{4,240},{8,252},{12,248},{16,228},{20,224},{24,236},{28,23... | collective-permute-start | bytes 294920 | tf_op jit(solution)/shard_map/stash_1_2/ppermute | solution.py:167
  151.1 8.0 %collective-permute-start.12 = (bf16[3,1,64,256]{3,2,1,0:T(8,128)(2,1)S(1)}, bf16[3,1,64,256]{3,2,1,0:T(8,128)(2,1)S(1)}, u32[]{:S(2)}, u32[]{:S(2)}) collective-permute-start(bf16[3,1,64,256]{3,2,1,0:T(8,128)(2,1)S(1)} %get-tuple-element.23), channel_id=1, source_target_pairs={{0,240},{4,244},{8,248},{12,252},{16,224},{20,228},{24,232},{28,23... | collective-permute-start | bytes 294920 | tf_op jit(solution)/shard_map/stash_0_2/ppermute | solution.py:167

commit v13 on v11

--- a/solution.py
+++ b/solution.py
@@ -11,7 +11,6 @@
 HEAD_DIM = 128
 FORWARD_STEPS = 2
 CHUNKS = ((0, 10), (12, 4), (10, 2))
-DETOUR = (0, 10)
 SCALE = HEAD_DIM ** (-0.5)
 EXPONENT = SCALE * math.log2(math.e)
 NT = (((1,), (1,)), ((), ()))
@@ -71,7 +70,7 @@
     )(qkv, segment)
 
 
-def backward_kernel(parts, around_from, carries, *refs):
+def backward_kernel(parts, carries, *refs):
     pieces, refs = refs[:parts], refs[parts:]
     upstream_ref, segment_ref, factor_ref = refs[:3]
     out_ref, stash = refs[-2:]
@@ -80,13 +79,9 @@
         refs[-2][...] = refs[3][...]
     mine = lax.axis_index("tensor")
     rows = pieces[0].shape[2]
-    if around_from is not None:
-        columns = slice(around_from, around_from + pieces[0].shape[3])
-        around = pieces[-1][:, 0, :, columns]
-        pieces = pieces[:-1]
     found = [piece[:, 0] for piece in pieces]
-    if around_from is not None:
-        found[0] = jnp.where(detoured(lax.axis_index("pipe")), around, found[0])
+    if parts > 4:
+        found[0] = jnp.where(detoured(lax.axis_index("pipe")), found.pop(), found[0])
     for k, piece in enumerate(found):
         start = pl.multiple_of((mine ^ k) * rows, rows)
         stash[:, pl.ds(start, rows), :] = piece
@@ -111,9 +106,7 @@
     first, heads = CHUNKS[chunk]
     step = heads * HEAD_DIM
     place = first // heads
-    around_from = None
-    if DETOUR[0] <= first and first + heads <= sum(DETOUR):
-        around_from = (first - DETOUR[0]) * HEAD_DIM
+    if around is not None:
         pieces = [*pieces, around]
     parts = len(pieces)
     operands = [*pieces, upstream, segment, factor]
@@ -136,7 +129,7 @@
         operands.append(earlier)
         in_specs.append(pl.BlockSpec(memory_space=pl.ANY))
     return pl.pallas_call(
-        functools.partial(backward_kernel, parts, around_from, carried is not None),
+        functools.partial(backward_kernel, parts, carried is not None),
         grid=(1,),
         in_specs=in_specs,
         out_specs=out_specs,
@@ -152,6 +145,34 @@
     )(*operands)
 
 
+def cut_kernel(spans, whole_ref, *refs):
+    outs, sems = refs[:-1], refs[-1]
+    width = whole_ref.shape[3] // lax.axis_size("tensor")
+    copies = []
+    for i, (k, first, heads) in enumerate(spans):
+        start = (lax.axis_index("tensor") ^ k) * width + first * HEAD_DIM
+        columns = pl.ds(pl.multiple_of(start, HEAD_DIM), heads * HEAD_DIM)
+        copies.append(pltpu.make_async_copy(whole_ref.at[:, :, :, columns], outs[i], sems.at[i]))
+    for copy in copies:
+        copy.start()
+    for copy in copies:
+        copy.wait()
+
+
+def cut_by_copy(whole, spans):
+    return pl.pallas_call(
+        functools.partial(cut_kernel, spans),
+        in_specs=[pl.BlockSpec(memory_space=pl.ANY)],
+        out_specs=[pl.BlockSpec(memory_space=pl.ANY)] * len(spans),
+        out_shape=[
+            jax.ShapeDtypeStruct((*whole.shape[:3], heads * HEAD_DIM), whole.dtype)
+            for _, _, heads in spans
+        ],
+        scratch_shapes=[pltpu.SemaphoreType.DMA((len(spans),))],
+        compiler_params=pltpu.CompilerParams(vmem_limit_bytes=60 * 1024 * 1024),
+    )(whole)
+
+
 def fetched(piece, k, leg="direct"):
     sections, tensors = lax.axis_size("pipe"), lax.axis_size("tensor")
     pairs = []
@@ -192,18 +213,22 @@
         first, heads = CHUNKS[chunk]
         pieces = []
         for k in range(tensors):
-            goes_around = k == 0 and DETOUR[0] <= first and first + heads <= sum(DETOUR)
             with jax.named_scope(f"stash_{k}_{chunk}"):
-                piece = cut(whole, k, first, heads)
-                pieces.append(fetched(piece, k, "direct" if goes_around else "all"))
+                pieces.append(fetched(cut(whole, k, first, heads), k, "all"))
         return pieces
 
     upstream = shifted(grad_out, -1)
+    (leading,) = cut_by_copy(parked, [(3, *CHUNKS[0])])
+    leading, parked = lax.optimization_barrier((leading, parked))
+    rest = cut_by_copy(parked, [(k, *CHUNKS[0]) for k in range(3)])
     with jax.named_scope("aside_0"):
-        around = fetched(cut(parked, 0, *DETOUR), 0, "aside")
+        around = fetched(rest[0], 0, "aside")
     with jax.named_scope("onward_0"):
         around = fetched(around, 0, "onward")
-    pieces = [fetched_chunk(parked, 0)]
+    pieces = [[]]
+    for k, piece in enumerate([*rest, leading]):
+        with jax.named_scope(f"stash_{k}_0"):
+            pieces[0].append(fetched(piece, k, "direct" if k == 0 else "all"))
     with jax.named_scope("forward_heads"):
         forward_out = forward(fwd_qkv, fwd_segments)
     received = shifted(forward_out, 1)
@@ -217,9 +242,9 @@
     parked, grads = lax.optimization_barrier((parked, grads))
     pieces.append(fetched_chunk(parked, 2))
     grads, received = backward(
-        1, pieces[1], around, upstream, bwd_segments, factor, grads, received
+        1, pieces[1], None, upstream, bwd_segments, factor, grads, received
     )
-    (grads,) = backward(2, pieces[2], around, upstream, bwd_segments, factor, grads)
+    (grads,) = backward(2, pieces[2], None, upstream, bwd_segments, factor, grads)
     return (received, grads)
 
 

time: 164 us -> 204 us (1.24)
  Pallas kernels: 18.3 us -> 80.2 us
  waiting for transfers between devices: 91.5 us -> 71.8 us
  local copies, waits for them, and re-layouts: 4.94 us -> 2.36 us
    pallas_call x3 -> x5, Pallas kernels: 13.1 us -> 75 us  [the longest x2 61.8 us: cut_by_copy(): pl.pallas_call(functools.partial(cut_kernel, spans), in_specs=[pl.BlockSp...]
    ppermute x14, waiting for transfers between devices: 91.5 us -> 71.8 us  [fetched(): return lax.ppermute(piece, AXES, pairs)]
    dynamic_slice x3 -> x2, local copies, waits for them, and re-layouts: 4.93 us -> 2.35 us  [cut(): return lax.dynamic_slice_in_dim(whole, start, heads * HEAD_DIM, axis=3)]
  transfers between devices with their start and end apart: 16 -> 16, of which waited for: 8 -> 7; matrix products, arithmetic and copies ran while one was open for 3% -> 1% of each run, Pallas kernels for 10% -> 38%
where the time goes in v13:
time: 204 us
  Pallas kernels  80.2 us (39%)
  waiting for transfers between devices  71.8 us (35%)
  starting transfers between devices  37.4 us (18%)
  blocking collectives  9.83 us (5%)
  local copies, waits for them, and re-layouts  2.36 us (1%)
    ppermute x14, waiting for transfers between devices, fetched(): return lax.ppermute(piece, AXES, pairs)  71.8 us
    pallas_call x2, Pallas kernels, cut_by_copy(): pl.pallas_call(functools.partial(cut_kernel, spans), in_specs=[pl.BlockSp...  61.8 us
    ppermute x14, starting transfers between devices, fetched(): return lax.ppermute(piece, AXES, pairs)  30 us
    pallas_call x3, Pallas kernels, backward(): pl.pallas_call(functools.partial(backward_kernel, parts, carried is not N...  13.2 us
    psum x1, blocking collectives, on_device(): token_total = lax.psum(tokens, 'dp')  9.83 us
    ppermute x2, starting transfers between devices, shifted(): lax.ppermute(array, 'pipe', [(p, (p + by) % sections) for p in range(sect...  7.41 us
    pallas_call x1, Pallas kernels, forward(): pl.pallas_call(forward_kernel, grid=(FORWARD_STEPS,), in_specs=[pl.BlockS...  5.18 us
  transfers between devices with their start and end apart: 16, of which 7 were waited for; matrix products, arithmetic and copies ran while one was open for 1% of the time, Pallas kernels for 38%

profile of v13, /device:TPU:1, one launch (start us, length us, event | category | flops | bytes accessed | tf_op | source)
XLA Modules:
  0.0 203.6 jit_solution(11542744207032414586)
XLA Ops:
  0.6 7.4 %collective-permute-start.5 = (bf16[1,256,2048]{2,1,0:T(8,128)(2,1)}, bf16[1,256,2048]{2,1,0:T(8,128)(2,1)S(1)}, u32[]{:S(2)}, u32[]{:S(2)}) collective-permute-start(bf16[1,256,2048]{2,1,0:T(8,128)(2,1)} %param.10), channel_id=1, source_target_pairs={{0,240},{16,0},{32,16},{48,32},{64,48},{80,64},{96,80},{112,96},{1... | collective-permute-start | bytes 3145736 | tf_op jit(solution)/shard_map/direct_grad/ppermute | solution.py:200
  8.0 16.0 %shard_map.77 = bf16[3,1,64,1280]{3,2,1,0:T(8,128)(2,1)} custom-call(bf16[3,1,64,8192]{3,2,1,0:T(8,128)(2,1)} %whole_ref.2), custom_call_target="tpu_custom_call" | custom-call | tf_op jit(solution)/shard_map/pallas_call | solution.py:163
  24.0 2.7 %collective-permute-start = (bf16[3,1,64,1280]{3,2,1,0:T(8,128)(2,1)}, bf16[3,1,64,1280]{3,2,1,0:T(8,128)(2,1)S(1)}, u32[]{:S(2)}, u32[]{:S(2)}) collective-permute-start(bf16[3,1,64,1280]{3,2,1,0:T(8,128)(2,1)} %shard_map.77), channel_id=1, source_target_pairs={{0,252},{4,248},{8,244},{12,240},{16,236},{20,232},{24,228},{28,22... | collective-permute-start | bytes 1474568 | tf_op jit(solution)/shard_map/stash_3_0/ppermute | solution.py:188
  26.8 45.8 %shard_map.78 = (bf16[3,1,64,1280]{3,2,1,0:T(8,128)(2,1)}, bf16[3,1,64,1280]{3,2,1,0:T(8,128)(2,1)}, bf16[3,1,64,1280]{3,2,1,0:T(8,128)(2,1)}) custom-call(bf16[3,1,64,8192]{3,2,1,0:T(8,128)(2,1)} %whole_ref.2), custom_call_target="tpu_custom_call" | custom-call | tf_op jit(solution)/shard_map/pallas_call | solution.py:163
  72.6 0.0 copy-start
  72.6 1.9 collective-permute-start.8
  74.5 1.5 collective-permute-start.10
  76.0 5.2 %forward_heads.1 = bf16[1,256,2048]{2,1,0:T(8,128)(2,1)} custom-call(bf16[3,1,256,2048]{3,2,1,0:T(8,128)(2,1)} %qkv_ref.1, s32[1,256]{1,0:T(1,128)} %segment_ref.1), custom_call_target="tpu_custom_call" | custom-call | flops 536870912 | bytes 4194304 | tf_op jit(solution)/shard_map/forward_heads/pallas_call | solution.py:54
  81.2 0.0 collective-permute-start.6
  81.2 0.0 collective-permute-done.refs_3_
  81.2 4.1 %collective-permute-start.9 = (bf16[3,1,64,1280]{3,2,1,0:T(8,128)(2,1)}, bf16[3,1,64,1280]{3,2,1,0:T(8,128)(2,1)}, u32[]{:S(2)}, u32[]{:S(2)}) collective-permute-start(bf16[3,1,64,1280]{3,2,1,0:T(8,128)(2,1)} %get-tuple-element.20), channel_id=1, source_target_pairs={{0,248},{4,252},{8,240},{12,244},{16,232},{20,236},{24,224},{28,22... | collective-permute-start | bytes 1474568 | tf_op jit(solution)/shard_map/stash_2_0/ppermute | solution.py:188
  85.3 20.9 %collective-permute-done.8.refs_1_ = bf16[3,1,64,1280]{3,2,1,0:T(8,128)(2,1)S(1)} collective-permute-done((bf16[3,1,64,1280]{3,2,1,0:T(8,128)(2,1)}, bf16[3,1,64,1280]{3,2,1,0:T(8,128)(2,1)S(1)}, u32[]{:S(2)}, u32[]{:S(2)}) %collective-permute-start.8) | collective-permute-done | bytes 491552 | tf_op jit(solution)/shard_map/stash_1_0/ppermute | solution.py:188
  106.2 6.4 %collective-permute-start.7 = (bf16[3,1,64,1280]{3,2,1,0:T(8,128)(2,1)}, bf16[3,1,64,1280]{3,2,1,0:T(8,128)(2,1)}, u32[]{:S(2)}, u32[]{:S(2)}) collective-permute-start(bf16[3,1,64,1280]{3,2,1,0:T(8,128)(2,1)} %get-tuple-element.18), channel_id=1, source_target_pairs={{0,240},{4,244},{8,248},{12,252},{16,224},{20,228},{24,232},{28,23... | collective-permute-start | bytes 1474568 | tf_op jit(solution)/shard_map/stash_0_0/ppermute | solution.py:188
  112.6 0.0 collective-permute-done.10
  112.6 1.5 collective-permute-start.11
  114.7 9.8 %psum.7 = f32[1]{0:T(128)} all-reduce(f32[1]{0:T(128)S(6)} %convert_element_type.3), channel_id=1, replica_groups=mesh['pipe'=16,'tensor'=4,'dp'=4] {'dp'}, use_global_device_ids=true, to_apply=%region_0.0 | all-reduce | flops 1 | bytes 8 | tf_op jit(solution)/shard_map/psum | solution.py:237
  125.2 1.3 constant_dynamic-slice_fusion.4
  126.5 15.3 %collective-permute-done.9.refs_2_ = bf16[3,1,64,1280]{3,2,1,0:T(8,128)(2,1)} collective-permute-done((bf16[3,1,64,1280]{3,2,1,0:T(8,128)(2,1)}, bf16[3,1,64,1280]{3,2,1,0:T(8,128)(2,1)}, u32[]{:S(2)}, u32[]{:S(2)}) %collective-permute-start.9) | collective-permute-done | bytes 491552 | tf_op jit(solution)/shard_map/stash_2_0/ppermute | solution.py:188
  141.8 0.0 collective-permute-start.4
  141.8 26.3 %collective-permute-done.7.refs_0_ = bf16[3,1,64,1280]{3,2,1,0:T(8,128)(2,1)} collective-permute-done((bf16[3,1,64,1280]{3,2,1,0:T(8,128)(2,1)}, bf16[3,1,64,1280]{3,2,1,0:T(8,128)(2,1)}, u32[]{:S(2)}, u32[]{:S(2)}) %collective-permute-start.7) | collective-permute-done | bytes 491552 | tf_op jit(solution)/shard_map/stash_0_0/ppermute | solution.py:188
  168.1 0.2 collective-permute-start.3
  168.3 0.0 collective-permute-done.11.refs_4_
  168.3 4.7 %collective-permute-start.2 = (bf16[3,1,64,512]{3,2,1,0:T(8,128)(2,1)S(1)}, bf16[3,1,64,512]{3,2,1,0:T(8,128)(2,1)S(1)}, u32[]{:S(2)}, u32[]{:S(2)}) collective-permute-start(bf16[3,1,64,512]{3,2,1,0:T(8,128)(2,1)S(1)} %get-tuple-element.32), channel_id=1, source_target_pairs={{0,244},{4,240},{8,252},{12,248},{16,228},{20,224},{24,236},{28,23... | collective-permute-start | bytes 589832 | tf_op jit(solution)/shard_map/stash_1_1/ppermute | solution.py:188
  173.0 0.0 collective-permute-done.5.refs_5_.refs_4_
  173.0 1.3 collective-permute-start.1
  174.3 0.0 copy-done
  174.3 7.7 %shard_map.79.refs_8_ = bf16[3,1,256,2048]{3,2,1,0:T(8,128)(2,1)} custom-call(bf16[3,1,64,1280]{3,2,1,0:T(8,128)(2,1)} %collective-permute-done.7.refs_0_, bf16[3,1,64,1280]{3,2,1,0:T(8,128)(2,1)S(1)} %collective-permute-done.8.refs_1_, bf16[3,1,64,1280]{3,2,1,0:T(8,128)(2,1)} %collective-permute-done.9.refs_2_, ...), custom_call_target="tpu_custom_call" | custom-call | flops 838860800 | bytes 4587520 | tf_op jit(solution)/shard_map/pallas_call | solution.py:131
  181.9 1.1 constant_dynamic-slice_fusion
  183.0 0.0 collective-permute-done.4.refs_3_
  183.0 3.0 %collective-permute-start.15 = (bf16[3,1,64,256]{3,2,1,0:T(8,128)(2,1)S(1)}, bf16[3,1,64,256]{3,2,1,0:T(8,128)(2,1)S(1)}, u32[]{:S(2)}, u32[]{:S(2)}) collective-permute-start(bf16[3,1,64,256]{3,2,1,0:T(8,128)(2,1)S(1)} %get-tuple-element.26), channel_id=1, source_target_pairs={{0,252},{4,248},{8,244},{12,240},{16,236},{20,232},{24,228},{28,22... | collective-permute-start | bytes 294920 | tf_op jit(solution)/shard_map/stash_3_2/ppermute | solution.py:188
  186.1 0.0 collective-permute-done.3.refs_2_
  186.1 2.4 %collective-permute-start.14 = (bf16[3,1,64,256]{3,2,1,0:T(8,128)(2,1)S(1)}, bf16[3,1,64,256]{3,2,1,0:T(8,128)(2,1)S(1)}, u32[]{:S(2)}, u32[]{:S(2)}) collective-permute-start(bf16[3,1,64,256]{3,2,1,0:T(8,128)(2,1)S(1)} %get-tuple-element.27), channel_id=1, source_target_pairs={{0,248},{4,252},{8,240},{12,244},{16,232},{20,236},{24,224},{28,22... | collective-permute-start | bytes 294920 | tf_op jit(solution)/shard_map/stash_2_2/ppermute | solution.py:188
  188.5 2.6 %collective-permute-done.2.refs_1_ = bf16[3,1,64,512]{3,2,1,0:T(8,128)(2,1)S(1)} collective-permute-done((bf16[3,1,64,512]{3,2,1,0:T(8,128)(2,1)S(1)}, bf16[3,1,64,512]{3,2,1,0:T(8,128)(2,1)S(1)}, u32[]{:S(2)}, u32[]{:S(2)}) %collective-permute-start.2) | collective-permute-done | bytes 196640 | tf_op jit(solution)/shard_map/stash_1_1/ppermute | solution.py:188
  191.1 0.2 collective-permute-start.13
  191.3 2.0 collective-permute-done.1.refs_0_
  193.3 0.0 collective-permute-start.12
  193.3 0.0 collective-permute-done.6.refs_7_
  193.3 3.5 %shard_map.80 = (bf16[3,1,256,2048]{3,2,1,0:T(8,128)(2,1)}, bf16[1,256,2048]{2,1,0:T(8,128)(2,1)}) custom-call(bf16[3,1,64,512]{3,2,1,0:T(8,128)(2,1)S(1)} %collective-permute-done.1.refs_0_, bf16[3,1,64,512]{3,2,1,0:T(8,128)(2,1)S(1)} %collective-permute-done.2.refs_1_, ...), custom_call_target="tpu_custom_call", output_to_operand_aliasing={{0}: (8, {})} | custom-call | flops 335544320 | bytes 1835008 | tf_op jit(solution)/shard_map/pallas_call | solution.py:131
  196.8 1.1 collective-permute-done.15.refs_3_
  197.9 0.0 collective-permute-done.14.refs_2_
  197.9 3.6 %collective-permute-done.13.refs_1_ = bf16[3,1,64,256]{3,2,1,0:T(8,128)(2,1)S(1)} collective-permute-done((bf16[3,1,64,256]{3,2,1,0:T(8,128)(2,1)S(1)}, bf16[3,1,64,256]{3,2,1,0:T(8,128)(2,1)S(1)}, u32[]{:S(2)}, u32[]{:S(2)}) %collective-permute-start.13) | collective-permute-done | bytes 98336 | tf_op jit(solution)/shard_map/stash_1_2/ppermute | solution.py:188
  201.5 0.0 collective-permute-done.12.refs_0_
  201.5 2.1 %shard_map.81 = bf16[3,1,256,2048]{3,2,1,0:T(8,128)(2,1)} custom-call(bf16[3,1,64,256]{3,2,1,0:T(8,128)(2,1)S(1)} %collective-permute-done.12.refs_0_, bf16[3,1,64,256]{3,2,1,0:T(8,128)(2,1)S(1)} %collective-permute-done.13.refs_1_, bf16[3,1,64,256]{3,2,1,0:T(8,128)(2,1)S(1)} %collective-permute-done.14.refs_2_, ...), custom_call_target="tpu_custom_call", output_to_operand_aliasing={{}: (7, {})} | custom-call | flops 167772160 | bytes 917504 | tf_op jit(solution)/shard_map/pallas_call | solution.py:131
Async XLA Ops:
  0.6 172.3 %collective-permute-start.5 = (bf16[1,256,2048]{2,1,0:T(8,128)(2,1)}, bf16[1,256,2048]{2,1,0:T(8,128)(2,1)S(1)}, u32[]{:S(2)}, u32[]{:S(2)}) collective-permute-start(bf16[1,256,2048]{2,1,0:T(8,128)(2,1)} %param.10), channel_id=1, source_target_pairs={{0,240},{16,0},{32,16},{48,32},{64,48},{80,64},{96,80},{112,96},{1... | collective-permute-start | bytes 3145736 | tf_op jit(solution)/shard_map/direct_grad/ppermute | solution.py:200
  24.0 57.1 %collective-permute-start = (bf16[3,1,64,1280]{3,2,1,0:T(8,128)(2,1)}, bf16[3,1,64,1280]{3,2,1,0:T(8,128)(2,1)S(1)}, u32[]{:S(2)}, u32[]{:S(2)}) collective-permute-start(bf16[3,1,64,1280]{3,2,1,0:T(8,128)(2,1)} %shard_map.77), channel_id=1, source_target_pairs={{0,252},{4,248},{8,244},{12,240},{16,236},{20,232},{24,228},{28,22... | collective-permute-start | bytes 1474568 | tf_op jit(solution)/shard_map/stash_3_0/ppermute | solution.py:188
  72.6 101.7 %copy-start = (s32[1,256]{1,0:T(1,128)S(1)}, s32[1,256]{1,0:T(1,128)}, u32[]{:S(2)}) copy-start(s32[1,256]{1,0:T(1,128)} %refs_5_.3) | copy-start | bytes 3076
  72.6 33.6 %collective-permute-start.8 = (bf16[3,1,64,1280]{3,2,1,0:T(8,128)(2,1)}, bf16[3,1,64,1280]{3,2,1,0:T(8,128)(2,1)S(1)}, u32[]{:S(2)}, u32[]{:S(2)}) collective-permute-start(bf16[3,1,64,1280]{3,2,1,0:T(8,128)(2,1)} %get-tuple-element.19), channel_id=1, source_target_pairs={{0,244},{4,240},{8,252},{12,248},{16,228},{20,224},{24,236},{28,23... | collective-permute-start | bytes 1474568 | tf_op jit(solution)/shard_map/stash_1_0/ppermute | solution.py:188
  74.5 38.0 %collective-permute-start.10 = (bf16[3,1,64,1280]{3,2,1,0:T(8,128)(2,1)}, bf16[3,1,64,1280]{3,2,1,0:T(8,128)(2,1)}, u32[]{:S(2)}, u32[]{:S(2)}) collective-permute-start(bf16[3,1,64,1280]{3,2,1,0:T(8,128)(2,1)} %get-tuple-element.18), channel_id=1, source_target_pairs={{32,48},{36,52},{40,56},{44,60},{80,64},{84,68},{88,72},{92,76},{1... | collective-permute-start | bytes 1474568 | tf_op jit(solution)/shard_map/aside_0/ppermute | solution.py:188
  81.2 112.1 %collective-permute-start.6 = (bf16[1,256,2048]{2,1,0:T(8,128)(2,1)}, bf16[1,256,2048]{2,1,0:T(8,128)(2,1)S(1)}, u32[]{:S(2)}, u32[]{:S(2)}) collective-permute-start(bf16[1,256,2048]{2,1,0:T(8,128)(2,1)} %forward_heads.1), channel_id=1, source_target_pairs={{0,16},{16,32},{32,48},{48,64},{64,80},{80,96},{96,112},{112,128},... | collective-permute-start | bytes 3145736 | tf_op jit(solution)/shard_map/direct_out/ppermute | solution.py:200
  81.2 60.6 %collective-permute-start.9 = (bf16[3,1,64,1280]{3,2,1,0:T(8,128)(2,1)}, bf16[3,1,64,1280]{3,2,1,0:T(8,128)(2,1)}, u32[]{:S(2)}, u32[]{:S(2)}) collective-permute-start(bf16[3,1,64,1280]{3,2,1,0:T(8,128)(2,1)} %get-tuple-element.20), channel_id=1, source_target_pairs={{0,248},{4,252},{8,240},{12,244},{16,232},{20,236},{24,224},{28,22... | collective-permute-start | bytes 1474568 | tf_op jit(solution)/shard_map/stash_2_0/ppermute | solution.py:188
  106.2 61.9 %collective-permute-start.7 = (bf16[3,1,64,1280]{3,2,1,0:T(8,128)(2,1)}, bf16[3,1,64,1280]{3,2,1,0:T(8,128)(2,1)}, u32[]{:S(2)}, u32[]{:S(2)}) collective-permute-start(bf16[3,1,64,1280]{3,2,1,0:T(8,128)(2,1)} %get-tuple-element.18), channel_id=1, source_target_pairs={{0,240},{4,244},{8,248},{12,252},{16,224},{20,228},{24,232},{28,23... | collective-permute-start | bytes 1474568 | tf_op jit(solution)/shard_map/stash_0_0/ppermute | solution.py:188
  112.6 55.7 %collective-permute-start.11 = (bf16[3,1,64,1280]{3,2,1,0:T(8,128)(2,1)}, bf16[3,1,64,1280]{3,2,1,0:T(8,128)(2,1)}, u32[]{:S(2)}, u32[]{:S(2)}) collective-permute-start(bf16[3,1,64,1280]{3,2,1,0:T(8,128)(2,1)} %collective-permute-done.10), channel_id=1, source_target_pairs={{48,208},{52,212},{56,216},{60,220},{64,160},{68,164},{72,168},{76... | collective-permute-start | bytes 1474568 | tf_op jit(solution)/shard_map/onward_0/ppermute | solution.py:188
  141.8 41.3 %collective-permute-start.4 = (bf16[3,1,64,512]{3,2,1,0:T(8,128)(2,1)S(1)}, bf16[3,1,64,512]{3,2,1,0:T(8,128)(2,1)S(1)}, u32[]{:S(2)}, u32[]{:S(2)}) collective-permute-start(bf16[3,1,64,512]{3,2,1,0:T(8,128)(2,1)S(1)} %get-tuple-element.30), channel_id=1, source_target_pairs={{0,252},{4,248},{8,244},{12,240},{16,236},{20,232},{24,228},{28,22... | collective-permute-start | bytes 589832 | tf_op jit(solution)/shard_map/stash_3_1/ppermute | solution.py:188
  168.1 18.0 %collective-permute-start.3 = (bf16[3,1,64,512]{3,2,1,0:T(8,128)(2,1)S(1)}, bf16[3,1,64,512]{3,2,1,0:T(8,128)(2,1)S(1)}, u32[]{:S(2)}, u32[]{:S(2)}) collective-permute-start(bf16[3,1,64,512]{3,2,1,0:T(8,128)(2,1)S(1)} %get-tuple-element.31), channel_id=1, source_target_pairs={{0,248},{4,252},{8,240},{12,244},{16,232},{20,236},{24,224},{28,22... | collective-permute-start | bytes 589832 | tf_op jit(solution)/shard_map/stash_2_1/ppermute | solution.py:188
  168.3 22.8 %collective-permute-start.2 = (bf16[3,1,64,512]{3,2,1,0:T(8,128)(2,1)S(1)}, bf16[3,1,64,512]{3,2,1,0:T(8,128)(2,1)S(1)}, u32[]{:S(2)}, u32[]{:S(2)}) collective-permute-start(bf16[3,1,64,512]{3,2,1,0:T(8,128)(2,1)S(1)} %get-tuple-element.32), channel_id=1, source_target_pairs={{0,244},{4,240},{8,252},{12,248},{16,228},{20,224},{24,236},{28,23... | collective-permute-start | bytes 589832 | tf_op jit(solution)/shard_map/stash_1_1/ppermute | solution.py:188
  173.0 20.3 %collective-permute-start.1 = (bf16[3,1,64,512]{3,2,1,0:T(8,128)(2,1)S(1)}, bf16[3,1,64,512]{3,2,1,0:T(8,128)(2,1)S(1)}, u32[]{:S(2)}, u32[]{:S(2)}) collective-permute-start(bf16[3,1,64,512]{3,2,1,0:T(8,128)(2,1)S(1)} %get-tuple-element.33), channel_id=1, source_target_pairs={{0,240},{4,244},{8,248},{12,252},{16,224},{20,228},{24,232},{28,23... | collective-permute-start | bytes 589832 | tf_op jit(solution)/shard_map/stash_0_1/ppermute | solution.py:188
  183.0 14.8 %collective-permute-start.15 = (bf16[3,1,64,256]{3,2,1,0:T(8,128)(2,1)S(1)}, bf16[3,1,64,256]{3,2,1,0:T(8,128)(2,1)S(1)}, u32[]{:S(2)}, u32[]{:S(2)}) collective-permute-start(bf16[3,1,64,256]{3,2,1,0:T(8,128)(2,1)S(1)} %get-tuple-element.26), channel_id=1, source_target_pairs={{0,252},{4,248},{8,244},{12,240},{16,236},{20,232},{24,228},{28,22... | collective-permute-start | bytes 294920 | tf_op jit(solution)/shard_map/stash_3_2/ppermute | solution.py:188
  186.1 11.8 %collective-permute-start.14 = (bf16[3,1,64,256]{3,2,1,0:T(8,128)(2,1)S(1)}, bf16[3,1,64,256]{3,2,1,0:T(8,128)(2,1)S(1)}, u32[]{:S(2)}, u32[]{:S(2)}) collective-permute-start(bf16[3,1,64,256]{3,2,1,0:T(8,128)(2,1)S(1)} %get-tuple-element.27), channel_id=1, source_target_pairs={{0,248},{4,252},{8,240},{12,244},{16,232},{20,236},{24,224},{28,22... | collective-permute-start | bytes 294920 | tf_op jit(solution)/shard_map/stash_2_2/ppermute | solution.py:188
  191.1 10.4 %collective-permute-start.13 = (bf16[3,1,64,256]{3,2,1,0:T(8,128)(2,1)S(1)}, bf16[3,1,64,256]{3,2,1,0:T(8,128)(2,1)S(1)}, u32[]{:S(2)}, u32[]{:S(2)}) collective-permute-start(bf16[3,1,64,256]{3,2,1,0:T(8,128)(2,1)S(1)} %get-tuple-element.28), channel_id=1, source_target_pairs={{0,244},{4,240},{8,252},{12,248},{16,228},{20,224},{24,236},{28,23... | collective-permute-start | bytes 294920 | tf_op jit(solution)/shard_map/stash_1_2/ppermute | solution.py:188
  193.3 8.2 %collective-permute-start.12 = (bf16[3,1,64,256]{3,2,1,0:T(8,128)(2,1)S(1)}, bf16[3,1,64,256]{3,2,1,0:T(8,128)(2,1)S(1)}, u32[]{:S(2)}, u32[]{:S(2)}) collective-permute-start(bf16[3,1,64,256]{3,2,1,0:T(8,128)(2,1)S(1)} %get-tuple-element.29), channel_id=1, source_target_pairs={{0,240},{4,244},{8,248},{12,252},{16,224},{20,228},{24,232},{28,23... | collective-permute-start | bytes 294920 | tf_op jit(solution)/shard_map/stash_0_2/ppermute | solution.py:188

commit v14 on v12

--- a/solution.py
+++ b/solution.py
@@ -219,7 +219,10 @@
     pieces.append(fetched_chunk(parked, 1, range(tensors)))
     (grads,) = backward(0, pieces[0], around, upstream, bwd_segments, factor, None)
     parked, grads = lax.optimization_barrier((parked, grads))
-    pieces.append(fetched_chunk(parked, 2, range(tensors)))
+    others = fetched_chunk(parked, 2, range(3))
+    parked, received = lax.optimization_barrier((parked, received))
+    final = fetched_chunk(parked, 2, [3])
+    pieces.append([*others, *final])
     grads, received = backward(
         1, pieces[1], around, upstream, bwd_segments, factor, grads, received
     )

time: 164 us -> 163 us (level)
  starting transfers between devices: 43.5 us -> 38.7 us
  waiting for transfers between devices: 80.8 us -> 84.8 us
    ppermute x14, starting transfers between devices: 42.1 us -> 37.2 us  [fetched(): return lax.ppermute(piece, AXES, pairs)]
    ppermute x14, waiting for transfers between devices: 80.8 us -> 84.8 us  [fetched(): return lax.ppermute(piece, AXES, pairs)]
    dynamic_slice x4 -> x5, local copies, waits for them, and re-layouts: 6.61 us -> 7.46 us  [cut(): return lax.dynamic_slice_in_dim(whole, start, heads * HEAD_DIM, axis=3)]
  transfers between devices with their start and end apart: 16 -> 16, of which waited for: 4 -> 5; matrix products, arithmetic and copies ran while one was open for 3% -> 3% of each run, Pallas kernels for 10% -> 10%
where the time goes in v14:
time: 163 us; the launch traced here: 161 us
  waiting for transfers between devices  84.8 us (52%)
  starting transfers between devices  38.7 us (24%)
  Pallas kernels  18.3 us (11%)
  blocking collectives  10 us (6%)
  local copies, waits for them, and re-layouts  7.46 us (5%)
  between operations  1.98 us (1%)
    ppermute x14, waiting for transfers between devices, fetched(): return lax.ppermute(piece, AXES, pairs)  84.8 us
    ppermute x14, starting transfers between devices, fetched(): return lax.ppermute(piece, AXES, pairs)  37.2 us
    pallas_call x3, Pallas kernels, backward(): pl.pallas_call(functools.partial(backward_kernel, parts, around_from, car...  13.1 us
    psum x1, blocking collectives, on_device(): token_total = lax.psum(tokens, 'dp')  10 us
    dynamic_slice x5, local copies, waits for them, and re-layouts, cut(): return lax.dynamic_slice_in_dim(whole, start, heads * HEAD_DIM, axis=3)  7.46 us
    pallas_call x1, Pallas kernels, forward(): pl.pallas_call(forward_kernel, grid=(FORWARD_STEPS,), in_specs=[pl.BlockS...  5.18 us
  transfers between devices with their start and end apart: 16, of which 5 were waited for; matrix products, arithmetic and copies ran while one was open for 3% of the time, Pallas kernels for 10%

profile of v14, /device:TPU:1, one launch (start us, length us, event | category | flops | bytes accessed | tf_op | source)
XLA Modules:
  0.0 161.3 jit_solution(12025092208262805015)
XLA Ops:
  0.6 1.9 %constant_dynamic-slice_fusion.11 = bf16[3,1,64,1280]{3,2,1,0:T(8,128)(2,1)} fusion(bf16[3,1,64,8192]{3,2,1,0:T(8,128)(2,1)} %param.8, s32[]{:T(128)S(6)} %select_n.37), kind=kLoop, calls=%fused_computation.11 | loop fusion | bytes 983044 | tf_op jit(solution)/shard_map/dynamic_slice | solution.py:189
  2.5 9.2 %collective-permute-start = (bf16[3,1,64,1280]{3,2,1,0:T(8,128)(2,1)}, bf16[3,1,64,1280]{3,2,1,0:T(8,128)(2,1)S(1)}, u32[]{:S(2)}, u32[]{:S(2)}) collective-permute-start(bf16[3,1,64,1280]{3,2,1,0:T(8,128)(2,1)} %constant_dynamic-slice_fusion.11), channel_id=1, source_target_pairs={{0,252},{4,248},{8,244},{12,240},{16,236},{20,232},{24,228},{28,22... | collective-permute-start | bytes 1474568 | tf_op jit(solution)/shard_map/stash_3_0/ppermute | solution.py:167
  11.7 0.0 collective-permute-start.5
  11.7 2.4 %constant_dynamic-slice_fusion.4 = (bf16[3,1,64,1280]{3,2,1,0:T(8,128)(2,1)S(1)}, bf16[3,1,64,1280]{3,2,1,0:T(8,128)(2,1)}, bf16[3,1,64,1280]{3,2,1,0:T(8,128)(2,1)}) fusion(bf16[3,1,64,8192]{3,2,1,0:T(8,128)(2,1)} %param.8, s32[]{:T(128)S(6)} %select_n.44, s32[]{:T(128)S(6)} %select_n.43, s32[]{:T(128)S(6)} %select_n.42), kind=kLoop, calls=%fused_computation.4 | loop fusion | bytes 2949132 | tf_op jit(solution)/shard_map/stash_2_0/dynamic_slice | solution.py:189
  14.1 0.0 copy-start
  14.1 0.0 collective-permute-start.8
  14.1 1.6 collective-permute-start.9
  15.7 5.2 %forward_heads.1 = bf16[1,256,2048]{2,1,0:T(8,128)(2,1)} custom-call(bf16[3,1,256,2048]{3,2,1,0:T(8,128)(2,1)} %qkv_ref.1, s32[1,256]{1,0:T(1,128)} %segment_ref.1), custom_call_target="tpu_custom_call" | custom-call | flops 536870912 | bytes 4194304 | tf_op jit(solution)/shard_map/forward_heads/pallas_call | solution.py:55
  20.8 1.5 collective-permute-start.11
  22.3 22.1 %collective-permute-done.refs_3_ = bf16[3,1,64,1280]{3,2,1,0:T(8,128)(2,1)S(1)} collective-permute-done((bf16[3,1,64,1280]{3,2,1,0:T(8,128)(2,1)}, bf16[3,1,64,1280]{3,2,1,0:T(8,128)(2,1)S(1)}, u32[]{:S(2)}, u32[]{:S(2)}) %collective-permute-start) | collective-permute-done | bytes 491552 | tf_op jit(solution)/shard_map/stash_3_0/ppermute | solution.py:167
  44.4 0.0 collective-permute-start.7
  44.4 43.2 %collective-permute-done.8.refs_2_ = bf16[3,1,64,1280]{3,2,1,0:T(8,128)(2,1)S(1)} collective-permute-done((bf16[3,1,64,1280]{3,2,1,0:T(8,128)(2,1)S(1)}, bf16[3,1,64,1280]{3,2,1,0:T(8,128)(2,1)S(1)}, u32[]{:S(2)}, u32[]{:S(2)}) %collective-permute-start.8) | collective-permute-done | bytes 491552 | tf_op jit(solution)/shard_map/stash_2_0/ppermute | solution.py:167
  87.6 4.9 %collective-permute-start.6 = (bf16[3,1,64,1280]{3,2,1,0:T(8,128)(2,1)}, bf16[3,1,64,1280]{3,2,1,0:T(8,128)(2,1)}, u32[]{:S(2)}, u32[]{:S(2)}) collective-permute-start(bf16[3,1,64,1280]{3,2,1,0:T(8,128)(2,1)} %get-tuple-element.29), channel_id=1, source_target_pairs={{0,240},{4,244},{8,248},{12,252},{16,224},{20,228},{24,232},{28,23... | collective-permute-start | bytes 1474568 | tf_op jit(solution)/shard_map/stash_0_0/ppermute | solution.py:167
  92.5 0.0 collective-permute-done.9
  92.5 1.5 collective-permute-start.10
  94.7 10.0 %psum.7 = f32[1]{0:T(128)} all-reduce(f32[1]{0:T(128)S(6)} %convert_element_type.3), channel_id=1, replica_groups=mesh['pipe'=16,'tensor'=4,'dp'=4] {'dp'}, use_global_device_ids=true, to_apply=%region_0.0 | all-reduce | flops 1 | bytes 8 | tf_op jit(solution)/shard_map/psum | solution.py:216
  105.3 1.3 constant_dynamic-slice_fusion.7
  106.6 0.0 collective-permute-done.7.refs_1_
  106.6 4.1 %collective-permute-start.4 = (bf16[3,1,64,512]{3,2,1,0:T(8,128)(2,1)S(1)}, bf16[3,1,64,512]{3,2,1,0:T(8,128)(2,1)S(1)}, u32[]{:S(2)}, u32[]{:S(2)}) collective-permute-start(bf16[3,1,64,512]{3,2,1,0:T(8,128)(2,1)S(1)} %get-tuple-element.30), channel_id=1, source_target_pairs={{0,252},{4,248},{8,244},{12,240},{16,236},{20,232},{24,228},{28,22... | collective-permute-start | bytes 589832 | tf_op jit(solution)/shard_map/stash_3_1/ppermute | solution.py:167
  110.7 15.8 %collective-permute-done.6.refs_0_ = bf16[3,1,64,1280]{3,2,1,0:T(8,128)(2,1)} collective-permute-done((bf16[3,1,64,1280]{3,2,1,0:T(8,128)(2,1)}, bf16[3,1,64,1280]{3,2,1,0:T(8,128)(2,1)}, u32[]{:S(2)}, u32[]{:S(2)}) %collective-permute-start.6) | collective-permute-done | bytes 491552 | tf_op jit(solution)/shard_map/stash_0_0/ppermute | solution.py:167
  126.5 2.7 %collective-permute-start.3 = (bf16[3,1,64,512]{3,2,1,0:T(8,128)(2,1)S(1)}, bf16[3,1,64,512]{3,2,1,0:T(8,128)(2,1)S(1)}, u32[]{:S(2)}, u32[]{:S(2)}) collective-permute-start(bf16[3,1,64,512]{3,2,1,0:T(8,128)(2,1)S(1)} %get-tuple-element.31), channel_id=1, source_target_pairs={{0,248},{4,252},{8,240},{12,244},{16,232},{20,236},{24,224},{28,22... | collective-permute-start | bytes 589832 | tf_op jit(solution)/shard_map/stash_2_1/ppermute | solution.py:167
  129.2 0.0 collective-permute-done.10.refs_4_
  129.2 2.0 %collective-permute-start.2 = (bf16[3,1,64,512]{3,2,1,0:T(8,128)(2,1)S(1)}, bf16[3,1,64,512]{3,2,1,0:T(8,128)(2,1)S(1)}, u32[]{:S(2)}, u32[]{:S(2)}) collective-permute-start(bf16[3,1,64,512]{3,2,1,0:T(8,128)(2,1)S(1)} %get-tuple-element.32), channel_id=1, source_target_pairs={{0,244},{4,240},{8,252},{12,248},{16,228},{20,224},{24,236},{28,23... | collective-permute-start | bytes 589832 | tf_op jit(solution)/shard_map/stash_1_1/ppermute | solution.py:167
  131.3 0.0 collective-permute-done.5.refs_5_.refs_4_
  131.3 2.1 %collective-permute-start.1 = (bf16[3,1,64,512]{3,2,1,0:T(8,128)(2,1)S(1)}, bf16[3,1,64,512]{3,2,1,0:T(8,128)(2,1)S(1)}, u32[]{:S(2)}, u32[]{:S(2)}) collective-permute-start(bf16[3,1,64,512]{3,2,1,0:T(8,128)(2,1)S(1)} %get-tuple-element.33), channel_id=1, source_target_pairs={{0,240},{4,244},{8,248},{12,252},{16,224},{20,228},{24,232},{28,23... | collective-permute-start | bytes 589832 | tf_op jit(solution)/shard_map/stash_0_1/ppermute | solution.py:167
  133.4 0.0 copy-done
  133.4 7.6 %shard_map.77.refs_8_ = bf16[3,1,256,2048]{3,2,1,0:T(8,128)(2,1)} custom-call(bf16[3,1,64,1280]{3,2,1,0:T(8,128)(2,1)} %collective-permute-done.6.refs_0_, bf16[3,1,64,1280]{3,2,1,0:T(8,128)(2,1)} %collective-permute-done.7.refs_1_, bf16[3,1,64,1280]{3,2,1,0:T(8,128)(2,1)S(1)} %collective-permute-done.8.refs_2_, ...), custom_call_target="tpu_custom_call" | custom-call | flops 838860800 | bytes 4587520 | tf_op jit(solution)/shard_map/pallas_call | solution.py:138
  141.0 0.0 collective-permute-done.11.refs_7_
  141.0 0.9 constant_dynamic-slice_fusion
  141.9 2.7 %collective-permute-start.15 = (bf16[3,1,64,256]{3,2,1,0:T(8,128)(2,1)S(1)}, bf16[3,1,64,256]{3,2,1,0:T(8,128)(2,1)S(1)}, u32[]{:S(2)}, u32[]{:S(2)}) collective-permute-start(bf16[3,1,64,256]{3,2,1,0:T(8,128)(2,1)S(1)} %constant_dynamic-slice_fusion), channel_id=1, source_target_pairs={{0,252},{4,248},{8,244},{12,240},{16,236},{20,232},{24,228},{28,22... | collective-permute-start | bytes 294920 | tf_op jit(solution)/shard_map/stash_3_2/ppermute | solution.py:167
  144.6 1.0 constant_dynamic-slice_fusion.1
  145.6 0.0 collective-permute-done.4.refs_3_
  145.6 2.2 %collective-permute-start.14 = (bf16[3,1,64,256]{3,2,1,0:T(8,128)(2,1)S(1)}, bf16[3,1,64,256]{3,2,1,0:T(8,128)(2,1)S(1)}, u32[]{:S(2)}, u32[]{:S(2)}) collective-permute-start(bf16[3,1,64,256]{3,2,1,0:T(8,128)(2,1)S(1)} %get-tuple-element.24), channel_id=1, source_target_pairs={{0,248},{4,252},{8,240},{12,244},{16,232},{20,236},{24,224},{28,22... | collective-permute-start | bytes 294920 | tf_op jit(solution)/shard_map/stash_2_2/ppermute | solution.py:167
  147.8 0.0 collective-permute-done.3.refs_2_
  147.8 0.9 collective-permute-start.13
  148.7 0.0 collective-permute-done.2.refs_1_
  148.7 3.3 %collective-permute-start.12 = (bf16[3,1,64,256]{3,2,1,0:T(8,128)(2,1)S(1)}, bf16[3,1,64,256]{3,2,1,0:T(8,128)(2,1)S(1)}, u32[]{:S(2)}, u32[]{:S(2)}) collective-permute-start(bf16[3,1,64,256]{3,2,1,0:T(8,128)(2,1)S(1)} %get-tuple-element.26), channel_id=1, source_target_pairs={{0,240},{4,244},{8,248},{12,252},{16,224},{20,228},{24,232},{28,23... | collective-permute-start | bytes 294920 | tf_op jit(solution)/shard_map/stash_0_2/ppermute | solution.py:167
  152.0 0.0 collective-permute-done.1.refs_0_
  152.0 3.5 %shard_map.78 = (bf16[3,1,256,2048]{3,2,1,0:T(8,128)(2,1)}, bf16[1,256,2048]{2,1,0:T(8,128)(2,1)}) custom-call(bf16[3,1,64,512]{3,2,1,0:T(8,128)(2,1)S(1)} %collective-permute-done.1.refs_0_, bf16[3,1,64,512]{3,2,1,0:T(8,128)(2,1)S(1)} %collective-permute-done.2.refs_1_, ...), custom_call_target="tpu_custom_call", output_to_operand_aliasing={{0}: (8, {})} | custom-call | flops 335544320 | bytes 1835008 | tf_op jit(solution)/shard_map/pallas_call | solution.py:138
  155.4 0.0 collective-permute-done.15.refs_3_
  155.4 0.0 collective-permute-done.14.refs_2_
  155.4 1.6 %collective-permute-done.13.refs_1_ = bf16[3,1,64,256]{3,2,1,0:T(8,128)(2,1)S(1)} collective-permute-done((bf16[3,1,64,256]{3,2,1,0:T(8,128)(2,1)S(1)}, bf16[3,1,64,256]{3,2,1,0:T(8,128)(2,1)S(1)}, u32[]{:S(2)}, u32[]{:S(2)}) %collective-permute-start.13) | collective-permute-done | bytes 98336 | tf_op jit(solution)/shard_map/stash_1_2/ppermute | solution.py:167
  157.1 2.1 %collective-permute-done.12.refs_0_ = bf16[3,1,64,256]{3,2,1,0:T(8,128)(2,1)S(1)} collective-permute-done((bf16[3,1,64,256]{3,2,1,0:T(8,128)(2,1)S(1)}, bf16[3,1,64,256]{3,2,1,0:T(8,128)(2,1)S(1)}, u32[]{:S(2)}, u32[]{:S(2)}) %collective-permute-start.12) | collective-permute-done | bytes 98336 | tf_op jit(solution)/shard_map/stash_0_2/ppermute | solution.py:167
  159.2 2.1 %shard_map.79 = bf16[3,1,256,2048]{3,2,1,0:T(8,128)(2,1)} custom-call(bf16[3,1,64,256]{3,2,1,0:T(8,128)(2,1)S(1)} %collective-permute-done.12.refs_0_, bf16[3,1,64,256]{3,2,1,0:T(8,128)(2,1)S(1)} %collective-permute-done.13.refs_1_, bf16[3,1,64,256]{3,2,1,0:T(8,128)(2,1)S(1)} %collective-permute-done.14.refs_2_, ...), custom_call_target="tpu_custom_call", output_to_operand_aliasing={{}: (7, {})} | custom-call | flops 167772160 | bytes 917504 | tf_op jit(solution)/shard_map/pallas_call | solution.py:138
Async XLA Ops:
  2.5 41.9 %collective-permute-start = (bf16[3,1,64,1280]{3,2,1,0:T(8,128)(2,1)}, bf16[3,1,64,1280]{3,2,1,0:T(8,128)(2,1)S(1)}, u32[]{:S(2)}, u32[]{:S(2)}) collective-permute-start(bf16[3,1,64,1280]{3,2,1,0:T(8,128)(2,1)} %constant_dynamic-slice_fusion.11), channel_id=1, source_target_pairs={{0,252},{4,248},{8,244},{12,240},{16,236},{20,232},{24,228},{28,22... | collective-permute-start | bytes 1474568 | tf_op jit(solution)/shard_map/stash_3_0/ppermute | solution.py:167
  11.7 119.6 %collective-permute-start.5 = (bf16[1,256,2048]{2,1,0:T(8,128)(2,1)}, bf16[1,256,2048]{2,1,0:T(8,128)(2,1)S(1)}, u32[]{:S(2)}, u32[]{:S(2)}) collective-permute-start(bf16[1,256,2048]{2,1,0:T(8,128)(2,1)} %param.10), channel_id=1, source_target_pairs={{0,240},{16,0},{32,16},{48,32},{64,48},{80,64},{96,80},{112,96},{1... | collective-permute-start | bytes 3145736 | tf_op jit(solution)/shard_map/direct_grad/ppermute | solution.py:179
  14.1 119.3 %copy-start = (s32[1,256]{1,0:T(1,128)S(1)}, s32[1,256]{1,0:T(1,128)}, u32[]{:S(2)}) copy-start(s32[1,256]{1,0:T(1,128)} %refs_5_.3) | copy-start | bytes 3076
  14.1 73.5 %collective-permute-start.8 = (bf16[3,1,64,1280]{3,2,1,0:T(8,128)(2,1)S(1)}, bf16[3,1,64,1280]{3,2,1,0:T(8,128)(2,1)S(1)}, u32[]{:S(2)}, u32[]{:S(2)}) collective-permute-start(bf16[3,1,64,1280]{3,2,1,0:T(8,128)(2,1)S(1)} %get-tuple-element.27), channel_id=1, source_target_pairs={{0,248},{4,252},{8,240},{12,244},{16,232},{20,236},{24,224},{28,22... | collective-permute-start | bytes 1474568 | tf_op jit(solution)/shard_map/stash_2_0/ppermute | solution.py:167
  14.1 78.4 %collective-permute-start.9 = (bf16[3,1,64,1280]{3,2,1,0:T(8,128)(2,1)}, bf16[3,1,64,1280]{3,2,1,0:T(8,128)(2,1)}, u32[]{:S(2)}, u32[]{:S(2)}) collective-permute-start(bf16[3,1,64,1280]{3,2,1,0:T(8,128)(2,1)} %get-tuple-element.29), channel_id=1, source_target_pairs={{32,48},{36,52},{40,56},{44,60},{80,64},{84,68},{88,72},{92,76},{1... | collective-permute-start | bytes 1474568 | tf_op jit(solution)/shard_map/aside_0/ppermute | solution.py:167
  20.8 120.2 %collective-permute-start.11 = (bf16[1,256,2048]{2,1,0:T(8,128)(2,1)}, bf16[1,256,2048]{2,1,0:T(8,128)(2,1)S(1)}, u32[]{:S(2)}, u32[]{:S(2)}) collective-permute-start(bf16[1,256,2048]{2,1,0:T(8,128)(2,1)} %forward_heads.1), channel_id=1, source_target_pairs={{0,16},{16,32},{32,48},{48,64},{64,80},{80,96},{96,112},{112,128},... | collective-permute-start | bytes 3145736 | tf_op jit(solution)/shard_map/direct_out/ppermute | solution.py:179
  44.4 62.2 %collective-permute-start.7 = (bf16[3,1,64,1280]{3,2,1,0:T(8,128)(2,1)}, bf16[3,1,64,1280]{3,2,1,0:T(8,128)(2,1)}, u32[]{:S(2)}, u32[]{:S(2)}) collective-permute-start(bf16[3,1,64,1280]{3,2,1,0:T(8,128)(2,1)} %get-tuple-element.28), channel_id=1, source_target_pairs={{0,244},{4,240},{8,252},{12,248},{16,228},{20,224},{24,236},{28,23... | collective-permute-start | bytes 1474568 | tf_op jit(solution)/shard_map/stash_1_0/ppermute | solution.py:167
  87.6 38.9 %collective-permute-start.6 = (bf16[3,1,64,1280]{3,2,1,0:T(8,128)(2,1)}, bf16[3,1,64,1280]{3,2,1,0:T(8,128)(2,1)}, u32[]{:S(2)}, u32[]{:S(2)}) collective-permute-start(bf16[3,1,64,1280]{3,2,1,0:T(8,128)(2,1)} %get-tuple-element.29), channel_id=1, source_target_pairs={{0,240},{4,244},{8,248},{12,252},{16,224},{20,228},{24,232},{28,23... | collective-permute-start | bytes 1474568 | tf_op jit(solution)/shard_map/stash_0_0/ppermute | solution.py:167
  92.5 36.7 %collective-permute-start.10 = (bf16[3,1,64,1280]{3,2,1,0:T(8,128)(2,1)}, bf16[3,1,64,1280]{3,2,1,0:T(8,128)(2,1)}, u32[]{:S(2)}, u32[]{:S(2)}) collective-permute-start(bf16[3,1,64,1280]{3,2,1,0:T(8,128)(2,1)} %collective-permute-done.9), channel_id=1, source_target_pairs={{48,208},{52,212},{56,216},{60,220},{64,160},{68,164},{72,168},{76... | collective-permute-start | bytes 1474568 | tf_op jit(solution)/shard_map/onward_0/ppermute | solution.py:167
  106.6 39.0 %collective-permute-start.4 = (bf16[3,1,64,512]{3,2,1,0:T(8,128)(2,1)S(1)}, bf16[3,1,64,512]{3,2,1,0:T(8,128)(2,1)S(1)}, u32[]{:S(2)}, u32[]{:S(2)}) collective-permute-start(bf16[3,1,64,512]{3,2,1,0:T(8,128)(2,1)S(1)} %get-tuple-element.30), channel_id=1, source_target_pairs={{0,252},{4,248},{8,244},{12,240},{16,236},{20,232},{24,228},{28,22... | collective-permute-start | bytes 589832 | tf_op jit(solution)/shard_map/stash_3_1/ppermute | solution.py:167
  126.5 21.3 %collective-permute-start.3 = (bf16[3,1,64,512]{3,2,1,0:T(8,128)(2,1)S(1)}, bf16[3,1,64,512]{3,2,1,0:T(8,128)(2,1)S(1)}, u32[]{:S(2)}, u32[]{:S(2)}) collective-permute-start(bf16[3,1,64,512]{3,2,1,0:T(8,128)(2,1)S(1)} %get-tuple-element.31), channel_id=1, source_target_pairs={{0,248},{4,252},{8,240},{12,244},{16,232},{20,236},{24,224},{28,22... | collective-permute-start | bytes 589832 | tf_op jit(solution)/shard_map/stash_2_1/ppermute | solution.py:167
  129.2 19.5 %collective-permute-start.2 = (bf16[3,1,64,512]{3,2,1,0:T(8,128)(2,1)S(1)}, bf16[3,1,64,512]{3,2,1,0:T(8,128)(2,1)S(1)}, u32[]{:S(2)}, u32[]{:S(2)}) collective-permute-start(bf16[3,1,64,512]{3,2,1,0:T(8,128)(2,1)S(1)} %get-tuple-element.32), channel_id=1, source_target_pairs={{0,244},{4,240},{8,252},{12,248},{16,228},{20,224},{24,236},{28,23... | collective-permute-start | bytes 589832 | tf_op jit(solution)/shard_map/stash_1_1/ppermute | solution.py:167
  131.3 20.7 %collective-permute-start.1 = (bf16[3,1,64,512]{3,2,1,0:T(8,128)(2,1)S(1)}, bf16[3,1,64,512]{3,2,1,0:T(8,128)(2,1)S(1)}, u32[]{:S(2)}, u32[]{:S(2)}) collective-permute-start(bf16[3,1,64,512]{3,2,1,0:T(8,128)(2,1)S(1)} %get-tuple-element.33), channel_id=1, source_target_pairs={{0,240},{4,244},{8,248},{12,252},{16,224},{20,228},{24,232},{28,23... | collective-permute-start | bytes 589832 | tf_op jit(solution)/shard_map/stash_0_1/ppermute | solution.py:167
  141.9 13.5 %collective-permute-start.15 = (bf16[3,1,64,256]{3,2,1,0:T(8,128)(2,1)S(1)}, bf16[3,1,64,256]{3,2,1,0:T(8,128)(2,1)S(1)}, u32[]{:S(2)}, u32[]{:S(2)}) collective-permute-start(bf16[3,1,64,256]{3,2,1,0:T(8,128)(2,1)S(1)} %constant_dynamic-slice_fusion), channel_id=1, source_target_pairs={{0,252},{4,248},{8,244},{12,240},{16,236},{20,232},{24,228},{28,22... | collective-permute-start | bytes 294920 | tf_op jit(solution)/shard_map/stash_3_2/ppermute | solution.py:167
  145.6 9.8 %collective-permute-start.14 = (bf16[3,1,64,256]{3,2,1,0:T(8,128)(2,1)S(1)}, bf16[3,1,64,256]{3,2,1,0:T(8,128)(2,1)S(1)}, u32[]{:S(2)}, u32[]{:S(2)}) collective-permute-start(bf16[3,1,64,256]{3,2,1,0:T(8,128)(2,1)S(1)} %get-tuple-element.24), channel_id=1, source_target_pairs={{0,248},{4,252},{8,240},{12,244},{16,232},{20,236},{24,224},{28,22... | collective-permute-start | bytes 294920 | tf_op jit(solution)/shard_map/stash_2_2/ppermute | solution.py:167
  147.8 9.3 %collective-permute-start.13 = (bf16[3,1,64,256]{3,2,1,0:T(8,128)(2,1)S(1)}, bf16[3,1,64,256]{3,2,1,0:T(8,128)(2,1)S(1)}, u32[]{:S(2)}, u32[]{:S(2)}) collective-permute-start(bf16[3,1,64,256]{3,2,1,0:T(8,128)(2,1)S(1)} %get-tuple-element.25), channel_id=1, source_target_pairs={{0,244},{4,240},{8,252},{12,248},{16,228},{20,224},{24,236},{28,23... | collective-permute-start | bytes 294920 | tf_op jit(solution)/shard_map/stash_1_2/ppermute | solution.py:167
  148.7 10.5 %collective-permute-start.12 = (bf16[3,1,64,256]{3,2,1,0:T(8,128)(2,1)S(1)}, bf16[3,1,64,256]{3,2,1,0:T(8,128)(2,1)S(1)}, u32[]{:S(2)}, u32[]{:S(2)}) collective-permute-start(bf16[3,1,64,256]{3,2,1,0:T(8,128)(2,1)S(1)} %get-tuple-element.26), channel_id=1, source_target_pairs={{0,240},{4,244},{8,248},{12,252},{16,224},{20,228},{24,232},{28,23... | collective-permute-start | bytes 294920 | tf_op jit(solution)/shard_map/stash_0_2/ppermute | solution.py:167

commit v15 on v14

--- a/solution.py
+++ b/solution.py
@@ -11,7 +11,7 @@
 HEAD_DIM = 128
 FORWARD_STEPS = 2
 CHUNKS = ((0, 10), (12, 4), (10, 2))
-DETOUR = (0, 10)
+DETOUR = (0, 12)
 SCALE = HEAD_DIM ** (-0.5)
 EXPONENT = SCALE * math.log2(math.e)
 NT = (((1,), (1,)), ((), ()))

time: 163 us -> 168 us (1.031)
  starting transfers between devices: 38.7 us -> 48.9 us
  waiting for transfers between devices: 84.8 us -> 77.5 us
  local copies, waits for them, and re-layouts: 7.46 us -> 10.4 us
    ppermute x14, starting transfers between devices: 37.2 us -> 46.4 us  [fetched(): return lax.ppermute(piece, AXES, pairs)]
    ppermute x14, waiting for transfers between devices: 84.8 us -> 77.5 us  [fetched(): return lax.ppermute(piece, AXES, pairs)]
    unnamed x2 -> x6, local copies, waits for them, and re-layouts: 0.01 us -> 1.84 us
    dynamic_slice x5 -> x6, local copies, waits for them, and re-layouts: 7.46 us -> 8.55 us  [cut(): return lax.dynamic_slice_in_dim(whole, start, heads * HEAD_DIM, axis=3)]
  transfers between devices with their start and end apart: 16 -> 16, of which waited for: 5 -> 3; matrix products, arithmetic and copies ran while one was open for 3% -> 4% of each run, Pallas kernels for 10% -> 10%
where the time goes in v15:
time: 168 us; the launch traced here: 167 us
  waiting for transfers between devices  77.5 us (46%)
  starting transfers between devices  48.9 us (29%)
  Pallas kernels  18.2 us (11%)
  local copies, waits for them, and re-layouts  10.4 us (6%)
  blocking collectives  9.63 us (6%)
  between operations  2.02 us (1%)
    ppermute x14, waiting for transfers between devices, fetched(): return lax.ppermute(piece, AXES, pairs)  77.5 us
    ppermute x14, starting transfers between devices, fetched(): return lax.ppermute(piece, AXES, pairs)  46.4 us
    pallas_call x3, Pallas kernels, backward(): pl.pallas_call(functools.partial(backward_kernel, parts, around_from, car...  13 us
    psum x1, blocking collectives, on_device(): token_total = lax.psum(tokens, 'dp')  9.63 us
    dynamic_slice x6, local copies, waits for them, and re-layouts, cut(): return lax.dynamic_slice_in_dim(whole, start, heads * HEAD_DIM, axis=3)  8.55 us
    pallas_call x1, Pallas kernels, forward(): pl.pallas_call(forward_kernel, grid=(FORWARD_STEPS,), in_specs=[pl.BlockS...  5.19 us
  transfers between devices with their start and end apart: 16, of which 3 were waited for; matrix products, arithmetic and copies ran while one was open for 4% of the time, Pallas kernels for 10%

profile of v15, /device:TPU:1, one launch (start us, length us, event | category | flops | bytes accessed | tf_op | source)
XLA Modules:
  0.0 166.7 jit_solution(18038419018334801467)
XLA Ops:
  0.6 1.9 %constant_dynamic-slice_fusion.12 = bf16[3,1,64,1280]{3,2,1,0:T(8,128)(2,1)} fusion(bf16[3,1,64,8192]{3,2,1,0:T(8,128)(2,1)} %param.8, s32[]{:T(128)S(6)} %select_n.37), kind=kLoop, calls=%fused_computation.12 | loop fusion | bytes 983044 | tf_op jit(solution)/shard_map/dynamic_slice | solution.py:189
  2.5 9.2 %collective-permute-start = (bf16[3,1,64,1280]{3,2,1,0:T(8,128)(2,1)}, bf16[3,1,64,1280]{3,2,1,0:T(8,128)(2,1)S(1)}, u32[]{:S(2)}, u32[]{:S(2)}) collective-permute-start(bf16[3,1,64,1280]{3,2,1,0:T(8,128)(2,1)} %constant_dynamic-slice_fusion.12), channel_id=1, source_target_pairs={{0,252},{4,248},{8,244},{12,240},{16,236},{20,232},{24,228},{28,22... | collective-permute-start | bytes 1474568 | tf_op jit(solution)/shard_map/stash_3_0/ppermute | solution.py:167
  11.7 1.1 constant_dynamic-slice_fusion.4
  12.8 1.5 collective-permute-start.9
  14.3 0.0 collective-permute-start.5
  14.3 2.4 %constant_dynamic-slice_fusion.5 = (bf16[3,1,64,1280]{3,2,1,0:T(8,128)(2,1)S(1)}, bf16[3,1,64,1280]{3,2,1,0:T(8,128)(2,1)}, bf16[3,1,64,1280]{3,2,1,0:T(8,128)(2,1)}) fusion(bf16[3,1,64,8192]{3,2,1,0:T(8,128)(2,1)} %param.8, s32[]{:T(128)S(6)} %select_n.44, s32[]{:T(128)S(6)} %select_n.43, s32[]{:T(128)S(6)} %select_n.42), kind=kLoop, calls=%fused_computation.5 | loop fusion | bytes 2949132 | tf_op jit(solution)/shard_map/stash_2_0/dynamic_slice | solution.py:189
  16.7 0.0 copy-start.2
  16.7 0.0 collective-permute-start.8
  16.7 5.2 %forward_heads.1 = bf16[1,256,2048]{2,1,0:T(8,128)(2,1)} custom-call(bf16[3,1,256,2048]{3,2,1,0:T(8,128)(2,1)} %qkv_ref.1, s32[1,256]{1,0:T(1,128)} %segment_ref.1), custom_call_target="tpu_custom_call" | custom-call | flops 536870912 | bytes 4194304 | tf_op jit(solution)/shard_map/forward_heads/pallas_call | solution.py:55
  21.9 2.5 %collective-permute-start.11 = (bf16[1,256,2048]{2,1,0:T(8,128)(2,1)}, bf16[1,256,2048]{2,1,0:T(8,128)(2,1)S(1)}, u32[]{:S(2)}, u32[]{:S(2)}) collective-permute-start(bf16[1,256,2048]{2,1,0:T(8,128)(2,1)} %forward_heads.1), channel_id=1, source_target_pairs={{0,16},{16,32},{32,48},{48,64},{64,80},{80,96},{96,112},{112,128},... | collective-permute-start | bytes 3145736 | tf_op jit(solution)/shard_map/direct_out/ppermute | solution.py:179
  24.4 0.0 collective-permute-done.9
  24.4 0.7 collective-permute-start.10
  25.1 19.3 %collective-permute-done.refs_3_ = bf16[3,1,64,1280]{3,2,1,0:T(8,128)(2,1)S(1)} collective-permute-done((bf16[3,1,64,1280]{3,2,1,0:T(8,128)(2,1)}, bf16[3,1,64,1280]{3,2,1,0:T(8,128)(2,1)S(1)}, u32[]{:S(2)}, u32[]{:S(2)}) %collective-permute-start) | collective-permute-done | bytes 491552 | tf_op jit(solution)/shard_map/stash_3_0/ppermute | solution.py:167
  44.4 0.0 collective-permute-start.7
  44.4 51.6 %collective-permute-done.8.refs_2_ = bf16[3,1,64,1280]{3,2,1,0:T(8,128)(2,1)S(1)} collective-permute-done((bf16[3,1,64,1280]{3,2,1,0:T(8,128)(2,1)S(1)}, bf16[3,1,64,1280]{3,2,1,0:T(8,128)(2,1)S(1)}, u32[]{:S(2)}, u32[]{:S(2)}) %collective-permute-start.8) | collective-permute-done | bytes 491552 | tf_op jit(solution)/shard_map/stash_2_0/ppermute | solution.py:167
  96.0 0.0 copy-start
  96.0 0.8 copy-done
  96.8 13.5 %collective-permute-start.6 = (bf16[3,1,64,1280]{3,2,1,0:T(8,128)(2,1)}, bf16[3,1,64,1280]{3,2,1,0:T(8,128)(2,1)}, u32[]{:S(2)}, u32[]{:S(2)}) collective-permute-start(bf16[3,1,64,1280]{3,2,1,0:T(8,128)(2,1)} %get-tuple-element.29), channel_id=1, source_target_pairs={{0,240},{4,244},{8,248},{12,252},{16,224},{20,228},{24,232},{28,23... | collective-permute-start | bytes 1474568 | tf_op jit(solution)/shard_map/stash_0_0/ppermute | solution.py:167
  110.9 9.6 %psum.7 = f32[1]{0:T(128)} all-reduce(f32[1]{0:T(128)S(6)} %convert_element_type.3), channel_id=1, replica_groups=mesh['pipe'=16,'tensor'=4,'dp'=4] {'dp'}, use_global_device_ids=true, to_apply=%region_0.0 | all-reduce | flops 1 | bytes 8 | tf_op jit(solution)/shard_map/psum | solution.py:216
  121.2 1.3 constant_dynamic-slice_fusion.8
  122.5 0.0 collective-permute-done.7.refs_1_
  122.5 2.8 %collective-permute-start.4 = (bf16[3,1,64,512]{3,2,1,0:T(8,128)(2,1)S(1)}, bf16[3,1,64,512]{3,2,1,0:T(8,128)(2,1)S(1)}, u32[]{:S(2)}, u32[]{:S(2)}) collective-permute-start(bf16[3,1,64,512]{3,2,1,0:T(8,128)(2,1)S(1)} %get-tuple-element.30), channel_id=1, source_target_pairs={{0,252},{4,248},{8,244},{12,240},{16,236},{20,232},{24,228},{28,22... | collective-permute-start | bytes 589832 | tf_op jit(solution)/shard_map/stash_3_1/ppermute | solution.py:167
  125.3 6.6 %collective-permute-done.6.refs_0_ = bf16[3,1,64,1280]{3,2,1,0:T(8,128)(2,1)} collective-permute-done((bf16[3,1,64,1280]{3,2,1,0:T(8,128)(2,1)}, bf16[3,1,64,1280]{3,2,1,0:T(8,128)(2,1)}, u32[]{:S(2)}, u32[]{:S(2)}) %collective-permute-start.6) | collective-permute-done | bytes 491552 | tf_op jit(solution)/shard_map/stash_0_0/ppermute | solution.py:167
  131.9 3.6 %collective-permute-start.3 = (bf16[3,1,64,512]{3,2,1,0:T(8,128)(2,1)S(1)}, bf16[3,1,64,512]{3,2,1,0:T(8,128)(2,1)S(1)}, u32[]{:S(2)}, u32[]{:S(2)}) collective-permute-start(bf16[3,1,64,512]{3,2,1,0:T(8,128)(2,1)S(1)} %get-tuple-element.31), channel_id=1, source_target_pairs={{0,248},{4,252},{8,240},{12,244},{16,232},{20,236},{24,224},{28,22... | collective-permute-start | bytes 589832 | tf_op jit(solution)/shard_map/stash_2_1/ppermute | solution.py:167
  135.5 0.0 collective-permute-done.5.refs_5_.refs_4_
  135.5 1.0 collective-permute-start.2
  136.5 0.0 collective-permute-done.10.refs_4_
  136.5 3.2 %collective-permute-start.1 = (bf16[3,1,64,512]{3,2,1,0:T(8,128)(2,1)S(1)}, bf16[3,1,64,512]{3,2,1,0:T(8,128)(2,1)S(1)}, u32[]{:S(2)}, u32[]{:S(2)}) collective-permute-start(bf16[3,1,64,512]{3,2,1,0:T(8,128)(2,1)S(1)} %get-tuple-element.33), channel_id=1, source_target_pairs={{0,240},{4,244},{8,248},{12,252},{16,224},{20,228},{24,232},{28,23... | collective-permute-start | bytes 589832 | tf_op jit(solution)/shard_map/stash_0_1/ppermute | solution.py:167
  139.7 0.0 copy-done.2
  139.7 0.0 copy-start.1
  139.7 1.0 copy-done.1
  140.7 7.4 %shard_map.77.refs_8_ = bf16[3,1,256,2048]{3,2,1,0:T(8,128)(2,1)} custom-call(bf16[3,1,64,1280]{3,2,1,0:T(8,128)(2,1)} %collective-permute-done.6.refs_0_, bf16[3,1,64,1280]{3,2,1,0:T(8,128)(2,1)} %collective-permute-done.7.refs_1_, bf16[3,1,64,1280]{3,2,1,0:T(8,128)(2,1)S(1)} %copy-done.1, bf16[3,1,64,1280]{3,2,1,0:T(8,128)(2,1)S(1)} %collective-permute-done.refs_3_, ...), custom_call_target="tpu_custom_call" | custom-call | flops 838860800 | bytes 4587520 | tf_op jit(solution)/shard_map/pallas_call | solution.py:138
  148.2 0.0 collective-permute-done.11.refs_7_
  148.2 0.9 constant_dynamic-slice_fusion
  149.1 1.6 collective-permute-start.15
  150.7 1.0 constant_dynamic-slice_fusion.1
  151.7 0.0 collective-permute-done.4.refs_3_
  151.8 3.2 %collective-permute-start.14 = (bf16[3,1,64,256]{3,2,1,0:T(8,128)(2,1)S(1)}, bf16[3,1,64,256]{3,2,1,0:T(8,128)(2,1)S(1)}, u32[]{:S(2)}, u32[]{:S(2)}) collective-permute-start(bf16[3,1,64,256]{3,2,1,0:T(8,128)(2,1)S(1)} %get-tuple-element.24), channel_id=1, source_target_pairs={{0,248},{4,252},{8,240},{12,244},{16,232},{20,236},{24,224},{28,22... | collective-permute-start | bytes 294920 | tf_op jit(solution)/shard_map/stash_2_2/ppermute | solution.py:167
  155.0 0.0 collective-permute-done.3.refs_2_
  155.0 0.0 collective-permute-start.13
  155.0 0.0 collective-permute-done.2.refs_1_
  155.0 6.1 %collective-permute-start.12 = (bf16[3,1,64,256]{3,2,1,0:T(8,128)(2,1)S(1)}, bf16[3,1,64,256]{3,2,1,0:T(8,128)(2,1)S(1)}, u32[]{:S(2)}, u32[]{:S(2)}) collective-permute-start(bf16[3,1,64,256]{3,2,1,0:T(8,128)(2,1)S(1)} %get-tuple-element.26), channel_id=1, source_target_pairs={{0,240},{4,244},{8,248},{12,252},{16,224},{20,228},{24,232},{28,23... | collective-permute-start | bytes 294920 | tf_op jit(solution)/shard_map/stash_0_2/ppermute | solution.py:167
  161.1 0.0 collective-permute-done.1.refs_0_
  161.1 3.5 %shard_map.78 = (bf16[3,1,256,2048]{3,2,1,0:T(8,128)(2,1)}, bf16[1,256,2048]{2,1,0:T(8,128)(2,1)}) custom-call(bf16[3,1,64,512]{3,2,1,0:T(8,128)(2,1)S(1)} %collective-permute-done.1.refs_0_, bf16[3,1,64,512]{3,2,1,0:T(8,128)(2,1)S(1)} %collective-permute-done.2.refs_1_, ...), custom_call_target="tpu_custom_call", output_to_operand_aliasing={{0}: (8, {})} | custom-call | flops 335544320 | bytes 1835008 | tf_op jit(solution)/shard_map/pallas_call | solution.py:138
  164.5 0.0 collective-permute-done.15.refs_3_
  164.5 0.0 collective-permute-done.14.refs_2_
  164.5 0.0 collective-permute-done.13.refs_1_
  164.6 0.0 collective-permute-done.12.refs_0_
  164.6 2.1 %shard_map.79 = bf16[3,1,256,2048]{3,2,1,0:T(8,128)(2,1)} custom-call(bf16[3,1,64,256]{3,2,1,0:T(8,128)(2,1)S(1)} %collective-permute-done.12.refs_0_, bf16[3,1,64,256]{3,2,1,0:T(8,128)(2,1)S(1)} %collective-permute-done.13.refs_1_, bf16[3,1,64,256]{3,2,1,0:T(8,128)(2,1)S(1)} %collective-permute-done.14.refs_2_, ...), custom_call_target="tpu_custom_call", output_to_operand_aliasing={{}: (8, {})} | custom-call | flops 167772160 | bytes 917504 | tf_op jit(solution)/shard_map/pallas_call | solution.py:138
Async XLA Ops:
  2.5 41.9 %collective-permute-start = (bf16[3,1,64,1280]{3,2,1,0:T(8,128)(2,1)}, bf16[3,1,64,1280]{3,2,1,0:T(8,128)(2,1)S(1)}, u32[]{:S(2)}, u32[]{:S(2)}) collective-permute-start(bf16[3,1,64,1280]{3,2,1,0:T(8,128)(2,1)} %constant_dynamic-slice_fusion.12), channel_id=1, source_target_pairs={{0,252},{4,248},{8,244},{12,240},{16,236},{20,232},{24,228},{28,22... | collective-permute-start | bytes 1474568 | tf_op jit(solution)/shard_map/stash_3_0/ppermute | solution.py:167
  12.8 11.6 %collective-permute-start.9 = (bf16[3,1,64,1536]{3,2,1,0:T(8,128)(2,1)S(1)}, bf16[3,1,64,1536]{3,2,1,0:T(8,128)(2,1)}, u32[]{:S(2)}, u32[]{:S(2)}) collective-permute-start(bf16[3,1,64,1536]{3,2,1,0:T(8,128)(2,1)S(1)} %constant_dynamic-slice_fusion.4), channel_id=1, source_target_pairs={{32,48},{36,52},{40,56},{44,60},{80,64},{84,68},{88,72},{92,76},{1... | collective-permute-start | bytes 1769480 | tf_op jit(solution)/shard_map/aside_0/ppermute | solution.py:167
  14.3 121.3 %collective-permute-start.5 = (bf16[1,256,2048]{2,1,0:T(8,128)(2,1)}, bf16[1,256,2048]{2,1,0:T(8,128)(2,1)S(1)}, u32[]{:S(2)}, u32[]{:S(2)}) collective-permute-start(bf16[1,256,2048]{2,1,0:T(8,128)(2,1)} %param.10), channel_id=1, source_target_pairs={{0,240},{16,0},{32,16},{48,32},{64,48},{80,64},{96,80},{112,96},{1... | collective-permute-start | bytes 3145736 | tf_op jit(solution)/shard_map/direct_grad/ppermute | solution.py:179
  16.7 123.1 %copy-start.2 = (s32[1,256]{1,0:T(1,128)S(1)}, s32[1,256]{1,0:T(1,128)}, u32[]{:S(2)}) copy-start(s32[1,256]{1,0:T(1,128)} %refs_6_.3) | copy-start | bytes 3076
  16.7 79.3 %collective-permute-start.8 = (bf16[3,1,64,1280]{3,2,1,0:T(8,128)(2,1)S(1)}, bf16[3,1,64,1280]{3,2,1,0:T(8,128)(2,1)S(1)}, u32[]{:S(2)}, u32[]{:S(2)}) collective-permute-start(bf16[3,1,64,1280]{3,2,1,0:T(8,128)(2,1)S(1)} %get-tuple-element.27), channel_id=1, source_target_pairs={{0,248},{4,252},{8,240},{12,244},{16,232},{20,236},{24,224},{28,22... | collective-permute-start | bytes 1474568 | tf_op jit(solution)/shard_map/stash_2_0/ppermute | solution.py:167
  21.9 126.3 %collective-permute-start.11 = (bf16[1,256,2048]{2,1,0:T(8,128)(2,1)}, bf16[1,256,2048]{2,1,0:T(8,128)(2,1)S(1)}, u32[]{:S(2)}, u32[]{:S(2)}) collective-permute-start(bf16[1,256,2048]{2,1,0:T(8,128)(2,1)} %forward_heads.1), channel_id=1, source_target_pairs={{0,16},{16,32},{32,48},{48,64},{64,80},{80,96},{96,112},{112,128},... | collective-permute-start | bytes 3145736 | tf_op jit(solution)/shard_map/direct_out/ppermute | solution.py:179
  24.4 112.1 %collective-permute-start.10 = (bf16[3,1,64,1536]{3,2,1,0:T(8,128)(2,1)}, bf16[3,1,64,1536]{3,2,1,0:T(8,128)(2,1)S(1)}, u32[]{:S(2)}, u32[]{:S(2)}) collective-permute-start(bf16[3,1,64,1536]{3,2,1,0:T(8,128)(2,1)} %collective-permute-done.9), channel_id=1, source_target_pairs={{48,208},{52,212},{56,216},{60,220},{64,160},{68,164},{72,168},{76... | collective-permute-start | bytes 1769480 | tf_op jit(solution)/shard_map/onward_0/ppermute | solution.py:167
  44.4 78.1 %collective-permute-start.7 = (bf16[3,1,64,1280]{3,2,1,0:T(8,128)(2,1)}, bf16[3,1,64,1280]{3,2,1,0:T(8,128)(2,1)}, u32[]{:S(2)}, u32[]{:S(2)}) collective-permute-start(bf16[3,1,64,1280]{3,2,1,0:T(8,128)(2,1)} %get-tuple-element.28), channel_id=1, source_target_pairs={{0,244},{4,240},{8,252},{12,248},{16,228},{20,224},{24,236},{28,23... | collective-permute-start | bytes 1474568 | tf_op jit(solution)/shard_map/stash_1_0/ppermute | solution.py:167
  96.0 0.8 copy-start
  96.8 35.1 %collective-permute-start.6 = (bf16[3,1,64,1280]{3,2,1,0:T(8,128)(2,1)}, bf16[3,1,64,1280]{3,2,1,0:T(8,128)(2,1)}, u32[]{:S(2)}, u32[]{:S(2)}) collective-permute-start(bf16[3,1,64,1280]{3,2,1,0:T(8,128)(2,1)} %get-tuple-element.29), channel_id=1, source_target_pairs={{0,240},{4,244},{8,248},{12,252},{16,224},{20,228},{24,232},{28,23... | collective-permute-start | bytes 1474568 | tf_op jit(solution)/shard_map/stash_0_0/ppermute | solution.py:167
  122.5 29.3 %collective-permute-start.4 = (bf16[3,1,64,512]{3,2,1,0:T(8,128)(2,1)S(1)}, bf16[3,1,64,512]{3,2,1,0:T(8,128)(2,1)S(1)}, u32[]{:S(2)}, u32[]{:S(2)}) collective-permute-start(bf16[3,1,64,512]{3,2,1,0:T(8,128)(2,1)S(1)} %get-tuple-element.30), channel_id=1, source_target_pairs={{0,252},{4,248},{8,244},{12,240},{16,236},{20,232},{24,228},{28,22... | collective-permute-start | bytes 589832 | tf_op jit(solution)/shard_map/stash_3_1/ppermute | solution.py:167
  131.9 23.1 %collective-permute-start.3 = (bf16[3,1,64,512]{3,2,1,0:T(8,128)(2,1)S(1)}, bf16[3,1,64,512]{3,2,1,0:T(8,128)(2,1)S(1)}, u32[]{:S(2)}, u32[]{:S(2)}) collective-permute-start(bf16[3,1,64,512]{3,2,1,0:T(8,128)(2,1)S(1)} %get-tuple-element.31), channel_id=1, source_target_pairs={{0,248},{4,252},{8,240},{12,244},{16,232},{20,236},{24,224},{28,22... | collective-permute-start | bytes 589832 | tf_op jit(solution)/shard_map/stash_2_1/ppermute | solution.py:167
  135.5 19.4 %collective-permute-start.2 = (bf16[3,1,64,512]{3,2,1,0:T(8,128)(2,1)S(1)}, bf16[3,1,64,512]{3,2,1,0:T(8,128)(2,1)S(1)}, u32[]{:S(2)}, u32[]{:S(2)}) collective-permute-start(bf16[3,1,64,512]{3,2,1,0:T(8,128)(2,1)S(1)} %get-tuple-element.32), channel_id=1, source_target_pairs={{0,244},{4,240},{8,252},{12,248},{16,228},{20,224},{24,236},{28,23... | collective-permute-start | bytes 589832 | tf_op jit(solution)/shard_map/stash_1_1/ppermute | solution.py:167
  136.5 24.5 %collective-permute-start.1 = (bf16[3,1,64,512]{3,2,1,0:T(8,128)(2,1)S(1)}, bf16[3,1,64,512]{3,2,1,0:T(8,128)(2,1)S(1)}, u32[]{:S(2)}, u32[]{:S(2)}) collective-permute-start(bf16[3,1,64,512]{3,2,1,0:T(8,128)(2,1)S(1)} %get-tuple-element.33), channel_id=1, source_target_pairs={{0,240},{4,244},{8,248},{12,252},{16,224},{20,228},{24,232},{28,23... | collective-permute-start | bytes 589832 | tf_op jit(solution)/shard_map/stash_0_1/ppermute | solution.py:167
  139.7 1.0 copy-start.1
  149.1 15.5 %collective-permute-start.15 = (bf16[3,1,64,256]{3,2,1,0:T(8,128)(2,1)S(1)}, bf16[3,1,64,256]{3,2,1,0:T(8,128)(2,1)S(1)}, u32[]{:S(2)}, u32[]{:S(2)}) collective-permute-start(bf16[3,1,64,256]{3,2,1,0:T(8,128)(2,1)S(1)} %constant_dynamic-slice_fusion), channel_id=1, source_target_pairs={{0,252},{4,248},{8,244},{12,240},{16,236},{20,232},{24,228},{28,22... | collective-permute-start | bytes 294920 | tf_op jit(solution)/shard_map/stash_3_2/ppermute | solution.py:167
  151.8 12.8 %collective-permute-start.14 = (bf16[3,1,64,256]{3,2,1,0:T(8,128)(2,1)S(1)}, bf16[3,1,64,256]{3,2,1,0:T(8,128)(2,1)S(1)}, u32[]{:S(2)}, u32[]{:S(2)}) collective-permute-start(bf16[3,1,64,256]{3,2,1,0:T(8,128)(2,1)S(1)} %get-tuple-element.24), channel_id=1, source_target_pairs={{0,248},{4,252},{8,240},{12,244},{16,232},{20,236},{24,224},{28,22... | collective-permute-start | bytes 294920 | tf_op jit(solution)/shard_map/stash_2_2/ppermute | solution.py:167
  155.0 9.6 %collective-permute-start.13 = (bf16[3,1,64,256]{3,2,1,0:T(8,128)(2,1)S(1)}, bf16[3,1,64,256]{3,2,1,0:T(8,128)(2,1)S(1)}, u32[]{:S(2)}, u32[]{:S(2)}) collective-permute-start(bf16[3,1,64,256]{3,2,1,0:T(8,128)(2,1)S(1)} %get-tuple-element.25), channel_id=1, source_target_pairs={{0,244},{4,240},{8,252},{12,248},{16,228},{20,224},{24,236},{28,23... | collective-permute-start | bytes 294920 | tf_op jit(solution)/shard_map/stash_1_2/ppermute | solution.py:167
  155.0 9.6 %collective-permute-start.12 = (bf16[3,1,64,256]{3,2,1,0:T(8,128)(2,1)S(1)}, bf16[3,1,64,256]{3,2,1,0:T(8,128)(2,1)S(1)}, u32[]{:S(2)}, u32[]{:S(2)}) collective-permute-start(bf16[3,1,64,256]{3,2,1,0:T(8,128)(2,1)S(1)} %get-tuple-element.26), channel_id=1, source_target_pairs={{0,240},{4,244},{8,248},{12,252},{16,224},{20,228},{24,232},{28,23... | collective-permute-start | bytes 294920 | tf_op jit(solution)/shard_map/stash_0_2/ppermute | solution.py:167

commit v16 on v14

--- a/solution.py
+++ b/solution.py
@@ -71,7 +71,7 @@
     )(qkv, segment)
 
 
-def backward_kernel(parts, around_from, carries, *refs):
+def backward_kernel(parts, around_from, goes, carries, *refs):
     pieces, refs = refs[:parts], refs[parts:]
     upstream_ref, segment_ref, factor_ref = refs[:3]
     out_ref, stash = refs[-2:]
@@ -86,7 +86,8 @@
         pieces = pieces[:-1]
     found = [piece[:, 0] for piece in pieces]
     if around_from is not None:
-        found[0] = jnp.where(detoured(lax.axis_index("pipe")), around, found[0])
+        source = lax.axis_size("pipe") - 1 - lax.axis_index("pipe")
+        found[0] = jnp.where(goes(source), around, found[0])
     for k, piece in enumerate(found):
         start = pl.multiple_of((mine ^ k) * rows, rows)
         stash[:, pl.ds(start, rows), :] = piece
@@ -112,8 +113,9 @@
     step = heads * HEAD_DIM
     place = first // heads
     around_from = None
-    if DETOUR[0] <= first and first + heads <= sum(DETOUR):
-        around_from = (first - DETOUR[0]) * HEAD_DIM
+    goes = detoured if chunk == 0 else detoured_late
+    if around is not None:
+        around_from = 0
         pieces = [*pieces, around]
     parts = len(pieces)
     operands = [*pieces, upstream, segment, factor]
@@ -136,7 +138,7 @@
         operands.append(earlier)
         in_specs.append(pl.BlockSpec(memory_space=pl.ANY))
     return pl.pallas_call(
-        functools.partial(backward_kernel, parts, around_from, carried is not None),
+        functools.partial(backward_kernel, parts, around_from, goes, carried is not None),
         grid=(1,),
         in_specs=in_specs,
         out_specs=out_specs,
@@ -152,8 +154,9 @@
     )(*operands)
 
 
-def fetched(piece, k, leg="direct"):
+def fetched(piece, k, leg="direct", goes=None):
     sections, tensors = lax.axis_size("pipe"), lax.axis_size("tensor")
+    goes = goes or detoured
     pairs = []
     for p in range(sections):
         for t in range(tensors):
@@ -162,7 +165,7 @@
                 end = p ^ 1
             if leg == "onward":
                 start = p ^ 1
-            if leg == "all" or (leg == "direct") != detoured(p):
+            if leg == "all" or (leg == "direct") != goes(p):
                 pairs.append((start * tensors + t, end * tensors + (t ^ k)))
     return lax.ppermute(piece, AXES, pairs)
 
@@ -173,6 +176,10 @@
     return (place == 2) | (place == half - 3)
 
 
+def detoured_late(section):
+    return section == lax.axis_size("pipe") - 3
+
+
 def shifted(array, by):
     sections = lax.axis_size("pipe")
     with jax.named_scope("direct_out" if by > 0 else "direct_grad"):
@@ -192,10 +199,10 @@
         first, heads = CHUNKS[chunk]
         pieces = []
         for k in partners:
-            goes_around = k == 0 and DETOUR[0] <= first and first + heads <= sum(DETOUR)
+            leg = "direct" if k == 0 and chunk != 1 else "all"
+            goes = detoured if chunk == 0 else detoured_late
             with jax.named_scope(f"stash_{k}_{chunk}"):
-                piece = cut(whole, k, first, heads)
-                pieces.append(fetched(piece, k, "direct" if goes_around else "all"))
+                pieces.append(fetched(cut(whole, k, first, heads), k, leg, goes))
         return pieces
 
     upstream = shifted(grad_out, -1)
@@ -221,12 +228,16 @@
     parked, grads = lax.optimization_barrier((parked, grads))
     others = fetched_chunk(parked, 2, range(3))
     parked, received = lax.optimization_barrier((parked, received))
+    with jax.named_scope("aside_2"):
+        late = fetched(cut(parked, 0, *CHUNKS[2]), 0, "aside", detoured_late)
+    with jax.named_scope("onward_2"):
+        late = fetched(late, 0, "onward", detoured_late)
     final = fetched_chunk(parked, 2, [3])
     pieces.append([*others, *final])
     grads, received = backward(
-        1, pieces[1], around, upstream, bwd_segments, factor, grads, received
+        1, pieces[1], None, upstream, bwd_segments, factor, grads, received
     )
-    (grads,) = backward(2, pieces[2], around, upstream, bwd_segments, factor, grads)
+    (grads,) = backward(2, pieces[2], late, upstream, bwd_segments, factor, grads)
     return (received, grads)
 
 

time: 163 us -> 164 us (level)
  starting transfers between devices: 38.7 us -> 44.3 us
  waiting for transfers between devices: 84.8 us -> 80.1 us
    ppermute x14 -> x16, starting transfers between devices: 37.2 us -> 42.9 us  [fetched(): return lax.ppermute(piece, AXES, pairs)]
    ppermute x14 -> x16, waiting for transfers between devices: 84.8 us -> 80.1 us  [fetched(): return lax.ppermute(piece, AXES, pairs)]
  transfers between devices with their start and end apart: 16 -> 18, of which waited for: 5 -> 3; matrix products, arithmetic and copies ran while one was open for 3% -> 3% of each run, Pallas kernels for 10% -> 10%
where the time goes in v16:
time: 164 us; the launch traced here: 162 us
  waiting for transfers between devices  80.1 us (49%)
  starting transfers between devices  44.3 us (27%)
  Pallas kernels  18.3 us (11%)
  blocking collectives  10.1 us (6%)
  local copies, waits for them, and re-layouts  7.54 us (5%)
  between operations  2.09 us (1%)
    ppermute x16, waiting for transfers between devices, fetched(): return lax.ppermute(piece, AXES, pairs)  80.1 us
    ppermute x16, starting transfers between devices, fetched(): return lax.ppermute(piece, AXES, pairs)  42.9 us
    pallas_call x3, Pallas kernels, backward(): pl.pallas_call(functools.partial(backward_kernel, parts, around_from, goe...  13.2 us
    psum x1, blocking collectives, on_device(): token_total = lax.psum(tokens, 'dp')  10.1 us
    dynamic_slice x5, local copies, waits for them, and re-layouts, cut(): return lax.dynamic_slice_in_dim(whole, start, heads * HEAD_DIM, axis=3)  7.54 us
    pallas_call x1, Pallas kernels, forward(): pl.pallas_call(forward_kernel, grid=(FORWARD_STEPS,), in_specs=[pl.BlockS...  5.18 us
  transfers between devices with their start and end apart: 18, of which 3 were waited for; matrix products, arithmetic and copies ran while one was open for 3% of the time, Pallas kernels for 10%

profile of v16, /device:TPU:1, one launch (start us, length us, event | category | flops | bytes accessed | tf_op | source)
XLA Modules:
  0.0 162.5 jit_solution(17858943040438355753)
XLA Ops:
  0.6 1.9 %constant_dynamic-slice_fusion.12 = bf16[3,1,64,1280]{3,2,1,0:T(8,128)(2,1)} fusion(bf16[3,1,64,8192]{3,2,1,0:T(8,128)(2,1)} %param.8, s32[]{:T(128)S(6)} %select_n.38), kind=kLoop, calls=%fused_computation.12 | loop fusion | bytes 983044 | tf_op jit(solution)/shard_map/dynamic_slice | solution.py:196
  2.5 9.2 %collective-permute-start = (bf16[3,1,64,1280]{3,2,1,0:T(8,128)(2,1)}, bf16[3,1,64,1280]{3,2,1,0:T(8,128)(2,1)S(1)}, u32[]{:S(2)}, u32[]{:S(2)}) collective-permute-start(bf16[3,1,64,1280]{3,2,1,0:T(8,128)(2,1)} %constant_dynamic-slice_fusion.12), channel_id=1, source_target_pairs={{0,252},{4,248},{8,244},{12,240},{16,236},{20,232},{24,228},{28,22... | collective-permute-start | bytes 1474568 | tf_op jit(solution)/shard_map/stash_3_0/ppermute | solution.py:170
  11.7 0.0 collective-permute-start.5
  11.7 2.4 %constant_dynamic-slice_fusion.5 = (bf16[3,1,64,1280]{3,2,1,0:T(8,128)(2,1)S(1)}, bf16[3,1,64,1280]{3,2,1,0:T(8,128)(2,1)}, bf16[3,1,64,1280]{3,2,1,0:T(8,128)(2,1)}) fusion(bf16[3,1,64,8192]{3,2,1,0:T(8,128)(2,1)} %param.8, s32[]{:T(128)S(6)} %select_n.45, s32[]{:T(128)S(6)} %select_n.44, s32[]{:T(128)S(6)} %select_n.43), kind=kLoop, calls=%fused_computation.5 | loop fusion | bytes 2949132 | tf_op jit(solution)/shard_map/stash_2_0/dynamic_slice | solution.py:196
  14.1 0.0 copy-start
  14.1 0.0 collective-permute-start.8
  14.1 1.6 collective-permute-start.9
  15.7 5.2 %forward_heads.1 = bf16[1,256,2048]{2,1,0:T(8,128)(2,1)} custom-call(bf16[3,1,256,2048]{3,2,1,0:T(8,128)(2,1)} %qkv_ref.1, s32[1,256]{1,0:T(1,128)} %segment_ref.1), custom_call_target="tpu_custom_call" | custom-call | flops 536870912 | bytes 4194304 | tf_op jit(solution)/shard_map/forward_heads/pallas_call | solution.py:55
  20.9 1.5 collective-permute-start.11
  22.3 22.1 %collective-permute-done.refs_3_ = bf16[3,1,64,1280]{3,2,1,0:T(8,128)(2,1)S(1)} collective-permute-done((bf16[3,1,64,1280]{3,2,1,0:T(8,128)(2,1)}, bf16[3,1,64,1280]{3,2,1,0:T(8,128)(2,1)S(1)}, u32[]{:S(2)}, u32[]{:S(2)}) %collective-permute-start) | collective-permute-done | bytes 491552 | tf_op jit(solution)/shard_map/stash_3_0/ppermute | solution.py:170
  44.4 0.0 collective-permute-start.7
  44.4 43.2 %collective-permute-done.8.refs_2_ = bf16[3,1,64,1280]{3,2,1,0:T(8,128)(2,1)S(1)} collective-permute-done((bf16[3,1,64,1280]{3,2,1,0:T(8,128)(2,1)S(1)}, bf16[3,1,64,1280]{3,2,1,0:T(8,128)(2,1)S(1)}, u32[]{:S(2)}, u32[]{:S(2)}) %collective-permute-start.8) | collective-permute-done | bytes 491552 | tf_op jit(solution)/shard_map/stash_2_0/ppermute | solution.py:170
  87.6 4.9 %collective-permute-start.6 = (bf16[3,1,64,1280]{3,2,1,0:T(8,128)(2,1)}, bf16[3,1,64,1280]{3,2,1,0:T(8,128)(2,1)}, u32[]{:S(2)}, u32[]{:S(2)}) collective-permute-start(bf16[3,1,64,1280]{3,2,1,0:T(8,128)(2,1)} %get-tuple-element.31), channel_id=1, source_target_pairs={{0,240},{4,244},{8,248},{12,252},{16,224},{20,228},{24,232},{28,23... | collective-permute-start | bytes 1474568 | tf_op jit(solution)/shard_map/stash_0_0/ppermute | solution.py:170
  92.5 0.0 collective-permute-done.9
  92.5 1.5 collective-permute-start.10
  94.6 10.1 %psum.7 = f32[1]{0:T(128)} all-reduce(f32[1]{0:T(128)S(6)} %convert_element_type.3), channel_id=1, replica_groups=mesh['pipe'=16,'tensor'=4,'dp'=4] {'dp'}, use_global_device_ids=true, to_apply=%region_0.0 | all-reduce | flops 1 | bytes 8 | tf_op jit(solution)/shard_map/psum | solution.py:223
  105.4 1.3 constant_dynamic-slice_fusion.8
  106.7 0.0 collective-permute-done.7.refs_1_
  106.7 4.1 %collective-permute-start.4 = (bf16[3,1,64,512]{3,2,1,0:T(8,128)(2,1)S(1)}, bf16[3,1,64,512]{3,2,1,0:T(8,128)(2,1)S(1)}, u32[]{:S(2)}, u32[]{:S(2)}) collective-permute-start(bf16[3,1,64,512]{3,2,1,0:T(8,128)(2,1)S(1)} %get-tuple-element.32), channel_id=1, source_target_pairs={{0,252},{4,248},{8,244},{12,240},{16,236},{20,232},{24,228},{28,22... | collective-permute-start | bytes 589832 | tf_op jit(solution)/shard_map/stash_3_1/ppermute | solution.py:170
  110.8 14.8 %collective-permute-done.6.refs_0_ = bf16[3,1,64,1280]{3,2,1,0:T(8,128)(2,1)} collective-permute-done((bf16[3,1,64,1280]{3,2,1,0:T(8,128)(2,1)}, bf16[3,1,64,1280]{3,2,1,0:T(8,128)(2,1)}, u32[]{:S(2)}, u32[]{:S(2)}) %collective-permute-start.6) | collective-permute-done | bytes 491552 | tf_op jit(solution)/shard_map/stash_0_0/ppermute | solution.py:170
  125.6 3.6 %collective-permute-start.3 = (bf16[3,1,64,512]{3,2,1,0:T(8,128)(2,1)S(1)}, bf16[3,1,64,512]{3,2,1,0:T(8,128)(2,1)S(1)}, u32[]{:S(2)}, u32[]{:S(2)}) collective-permute-start(bf16[3,1,64,512]{3,2,1,0:T(8,128)(2,1)S(1)} %get-tuple-element.33), channel_id=1, source_target_pairs={{0,248},{4,252},{8,240},{12,244},{16,232},{20,236},{24,224},{28,22... | collective-permute-start | bytes 589832 | tf_op jit(solution)/shard_map/stash_2_1/ppermute | solution.py:170
  129.2 0.0 collective-permute-done.10.refs_4_
  129.2 1.0 collective-permute-start.2
  130.2 0.0 collective-permute-done.5.refs_5_.refs_4_
  130.2 3.2 %collective-permute-start.1 = (bf16[3,1,64,512]{3,2,1,0:T(8,128)(2,1)S(1)}, bf16[3,1,64,512]{3,2,1,0:T(8,128)(2,1)S(1)}, u32[]{:S(2)}, u32[]{:S(2)}) collective-permute-start(bf16[3,1,64,512]{3,2,1,0:T(8,128)(2,1)S(1)} %get-tuple-element.35), channel_id=1, source_target_pairs={{0,240},{4,244},{8,248},{12,252},{16,224},{20,228},{24,232},{28,23... | collective-permute-start | bytes 589832 | tf_op jit(solution)/shard_map/stash_0_1/ppermute | solution.py:170
  133.4 0.0 copy-done
  133.4 7.6 %shard_map.77.refs_8_ = bf16[3,1,256,2048]{3,2,1,0:T(8,128)(2,1)} custom-call(bf16[3,1,64,1280]{3,2,1,0:T(8,128)(2,1)} %collective-permute-done.6.refs_0_, bf16[3,1,64,1280]{3,2,1,0:T(8,128)(2,1)} %collective-permute-done.7.refs_1_, bf16[3,1,64,1280]{3,2,1,0:T(8,128)(2,1)S(1)} %collective-permute-done.8.refs_2_, ...), custom_call_target="tpu_custom_call" | custom-call | flops 838860800 | bytes 4587520 | tf_op jit(solution)/shard_map/pallas_call | solution.py:140
  141.0 0.0 collective-permute-done.11.refs_7_
  141.0 1.0 constant_dynamic-slice_fusion
  142.0 0.8 collective-permute-start.16
  142.8 1.0 constant_dynamic-slice_fusion.2
  143.8 0.0 collective-permute-done.4.refs_3_
  143.9 1.7 %collective-permute-start.15 = (bf16[3,1,64,256]{3,2,1,0:T(8,128)(2,1)S(1)}, bf16[3,1,64,256]{3,2,1,0:T(8,128)(2,1)S(1)}, u32[]{:S(2)}, u32[]{:S(2)}) collective-permute-start(bf16[3,1,64,256]{3,2,1,0:T(8,128)(2,1)S(1)} %get-tuple-element.25), channel_id=1, source_target_pairs={{0,252},{4,248},{8,244},{12,240},{16,236},{20,232},{24,228},{28,22... | collective-permute-start | bytes 294920 | tf_op jit(solution)/shard_map/stash_3_2/ppermute | solution.py:170
  145.6 0.0 collective-permute-done.3.refs_2_
  145.6 3.1 %collective-permute-start.14 = (bf16[3,1,64,256]{3,2,1,0:T(8,128)(2,1)S(1)}, bf16[3,1,64,256]{3,2,1,0:T(8,128)(2,1)S(1)}, u32[]{:S(2)}, u32[]{:S(2)}) collective-permute-start(bf16[3,1,64,256]{3,2,1,0:T(8,128)(2,1)S(1)} %get-tuple-element.26), channel_id=1, source_target_pairs={{0,248},{4,252},{8,240},{12,244},{16,232},{20,236},{24,224},{28,22... | collective-permute-start | bytes 294920 | tf_op jit(solution)/shard_map/stash_2_2/ppermute | solution.py:170
  148.7 0.0 collective-permute-done.2.refs_1_
  148.7 1.6 collective-permute-start.13
  150.3 0.0 collective-permute-done.1.refs_0_
  150.3 5.8 %collective-permute-start.12 = (bf16[3,1,64,256]{3,2,1,0:T(8,128)(2,1)S(1)}, bf16[3,1,64,256]{3,2,1,0:T(8,128)(2,1)S(1)}, u32[]{:S(2)}, u32[]{:S(2)}) collective-permute-start(bf16[3,1,64,256]{3,2,1,0:T(8,128)(2,1)S(1)} %get-tuple-element.28), channel_id=1, source_target_pairs={{0,240},{4,244},{8,248},{12,252},{16,224},{20,228},{24,232},{28,23... | collective-permute-start | bytes 294920 | tf_op jit(solution)/shard_map/stash_0_2/ppermute | solution.py:170
  156.2 0.0 collective-permute-done.16
  156.2 0.7 collective-permute-start.17
  156.9 3.5 %shard_map.78 = (bf16[3,1,256,2048]{3,2,1,0:T(8,128)(2,1)}, bf16[1,256,2048]{2,1,0:T(8,128)(2,1)}) custom-call(bf16[3,1,64,512]{3,2,1,0:T(8,128)(2,1)S(1)} %collective-permute-done.1.refs_0_, bf16[3,1,64,512]{3,2,1,0:T(8,128)(2,1)S(1)} %collective-permute-done.2.refs_1_, ...), custom_call_target="tpu_custom_call", output_to_operand_aliasing={{0}: (8, {})} | custom-call | flops 335544320 | bytes 1835008 | tf_op jit(solution)/shard_map/pallas_call | solution.py:140
  160.3 0.0 collective-permute-done.15.refs_3_
  160.3 0.0 collective-permute-done.14.refs_2_
  160.3 0.0 collective-permute-done.13.refs_1_
  160.3 0.0 collective-permute-done.12.refs_0_
  160.4 0.0 collective-permute-done.17.refs_4_
  160.4 2.1 %shard_map.79 = bf16[3,1,256,2048]{3,2,1,0:T(8,128)(2,1)} custom-call(bf16[3,1,64,256]{3,2,1,0:T(8,128)(2,1)S(1)} %collective-permute-done.12.refs_0_, bf16[3,1,64,256]{3,2,1,0:T(8,128)(2,1)S(1)} %collective-permute-done.13.refs_1_, bf16[3,1,64,256]{3,2,1,0:T(8,128)(2,1)S(1)} %collective-permute-done.14.refs_2_, ...), custom_call_target="tpu_custom_call", output_to_operand_aliasing={{}: (8, {})} | custom-call | flops 167772160 | bytes 917504 | tf_op jit(solution)/shard_map/pallas_call | solution.py:140
Async XLA Ops:
  2.5 41.9 %collective-permute-start = (bf16[3,1,64,1280]{3,2,1,0:T(8,128)(2,1)}, bf16[3,1,64,1280]{3,2,1,0:T(8,128)(2,1)S(1)}, u32[]{:S(2)}, u32[]{:S(2)}) collective-permute-start(bf16[3,1,64,1280]{3,2,1,0:T(8,128)(2,1)} %constant_dynamic-slice_fusion.12), channel_id=1, source_target_pairs={{0,252},{4,248},{8,244},{12,240},{16,236},{20,232},{24,228},{28,22... | collective-permute-start | bytes 1474568 | tf_op jit(solution)/shard_map/stash_3_0/ppermute | solution.py:170
  11.7 118.5 %collective-permute-start.5 = (bf16[1,256,2048]{2,1,0:T(8,128)(2,1)}, bf16[1,256,2048]{2,1,0:T(8,128)(2,1)S(1)}, u32[]{:S(2)}, u32[]{:S(2)}) collective-permute-start(bf16[1,256,2048]{2,1,0:T(8,128)(2,1)} %param.10), channel_id=1, source_target_pairs={{0,240},{16,0},{32,16},{48,32},{64,48},{80,64},{96,80},{112,96},{1... | collective-permute-start | bytes 3145736 | tf_op jit(solution)/shard_map/direct_grad/ppermute | solution.py:186
  14.1 119.3 %copy-start = (s32[1,256]{1,0:T(1,128)S(1)}, s32[1,256]{1,0:T(1,128)}, u32[]{:S(2)}) copy-start(s32[1,256]{1,0:T(1,128)} %refs_6_.3) | copy-start | bytes 3076
  14.1 73.5 %collective-permute-start.8 = (bf16[3,1,64,1280]{3,2,1,0:T(8,128)(2,1)S(1)}, bf16[3,1,64,1280]{3,2,1,0:T(8,128)(2,1)S(1)}, u32[]{:S(2)}, u32[]{:S(2)}) collective-permute-start(bf16[3,1,64,1280]{3,2,1,0:T(8,128)(2,1)S(1)} %get-tuple-element.29), channel_id=1, source_target_pairs={{0,248},{4,252},{8,240},{12,244},{16,232},{20,236},{24,224},{28,22... | collective-permute-start | bytes 1474568 | tf_op jit(solution)/shard_map/stash_2_0/ppermute | solution.py:170
  14.1 78.4 %collective-permute-start.9 = (bf16[3,1,64,1280]{3,2,1,0:T(8,128)(2,1)}, bf16[3,1,64,1280]{3,2,1,0:T(8,128)(2,1)}, u32[]{:S(2)}, u32[]{:S(2)}) collective-permute-start(bf16[3,1,64,1280]{3,2,1,0:T(8,128)(2,1)} %get-tuple-element.31), channel_id=1, source_target_pairs={{32,48},{36,52},{40,56},{44,60},{80,64},{84,68},{88,72},{92,76},{1... | collective-permute-start | bytes 1474568 | tf_op jit(solution)/shard_map/aside_0/ppermute | solution.py:170
  20.9 120.2 %collective-permute-start.11 = (bf16[1,256,2048]{2,1,0:T(8,128)(2,1)}, bf16[1,256,2048]{2,1,0:T(8,128)(2,1)S(1)}, u32[]{:S(2)}, u32[]{:S(2)}) collective-permute-start(bf16[1,256,2048]{2,1,0:T(8,128)(2,1)} %forward_heads.1), channel_id=1, source_target_pairs={{0,16},{16,32},{32,48},{48,64},{64,80},{80,96},{96,112},{112,128},... | collective-permute-start | bytes 3145736 | tf_op jit(solution)/shard_map/direct_out/ppermute | solution.py:186
  44.4 62.3 %collective-permute-start.7 = (bf16[3,1,64,1280]{3,2,1,0:T(8,128)(2,1)}, bf16[3,1,64,1280]{3,2,1,0:T(8,128)(2,1)}, u32[]{:S(2)}, u32[]{:S(2)}) collective-permute-start(bf16[3,1,64,1280]{3,2,1,0:T(8,128)(2,1)} %get-tuple-element.30), channel_id=1, source_target_pairs={{0,244},{4,240},{8,252},{12,248},{16,228},{20,224},{24,236},{28,23... | collective-permute-start | bytes 1474568 | tf_op jit(solution)/shard_map/stash_1_0/ppermute | solution.py:170
  87.6 38.0 %collective-permute-start.6 = (bf16[3,1,64,1280]{3,2,1,0:T(8,128)(2,1)}, bf16[3,1,64,1280]{3,2,1,0:T(8,128)(2,1)}, u32[]{:S(2)}, u32[]{:S(2)}) collective-permute-start(bf16[3,1,64,1280]{3,2,1,0:T(8,128)(2,1)} %get-tuple-element.31), channel_id=1, source_target_pairs={{0,240},{4,244},{8,248},{12,252},{16,224},{20,228},{24,232},{28,23... | collective-permute-start | bytes 1474568 | tf_op jit(solution)/shard_map/stash_0_0/ppermute | solution.py:170
  92.5 36.7 %collective-permute-start.10 = (bf16[3,1,64,1280]{3,2,1,0:T(8,128)(2,1)}, bf16[3,1,64,1280]{3,2,1,0:T(8,128)(2,1)}, u32[]{:S(2)}, u32[]{:S(2)}) collective-permute-start(bf16[3,1,64,1280]{3,2,1,0:T(8,128)(2,1)} %collective-permute-done.9), channel_id=1, source_target_pairs={{48,208},{52,212},{56,216},{60,220},{64,160},{68,164},{72,168},{76... | collective-permute-start | bytes 1474568 | tf_op jit(solution)/shard_map/onward_0/ppermute | solution.py:170
  106.7 37.2 %collective-permute-start.4 = (bf16[3,1,64,512]{3,2,1,0:T(8,128)(2,1)S(1)}, bf16[3,1,64,512]{3,2,1,0:T(8,128)(2,1)S(1)}, u32[]{:S(2)}, u32[]{:S(2)}) collective-permute-start(bf16[3,1,64,512]{3,2,1,0:T(8,128)(2,1)S(1)} %get-tuple-element.32), channel_id=1, source_target_pairs={{0,252},{4,248},{8,244},{12,240},{16,236},{20,232},{24,228},{28,22... | collective-permute-start | bytes 589832 | tf_op jit(solution)/shard_map/stash_3_1/ppermute | solution.py:170
  125.6 20.0 %collective-permute-start.3 = (bf16[3,1,64,512]{3,2,1,0:T(8,128)(2,1)S(1)}, bf16[3,1,64,512]{3,2,1,0:T(8,128)(2,1)S(1)}, u32[]{:S(2)}, u32[]{:S(2)}) collective-permute-start(bf16[3,1,64,512]{3,2,1,0:T(8,128)(2,1)S(1)} %get-tuple-element.33), channel_id=1, source_target_pairs={{0,248},{4,252},{8,240},{12,244},{16,232},{20,236},{24,224},{28,22... | collective-permute-start | bytes 589832 | tf_op jit(solution)/shard_map/stash_2_1/ppermute | solution.py:170
  129.2 19.5 %collective-permute-start.2 = (bf16[3,1,64,512]{3,2,1,0:T(8,128)(2,1)S(1)}, bf16[3,1,64,512]{3,2,1,0:T(8,128)(2,1)S(1)}, u32[]{:S(2)}, u32[]{:S(2)}) collective-permute-start(bf16[3,1,64,512]{3,2,1,0:T(8,128)(2,1)S(1)} %get-tuple-element.34), channel_id=1, source_target_pairs={{0,244},{4,240},{8,252},{12,248},{16,228},{20,224},{24,236},{28,23... | collective-permute-start | bytes 589832 | tf_op jit(solution)/shard_map/stash_1_1/ppermute | solution.py:170
  130.2 20.1 %collective-permute-start.1 = (bf16[3,1,64,512]{3,2,1,0:T(8,128)(2,1)S(1)}, bf16[3,1,64,512]{3,2,1,0:T(8,128)(2,1)S(1)}, u32[]{:S(2)}, u32[]{:S(2)}) collective-permute-start(bf16[3,1,64,512]{3,2,1,0:T(8,128)(2,1)S(1)} %get-tuple-element.35), channel_id=1, source_target_pairs={{0,240},{4,244},{8,248},{12,252},{16,224},{20,228},{24,232},{28,23... | collective-permute-start | bytes 589832 | tf_op jit(solution)/shard_map/stash_0_1/ppermute | solution.py:170
  142.0 14.2 %collective-permute-start.16 = (bf16[3,1,64,256]{3,2,1,0:T(8,128)(2,1)S(1)}, bf16[3,1,64,256]{3,2,1,0:T(8,128)(2,1)S(1)}, u32[]{:S(2)}, u32[]{:S(2)}) collective-permute-start(bf16[3,1,64,256]{3,2,1,0:T(8,128)(2,1)S(1)} %get-tuple-element.24), channel_id=1, source_target_pairs={{208,192},{212,196},{216,200},{220,204},{209,193},{213,197},{217,2... | collective-permute-start | bytes 294920 | tf_op jit(solution)/shard_map/aside_2/ppermute | solution.py:170
  143.9 16.5 %collective-permute-start.15 = (bf16[3,1,64,256]{3,2,1,0:T(8,128)(2,1)S(1)}, bf16[3,1,64,256]{3,2,1,0:T(8,128)(2,1)S(1)}, u32[]{:S(2)}, u32[]{:S(2)}) collective-permute-start(bf16[3,1,64,256]{3,2,1,0:T(8,128)(2,1)S(1)} %get-tuple-element.25), channel_id=1, source_target_pairs={{0,252},{4,248},{8,244},{12,240},{16,236},{20,232},{24,228},{28,22... | collective-permute-start | bytes 294920 | tf_op jit(solution)/shard_map/stash_3_2/ppermute | solution.py:170
  145.6 14.7 %collective-permute-start.14 = (bf16[3,1,64,256]{3,2,1,0:T(8,128)(2,1)S(1)}, bf16[3,1,64,256]{3,2,1,0:T(8,128)(2,1)S(1)}, u32[]{:S(2)}, u32[]{:S(2)}) collective-permute-start(bf16[3,1,64,256]{3,2,1,0:T(8,128)(2,1)S(1)} %get-tuple-element.26), channel_id=1, source_target_pairs={{0,248},{4,252},{8,240},{12,244},{16,232},{20,236},{24,224},{28,22... | collective-permute-start | bytes 294920 | tf_op jit(solution)/shard_map/stash_2_2/ppermute | solution.py:170
  148.7 11.6 %collective-permute-start.13 = (bf16[3,1,64,256]{3,2,1,0:T(8,128)(2,1)S(1)}, bf16[3,1,64,256]{3,2,1,0:T(8,128)(2,1)S(1)}, u32[]{:S(2)}, u32[]{:S(2)}) collective-permute-start(bf16[3,1,64,256]{3,2,1,0:T(8,128)(2,1)S(1)} %get-tuple-element.27), channel_id=1, source_target_pairs={{0,244},{4,240},{8,252},{12,248},{16,228},{20,224},{24,236},{28,23... | collective-permute-start | bytes 294920 | tf_op jit(solution)/shard_map/stash_1_2/ppermute | solution.py:170
  150.3 10.0 %collective-permute-start.12 = (bf16[3,1,64,256]{3,2,1,0:T(8,128)(2,1)S(1)}, bf16[3,1,64,256]{3,2,1,0:T(8,128)(2,1)S(1)}, u32[]{:S(2)}, u32[]{:S(2)}) collective-permute-start(bf16[3,1,64,256]{3,2,1,0:T(8,128)(2,1)S(1)} %get-tuple-element.28), channel_id=1, source_target_pairs={{0,240},{4,244},{8,248},{12,252},{16,224},{20,228},{24,232},{28,23... | collective-permute-start | bytes 294920 | tf_op jit(solution)/shard_map/stash_0_2/ppermute | solution.py:170
  156.2 4.2 %collective-permute-start.17 = (bf16[3,1,64,256]{3,2,1,0:T(8,128)(2,1)S(1)}, bf16[3,1,64,256]{3,2,1,0:T(8,128)(2,1)S(1)}, u32[]{:S(2)}, u32[]{:S(2)}) collective-permute-start(bf16[3,1,64,256]{3,2,1,0:T(8,128)(2,1)S(1)} %collective-permute-done.16), channel_id=1, source_target_pairs={{192,32},{196,36},{200,40},{204,44},{193,33},{197,37},{201,41},{20... | collective-permute-start | bytes 294920 | tf_op jit(solution)/shard_map/onward_2/ppermute | solution.py:170

commit v17 on v16

--- a/solution.py
+++ b/solution.py
@@ -230,13 +230,15 @@
     parked, received = lax.optimization_barrier((parked, received))
     with jax.named_scope("aside_2"):
         late = fetched(cut(parked, 0, *CHUNKS[2]), 0, "aside", detoured_late)
-    with jax.named_scope("onward_2"):
-        late = fetched(late, 0, "onward", detoured_late)
     final = fetched_chunk(parked, 2, [3])
     pieces.append([*others, *final])
+    late, grads = lax.optimization_barrier((late, grads))
     grads, received = backward(
         1, pieces[1], None, upstream, bwd_segments, factor, grads, received
     )
+    late, grads = lax.optimization_barrier((late, grads))
+    with jax.named_scope("onward_2"):
+        late = fetched(late, 0, "onward", detoured_late)
     (grads,) = backward(2, pieces[2], late, upstream, bwd_segments, factor, grads)
     return (received, grads)
 

time: 164 us -> 162 us (0.988)
  transfers between devices with their start and end apart: 18 -> 18, of which waited for: 3 -> 3; matrix products, arithmetic and copies ran while one was open for 3% -> 4% of each run, Pallas kernels for 10% -> 10%
where the time goes in v17:
time: 162 us; the launch traced here: 161 us
  waiting for transfers between devices  80.1 us (49%)
  starting transfers between devices  42.9 us (26%)
  Pallas kernels  18.3 us (11%)
  blocking collectives  10.1 us (6%)
  local copies, waits for them, and re-layouts  7.54 us (5%)
  between operations  2.12 us (1%)
    ppermute x16, waiting for transfers between devices, fetched(): return lax.ppermute(piece, AXES, pairs)  80.1 us
    ppermute x16, starting transfers between devices, fetched(): return lax.ppermute(piece, AXES, pairs)  41.5 us
    pallas_call x3, Pallas kernels, backward(): pl.pallas_call(functools.partial(backward_kernel, parts, around_from, goe...  13.2 us
    psum x1, blocking collectives, on_device(): token_total = lax.psum(tokens, 'dp')  10.1 us
    dynamic_slice x5, local copies, waits for them, and re-layouts, cut(): return lax.dynamic_slice_in_dim(whole, start, heads * HEAD_DIM, axis=3)  7.54 us
    pallas_call x1, Pallas kernels, forward(): pl.pallas_call(forward_kernel, grid=(FORWARD_STEPS,), in_specs=[pl.BlockS...  5.18 us
  transfers between devices with their start and end apart: 18, of which 3 were waited for; matrix products, arithmetic and copies ran while one was open for 4% of the time, Pallas kernels for 10%

profile of v17, /device:TPU:1, one launch (start us, length us, event | category | flops | bytes accessed | tf_op | source)
XLA Modules:
  0.0 161.1 jit_solution(14599401902290368755)
XLA Ops:
  0.6 1.9 %constant_dynamic-slice_fusion.12 = bf16[3,1,64,1280]{3,2,1,0:T(8,128)(2,1)} fusion(bf16[3,1,64,8192]{3,2,1,0:T(8,128)(2,1)} %param.8, s32[]{:T(128)S(6)} %select_n.38), kind=kLoop, calls=%fused_computation.12 | loop fusion | bytes 983044 | tf_op jit(solution)/shard_map/dynamic_slice | solution.py:196
  2.5 9.2 %collective-permute-start = (bf16[3,1,64,1280]{3,2,1,0:T(8,128)(2,1)}, bf16[3,1,64,1280]{3,2,1,0:T(8,128)(2,1)S(1)}, u32[]{:S(2)}, u32[]{:S(2)}) collective-permute-start(bf16[3,1,64,1280]{3,2,1,0:T(8,128)(2,1)} %constant_dynamic-slice_fusion.12), channel_id=1, source_target_pairs={{0,252},{4,248},{8,244},{12,240},{16,236},{20,232},{24,228},{28,22... | collective-permute-start | bytes 1474568 | tf_op jit(solution)/shard_map/stash_3_0/ppermute | solution.py:170
  11.7 0.0 collective-permute-start.5
  11.7 2.4 %constant_dynamic-slice_fusion.5 = (bf16[3,1,64,1280]{3,2,1,0:T(8,128)(2,1)S(1)}, bf16[3,1,64,1280]{3,2,1,0:T(8,128)(2,1)}, bf16[3,1,64,1280]{3,2,1,0:T(8,128)(2,1)}) fusion(bf16[3,1,64,8192]{3,2,1,0:T(8,128)(2,1)} %param.8, s32[]{:T(128)S(6)} %select_n.45, s32[]{:T(128)S(6)} %select_n.44, s32[]{:T(128)S(6)} %select_n.43), kind=kLoop, calls=%fused_computation.5 | loop fusion | bytes 2949132 | tf_op jit(solution)/shard_map/stash_2_0/dynamic_slice | solution.py:196
  14.1 0.0 copy-start
  14.1 0.0 collective-permute-start.8
  14.1 1.6 collective-permute-start.9
  15.7 5.2 %forward_heads.1 = bf16[1,256,2048]{2,1,0:T(8,128)(2,1)} custom-call(bf16[3,1,256,2048]{3,2,1,0:T(8,128)(2,1)} %qkv_ref.1, s32[1,256]{1,0:T(1,128)} %segment_ref.1), custom_call_target="tpu_custom_call" | custom-call | flops 536870912 | bytes 4194304 | tf_op jit(solution)/shard_map/forward_heads/pallas_call | solution.py:55
  20.9 1.5 collective-permute-start.11
  22.3 22.1 %collective-permute-done.refs_3_ = bf16[3,1,64,1280]{3,2,1,0:T(8,128)(2,1)S(1)} collective-permute-done((bf16[3,1,64,1280]{3,2,1,0:T(8,128)(2,1)}, bf16[3,1,64,1280]{3,2,1,0:T(8,128)(2,1)S(1)}, u32[]{:S(2)}, u32[]{:S(2)}) %collective-permute-start) | collective-permute-done | bytes 491552 | tf_op jit(solution)/shard_map/stash_3_0/ppermute | solution.py:170
  44.4 0.0 collective-permute-start.7
  44.4 43.2 %collective-permute-done.8.refs_2_ = bf16[3,1,64,1280]{3,2,1,0:T(8,128)(2,1)S(1)} collective-permute-done((bf16[3,1,64,1280]{3,2,1,0:T(8,128)(2,1)S(1)}, bf16[3,1,64,1280]{3,2,1,0:T(8,128)(2,1)S(1)}, u32[]{:S(2)}, u32[]{:S(2)}) %collective-permute-start.8) | collective-permute-done | bytes 491552 | tf_op jit(solution)/shard_map/stash_2_0/ppermute | solution.py:170
  87.6 4.9 %collective-permute-start.6 = (bf16[3,1,64,1280]{3,2,1,0:T(8,128)(2,1)}, bf16[3,1,64,1280]{3,2,1,0:T(8,128)(2,1)}, u32[]{:S(2)}, u32[]{:S(2)}) collective-permute-start(bf16[3,1,64,1280]{3,2,1,0:T(8,128)(2,1)} %get-tuple-element.39), channel_id=1, source_target_pairs={{0,240},{4,244},{8,248},{12,252},{16,224},{20,228},{24,232},{28,23... | collective-permute-start | bytes 1474568 | tf_op jit(solution)/shard_map/stash_0_0/ppermute | solution.py:170
  92.5 0.0 collective-permute-done.9
  92.5 1.5 collective-permute-start.10
  94.6 10.1 %psum.7 = f32[1]{0:T(128)} all-reduce(f32[1]{0:T(128)S(6)} %convert_element_type.3), channel_id=1, replica_groups=mesh['pipe'=16,'tensor'=4,'dp'=4] {'dp'}, use_global_device_ids=true, to_apply=%region_0.0 | all-reduce | flops 1 | bytes 8 | tf_op jit(solution)/shard_map/psum | solution.py:223
  105.4 1.3 constant_dynamic-slice_fusion.8
  106.7 0.0 collective-permute-done.7.refs_1_
  106.7 4.1 %collective-permute-start.4 = (bf16[3,1,64,512]{3,2,1,0:T(8,128)(2,1)S(1)}, bf16[3,1,64,512]{3,2,1,0:T(8,128)(2,1)S(1)}, u32[]{:S(2)}, u32[]{:S(2)}) collective-permute-start(bf16[3,1,64,512]{3,2,1,0:T(8,128)(2,1)S(1)} %get-tuple-element.40), channel_id=1, source_target_pairs={{0,252},{4,248},{8,244},{12,240},{16,236},{20,232},{24,228},{28,22... | collective-permute-start | bytes 589832 | tf_op jit(solution)/shard_map/stash_3_1/ppermute | solution.py:170
  110.8 14.8 %collective-permute-done.6.refs_0_ = bf16[3,1,64,1280]{3,2,1,0:T(8,128)(2,1)} collective-permute-done((bf16[3,1,64,1280]{3,2,1,0:T(8,128)(2,1)}, bf16[3,1,64,1280]{3,2,1,0:T(8,128)(2,1)}, u32[]{:S(2)}, u32[]{:S(2)}) %collective-permute-start.6) | collective-permute-done | bytes 491552 | tf_op jit(solution)/shard_map/stash_0_0/ppermute | solution.py:170
  125.6 3.6 %collective-permute-start.3 = (bf16[3,1,64,512]{3,2,1,0:T(8,128)(2,1)S(1)}, bf16[3,1,64,512]{3,2,1,0:T(8,128)(2,1)S(1)}, u32[]{:S(2)}, u32[]{:S(2)}) collective-permute-start(bf16[3,1,64,512]{3,2,1,0:T(8,128)(2,1)S(1)} %get-tuple-element.41), channel_id=1, source_target_pairs={{0,248},{4,252},{8,240},{12,244},{16,232},{20,236},{24,224},{28,22... | collective-permute-start | bytes 589832 | tf_op jit(solution)/shard_map/stash_2_1/ppermute | solution.py:170
  129.2 0.0 collective-permute-done.10.refs_4_
  129.2 1.0 collective-permute-start.2
  130.2 0.0 collective-permute-done.5.refs_5_.refs_4_
  130.2 3.2 %collective-permute-start.1 = (bf16[3,1,64,512]{3,2,1,0:T(8,128)(2,1)S(1)}, bf16[3,1,64,512]{3,2,1,0:T(8,128)(2,1)S(1)}, u32[]{:S(2)}, u32[]{:S(2)}) collective-permute-start(bf16[3,1,64,512]{3,2,1,0:T(8,128)(2,1)S(1)} %get-tuple-element.43), channel_id=1, source_target_pairs={{0,240},{4,244},{8,248},{12,252},{16,224},{20,228},{24,232},{28,23... | collective-permute-start | bytes 589832 | tf_op jit(solution)/shard_map/stash_0_1/ppermute | solution.py:170
  133.4 0.0 copy-done
  133.4 7.6 %shard_map.77.refs_8_ = bf16[3,1,256,2048]{3,2,1,0:T(8,128)(2,1)} custom-call(bf16[3,1,64,1280]{3,2,1,0:T(8,128)(2,1)} %collective-permute-done.6.refs_0_, bf16[3,1,64,1280]{3,2,1,0:T(8,128)(2,1)} %collective-permute-done.7.refs_1_, bf16[3,1,64,1280]{3,2,1,0:T(8,128)(2,1)S(1)} %collective-permute-done.8.refs_2_, ...), custom_call_target="tpu_custom_call" | custom-call | flops 838860800 | bytes 4587520 | tf_op jit(solution)/shard_map/pallas_call | solution.py:140
  141.0 0.0 collective-permute-done.11.refs_7_
  141.0 1.0 constant_dynamic-slice_fusion
  142.0 0.8 collective-permute-start.12
  142.8 1.0 constant_dynamic-slice_fusion.1
  143.8 0.0 collective-permute-done.12
  143.9 1.7 %collective-permute-start.16 = (bf16[3,1,64,256]{3,2,1,0:T(8,128)(2,1)S(1)}, bf16[3,1,64,256]{3,2,1,0:T(8,128)(2,1)S(1)}, u32[]{:S(2)}, u32[]{:S(2)}) collective-permute-start(bf16[3,1,64,256]{3,2,1,0:T(8,128)(2,1)S(1)} %get-tuple-element.32), channel_id=1, source_target_pairs={{0,252},{4,248},{8,244},{12,240},{16,236},{20,232},{24,228},{28,22... | collective-permute-start | bytes 294920 | tf_op jit(solution)/shard_map/stash_3_2/ppermute | solution.py:170
  145.6 0.0 collective-permute-done.4.refs_3_
  145.6 3.1 %collective-permute-start.15 = (bf16[3,1,64,256]{3,2,1,0:T(8,128)(2,1)S(1)}, bf16[3,1,64,256]{3,2,1,0:T(8,128)(2,1)S(1)}, u32[]{:S(2)}, u32[]{:S(2)}) collective-permute-start(bf16[3,1,64,256]{3,2,1,0:T(8,128)(2,1)S(1)} %get-tuple-element.34), channel_id=1, source_target_pairs={{0,248},{4,252},{8,240},{12,244},{16,232},{20,236},{24,224},{28,22... | collective-permute-start | bytes 294920 | tf_op jit(solution)/shard_map/stash_2_2/ppermute | solution.py:170
  148.7 0.0 collective-permute-done.3.refs_2_
  148.7 0.0 collective-permute-start.14
  148.7 0.0 collective-permute-done.2.refs_1_
  148.7 6.1 %collective-permute-start.13 = (bf16[3,1,64,256]{3,2,1,0:T(8,128)(2,1)S(1)}, bf16[3,1,64,256]{3,2,1,0:T(8,128)(2,1)S(1)}, u32[]{:S(2)}, u32[]{:S(2)}) collective-permute-start(bf16[3,1,64,256]{3,2,1,0:T(8,128)(2,1)S(1)} %get-tuple-element.36), channel_id=1, source_target_pairs={{0,240},{4,244},{8,248},{12,252},{16,224},{20,228},{24,232},{28,23... | collective-permute-start | bytes 294920 | tf_op jit(solution)/shard_map/stash_0_2/ppermute | solution.py:170
  154.8 0.0 collective-permute-done.1.refs_0_
  154.8 3.5 %shard_map.78 = (bf16[3,1,256,2048]{3,2,1,0:T(8,128)(2,1)}, bf16[1,256,2048]{2,1,0:T(8,128)(2,1)}) custom-call(bf16[3,1,64,512]{3,2,1,0:T(8,128)(2,1)S(1)} %collective-permute-done.1.refs_0_, bf16[3,1,64,512]{3,2,1,0:T(8,128)(2,1)S(1)} %collective-permute-done.2.refs_1_, ...), custom_call_target="tpu_custom_call", output_to_operand_aliasing={{0}: (8, {})} | custom-call | flops 335544320 | bytes 1835008 | tf_op jit(solution)/shard_map/pallas_call | solution.py:140
  158.3 0.7 collective-permute-start.17
  159.0 0.0 collective-permute-done.16.refs_3_
  159.0 0.0 collective-permute-done.15.refs_2_
  159.0 0.0 collective-permute-done.14.refs_1_
  159.0 0.0 collective-permute-done.13.refs_0_
  159.0 0.0 collective-permute-done.17.refs_4_
  159.0 2.1 %shard_map.79 = bf16[3,1,256,2048]{3,2,1,0:T(8,128)(2,1)} custom-call(bf16[3,1,64,256]{3,2,1,0:T(8,128)(2,1)S(1)} %collective-permute-done.13.refs_0_, bf16[3,1,64,256]{3,2,1,0:T(8,128)(2,1)S(1)} %collective-permute-done.14.refs_1_, bf16[3,1,64,256]{3,2,1,0:T(8,128)(2,1)S(1)} %collective-permute-done.15.refs_2_, ...), custom_call_target="tpu_custom_call", output_to_operand_aliasing={{}: (8, {})} | custom-call | flops 167772160 | bytes 917504 | tf_op jit(solution)/shard_map/pallas_call | solution.py:140
Async XLA Ops:
  2.5 41.9 %collective-permute-start = (bf16[3,1,64,1280]{3,2,1,0:T(8,128)(2,1)}, bf16[3,1,64,1280]{3,2,1,0:T(8,128)(2,1)S(1)}, u32[]{:S(2)}, u32[]{:S(2)}) collective-permute-start(bf16[3,1,64,1280]{3,2,1,0:T(8,128)(2,1)} %constant_dynamic-slice_fusion.12), channel_id=1, source_target_pairs={{0,252},{4,248},{8,244},{12,240},{16,236},{20,232},{24,228},{28,22... | collective-permute-start | bytes 1474568 | tf_op jit(solution)/shard_map/stash_3_0/ppermute | solution.py:170
  11.7 118.5 %collective-permute-start.5 = (bf16[1,256,2048]{2,1,0:T(8,128)(2,1)}, bf16[1,256,2048]{2,1,0:T(8,128)(2,1)S(1)}, u32[]{:S(2)}, u32[]{:S(2)}) collective-permute-start(bf16[1,256,2048]{2,1,0:T(8,128)(2,1)} %param.10), channel_id=1, source_target_pairs={{0,240},{16,0},{32,16},{48,32},{64,48},{80,64},{96,80},{112,96},{1... | collective-permute-start | bytes 3145736 | tf_op jit(solution)/shard_map/direct_grad/ppermute | solution.py:186
  14.1 119.3 %copy-start = (s32[1,256]{1,0:T(1,128)S(1)}, s32[1,256]{1,0:T(1,128)}, u32[]{:S(2)}) copy-start(s32[1,256]{1,0:T(1,128)} %refs_6_.3) | copy-start | bytes 3076
  14.1 73.5 %collective-permute-start.8 = (bf16[3,1,64,1280]{3,2,1,0:T(8,128)(2,1)S(1)}, bf16[3,1,64,1280]{3,2,1,0:T(8,128)(2,1)S(1)}, u32[]{:S(2)}, u32[]{:S(2)}) collective-permute-start(bf16[3,1,64,1280]{3,2,1,0:T(8,128)(2,1)S(1)} %get-tuple-element.37), channel_id=1, source_target_pairs={{0,248},{4,252},{8,240},{12,244},{16,232},{20,236},{24,224},{28,22... | collective-permute-start | bytes 1474568 | tf_op jit(solution)/shard_map/stash_2_0/ppermute | solution.py:170
  14.1 78.4 %collective-permute-start.9 = (bf16[3,1,64,1280]{3,2,1,0:T(8,128)(2,1)}, bf16[3,1,64,1280]{3,2,1,0:T(8,128)(2,1)}, u32[]{:S(2)}, u32[]{:S(2)}) collective-permute-start(bf16[3,1,64,1280]{3,2,1,0:T(8,128)(2,1)} %get-tuple-element.39), channel_id=1, source_target_pairs={{32,48},{36,52},{40,56},{44,60},{80,64},{84,68},{88,72},{92,76},{1... | collective-permute-start | bytes 1474568 | tf_op jit(solution)/shard_map/aside_0/ppermute | solution.py:170
  20.9 120.2 %collective-permute-start.11 = (bf16[1,256,2048]{2,1,0:T(8,128)(2,1)}, bf16[1,256,2048]{2,1,0:T(8,128)(2,1)S(1)}, u32[]{:S(2)}, u32[]{:S(2)}) collective-permute-start(bf16[1,256,2048]{2,1,0:T(8,128)(2,1)} %forward_heads.1), channel_id=1, source_target_pairs={{0,16},{16,32},{32,48},{48,64},{64,80},{80,96},{96,112},{112,128},... | collective-permute-start | bytes 3145736 | tf_op jit(solution)/shard_map/direct_out/ppermute | solution.py:186
  44.4 62.3 %collective-permute-start.7 = (bf16[3,1,64,1280]{3,2,1,0:T(8,128)(2,1)}, bf16[3,1,64,1280]{3,2,1,0:T(8,128)(2,1)}, u32[]{:S(2)}, u32[]{:S(2)}) collective-permute-start(bf16[3,1,64,1280]{3,2,1,0:T(8,128)(2,1)} %get-tuple-element.38), channel_id=1, source_target_pairs={{0,244},{4,240},{8,252},{12,248},{16,228},{20,224},{24,236},{28,23... | collective-permute-start | bytes 1474568 | tf_op jit(solution)/shard_map/stash_1_0/ppermute | solution.py:170
  87.6 38.0 %collective-permute-start.6 = (bf16[3,1,64,1280]{3,2,1,0:T(8,128)(2,1)}, bf16[3,1,64,1280]{3,2,1,0:T(8,128)(2,1)}, u32[]{:S(2)}, u32[]{:S(2)}) collective-permute-start(bf16[3,1,64,1280]{3,2,1,0:T(8,128)(2,1)} %get-tuple-element.39), channel_id=1, source_target_pairs={{0,240},{4,244},{8,248},{12,252},{16,224},{20,228},{24,232},{28,23... | collective-permute-start | bytes 1474568 | tf_op jit(solution)/shard_map/stash_0_0/ppermute | solution.py:170
  92.5 36.7 %collective-permute-start.10 = (bf16[3,1,64,1280]{3,2,1,0:T(8,128)(2,1)}, bf16[3,1,64,1280]{3,2,1,0:T(8,128)(2,1)}, u32[]{:S(2)}, u32[]{:S(2)}) collective-permute-start(bf16[3,1,64,1280]{3,2,1,0:T(8,128)(2,1)} %collective-permute-done.9), channel_id=1, source_target_pairs={{48,208},{52,212},{56,216},{60,220},{64,160},{68,164},{72,168},{76... | collective-permute-start | bytes 1474568 | tf_op jit(solution)/shard_map/onward_0/ppermute | solution.py:170
  106.7 38.9 %collective-permute-start.4 = (bf16[3,1,64,512]{3,2,1,0:T(8,128)(2,1)S(1)}, bf16[3,1,64,512]{3,2,1,0:T(8,128)(2,1)S(1)}, u32[]{:S(2)}, u32[]{:S(2)}) collective-permute-start(bf16[3,1,64,512]{3,2,1,0:T(8,128)(2,1)S(1)} %get-tuple-element.40), channel_id=1, source_target_pairs={{0,252},{4,248},{8,244},{12,240},{16,236},{20,232},{24,228},{28,22... | collective-permute-start | bytes 589832 | tf_op jit(solution)/shard_map/stash_3_1/ppermute | solution.py:170
  125.6 23.1 %collective-permute-start.3 = (bf16[3,1,64,512]{3,2,1,0:T(8,128)(2,1)S(1)}, bf16[3,1,64,512]{3,2,1,0:T(8,128)(2,1)S(1)}, u32[]{:S(2)}, u32[]{:S(2)}) collective-permute-start(bf16[3,1,64,512]{3,2,1,0:T(8,128)(2,1)S(1)} %get-tuple-element.41), channel_id=1, source_target_pairs={{0,248},{4,252},{8,240},{12,244},{16,232},{20,236},{24,224},{28,22... | collective-permute-start | bytes 589832 | tf_op jit(solution)/shard_map/stash_2_1/ppermute | solution.py:170
  129.2 19.5 %collective-permute-start.2 = (bf16[3,1,64,512]{3,2,1,0:T(8,128)(2,1)S(1)}, bf16[3,1,64,512]{3,2,1,0:T(8,128)(2,1)S(1)}, u32[]{:S(2)}, u32[]{:S(2)}) collective-permute-start(bf16[3,1,64,512]{3,2,1,0:T(8,128)(2,1)S(1)} %get-tuple-element.42), channel_id=1, source_target_pairs={{0,244},{4,240},{8,252},{12,248},{16,228},{20,224},{24,236},{28,23... | collective-permute-start | bytes 589832 | tf_op jit(solution)/shard_map/stash_1_1/ppermute | solution.py:170
  130.2 24.6 %collective-permute-start.1 = (bf16[3,1,64,512]{3,2,1,0:T(8,128)(2,1)S(1)}, bf16[3,1,64,512]{3,2,1,0:T(8,128)(2,1)S(1)}, u32[]{:S(2)}, u32[]{:S(2)}) collective-permute-start(bf16[3,1,64,512]{3,2,1,0:T(8,128)(2,1)S(1)} %get-tuple-element.43), channel_id=1, source_target_pairs={{0,240},{4,244},{8,248},{12,252},{16,224},{20,228},{24,232},{28,23... | collective-permute-start | bytes 589832 | tf_op jit(solution)/shard_map/stash_0_1/ppermute | solution.py:170
  142.0 1.9 %collective-permute-start.12 = (bf16[3,1,64,256]{3,2,1,0:T(8,128)(2,1)S(1)}, bf16[3,1,64,256]{3,2,1,0:T(8,128)(2,1)S(1)}, u32[]{:S(2)}, u32[]{:S(2)}) collective-permute-start(bf16[3,1,64,256]{3,2,1,0:T(8,128)(2,1)S(1)} %get-tuple-element.33), channel_id=1, source_target_pairs={{208,192},{212,196},{216,200},{220,204},{209,193},{213,197},{217,2... | collective-permute-start | bytes 294920 | tf_op jit(solution)/shard_map/aside_2/ppermute | solution.py:170
  143.9 15.1 %collective-permute-start.16 = (bf16[3,1,64,256]{3,2,1,0:T(8,128)(2,1)S(1)}, bf16[3,1,64,256]{3,2,1,0:T(8,128)(2,1)S(1)}, u32[]{:S(2)}, u32[]{:S(2)}) collective-permute-start(bf16[3,1,64,256]{3,2,1,0:T(8,128)(2,1)S(1)} %get-tuple-element.32), channel_id=1, source_target_pairs={{0,252},{4,248},{8,244},{12,240},{16,236},{20,232},{24,228},{28,22... | collective-permute-start | bytes 294920 | tf_op jit(solution)/shard_map/stash_3_2/ppermute | solution.py:170
  145.6 13.4 %collective-permute-start.15 = (bf16[3,1,64,256]{3,2,1,0:T(8,128)(2,1)S(1)}, bf16[3,1,64,256]{3,2,1,0:T(8,128)(2,1)S(1)}, u32[]{:S(2)}, u32[]{:S(2)}) collective-permute-start(bf16[3,1,64,256]{3,2,1,0:T(8,128)(2,1)S(1)} %get-tuple-element.34), channel_id=1, source_target_pairs={{0,248},{4,252},{8,240},{12,244},{16,232},{20,236},{24,224},{28,22... | collective-permute-start | bytes 294920 | tf_op jit(solution)/shard_map/stash_2_2/ppermute | solution.py:170
  148.7 10.3 %collective-permute-start.14 = (bf16[3,1,64,256]{3,2,1,0:T(8,128)(2,1)S(1)}, bf16[3,1,64,256]{3,2,1,0:T(8,128)(2,1)S(1)}, u32[]{:S(2)}, u32[]{:S(2)}) collective-permute-start(bf16[3,1,64,256]{3,2,1,0:T(8,128)(2,1)S(1)} %get-tuple-element.35), channel_id=1, source_target_pairs={{0,244},{4,240},{8,252},{12,248},{16,228},{20,224},{24,236},{28,23... | collective-permute-start | bytes 294920 | tf_op jit(solution)/shard_map/stash_1_2/ppermute | solution.py:170
  148.7 10.3 %collective-permute-start.13 = (bf16[3,1,64,256]{3,2,1,0:T(8,128)(2,1)S(1)}, bf16[3,1,64,256]{3,2,1,0:T(8,128)(2,1)S(1)}, u32[]{:S(2)}, u32[]{:S(2)}) collective-permute-start(bf16[3,1,64,256]{3,2,1,0:T(8,128)(2,1)S(1)} %get-tuple-element.36), channel_id=1, source_target_pairs={{0,240},{4,244},{8,248},{12,252},{16,224},{20,228},{24,232},{28,23... | collective-permute-start | bytes 294920 | tf_op jit(solution)/shard_map/stash_0_2/ppermute | solution.py:170
  158.3 0.7 collective-permute-start.17

commit v18 on v17

--- a/solution.py
+++ b/solution.py
@@ -91,7 +91,12 @@
     for k, piece in enumerate(found):
         start = pl.multiple_of((mine ^ k) * rows, rows)
         stash[:, pl.ds(start, rows), :] = piece
-    outside = outside_of(segment_ref)
+    if segment_ref.shape[0] == 1:
+        outside = outside_of(segment_ref)
+        out_ref = refs[-3]
+        refs[-2][...] = outside
+    else:
+        outside = segment_ref[...]
     factor = factor_ref[0]
     for start in range(0, upstream_ref.shape[2], HEAD_DIM):
         head = slice(start, start + HEAD_DIM)
@@ -121,11 +126,14 @@
     operands = [*pieces, upstream, segment, factor]
     in_specs = [pl.BlockSpec(memory_space=pltpu.VMEM)] * parts + [
         pl.BlockSpec((1, length, step), lambda i: (0, 0, place)),
-        pl.BlockSpec((1, length), lambda i: (0, 0)),
+        pl.BlockSpec(segment.shape, lambda i: (0, 0)),
         pl.BlockSpec(memory_space=pltpu.SMEM),
     ]
     out_specs = [pl.BlockSpec((3, 1, length, step), lambda i: (0, 0, 0, place))]
     out_shape = [jax.ShapeDtypeStruct((3, 1, length, width), jnp.bfloat16)]
+    if segment.shape[0] == 1:
+        out_specs.append(pl.BlockSpec((length, length), lambda i: (0, 0)))
+        out_shape.append(jax.ShapeDtypeStruct((length, length), jnp.float32))
     if carried is not None:
         whole = pl.BlockSpec(carried.shape, lambda i: (0, 0, 0))
         operands.append(carried)
@@ -224,7 +232,7 @@
     factor = jnp.float32(lax.axis_size("dp") * length) / token_total
     parked, token_total = lax.optimization_barrier((parked, token_total))
     pieces.append(fetched_chunk(parked, 1, range(tensors)))
-    (grads,) = backward(0, pieces[0], around, upstream, bwd_segments, factor, None)
+    grads, outside = backward(0, pieces[0], around, upstream, bwd_segments, factor, None)
     parked, grads = lax.optimization_barrier((parked, grads))
     others = fetched_chunk(parked, 2, range(3))
     parked, received = lax.optimization_barrier((parked, received))
@@ -234,12 +242,12 @@
     pieces.append([*others, *final])
     late, grads = lax.optimization_barrier((late, grads))
     grads, received = backward(
-        1, pieces[1], None, upstream, bwd_segments, factor, grads, received
+        1, pieces[1], None, upstream, outside, factor, grads, received
     )
     late, grads = lax.optimization_barrier((late, grads))
     with jax.named_scope("onward_2"):
         late = fetched(late, 0, "onward", detoured_late)
-    (grads,) = backward(2, pieces[2], late, upstream, bwd_segments, factor, grads)
+    (grads,) = backward(2, pieces[2], late, upstream, outside, factor, grads)
     return (received, grads)
 
 

time: 162 us -> 162 us (level)
  no operation moved by 1% of the time
where the time goes in v18:
time: 162 us; the launch traced here: 161 us
  waiting for transfers between devices  80.2 us (50%)
  starting transfers between devices  43 us (27%)
  Pallas kernels  18.3 us (11%)
  blocking collectives  10 us (6%)
  local copies, waits for them, and re-layouts  7.53 us (5%)
  between operations  2.05 us (1%)
    ppermute x16, waiting for transfers between devices, fetched(): return lax.ppermute(piece, AXES, pairs)  80.2 us
    ppermute x16, starting transfers between devices, fetched(): return lax.ppermute(piece, AXES, pairs)  41.5 us
    pallas_call x3, Pallas kernels, backward(): pl.pallas_call(functools.partial(backward_kernel, parts, around_from, goe...  13.1 us
    psum x1, blocking collectives, on_device(): token_total = lax.psum(tokens, 'dp')  10 us
    dynamic_slice x5, local copies, waits for them, and re-layouts, cut(): return lax.dynamic_slice_in_dim(whole, start, heads * HEAD_DIM, axis=3)  7.53 us
    pallas_call x1, Pallas kernels, forward(): pl.pallas_call(forward_kernel, grid=(FORWARD_STEPS,), in_specs=[pl.BlockS...  5.18 us
  transfers between devices with their start and end apart: 18, of which 3 were waited for; matrix products, arithmetic and copies ran while one was open for 4% of the time, Pallas kernels for 10%

profile of v18, /device:TPU:1, one launch (start us, length us, event | category | flops | bytes accessed | tf_op | source)
XLA Modules:
  0.0 161.1 jit_solution(1619840021762069816)
XLA Ops:
  0.6 1.9 %constant_dynamic-slice_fusion.12 = bf16[3,1,64,1280]{3,2,1,0:T(8,128)(2,1)} fusion(bf16[3,1,64,8192]{3,2,1,0:T(8,128)(2,1)} %param.8, s32[]{:T(128)S(6)} %select_n.38), kind=kLoop, calls=%fused_computation.12 | loop fusion | bytes 983044 | tf_op jit(solution)/shard_map/dynamic_slice | solution.py:204
  2.5 9.2 %collective-permute-start = (bf16[3,1,64,1280]{3,2,1,0:T(8,128)(2,1)}, bf16[3,1,64,1280]{3,2,1,0:T(8,128)(2,1)S(1)}, u32[]{:S(2)}, u32[]{:S(2)}) collective-permute-start(bf16[3,1,64,1280]{3,2,1,0:T(8,128)(2,1)} %constant_dynamic-slice_fusion.12), channel_id=1, source_target_pairs={{0,252},{4,248},{8,244},{12,240},{16,236},{20,232},{24,228},{28,22... | collective-permute-start | bytes 1474568 | tf_op jit(solution)/shard_map/stash_3_0/ppermute | solution.py:178
  11.7 0.0 collective-permute-start.5
  11.7 2.4 %constant_dynamic-slice_fusion.5 = (bf16[3,1,64,1280]{3,2,1,0:T(8,128)(2,1)S(1)}, bf16[3,1,64,1280]{3,2,1,0:T(8,128)(2,1)}, bf16[3,1,64,1280]{3,2,1,0:T(8,128)(2,1)}) fusion(bf16[3,1,64,8192]{3,2,1,0:T(8,128)(2,1)} %param.8, s32[]{:T(128)S(6)} %select_n.45, s32[]{:T(128)S(6)} %select_n.44, s32[]{:T(128)S(6)} %select_n.43), kind=kLoop, calls=%fused_computation.5 | loop fusion | bytes 2949132 | tf_op jit(solution)/shard_map/stash_2_0/dynamic_slice | solution.py:204
  14.1 0.0 copy-start
  14.1 0.0 collective-permute-start.8
  14.1 1.6 collective-permute-start.9
  15.7 5.2 %forward_heads.1 = bf16[1,256,2048]{2,1,0:T(8,128)(2,1)} custom-call(bf16[3,1,256,2048]{3,2,1,0:T(8,128)(2,1)} %qkv_ref.1, s32[1,256]{1,0:T(1,128)} %segment_ref.1), custom_call_target="tpu_custom_call" | custom-call | flops 536870912 | bytes 4194304 | tf_op jit(solution)/shard_map/forward_heads/pallas_call | solution.py:55
  20.8 1.5 collective-permute-start.11
  22.3 22.1 %collective-permute-done.refs_3_ = bf16[3,1,64,1280]{3,2,1,0:T(8,128)(2,1)S(1)} collective-permute-done((bf16[3,1,64,1280]{3,2,1,0:T(8,128)(2,1)}, bf16[3,1,64,1280]{3,2,1,0:T(8,128)(2,1)S(1)}, u32[]{:S(2)}, u32[]{:S(2)}) %collective-permute-start) | collective-permute-done | bytes 491552 | tf_op jit(solution)/shard_map/stash_3_0/ppermute | solution.py:178
  44.4 0.0 collective-permute-start.7
  44.4 43.2 %collective-permute-done.8.refs_2_ = bf16[3,1,64,1280]{3,2,1,0:T(8,128)(2,1)S(1)} collective-permute-done((bf16[3,1,64,1280]{3,2,1,0:T(8,128)(2,1)S(1)}, bf16[3,1,64,1280]{3,2,1,0:T(8,128)(2,1)S(1)}, u32[]{:S(2)}, u32[]{:S(2)}) %collective-permute-start.8) | collective-permute-done | bytes 491552 | tf_op jit(solution)/shard_map/stash_2_0/ppermute | solution.py:178
  87.6 4.9 %collective-permute-start.6 = (bf16[3,1,64,1280]{3,2,1,0:T(8,128)(2,1)}, bf16[3,1,64,1280]{3,2,1,0:T(8,128)(2,1)}, u32[]{:S(2)}, u32[]{:S(2)}) collective-permute-start(bf16[3,1,64,1280]{3,2,1,0:T(8,128)(2,1)} %get-tuple-element.43), channel_id=1, source_target_pairs={{0,240},{4,244},{8,248},{12,252},{16,224},{20,228},{24,232},{28,23... | collective-permute-start | bytes 1474568 | tf_op jit(solution)/shard_map/stash_0_0/ppermute | solution.py:178
  92.5 0.0 collective-permute-done.9
  92.5 1.5 collective-permute-start.10
  94.7 10.0 %psum.7 = f32[1]{0:T(128)} all-reduce(f32[1]{0:T(128)S(6)} %convert_element_type.3), channel_id=1, replica_groups=mesh['pipe'=16,'tensor'=4,'dp'=4] {'dp'}, use_global_device_ids=true, to_apply=%region_0.0 | all-reduce | flops 1 | bytes 8 | tf_op jit(solution)/shard_map/psum | solution.py:231
  105.3 1.3 constant_dynamic-slice_fusion.8
  106.6 0.0 collective-permute-done.7.refs_1_
  106.6 4.1 %collective-permute-start.4 = (bf16[3,1,64,512]{3,2,1,0:T(8,128)(2,1)S(1)}, bf16[3,1,64,512]{3,2,1,0:T(8,128)(2,1)S(1)}, u32[]{:S(2)}, u32[]{:S(2)}) collective-permute-start(bf16[3,1,64,512]{3,2,1,0:T(8,128)(2,1)S(1)} %get-tuple-element.44), channel_id=1, source_target_pairs={{0,252},{4,248},{8,244},{12,240},{16,236},{20,232},{24,228},{28,22... | collective-permute-start | bytes 589832 | tf_op jit(solution)/shard_map/stash_3_1/ppermute | solution.py:178
  110.7 14.9 %collective-permute-done.6.refs_0_ = bf16[3,1,64,1280]{3,2,1,0:T(8,128)(2,1)} collective-permute-done((bf16[3,1,64,1280]{3,2,1,0:T(8,128)(2,1)}, bf16[3,1,64,1280]{3,2,1,0:T(8,128)(2,1)}, u32[]{:S(2)}, u32[]{:S(2)}) %collective-permute-start.6) | collective-permute-done | bytes 491552 | tf_op jit(solution)/shard_map/stash_0_0/ppermute | solution.py:178
  125.6 3.6 %collective-permute-start.3 = (bf16[3,1,64,512]{3,2,1,0:T(8,128)(2,1)S(1)}, bf16[3,1,64,512]{3,2,1,0:T(8,128)(2,1)S(1)}, u32[]{:S(2)}, u32[]{:S(2)}) collective-permute-start(bf16[3,1,64,512]{3,2,1,0:T(8,128)(2,1)S(1)} %get-tuple-element.45), channel_id=1, source_target_pairs={{0,248},{4,252},{8,240},{12,244},{16,232},{20,236},{24,224},{28,22... | collective-permute-start | bytes 589832 | tf_op jit(solution)/shard_map/stash_2_1/ppermute | solution.py:178
  129.2 0.0 collective-permute-done.10.refs_4_
  129.2 1.0 collective-permute-start.2
  130.2 0.0 collective-permute-done.5.refs_5_.refs_4_
  130.2 3.2 %collective-permute-start.1 = (bf16[3,1,64,512]{3,2,1,0:T(8,128)(2,1)S(1)}, bf16[3,1,64,512]{3,2,1,0:T(8,128)(2,1)S(1)}, u32[]{:S(2)}, u32[]{:S(2)}) collective-permute-start(bf16[3,1,64,512]{3,2,1,0:T(8,128)(2,1)S(1)} %get-tuple-element.47), channel_id=1, source_target_pairs={{0,240},{4,244},{8,248},{12,252},{16,224},{20,228},{24,232},{28,23... | collective-permute-start | bytes 589832 | tf_op jit(solution)/shard_map/stash_0_1/ppermute | solution.py:178
  133.4 0.0 copy-done
  133.4 7.6 %shard_map.77 = (bf16[3,1,256,2048]{3,2,1,0:T(8,128)(2,1)}, f32[256,256]{1,0:T(8,128)S(1)}) custom-call(bf16[3,1,64,1280]{3,2,1,0:T(8,128)(2,1)} %collective-permute-done.6.refs_0_, bf16[3,1,64,1280]{3,2,1,0:T(8,128)(2,1)} %collective-permute-done.7.refs_1_, bf16[3,1,64,1280]{3,2,1,0:T(8,128)(2,1)S(1)} %collective-permute-done.8.refs_2_, ...), custom_call_target="tpu_custom_call" | custom-call | flops 838860800 | bytes 4587520 | tf_op jit(solution)/shard_map/pallas_call | solution.py:148
  141.0 0.0 collective-permute-done.11.refs_7_
  141.0 1.0 constant_dynamic-slice_fusion
  142.0 0.8 collective-permute-start.12
  142.8 1.0 constant_dynamic-slice_fusion.1
  143.9 0.0 collective-permute-done.12
  143.9 1.7 %collective-permute-start.16 = (bf16[3,1,64,256]{3,2,1,0:T(8,128)(2,1)S(1)}, bf16[3,1,64,256]{3,2,1,0:T(8,128)(2,1)S(1)}, u32[]{:S(2)}, u32[]{:S(2)}) collective-permute-start(bf16[3,1,64,256]{3,2,1,0:T(8,128)(2,1)S(1)} %get-tuple-element.36), channel_id=1, source_target_pairs={{0,252},{4,248},{8,244},{12,240},{16,236},{20,232},{24,228},{28,22... | collective-permute-start | bytes 294920 | tf_op jit(solution)/shard_map/stash_3_2/ppermute | solution.py:178
  145.6 0.0 collective-permute-done.4.refs_3_
  145.6 3.1 %collective-permute-start.15 = (bf16[3,1,64,256]{3,2,1,0:T(8,128)(2,1)S(1)}, bf16[3,1,64,256]{3,2,1,0:T(8,128)(2,1)S(1)}, u32[]{:S(2)}, u32[]{:S(2)}) collective-permute-start(bf16[3,1,64,256]{3,2,1,0:T(8,128)(2,1)S(1)} %get-tuple-element.38), channel_id=1, source_target_pairs={{0,248},{4,252},{8,240},{12,244},{16,232},{20,236},{24,224},{28,22... | collective-permute-start | bytes 294920 | tf_op jit(solution)/shard_map/stash_2_2/ppermute | solution.py:178
  148.7 0.0 collective-permute-done.3.refs_2_
  148.7 0.0 collective-permute-start.14
  148.7 0.0 collective-permute-done.2.refs_1_
  148.7 6.1 %collective-permute-start.13 = (bf16[3,1,64,256]{3,2,1,0:T(8,128)(2,1)S(1)}, bf16[3,1,64,256]{3,2,1,0:T(8,128)(2,1)S(1)}, u32[]{:S(2)}, u32[]{:S(2)}) collective-permute-start(bf16[3,1,64,256]{3,2,1,0:T(8,128)(2,1)S(1)} %get-tuple-element.40), channel_id=1, source_target_pairs={{0,240},{4,244},{8,248},{12,252},{16,224},{20,228},{24,232},{28,23... | collective-permute-start | bytes 294920 | tf_op jit(solution)/shard_map/stash_0_2/ppermute | solution.py:178
  154.8 0.0 collective-permute-done.1.refs_0_
  154.8 3.5 %shard_map.78 = (bf16[3,1,256,2048]{3,2,1,0:T(8,128)(2,1)}, bf16[1,256,2048]{2,1,0:T(8,128)(2,1)}) custom-call(bf16[3,1,64,512]{3,2,1,0:T(8,128)(2,1)S(1)} %collective-permute-done.1.refs_0_, bf16[3,1,64,512]{3,2,1,0:T(8,128)(2,1)S(1)} %collective-permute-done.2.refs_1_, ...), custom_call_target="tpu_custom_call", output_to_operand_aliasing={{0}: (8, {})} | custom-call | flops 335544320 | bytes 1835008 | tf_op jit(solution)/shard_map/pallas_call | solution.py:148
  158.3 0.7 collective-permute-start.17
  158.9 0.0 collective-permute-done.16.refs_3_
  159.0 0.0 collective-permute-done.15.refs_2_
  159.0 0.0 collective-permute-done.14.refs_1_
  159.0 0.0 collective-permute-done.13.refs_0_
  159.0 0.0 collective-permute-done.17.refs_4_
  159.0 2.1 %shard_map.79 = bf16[3,1,256,2048]{3,2,1,0:T(8,128)(2,1)} custom-call(bf16[3,1,64,256]{3,2,1,0:T(8,128)(2,1)S(1)} %collective-permute-done.13.refs_0_, bf16[3,1,64,256]{3,2,1,0:T(8,128)(2,1)S(1)} %collective-permute-done.14.refs_1_, bf16[3,1,64,256]{3,2,1,0:T(8,128)(2,1)S(1)} %collective-permute-done.15.refs_2_, ...), custom_call_target="tpu_custom_call", output_to_operand_aliasing={{}: (8, {})} | custom-call | flops 167772160 | bytes 917504 | tf_op jit(solution)/shard_map/pallas_call | solution.py:148
Async XLA Ops:
  2.5 41.9 %collective-permute-start = (bf16[3,1,64,1280]{3,2,1,0:T(8,128)(2,1)}, bf16[3,1,64,1280]{3,2,1,0:T(8,128)(2,1)S(1)}, u32[]{:S(2)}, u32[]{:S(2)}) collective-permute-start(bf16[3,1,64,1280]{3,2,1,0:T(8,128)(2,1)} %constant_dynamic-slice_fusion.12), channel_id=1, source_target_pairs={{0,252},{4,248},{8,244},{12,240},{16,236},{20,232},{24,228},{28,22... | collective-permute-start | bytes 1474568 | tf_op jit(solution)/shard_map/stash_3_0/ppermute | solution.py:178
  11.7 118.5 %collective-permute-start.5 = (bf16[1,256,2048]{2,1,0:T(8,128)(2,1)}, bf16[1,256,2048]{2,1,0:T(8,128)(2,1)S(1)}, u32[]{:S(2)}, u32[]{:S(2)}) collective-permute-start(bf16[1,256,2048]{2,1,0:T(8,128)(2,1)} %param.10), channel_id=1, source_target_pairs={{0,240},{16,0},{32,16},{48,32},{64,48},{80,64},{96,80},{112,96},{1... | collective-permute-start | bytes 3145736 | tf_op jit(solution)/shard_map/direct_grad/ppermute | solution.py:194
  14.1 119.3 %copy-start = (s32[1,256]{1,0:T(1,128)S(1)}, s32[1,256]{1,0:T(1,128)}, u32[]{:S(2)}) copy-start(s32[1,256]{1,0:T(1,128)} %refs_6_.1) | copy-start | bytes 3076
  14.1 73.5 %collective-permute-start.8 = (bf16[3,1,64,1280]{3,2,1,0:T(8,128)(2,1)S(1)}, bf16[3,1,64,1280]{3,2,1,0:T(8,128)(2,1)S(1)}, u32[]{:S(2)}, u32[]{:S(2)}) collective-permute-start(bf16[3,1,64,1280]{3,2,1,0:T(8,128)(2,1)S(1)} %get-tuple-element.41), channel_id=1, source_target_pairs={{0,248},{4,252},{8,240},{12,244},{16,232},{20,236},{24,224},{28,22... | collective-permute-start | bytes 1474568 | tf_op jit(solution)/shard_map/stash_2_0/ppermute | solution.py:178
  14.1 78.4 %collective-permute-start.9 = (bf16[3,1,64,1280]{3,2,1,0:T(8,128)(2,1)}, bf16[3,1,64,1280]{3,2,1,0:T(8,128)(2,1)}, u32[]{:S(2)}, u32[]{:S(2)}) collective-permute-start(bf16[3,1,64,1280]{3,2,1,0:T(8,128)(2,1)} %get-tuple-element.43), channel_id=1, source_target_pairs={{32,48},{36,52},{40,56},{44,60},{80,64},{84,68},{88,72},{92,76},{1... | collective-permute-start | bytes 1474568 | tf_op jit(solution)/shard_map/aside_0/ppermute | solution.py:178
  20.8 120.2 %collective-permute-start.11 = (bf16[1,256,2048]{2,1,0:T(8,128)(2,1)}, bf16[1,256,2048]{2,1,0:T(8,128)(2,1)S(1)}, u32[]{:S(2)}, u32[]{:S(2)}) collective-permute-start(bf16[1,256,2048]{2,1,0:T(8,128)(2,1)} %forward_heads.1), channel_id=1, source_target_pairs={{0,16},{16,32},{32,48},{48,64},{64,80},{80,96},{96,112},{112,128},... | collective-permute-start | bytes 3145736 | tf_op jit(solution)/shard_map/direct_out/ppermute | solution.py:194
  44.4 62.2 %collective-permute-start.7 = (bf16[3,1,64,1280]{3,2,1,0:T(8,128)(2,1)}, bf16[3,1,64,1280]{3,2,1,0:T(8,128)(2,1)}, u32[]{:S(2)}, u32[]{:S(2)}) collective-permute-start(bf16[3,1,64,1280]{3,2,1,0:T(8,128)(2,1)} %get-tuple-element.42), channel_id=1, source_target_pairs={{0,244},{4,240},{8,252},{12,248},{16,228},{20,224},{24,236},{28,23... | collective-permute-start | bytes 1474568 | tf_op jit(solution)/shard_map/stash_1_0/ppermute | solution.py:178
  87.6 38.0 %collective-permute-start.6 = (bf16[3,1,64,1280]{3,2,1,0:T(8,128)(2,1)}, bf16[3,1,64,1280]{3,2,1,0:T(8,128)(2,1)}, u32[]{:S(2)}, u32[]{:S(2)}) collective-permute-start(bf16[3,1,64,1280]{3,2,1,0:T(8,128)(2,1)} %get-tuple-element.43), channel_id=1, source_target_pairs={{0,240},{4,244},{8,248},{12,252},{16,224},{20,228},{24,232},{28,23... | collective-permute-start | bytes 1474568 | tf_op jit(solution)/shard_map/stash_0_0/ppermute | solution.py:178
  92.5 36.7 %collective-permute-start.10 = (bf16[3,1,64,1280]{3,2,1,0:T(8,128)(2,1)}, bf16[3,1,64,1280]{3,2,1,0:T(8,128)(2,1)}, u32[]{:S(2)}, u32[]{:S(2)}) collective-permute-start(bf16[3,1,64,1280]{3,2,1,0:T(8,128)(2,1)} %collective-permute-done.9), channel_id=1, source_target_pairs={{48,208},{52,212},{56,216},{60,220},{64,160},{68,164},{72,168},{76... | collective-permute-start | bytes 1474568 | tf_op jit(solution)/shard_map/onward_0/ppermute | solution.py:178
  106.6 39.0 %collective-permute-start.4 = (bf16[3,1,64,512]{3,2,1,0:T(8,128)(2,1)S(1)}, bf16[3,1,64,512]{3,2,1,0:T(8,128)(2,1)S(1)}, u32[]{:S(2)}, u32[]{:S(2)}) collective-permute-start(bf16[3,1,64,512]{3,2,1,0:T(8,128)(2,1)S(1)} %get-tuple-element.44), channel_id=1, source_target_pairs={{0,252},{4,248},{8,244},{12,240},{16,236},{20,232},{24,228},{28,22... | collective-permute-start | bytes 589832 | tf_op jit(solution)/shard_map/stash_3_1/ppermute | solution.py:178
  125.6 23.1 %collective-permute-start.3 = (bf16[3,1,64,512]{3,2,1,0:T(8,128)(2,1)S(1)}, bf16[3,1,64,512]{3,2,1,0:T(8,128)(2,1)S(1)}, u32[]{:S(2)}, u32[]{:S(2)}) collective-permute-start(bf16[3,1,64,512]{3,2,1,0:T(8,128)(2,1)S(1)} %get-tuple-element.45), channel_id=1, source_target_pairs={{0,248},{4,252},{8,240},{12,244},{16,232},{20,236},{24,224},{28,22... | collective-permute-start | bytes 589832 | tf_op jit(solution)/shard_map/stash_2_1/ppermute | solution.py:178
  129.2 19.5 %collective-permute-start.2 = (bf16[3,1,64,512]{3,2,1,0:T(8,128)(2,1)S(1)}, bf16[3,1,64,512]{3,2,1,0:T(8,128)(2,1)S(1)}, u32[]{:S(2)}, u32[]{:S(2)}) collective-permute-start(bf16[3,1,64,512]{3,2,1,0:T(8,128)(2,1)S(1)} %get-tuple-element.46), channel_id=1, source_target_pairs={{0,244},{4,240},{8,252},{12,248},{16,228},{20,224},{24,236},{28,23... | collective-permute-start | bytes 589832 | tf_op jit(solution)/shard_map/stash_1_1/ppermute | solution.py:178
  130.2 24.6 %collective-permute-start.1 = (bf16[3,1,64,512]{3,2,1,0:T(8,128)(2,1)S(1)}, bf16[3,1,64,512]{3,2,1,0:T(8,128)(2,1)S(1)}, u32[]{:S(2)}, u32[]{:S(2)}) collective-permute-start(bf16[3,1,64,512]{3,2,1,0:T(8,128)(2,1)S(1)} %get-tuple-element.47), channel_id=1, source_target_pairs={{0,240},{4,244},{8,248},{12,252},{16,224},{20,228},{24,232},{28,23... | collective-permute-start | bytes 589832 | tf_op jit(solution)/shard_map/stash_0_1/ppermute | solution.py:178
  142.0 1.9 %collective-permute-start.12 = (bf16[3,1,64,256]{3,2,1,0:T(8,128)(2,1)S(1)}, bf16[3,1,64,256]{3,2,1,0:T(8,128)(2,1)S(1)}, u32[]{:S(2)}, u32[]{:S(2)}) collective-permute-start(bf16[3,1,64,256]{3,2,1,0:T(8,128)(2,1)S(1)} %get-tuple-element.37), channel_id=1, source_target_pairs={{208,192},{212,196},{216,200},{220,204},{209,193},{213,197},{217,2... | collective-permute-start | bytes 294920 | tf_op jit(solution)/shard_map/aside_2/ppermute | solution.py:178
  143.9 15.1 %collective-permute-start.16 = (bf16[3,1,64,256]{3,2,1,0:T(8,128)(2,1)S(1)}, bf16[3,1,64,256]{3,2,1,0:T(8,128)(2,1)S(1)}, u32[]{:S(2)}, u32[]{:S(2)}) collective-permute-start(bf16[3,1,64,256]{3,2,1,0:T(8,128)(2,1)S(1)} %get-tuple-element.36), channel_id=1, source_target_pairs={{0,252},{4,248},{8,244},{12,240},{16,236},{20,232},{24,228},{28,22... | collective-permute-start | bytes 294920 | tf_op jit(solution)/shard_map/stash_3_2/ppermute | solution.py:178
  145.6 13.4 %collective-permute-start.15 = (bf16[3,1,64,256]{3,2,1,0:T(8,128)(2,1)S(1)}, bf16[3,1,64,256]{3,2,1,0:T(8,128)(2,1)S(1)}, u32[]{:S(2)}, u32[]{:S(2)}) collective-permute-start(bf16[3,1,64,256]{3,2,1,0:T(8,128)(2,1)S(1)} %get-tuple-element.38), channel_id=1, source_target_pairs={{0,248},{4,252},{8,240},{12,244},{16,232},{20,236},{24,224},{28,22... | collective-permute-start | bytes 294920 | tf_op jit(solution)/shard_map/stash_2_2/ppermute | solution.py:178
  148.7 10.3 %collective-permute-start.14 = (bf16[3,1,64,256]{3,2,1,0:T(8,128)(2,1)S(1)}, bf16[3,1,64,256]{3,2,1,0:T(8,128)(2,1)S(1)}, u32[]{:S(2)}, u32[]{:S(2)}) collective-permute-start(bf16[3,1,64,256]{3,2,1,0:T(8,128)(2,1)S(1)} %get-tuple-element.39), channel_id=1, source_target_pairs={{0,244},{4,240},{8,252},{12,248},{16,228},{20,224},{24,236},{28,23... | collective-permute-start | bytes 294920 | tf_op jit(solution)/shard_map/stash_1_2/ppermute | solution.py:178
  148.7 10.3 %collective-permute-start.13 = (bf16[3,1,64,256]{3,2,1,0:T(8,128)(2,1)S(1)}, bf16[3,1,64,256]{3,2,1,0:T(8,128)(2,1)S(1)}, u32[]{:S(2)}, u32[]{:S(2)}) collective-permute-start(bf16[3,1,64,256]{3,2,1,0:T(8,128)(2,1)S(1)} %get-tuple-element.40), channel_id=1, source_target_pairs={{0,240},{4,244},{8,248},{12,252},{16,224},{20,228},{24,232},{28,23... | collective-permute-start | bytes 294920 | tf_op jit(solution)/shard_map/stash_0_2/ppermute | solution.py:178
  158.3 0.7 collective-permute-start.17

commit v19 on v18

--- a/solution.py
+++ b/solution.py
@@ -10,7 +10,7 @@
 
 HEAD_DIM = 128
 FORWARD_STEPS = 2
-CHUNKS = ((0, 10), (12, 4), (10, 2))
+CHUNKS = ((0, 10), (10, 5), (15, 1))
 DETOUR = (0, 10)
 SCALE = HEAD_DIM ** (-0.5)
 EXPONENT = SCALE * math.log2(math.e)

time: 162 us -> 165 us (1.019)
  waiting for transfers between devices: 80.2 us -> 84.3 us
    ppermute x16, waiting for transfers between devices: 80.2 us -> 84.3 us  [fetched(): return lax.ppermute(piece, AXES, pairs)]
  transfers between devices with their start and end apart: 18 -> 18, of which waited for: 3 -> 3; matrix products, arithmetic and copies ran while one was open for 4% -> 3% of each run, Pallas kernels for 10% -> 10%
where the time goes in v19:
time: 165 us
  waiting for transfers between devices  84.3 us (51%)
  starting transfers between devices  42.9 us (26%)
  Pallas kernels  18.3 us (11%)
  blocking collectives  10 us (6%)
  local copies, waits for them, and re-layouts  7.38 us (4%)
  between operations  2.05 us (1%)
    ppermute x16, waiting for transfers between devices, fetched(): return lax.ppermute(piece, AXES, pairs)  84.3 us
    ppermute x16, starting transfers between devices, fetched(): return lax.ppermute(piece, AXES, pairs)  41.5 us
    pallas_call x3, Pallas kernels, backward(): pl.pallas_call(functools.partial(backward_kernel, parts, around_from, goe...  13.1 us
    psum x1, blocking collectives, on_device(): token_total = lax.psum(tokens, 'dp')  10 us
    dynamic_slice x5, local copies, waits for them, and re-layouts, cut(): return lax.dynamic_slice_in_dim(whole, start, heads * HEAD_DIM, axis=3)  7.38 us
    pallas_call x1, Pallas kernels, forward(): pl.pallas_call(forward_kernel, grid=(FORWARD_STEPS,), in_specs=[pl.BlockS...  5.18 us
  transfers between devices with their start and end apart: 18, of which 3 were waited for; matrix products, arithmetic and copies ran while one was open for 3% of the time, Pallas kernels for 10%

profile of v19, /device:TPU:1, one launch (start us, length us, event | category | flops | bytes accessed | tf_op | source)
XLA Modules:
  0.0 165.0 jit_solution(8161642468606055764)
XLA Ops:
  0.6 1.9 %constant_dynamic-slice_fusion.12 = bf16[3,1,64,1280]{3,2,1,0:T(8,128)(2,1)} fusion(bf16[3,1,64,8192]{3,2,1,0:T(8,128)(2,1)} %param.8, s32[]{:T(128)S(6)} %select_n.38), kind=kLoop, calls=%fused_computation.12 | loop fusion | bytes 983044 | tf_op jit(solution)/shard_map/dynamic_slice | solution.py:204
  2.5 9.2 %collective-permute-start = (bf16[3,1,64,1280]{3,2,1,0:T(8,128)(2,1)}, bf16[3,1,64,1280]{3,2,1,0:T(8,128)(2,1)S(1)}, u32[]{:S(2)}, u32[]{:S(2)}) collective-permute-start(bf16[3,1,64,1280]{3,2,1,0:T(8,128)(2,1)} %constant_dynamic-slice_fusion.12), channel_id=1, source_target_pairs={{0,252},{4,248},{8,244},{12,240},{16,236},{20,232},{24,228},{28,22... | collective-permute-start | bytes 1474568 | tf_op jit(solution)/shard_map/stash_3_0/ppermute | solution.py:178
  11.7 0.0 collective-permute-start.5
  11.7 2.4 %constant_dynamic-slice_fusion.5 = (bf16[3,1,64,1280]{3,2,1,0:T(8,128)(2,1)S(1)}, bf16[3,1,64,1280]{3,2,1,0:T(8,128)(2,1)}, bf16[3,1,64,1280]{3,2,1,0:T(8,128)(2,1)}) fusion(bf16[3,1,64,8192]{3,2,1,0:T(8,128)(2,1)} %param.8, s32[]{:T(128)S(6)} %select_n.45, s32[]{:T(128)S(6)} %select_n.44, s32[]{:T(128)S(6)} %select_n.43), kind=kLoop, calls=%fused_computation.5 | loop fusion | bytes 2949132 | tf_op jit(solution)/shard_map/stash_2_0/dynamic_slice | solution.py:204
  14.1 0.0 copy-start
  14.1 0.0 collective-permute-start.8
  14.1 1.6 collective-permute-start.9
  15.7 5.2 %forward_heads.1 = bf16[1,256,2048]{2,1,0:T(8,128)(2,1)} custom-call(bf16[3,1,256,2048]{3,2,1,0:T(8,128)(2,1)} %qkv_ref.1, s32[1,256]{1,0:T(1,128)} %segment_ref.1), custom_call_target="tpu_custom_call" | custom-call | flops 536870912 | bytes 4194304 | tf_op jit(solution)/shard_map/forward_heads/pallas_call | solution.py:55
  20.8 1.5 collective-permute-start.11
  22.3 22.1 %collective-permute-done.refs_3_ = bf16[3,1,64,1280]{3,2,1,0:T(8,128)(2,1)S(1)} collective-permute-done((bf16[3,1,64,1280]{3,2,1,0:T(8,128)(2,1)}, bf16[3,1,64,1280]{3,2,1,0:T(8,128)(2,1)S(1)}, u32[]{:S(2)}, u32[]{:S(2)}) %collective-permute-start) | collective-permute-done | bytes 491552 | tf_op jit(solution)/shard_map/stash_3_0/ppermute | solution.py:178
  44.4 0.0 collective-permute-start.7
  44.4 43.2 %collective-permute-done.8.refs_2_ = bf16[3,1,64,1280]{3,2,1,0:T(8,128)(2,1)S(1)} collective-permute-done((bf16[3,1,64,1280]{3,2,1,0:T(8,128)(2,1)S(1)}, bf16[3,1,64,1280]{3,2,1,0:T(8,128)(2,1)S(1)}, u32[]{:S(2)}, u32[]{:S(2)}) %collective-permute-start.8) | collective-permute-done | bytes 491552 | tf_op jit(solution)/shard_map/stash_2_0/ppermute | solution.py:178
  87.6 4.9 %collective-permute-start.6 = (bf16[3,1,64,1280]{3,2,1,0:T(8,128)(2,1)}, bf16[3,1,64,1280]{3,2,1,0:T(8,128)(2,1)}, u32[]{:S(2)}, u32[]{:S(2)}) collective-permute-start(bf16[3,1,64,1280]{3,2,1,0:T(8,128)(2,1)} %get-tuple-element.43), channel_id=1, source_target_pairs={{0,240},{4,244},{8,248},{12,252},{16,224},{20,228},{24,232},{28,23... | collective-permute-start | bytes 1474568 | tf_op jit(solution)/shard_map/stash_0_0/ppermute | solution.py:178
  92.5 0.0 collective-permute-done.9
  92.5 1.5 collective-permute-start.10
  94.7 10.0 %psum.7 = f32[1]{0:T(128)} all-reduce(f32[1]{0:T(128)S(6)} %convert_element_type.3), channel_id=1, replica_groups=mesh['pipe'=16,'tensor'=4,'dp'=4] {'dp'}, use_global_device_ids=true, to_apply=%region_0.0 | all-reduce | flops 1 | bytes 8 | tf_op jit(solution)/shard_map/psum | solution.py:231
  105.3 1.4 constant_dynamic-slice_fusion.8
  106.7 0.0 collective-permute-done.7.refs_1_
  106.7 4.1 %collective-permute-start.4 = (bf16[3,1,64,640]{3,2,1,0:T(8,128)(2,1)S(1)}, bf16[3,1,64,640]{3,2,1,0:T(8,128)(2,1)S(1)}, u32[]{:S(2)}, u32[]{:S(2)}) collective-permute-start(bf16[3,1,64,640]{3,2,1,0:T(8,128)(2,1)S(1)} %get-tuple-element.44), channel_id=1, source_target_pairs={{0,252},{4,248},{8,244},{12,240},{16,236},{20,232},{24,228},{28,22... | collective-permute-start | bytes 737288 | tf_op jit(solution)/shard_map/stash_3_1/ppermute | solution.py:178
  110.8 19.0 %collective-permute-done.6.refs_0_ = bf16[3,1,64,1280]{3,2,1,0:T(8,128)(2,1)} collective-permute-done((bf16[3,1,64,1280]{3,2,1,0:T(8,128)(2,1)}, bf16[3,1,64,1280]{3,2,1,0:T(8,128)(2,1)}, u32[]{:S(2)}, u32[]{:S(2)}) %collective-permute-start.6) | collective-permute-done | bytes 491552 | tf_op jit(solution)/shard_map/stash_0_0/ppermute | solution.py:178
  129.8 3.7 %collective-permute-start.3 = (bf16[3,1,64,640]{3,2,1,0:T(8,128)(2,1)S(1)}, bf16[3,1,64,640]{3,2,1,0:T(8,128)(2,1)S(1)}, u32[]{:S(2)}, u32[]{:S(2)}) collective-permute-start(bf16[3,1,64,640]{3,2,1,0:T(8,128)(2,1)S(1)} %get-tuple-element.45), channel_id=1, source_target_pairs={{0,248},{4,252},{8,240},{12,244},{16,232},{20,236},{24,224},{28,22... | collective-permute-start | bytes 737288 | tf_op jit(solution)/shard_map/stash_2_1/ppermute | solution.py:178
  133.5 0.0 collective-permute-done.10.refs_4_
  133.5 1.0 collective-permute-start.2
  134.4 0.0 collective-permute-done.5.refs_5_.refs_4_
  134.4 3.2 %collective-permute-start.1 = (bf16[3,1,64,640]{3,2,1,0:T(8,128)(2,1)S(1)}, bf16[3,1,64,640]{3,2,1,0:T(8,128)(2,1)S(1)}, u32[]{:S(2)}, u32[]{:S(2)}) collective-permute-start(bf16[3,1,64,640]{3,2,1,0:T(8,128)(2,1)S(1)} %get-tuple-element.47), channel_id=1, source_target_pairs={{0,240},{4,244},{8,248},{12,252},{16,224},{20,228},{24,232},{28,23... | collective-permute-start | bytes 737288 | tf_op jit(solution)/shard_map/stash_0_1/ppermute | solution.py:178
  137.6 0.0 copy-done
  137.6 7.6 %shard_map.77 = (bf16[3,1,256,2048]{3,2,1,0:T(8,128)(2,1)}, f32[256,256]{1,0:T(8,128)S(1)}) custom-call(bf16[3,1,64,1280]{3,2,1,0:T(8,128)(2,1)} %collective-permute-done.6.refs_0_, bf16[3,1,64,1280]{3,2,1,0:T(8,128)(2,1)} %collective-permute-done.7.refs_1_, bf16[3,1,64,1280]{3,2,1,0:T(8,128)(2,1)S(1)} %collective-permute-done.8.refs_2_, ...), custom_call_target="tpu_custom_call" | custom-call | flops 838860800 | bytes 4587520 | tf_op jit(solution)/shard_map/pallas_call | solution.py:148
  145.2 0.0 collective-permute-done.11.refs_7_
  145.2 0.8 constant_dynamic-slice_fusion
  146.1 0.8 collective-permute-start.12
  146.9 0.9 constant_dynamic-slice_fusion.1
  147.8 0.0 collective-permute-done.12
  147.8 1.7 %collective-permute-start.16 = (bf16[3,1,64,128]{3,2,1,0:T(8,128)(2,1)S(1)}, bf16[3,1,64,128]{3,2,1,0:T(8,128)(2,1)S(1)}, u32[]{:S(2)}, u32[]{:S(2)}) collective-permute-start(bf16[3,1,64,128]{3,2,1,0:T(8,128)(2,1)S(1)} %get-tuple-element.36), channel_id=1, source_target_pairs={{0,252},{4,248},{8,244},{12,240},{16,236},{20,232},{24,228},{28,22... | collective-permute-start | bytes 147464 | tf_op jit(solution)/shard_map/stash_3_2/ppermute | solution.py:178
  149.5 0.0 collective-permute-done.4.refs_3_
  149.5 3.1 %collective-permute-start.15 = (bf16[3,1,64,128]{3,2,1,0:T(8,128)(2,1)S(1)}, bf16[3,1,64,128]{3,2,1,0:T(8,128)(2,1)S(1)}, u32[]{:S(2)}, u32[]{:S(2)}) collective-permute-start(bf16[3,1,64,128]{3,2,1,0:T(8,128)(2,1)S(1)} %get-tuple-element.38), channel_id=1, source_target_pairs={{0,248},{4,252},{8,240},{12,244},{16,232},{20,236},{24,224},{28,22... | collective-permute-start | bytes 147464 | tf_op jit(solution)/shard_map/stash_2_2/ppermute | solution.py:178
  152.6 0.0 collective-permute-done.3.refs_2_
  152.6 0.0 collective-permute-start.14
  152.6 0.0 collective-permute-done.2.refs_1_
  152.6 6.1 %collective-permute-start.13 = (bf16[3,1,64,128]{3,2,1,0:T(8,128)(2,1)S(1)}, bf16[3,1,64,128]{3,2,1,0:T(8,128)(2,1)S(1)}, u32[]{:S(2)}, u32[]{:S(2)}) collective-permute-start(bf16[3,1,64,128]{3,2,1,0:T(8,128)(2,1)S(1)} %get-tuple-element.40), channel_id=1, source_target_pairs={{0,240},{4,244},{8,248},{12,252},{16,224},{20,228},{24,232},{28,23... | collective-permute-start | bytes 147464 | tf_op jit(solution)/shard_map/stash_0_2/ppermute | solution.py:178
  158.7 0.0 collective-permute-done.1.refs_0_
  158.7 4.0 %shard_map.78 = (bf16[3,1,256,2048]{3,2,1,0:T(8,128)(2,1)}, bf16[1,256,2048]{2,1,0:T(8,128)(2,1)}) custom-call(bf16[3,1,64,640]{3,2,1,0:T(8,128)(2,1)S(1)} %collective-permute-done.1.refs_0_, bf16[3,1,64,640]{3,2,1,0:T(8,128)(2,1)S(1)} %collective-permute-done.2.refs_1_, ...), custom_call_target="tpu_custom_call", output_to_operand_aliasing={{0}: (8, {})} | custom-call | flops 419430400 | bytes 2293760 | tf_op jit(solution)/shard_map/pallas_call | solution.py:148
  162.7 0.7 collective-permute-start.17
  163.4 0.0 collective-permute-done.16.refs_3_
  163.4 0.0 collective-permute-done.15.refs_2_
  163.4 0.0 collective-permute-done.14.refs_1_
  163.4 0.0 collective-permute-done.13.refs_0_
  163.4 0.0 collective-permute-done.17.refs_4_
  163.4 1.5 shard_map.79
Async XLA Ops:
  2.5 41.9 %collective-permute-start = (bf16[3,1,64,1280]{3,2,1,0:T(8,128)(2,1)}, bf16[3,1,64,1280]{3,2,1,0:T(8,128)(2,1)S(1)}, u32[]{:S(2)}, u32[]{:S(2)}) collective-permute-start(bf16[3,1,64,1280]{3,2,1,0:T(8,128)(2,1)} %constant_dynamic-slice_fusion.12), channel_id=1, source_target_pairs={{0,252},{4,248},{8,244},{12,240},{16,236},{20,232},{24,228},{28,22... | collective-permute-start | bytes 1474568 | tf_op jit(solution)/shard_map/stash_3_0/ppermute | solution.py:178
  11.7 122.7 %collective-permute-start.5 = (bf16[1,256,2048]{2,1,0:T(8,128)(2,1)}, bf16[1,256,2048]{2,1,0:T(8,128)(2,1)S(1)}, u32[]{:S(2)}, u32[]{:S(2)}) collective-permute-start(bf16[1,256,2048]{2,1,0:T(8,128)(2,1)} %param.10), channel_id=1, source_target_pairs={{0,240},{16,0},{32,16},{48,32},{64,48},{80,64},{96,80},{112,96},{1... | collective-permute-start | bytes 3145736 | tf_op jit(solution)/shard_map/direct_grad/ppermute | solution.py:194
  14.1 123.6 %copy-start = (s32[1,256]{1,0:T(1,128)S(1)}, s32[1,256]{1,0:T(1,128)}, u32[]{:S(2)}) copy-start(s32[1,256]{1,0:T(1,128)} %refs_6_.1) | copy-start | bytes 3076
  14.1 73.5 %collective-permute-start.8 = (bf16[3,1,64,1280]{3,2,1,0:T(8,128)(2,1)S(1)}, bf16[3,1,64,1280]{3,2,1,0:T(8,128)(2,1)S(1)}, u32[]{:S(2)}, u32[]{:S(2)}) collective-permute-start(bf16[3,1,64,1280]{3,2,1,0:T(8,128)(2,1)S(1)} %get-tuple-element.41), channel_id=1, source_target_pairs={{0,248},{4,252},{8,240},{12,244},{16,232},{20,236},{24,224},{28,22... | collective-permute-start | bytes 1474568 | tf_op jit(solution)/shard_map/stash_2_0/ppermute | solution.py:178
  14.1 78.4 %collective-permute-start.9 = (bf16[3,1,64,1280]{3,2,1,0:T(8,128)(2,1)}, bf16[3,1,64,1280]{3,2,1,0:T(8,128)(2,1)}, u32[]{:S(2)}, u32[]{:S(2)}) collective-permute-start(bf16[3,1,64,1280]{3,2,1,0:T(8,128)(2,1)} %get-tuple-element.43), channel_id=1, source_target_pairs={{32,48},{36,52},{40,56},{44,60},{80,64},{84,68},{88,72},{92,76},{1... | collective-permute-start | bytes 1474568 | tf_op jit(solution)/shard_map/aside_0/ppermute | solution.py:178
  20.8 124.4 %collective-permute-start.11 = (bf16[1,256,2048]{2,1,0:T(8,128)(2,1)}, bf16[1,256,2048]{2,1,0:T(8,128)(2,1)S(1)}, u32[]{:S(2)}, u32[]{:S(2)}) collective-permute-start(bf16[1,256,2048]{2,1,0:T(8,128)(2,1)} %forward_heads.1), channel_id=1, source_target_pairs={{0,16},{16,32},{32,48},{48,64},{64,80},{80,96},{96,112},{112,128},... | collective-permute-start | bytes 3145736 | tf_op jit(solution)/shard_map/direct_out/ppermute | solution.py:194
  44.4 62.3 %collective-permute-start.7 = (bf16[3,1,64,1280]{3,2,1,0:T(8,128)(2,1)}, bf16[3,1,64,1280]{3,2,1,0:T(8,128)(2,1)}, u32[]{:S(2)}, u32[]{:S(2)}) collective-permute-start(bf16[3,1,64,1280]{3,2,1,0:T(8,128)(2,1)} %get-tuple-element.42), channel_id=1, source_target_pairs={{0,244},{4,240},{8,252},{12,248},{16,228},{20,224},{24,236},{28,23... | collective-permute-start | bytes 1474568 | tf_op jit(solution)/shard_map/stash_1_0/ppermute | solution.py:178
  87.6 42.2 %collective-permute-start.6 = (bf16[3,1,64,1280]{3,2,1,0:T(8,128)(2,1)}, bf16[3,1,64,1280]{3,2,1,0:T(8,128)(2,1)}, u32[]{:S(2)}, u32[]{:S(2)}) collective-permute-start(bf16[3,1,64,1280]{3,2,1,0:T(8,128)(2,1)} %get-tuple-element.43), channel_id=1, source_target_pairs={{0,240},{4,244},{8,248},{12,252},{16,224},{20,228},{24,232},{28,23... | collective-permute-start | bytes 1474568 | tf_op jit(solution)/shard_map/stash_0_0/ppermute | solution.py:178
  92.5 40.9 %collective-permute-start.10 = (bf16[3,1,64,1280]{3,2,1,0:T(8,128)(2,1)}, bf16[3,1,64,1280]{3,2,1,0:T(8,128)(2,1)}, u32[]{:S(2)}, u32[]{:S(2)}) collective-permute-start(bf16[3,1,64,1280]{3,2,1,0:T(8,128)(2,1)} %collective-permute-done.9), channel_id=1, source_target_pairs={{48,208},{52,212},{56,216},{60,220},{64,160},{68,164},{72,168},{76... | collective-permute-start | bytes 1474568 | tf_op jit(solution)/shard_map/onward_0/ppermute | solution.py:178
  106.7 42.8 %collective-permute-start.4 = (bf16[3,1,64,640]{3,2,1,0:T(8,128)(2,1)S(1)}, bf16[3,1,64,640]{3,2,1,0:T(8,128)(2,1)S(1)}, u32[]{:S(2)}, u32[]{:S(2)}) collective-permute-start(bf16[3,1,64,640]{3,2,1,0:T(8,128)(2,1)S(1)} %get-tuple-element.44), channel_id=1, source_target_pairs={{0,252},{4,248},{8,244},{12,240},{16,236},{20,232},{24,228},{28,22... | collective-permute-start | bytes 737288 | tf_op jit(solution)/shard_map/stash_3_1/ppermute | solution.py:178
  129.8 22.8 %collective-permute-start.3 = (bf16[3,1,64,640]{3,2,1,0:T(8,128)(2,1)S(1)}, bf16[3,1,64,640]{3,2,1,0:T(8,128)(2,1)S(1)}, u32[]{:S(2)}, u32[]{:S(2)}) collective-permute-start(bf16[3,1,64,640]{3,2,1,0:T(8,128)(2,1)S(1)} %get-tuple-element.45), channel_id=1, source_target_pairs={{0,248},{4,252},{8,240},{12,244},{16,232},{20,236},{24,224},{28,22... | collective-permute-start | bytes 737288 | tf_op jit(solution)/shard_map/stash_2_1/ppermute | solution.py:178
  133.5 19.2 %collective-permute-start.2 = (bf16[3,1,64,640]{3,2,1,0:T(8,128)(2,1)S(1)}, bf16[3,1,64,640]{3,2,1,0:T(8,128)(2,1)S(1)}, u32[]{:S(2)}, u32[]{:S(2)}) collective-permute-start(bf16[3,1,64,640]{3,2,1,0:T(8,128)(2,1)S(1)} %get-tuple-element.46), channel_id=1, source_target_pairs={{0,244},{4,240},{8,252},{12,248},{16,228},{20,224},{24,236},{28,23... | collective-permute-start | bytes 737288 | tf_op jit(solution)/shard_map/stash_1_1/ppermute | solution.py:178
  134.4 24.3 %collective-permute-start.1 = (bf16[3,1,64,640]{3,2,1,0:T(8,128)(2,1)S(1)}, bf16[3,1,64,640]{3,2,1,0:T(8,128)(2,1)S(1)}, u32[]{:S(2)}, u32[]{:S(2)}) collective-permute-start(bf16[3,1,64,640]{3,2,1,0:T(8,128)(2,1)S(1)} %get-tuple-element.47), channel_id=1, source_target_pairs={{0,240},{4,244},{8,248},{12,252},{16,224},{20,228},{24,232},{28,23... | collective-permute-start | bytes 737288 | tf_op jit(solution)/shard_map/stash_0_1/ppermute | solution.py:178
  146.1 1.7 %collective-permute-start.12 = (bf16[3,1,64,128]{3,2,1,0:T(8,128)(2,1)S(1)}, bf16[3,1,64,128]{3,2,1,0:T(8,128)(2,1)S(1)}, u32[]{:S(2)}, u32[]{:S(2)}) collective-permute-start(bf16[3,1,64,128]{3,2,1,0:T(8,128)(2,1)S(1)} %get-tuple-element.37), channel_id=1, source_target_pairs={{208,192},{212,196},{216,200},{220,204},{209,193},{213,197},{217,2... | collective-permute-start | bytes 147464 | tf_op jit(solution)/shard_map/aside_2/ppermute | solution.py:178
  147.8 15.6 %collective-permute-start.16 = (bf16[3,1,64,128]{3,2,1,0:T(8,128)(2,1)S(1)}, bf16[3,1,64,128]{3,2,1,0:T(8,128)(2,1)S(1)}, u32[]{:S(2)}, u32[]{:S(2)}) collective-permute-start(bf16[3,1,64,128]{3,2,1,0:T(8,128)(2,1)S(1)} %get-tuple-element.36), channel_id=1, source_target_pairs={{0,252},{4,248},{8,244},{12,240},{16,236},{20,232},{24,228},{28,22... | collective-permute-start | bytes 147464 | tf_op jit(solution)/shard_map/stash_3_2/ppermute | solution.py:178
  149.5 13.9 %collective-permute-start.15 = (bf16[3,1,64,128]{3,2,1,0:T(8,128)(2,1)S(1)}, bf16[3,1,64,128]{3,2,1,0:T(8,128)(2,1)S(1)}, u32[]{:S(2)}, u32[]{:S(2)}) collective-permute-start(bf16[3,1,64,128]{3,2,1,0:T(8,128)(2,1)S(1)} %get-tuple-element.38), channel_id=1, source_target_pairs={{0,248},{4,252},{8,240},{12,244},{16,232},{20,236},{24,224},{28,22... | collective-permute-start | bytes 147464 | tf_op jit(solution)/shard_map/stash_2_2/ppermute | solution.py:178
  152.6 10.8 %collective-permute-start.14 = (bf16[3,1,64,128]{3,2,1,0:T(8,128)(2,1)S(1)}, bf16[3,1,64,128]{3,2,1,0:T(8,128)(2,1)S(1)}, u32[]{:S(2)}, u32[]{:S(2)}) collective-permute-start(bf16[3,1,64,128]{3,2,1,0:T(8,128)(2,1)S(1)} %get-tuple-element.39), channel_id=1, source_target_pairs={{0,244},{4,240},{8,252},{12,248},{16,228},{20,224},{24,236},{28,23... | collective-permute-start | bytes 147464 | tf_op jit(solution)/shard_map/stash_1_2/ppermute | solution.py:178
  152.6 10.8 %collective-permute-start.13 = (bf16[3,1,64,128]{3,2,1,0:T(8,128)(2,1)S(1)}, bf16[3,1,64,128]{3,2,1,0:T(8,128)(2,1)S(1)}, u32[]{:S(2)}, u32[]{:S(2)}) collective-permute-start(bf16[3,1,64,128]{3,2,1,0:T(8,128)(2,1)S(1)} %get-tuple-element.40), channel_id=1, source_target_pairs={{0,240},{4,244},{8,248},{12,252},{16,224},{20,228},{24,232},{28,23... | collective-permute-start | bytes 147464 | tf_op jit(solution)/shard_map/stash_0_2/ppermute | solution.py:178
  162.7 0.7 collective-permute-start.17
